TPU v7x, 32 devices: a whole 2x2x4 slice. The times are simulated.
32 devices in a mesh: group: 4 (over x, core), seq: 8 (over z, y).
Axes of the slice: x: 2, y: 2, z: 4, core: 2. Of those that a mesh axis runs over, the one named last changes fastest.
Arguments:
- source_short: bfloat16 [128, 128, 512], P(('group', 'seq')), may hold values from -6 to 6
- target_short: bfloat16 [128, 128, 512], P(('group', 'seq')), may hold values from -6 to 6
- source_segment: int32 [128, 128], P(('group', 'seq')), may hold values from 0 to 7, never falling along the last dimension, each value on 1 to 32 neighbouring positions
- target_segment: int32 [128, 128], P(('group', 'seq')), may hold values from 0 to 7, never falling along the last dimension, each value on 1 to 32 neighbouring positions
- source_long: bfloat16 [8, 1024, 512], P('group', 'seq'), may hold values from -6 to 6
- target_long: bfloat16 [8, 1024, 512], P('group', 'seq'), may hold values from -6 to 6
- source_length: int32 [8], P('group'), may hold values from 1 to 1024, as said below
- target_length: int32 [8], P('group'), may hold values from 1 to 1024, as said below
- cotangent_short: bfloat16 [128, 128, 512], P(('group', 'seq')), may hold values from -6 to 6
- cotangent_long: bfloat16 [8, 1024, 512], P('group', 'seq'), may hold values from -6 to 6
- encoder_project: bfloat16 [3, 512, 512], replicated, may hold values from -0.25 to 0.25
- encoder_output: bfloat16 [512, 512], replicated, may hold values from -1 to 1
- encoder_up: bfloat16 [512, 2048], replicated, may hold values from -0.25 to 0.25
- encoder_down: bfloat16 [2048, 512], replicated, may hold values from -0.125 to 0.125
- encoder_gain: float32 [2, 512], replicated, may hold values from 0.1 to 1.9
- encoder_bias: float32 [2, 512], replicated, may hold values from -3 to 3
- decoder_project: bfloat16 [3, 512, 512], replicated, may hold values from -0.25 to 0.25
- decoder_output: bfloat16 [512, 512], replicated, may hold values from -1 to 1
- cross_project: bfloat16 [3, 512, 512], replicated, may hold values from -0.25 to 0.25
- cross_output: bfloat16 [512, 512], replicated, may hold values from -1 to 1
- decoder_up: bfloat16 [512, 2048], replicated, may hold values from -0.25 to 0.25
- decoder_down: bfloat16 [2048, 512], replicated, may hold values from -0.125 to 0.125
- decoder_gain: float32 [3, 512], replicated, may hold values from 0.1 to 1.9
- decoder_bias: float32 [3, 512], replicated, may hold values from -3 to 3
Outputs:
- output_short: float32 [128, 128, 512], P(('group', 'seq'))
- output_long: float32 [8, 1024, 512], P('group', 'seq')
- grad_source_short: float32 [128, 128, 512], P(('group', 'seq'))
- grad_target_short: float32 [128, 128, 512], P(('group', 'seq'))
- grad_source_long: float32 [8, 1024, 512], P('group', 'seq')
- grad_target_long: float32 [8, 1024, 512], P('group', 'seq')
- grad_encoder_project: float32 [3, 512, 512], replicated
- grad_encoder_output: float32 [512, 512], replicated
- grad_encoder_up: float32 [512, 2048], replicated
- grad_encoder_down: float32 [2048, 512], replicated
- grad_encoder_gain: float32 [2, 512], replicated
- grad_encoder_bias: float32 [2, 512], replicated
- grad_decoder_project: float32 [3, 512, 512], replicated
- grad_decoder_output: float32 [512, 512], replicated
- grad_cross_project: float32 [3, 512, 512], replicated
- grad_cross_output: float32 [512, 512], replicated
- grad_decoder_up: float32 [512, 2048], replicated
- grad_decoder_down: float32 [2048, 512], replicated
- grad_decoder_gain: float32 [3, 512], replicated
- grad_decoder_bias: float32 [3, 512], replicated
Inputs may be any that keep to these rules, and one draw needn't show every extreme that they name: `source_length`: each group's 2 source sequences (and likewise its target sequences) include one of exactly 1024 tokens; the others are shorter, most much shorter. `target_length`: each group's 2 target sequences include one of exactly 1024 tokens; the others are shorter, most much shorter. `source_segment`: every block holds each of the 8 sentence numbers, in rising runs of at most 32 positions. `target_segment`: as for source_segment.
All inputs are finite; a program needn't handle non-finite values.
Results may differ from a plain program's by a relative error of at most 0.04.
Values may be sent and summed in bfloat16 or wider, within the bound.
No kernel may reach another device: no remote copies, remote signals or barrier semaphores. Data moves between devices by JAX's collectives and lax.ppermute only.
A program may use at most 448 MiB of HBM per device.

v0:
```python
import jax
import jax.numpy as jnp
from jax import lax
from jax.sharding import PartitionSpec as P

HEADS = 8
HEAD_DIM = 64


FLOOR_SCORE = -1e30
EPSILON = 1e-05


def split_heads(matrix):
    return matrix.reshape(matrix.shape[0], matrix.shape[1], HEADS, HEAD_DIM)


def join_heads(tensor):
    return jnp.transpose(tensor, (0, 2, 1, 3)).reshape(
        tensor.shape[0], tensor.shape[2], HEADS * HEAD_DIM
    )


def rows_times(rows, matrix):
    return jnp.einsum("bsd,de->bse", rows, matrix, preferred_element_type=jnp.float32)


def rows_times_transposed(rows, matrix):
    return jnp.einsum("bse,de->bsd", rows, matrix, preferred_element_type=jnp.float32)


def outer_sum(left_rows, right_rows):
    return jnp.einsum("bsd,bse->de", left_rows, right_rows, preferred_element_type=jnp.float32)


def masked_scores(queries, key_rows, allowed):
    scores = jnp.einsum(
        "bqhd,bkhd->bhqk",
        split_heads(queries),
        split_heads(key_rows),
        preferred_element_type=jnp.float32,
    )
    return jnp.where(allowed[:, None], scores, FLOOR_SCORE)


def forward_step(running, queries, key_rows, value_rows, allowed):
    row_max, totals, accumulated = running
    scores = masked_scores(queries, key_rows, allowed)
    new_max = jnp.maximum(row_max, jnp.max(scores, axis=-1))
    weights = jnp.where(allowed[:, None], jnp.exp(scores - new_max[..., None]), 0.0)
    totals = jnp.sum(weights, axis=-1)
    update = jnp.einsum(
        "bhqk,bkhd->bhqd",
        weights.astype(jnp.bfloat16),
        split_heads(value_rows),
        preferred_element_type=jnp.float32,
    )
    return (new_max, totals, update)


def score_grads(queries, key_rows, value_rows, grad_out, log_total, row_delta, allowed):
    scores = masked_scores(queries, key_rows, allowed)
    weights = jnp.where(allowed[:, None], jnp.exp(scores - log_total[..., None]), 0.0)
    grad_weights = jnp.einsum(
        "bqhd,bkhd->bhqk",
        split_heads(grad_out),
        split_heads(value_rows),
        preferred_element_type=jnp.float32,
    )
    grad_scores = (weights * (grad_weights - row_delta[..., None])).astype(jnp.bfloat16)
    return (weights.astype(jnp.bfloat16), grad_scores)


def query_term(queries, key_rows, value_rows, grad_out, log_total, row_delta, allowed):
    weights, grad_scores = score_grads(
        queries, key_rows, value_rows, grad_out, log_total, row_delta, allowed
    )
    query_part = jnp.einsum(
        "bhqk,bkhd->bqhd", grad_scores, split_heads(key_rows), preferred_element_type=jnp.float32
    )
    return query_part.reshape(queries.shape)


def key_value_terms(queries, key_rows, value_rows, grad_out, log_total, row_delta, allowed):
    weights, grad_scores = score_grads(
        queries, key_rows, value_rows, grad_out, log_total, row_delta, allowed
    )
    key_part = jnp.einsum(
        "bhqk,bqhd->bkhd", grad_scores, split_heads(queries), preferred_element_type=jnp.float32
    )
    value_part = jnp.einsum(
        "bhqk,bqhd->bkhd", weights, split_heads(grad_out), preferred_element_type=jnp.float32
    )
    return (key_part.reshape(key_rows.shape), value_part.reshape(key_rows.shape))


def backward_terms(queries, key_rows, value_rows, grad_out, log_total, row_delta, allowed):
    weights, grad_scores = score_grads(
        queries, key_rows, value_rows, grad_out, log_total, row_delta, allowed
    )
    query_part = jnp.einsum(
        "bhqk,bkhd->bqhd", grad_scores, split_heads(key_rows), preferred_element_type=jnp.float32
    )
    key_part = jnp.einsum(
        "bhqk,bqhd->bkhd", grad_scores, split_heads(queries), preferred_element_type=jnp.float32
    )
    value_part = jnp.einsum(
        "bhqk,bqhd->bkhd", weights, split_heads(grad_out), preferred_element_type=jnp.float32
    )
    return (
        query_part.reshape(queries.shape),
        key_part.reshape(key_rows.shape),
        value_part.reshape(key_rows.shape),
    )


def attend_forward(queries, key_rows, value_rows, allowed_of, spread):
    batch_size, row_count, _ = queries.shape
    start_state = (
        jnp.full((batch_size, HEADS, row_count), FLOOR_SCORE, jnp.float32),
        jnp.zeros((batch_size, HEADS, row_count), jnp.float32),
        jnp.zeros((batch_size, HEADS, row_count, HEAD_DIM), jnp.float32),
    )
    kept = (key_rows, value_rows)
    if not spread:
        final_state = forward_step(
            start_state,
            queries,
            key_rows,
            value_rows,
            allowed_of(0, row_count, 0, key_rows.shape[1]),
        )
    else:
        query_start = lax.axis_index("seq") * row_count
        pieces = (
            lax.all_gather(key_rows, "seq", axis=1, tiled=True),
            lax.all_gather(value_rows, "seq", axis=1, tiled=True),
        )
        final_state = forward_step(
            start_state,
            queries,
            pieces[0],
            pieces[1],
            allowed_of(query_start, row_count, jnp.int32(0), pieces[0].shape[1]),
        )
    row_max, totals, accumulated = final_state
    return (join_heads(accumulated / totals[..., None]), row_max + jnp.log(totals), kept)


def attend_backward(
    queries, key_rows, value_rows, grad_out, outputs, log_total, allowed_of, spread
):
    batch_size, row_count, feature_count = queries.shape
    products = (grad_out.astype(jnp.float32) * outputs).reshape(
        batch_size, row_count, HEADS, HEAD_DIM
    )
    row_delta = jnp.transpose(jnp.sum(products, axis=-1), (0, 2, 1))
    if not spread:
        return backward_terms(
            queries,
            key_rows,
            value_rows,
            grad_out,
            log_total,
            row_delta,
            allowed_of(0, row_count, 0, row_count),
        )
    query_start = lax.axis_index("seq") * row_count
    pieces = (
        lax.all_gather(key_rows, "seq", axis=1, tiled=True),
        lax.all_gather(value_rows, "seq", axis=1, tiled=True),
    )
    grad_queries = query_term(
        queries,
        pieces[0],
        pieces[1],
        grad_out,
        log_total,
        row_delta,
        allowed_of(query_start, row_count, jnp.int32(0), pieces[0].shape[1]),
    )
    own_rows = (
        queries.astype(jnp.float32),
        grad_out.astype(jnp.float32),
        jnp.transpose(log_total, (0, 2, 1)),
        jnp.transpose(row_delta, (0, 2, 1)),
    )
    pieces = (
        lax.all_gather(own_rows[0], "seq", axis=1, tiled=True),
        lax.all_gather(own_rows[1], "seq", axis=1, tiled=True),
        lax.all_gather(own_rows[2], "seq", axis=1, tiled=True),
        lax.all_gather(own_rows[3], "seq", axis=1, tiled=True),
    )
    piece_queries = pieces[0].astype(jnp.bfloat16)
    piece_grads = pieces[1].astype(jnp.bfloat16)
    piece_total = jnp.transpose(pieces[2], (0, 2, 1))
    piece_delta = jnp.transpose(pieces[3], (0, 2, 1))
    key_part, value_part = key_value_terms(
        piece_queries,
        key_rows,
        value_rows,
        piece_grads,
        piece_total,
        piece_delta,
        allowed_of(jnp.int32(0), piece_queries.shape[1], query_start, row_count),
    )
    return (grad_queries, key_part, value_part)


def fixed_allowed(table):

    def allowed_of(query_start, query_count, key_start, key_count):
        return table

    return allowed_of


def length_allowed(lengths, causal):

    def allowed_of(query_start, query_count, key_start, key_count):
        key_index = key_start + jnp.arange(key_count, dtype=jnp.int32)
        allowed = key_index[None, None, :] < lengths[:, None, None]
        if causal:
            query_index = query_start + jnp.arange(query_count, dtype=jnp.int32)
            allowed = allowed & (key_index[None, None, :] <= query_index[None, :, None])
        return jnp.broadcast_to(allowed, (lengths.shape[0], query_count, key_count))

    return allowed_of


def norm_forward(residual, gain_row, bias_row):
    centred = residual - jnp.mean(residual, axis=-1, keepdims=True)
    inverse_std = lax.rsqrt(jnp.mean(centred * centred, axis=-1, keepdims=True) + EPSILON)
    normed = centred * inverse_std
    return (normed * gain_row + bias_row, (normed, inverse_std))


def norm_backward(upstream, stored, gain_row):
    normed, inverse_std = stored
    scaled = upstream * gain_row
    grad_residual = inverse_std * (
        scaled
        - jnp.mean(scaled, axis=-1, keepdims=True)
        - normed * jnp.mean(scaled * normed, axis=-1, keepdims=True)
    )
    return (grad_residual, jnp.sum(upstream * normed, axis=(0, 1)), jnp.sum(upstream, axis=(0, 1)))


def attention_forward(query_in, context_in, project, output_weight, allowed_of, spread):
    queries = (rows_times(query_in, project[0]) * HEAD_DIM ** (-0.5)).astype(jnp.bfloat16)
    key_rows = rows_times(context_in, project[1]).astype(jnp.bfloat16)
    value_rows = rows_times(context_in, project[2]).astype(jnp.bfloat16)
    outputs, log_total, kept = attend_forward(queries, key_rows, value_rows, allowed_of, spread)
    rounded = outputs.astype(jnp.bfloat16)
    return (
        rows_times(rounded, output_weight),
        (queries, key_rows, value_rows, outputs, rounded, log_total, kept),
    )


def attention_backward(
    upstream, query_in, context_in, project, output_weight, stored, allowed_of, spread
):
    queries, key_rows, value_rows, outputs, rounded, log_total, kept = stored
    branch_grad = upstream.astype(jnp.bfloat16)
    grad_output_weight = outer_sum(rounded, branch_grad)
    grad_out = rows_times_transposed(branch_grad, output_weight).astype(jnp.bfloat16)
    grad_queries, grad_keys, grad_values = attend_backward(
        queries, key_rows, value_rows, grad_out, outputs, log_total, allowed_of, spread
    )
    query_grad = grad_queries.astype(jnp.bfloat16) * HEAD_DIM ** (-0.5)
    key_grad = grad_keys.astype(jnp.bfloat16)
    value_grad = grad_values.astype(jnp.bfloat16)
    grad_project = jnp.stack(
        [
            outer_sum(query_in, query_grad),
            outer_sum(context_in, key_grad),
            outer_sum(context_in, value_grad),
        ]
    )
    grad_query_in = rows_times_transposed(query_grad, project[0])
    grad_context_in = rows_times_transposed(key_grad, project[1]) + rows_times_transposed(
        value_grad, project[2]
    )
    return (grad_query_in, grad_context_in, grad_project, grad_output_weight)


def ffn_forward(normed_in, up_weight, down_weight):
    rounded_in = normed_in.astype(jnp.bfloat16)
    hidden = rows_times(rounded_in, up_weight)
    active = jax.nn.silu(hidden).astype(jnp.bfloat16)
    return (rows_times(active, down_weight), (rounded_in, hidden, active))


def ffn_backward(upstream, stored, up_weight, down_weight):
    rounded_in, hidden, active = stored
    branch_grad = upstream.astype(jnp.bfloat16)
    grad_down = outer_sum(active, branch_grad)
    sigmoid = jax.nn.sigmoid(hidden)
    hidden_grad = (
        rows_times_transposed(branch_grad, down_weight) * sigmoid * (1.0 + hidden * (1.0 - sigmoid))
    ).astype(jnp.bfloat16)
    return (
        rows_times_transposed(hidden_grad, up_weight),
        outer_sum(rounded_in, hidden_grad),
        grad_down,
    )


def layer_forward(source, target, masks, spread, params):
    (
        encoder_project,
        encoder_output,
        encoder_up,
        encoder_down,
        encoder_gain,
        encoder_bias,
        decoder_project,
        decoder_output,
        cross_project,
        cross_output,
        decoder_up,
        decoder_down,
        decoder_gain,
        decoder_bias,
    ) = params
    encoder_mask, self_mask, cross_mask = masks
    branch_one, attend_one = attention_forward(
        source, source, encoder_project, encoder_output, encoder_mask, spread
    )
    first, norm_one = norm_forward(
        source.astype(jnp.float32) + branch_one, encoder_gain[0], encoder_bias[0]
    )
    branch_two, ffn_one = ffn_forward(first, encoder_up, encoder_down)
    encoded, norm_two = norm_forward(first + branch_two, encoder_gain[1], encoder_bias[1])
    encoded_low = encoded.astype(jnp.bfloat16)
    branch_three, attend_two = attention_forward(
        target, target, decoder_project, decoder_output, self_mask, spread
    )
    upper, norm_three = norm_forward(
        target.astype(jnp.float32) + branch_three, decoder_gain[0], decoder_bias[0]
    )
    upper_low = upper.astype(jnp.bfloat16)
    branch_four, attend_three = attention_forward(
        upper_low, encoded_low, cross_project, cross_output, cross_mask, spread
    )
    middle, norm_four = norm_forward(upper + branch_four, decoder_gain[1], decoder_bias[1])
    branch_five, ffn_two = ffn_forward(middle, decoder_up, decoder_down)
    final, norm_five = norm_forward(middle + branch_five, decoder_gain[2], decoder_bias[2])
    stored = (
        attend_one,
        norm_one,
        ffn_one,
        norm_two,
        encoded_low,
        attend_two,
        norm_three,
        upper_low,
        attend_three,
        norm_four,
        ffn_two,
        norm_five,
    )
    return (final, stored)


def layer_backward(cotangent, source, target, stored, masks, spread, params):
    (
        encoder_project,
        encoder_output,
        encoder_up,
        encoder_down,
        encoder_gain,
        encoder_bias,
        decoder_project,
        decoder_output,
        cross_project,
        cross_output,
        decoder_up,
        decoder_down,
        decoder_gain,
        decoder_bias,
    ) = params
    encoder_mask, self_mask, cross_mask = masks
    (
        attend_one,
        norm_one,
        ffn_one,
        norm_two,
        encoded_low,
        attend_two,
        norm_three,
        upper_low,
        attend_three,
        norm_four,
        ffn_two,
        norm_five,
    ) = stored
    upstream, gain_five, bias_five = norm_backward(
        cotangent.astype(jnp.float32), norm_five, decoder_gain[2]
    )
    grad_middle, grad_dec_up, grad_dec_down = ffn_backward(
        upstream, ffn_two, decoder_up, decoder_down
    )
    upstream, gain_four, bias_four = norm_backward(
        grad_middle + upstream, norm_four, decoder_gain[1]
    )
    grad_upper, grad_encoded, grad_cross_project, grad_cross_output = attention_backward(
        upstream,
        upper_low,
        encoded_low,
        cross_project,
        cross_output,
        attend_three,
        cross_mask,
        spread,
    )
    upstream, gain_three, bias_three = norm_backward(
        upstream + grad_upper, norm_three, decoder_gain[0]
    )
    query_side, context_side, grad_dec_project, grad_dec_output = attention_backward(
        upstream, target, target, decoder_project, decoder_output, attend_two, self_mask, spread
    )
    grad_target = upstream + query_side + context_side
    upstream, gain_two, bias_two = norm_backward(grad_encoded, norm_two, encoder_gain[1])
    grad_first, grad_enc_up, grad_enc_down = ffn_backward(
        upstream, ffn_one, encoder_up, encoder_down
    )
    upstream, gain_one, bias_one = norm_backward(grad_first + upstream, norm_one, encoder_gain[0])
    query_side, context_side, grad_enc_project, grad_enc_output = attention_backward(
        upstream, source, source, encoder_project, encoder_output, attend_one, encoder_mask, spread
    )
    grad_source = upstream + query_side + context_side
    grads = (
        grad_enc_project,
        grad_enc_output,
        grad_enc_up,
        grad_enc_down,
        jnp.stack([gain_one, gain_two]),
        jnp.stack([bias_one, bias_two]),
        grad_dec_project,
        grad_dec_output,
        grad_cross_project,
        grad_cross_output,
        grad_dec_up,
        grad_dec_down,
        jnp.stack([gain_three, gain_four, gain_five]),
        jnp.stack([bias_three, bias_four, bias_five]),
    )
    return (grad_source, grad_target, grads)


def shards(
    source_short,
    target_short,
    source_segment,
    target_segment,
    source_long,
    target_long,
    source_length,
    target_length,
    cotangent_short,
    cotangent_long,
    encoder_project,
    encoder_output,
    encoder_up,
    encoder_down,
    encoder_gain,
    encoder_bias,
    decoder_project,
    decoder_output,
    cross_project,
    cross_output,
    decoder_up,
    decoder_down,
    decoder_gain,
    decoder_bias,
):
    params = (
        encoder_project,
        encoder_output,
        encoder_up,
        encoder_down,
        encoder_gain,
        encoder_bias,
        decoder_project,
        decoder_output,
        cross_project,
        cross_output,
        decoder_up,
        decoder_down,
        decoder_gain,
        decoder_bias,
    )
    block_rows = source_segment.shape[1]
    causal = jnp.arange(block_rows)[:, None] >= jnp.arange(block_rows)[None, :]
    short_tables = (
        fixed_allowed(source_segment[:, :, None] == source_segment[:, None, :]),
        fixed_allowed((target_segment[:, :, None] == target_segment[:, None, :]) & causal[None]),
        fixed_allowed(target_segment[:, :, None] == source_segment[:, None, :]),
    )
    long_tables = (
        length_allowed(source_length, False),
        length_allowed(target_length, True),
        length_allowed(source_length, False),
    )
    final_short, stored_short = layer_forward(
        source_short, target_short, short_tables, False, params
    )
    final_long, stored_long = layer_forward(source_long, target_long, long_tables, True, params)
    source_grad_short, target_grad_short, grads_short = layer_backward(
        cotangent_short, source_short, target_short, stored_short, short_tables, False, params
    )
    source_grad_long, target_grad_long, grads_long = layer_backward(
        cotangent_long, source_long, target_long, stored_long, long_tables, True, params
    )
    local_grads = tuple(
        (short_term + long_term for short_term, long_term in zip(grads_short, grads_long))
    )
    summed = lax.psum(local_grads, ("group", "seq"))
    return (
        final_short,
        final_long,
        source_grad_short,
        target_grad_short,
        source_grad_long,
        target_grad_long,
    ) + tuple(summed)


def solution(mesh):
    in_specs = (
        P(("group", "seq"), None, None),
        P(("group", "seq"), None, None),
        P(("group", "seq"), None),
        P(("group", "seq"), None),
        P("group", "seq", None),
        P("group", "seq", None),
        P("group"),
        P("group"),
        P(("group", "seq"), None, None),
        P("group", "seq", None),
        P(),
        P(),
        P(),
        P(),
        P(),
        P(),
        P(),
        P(),
        P(),
        P(),
        P(),
        P(),
        P(),
        P(),
    )
    out_specs = (
        P(("group", "seq"), None, None),
        P("group", "seq", None),
        P(("group", "seq"), None, None),
        P(("group", "seq"), None, None),
        P("group", "seq", None),
        P("group", "seq", None),
        P(),
        P(),
        P(),
        P(),
        P(),
        P(),
        P(),
        P(),
        P(),
        P(),
        P(),
        P(),
        P(),
        P(),
    )
    return jax.shard_map(shards, mesh=mesh, in_specs=in_specs, out_specs=out_specs, check_vma=False)
```

profile of v0, /device:TPU:0, one launch (start us, length us, event | category | flops | bytes accessed | tf_op | source)
XLA Modules:
  0.0 1226.7 jit_solution(7167964118099449601)
XLA Ops:
  42.9 2.9 select_reduce_fusion.4
  50.8 4.2 fusion.83
  81.5 3.2 select_reduce_fusion.3
  90.8 2.6 fusion.97
  118.0 3.5 convolution_convert_fusion.16
  138.7 3.3 multiply_reduce_fusion.1
  143.9 2.7 multiply_reduce_fusion.2
  150.4 3.1 multiply_reduce_fusion.3
  164.5 2.8 multiply_convert_fusion.16
  182.0 3.7 multiply_convert_fusion.17
  185.7 4.0 copy.180
  189.7 3.0 select_reduce_fusion.1
  193.3 2.8 copy-done.2
  196.0 2.6 fusion.2
  198.7 4.0 copy.181
  202.7 6.0 fusion.202
  217.9 3.0 convolution_bitcast_fusion.20
  248.7 4.0 copy.175
  252.7 6.4 select_reduce_fusion.2
  263.7 3.9 copy.176
  267.6 5.6 fusion
  273.7 3.6 fusion.205
  283.8 34.2 %all_gather.75 = f32[2,1024,8]{1,2,0:T(8,128)} all-gather(f32[2,128,8]{1,2,0:T(8,128)S(1)} %bitcast_add_fusion.4), channel_id=1, replica_groups=mesh['group'=4,'seq'=8] {'seq'}, dimensions={1}, use_global_device_ids=true | all-gather | bytes 73728 | tf_op jit(solution)/shard_map/all_gather | solution.py:191
  318.0 31.1 %all_gather.71 = f32[2,1024,8]{1,2,0:T(8,128)S(1)} all-gather(f32[2,128,8]{1,2,0:T(8,128)S(1)} %bitcast_add_fusion.5), channel_id=1, replica_groups=mesh['group'=4,'seq'=8] {'seq'}, dimensions={1}, use_global_device_ids=true | all-gather | bytes 73728 | tf_op jit(solution)/shard_map/all_gather | solution.py:191
  349.1 4.0 copy.240
  353.1 6.3 fusion.409
  359.4 4.0 copy.228
  363.4 6.3 fusion.408
  369.7 3.9 copy.183
  373.6 3.0 select_reduce_fusion
  376.6 3.3 copy-done.4
  382.0 31.5 %all-gather.23.cloned.1.call-done = bf16[2,1024,512]{2,1,0:T(8,128)(2,1)} async-done(((bf16[2,128,512]{2,1,0:T(8,128)(2,1)}), bf16[2,1024,512]{2,1,0:T(8,128)(2,1)}) %all-gather.23.cloned.1.call-update) | async-done | bytes 2097168 | tf_op jit(solution)/shard_map/all_gather | solution.py:137
  413.5 3.9 copy.184
  417.4 5.9 fusion.199
  431.7 3.4 fusion.53
  443.8 8.5 fusion.164
  459.4 32.4 %all_gather.69 = f32[2,1024,8]{1,2,0:T(8,128)} all-gather(f32[2,128,8]{1,2,0:T(8,128)S(1)} %bitcast_reduce_fusion.5), channel_id=1, replica_groups=mesh['group'=4,'seq'=8] {'seq'}, dimensions={1}, use_global_device_ids=true | all-gather | bytes 73728 | tf_op jit(solution)/shard_map/all_gather | solution.py:192
  491.8 32.5 %all_gather.67 = f32[2,1024,8]{1,2,0:T(8,128)} all-gather(f32[2,128,8]{1,2,0:T(8,128)S(1)} %bitcast_add_fusion.6), channel_id=1, replica_groups=mesh['group'=4,'seq'=8] {'seq'}, dimensions={1}, use_global_device_ids=true | all-gather | bytes 73728 | tf_op jit(solution)/shard_map/all_gather | solution.py:191
  533.0 3.5 bitcast_add_fusion.1
  536.5 3.6 bitcast_add_fusion
  541.5 32.5 %all_gather.77 = f32[2,1024,8]{1,2,0:T(8,128)} all-gather(f32[2,128,8]{1,2,0:T(8,128)S(1)} %bitcast_reduce_fusion.3), channel_id=1, replica_groups=mesh['group'=4,'seq'=8] {'seq'}, dimensions={1}, use_global_device_ids=true | all-gather | bytes 73728 | tf_op jit(solution)/shard_map/all_gather | solution.py:192
  574.0 8.0 fusion.162
  583.4 3.2 copy.216
  586.6 4.7 fusion.407
  591.3 3.0 copy.218
  594.3 6.6 fusion.156
  601.0 9.1 fusion.147
  621.0 3.9 copy.242
  624.9 5.9 fusion.151
  632.1 9.0 fusion.144
  642.7 32.7 %all_gather.73 = f32[2,1024,8]{1,2,0:T(8,128)} all-gather(f32[2,128,8]{1,2,0:T(8,128)S(1)} %bitcast_reduce_fusion.4), channel_id=1, replica_groups=mesh['group'=4,'seq'=8] {'seq'}, dimensions={1}, use_global_device_ids=true | all-gather | bytes 73728 | tf_op jit(solution)/shard_map/all_gather | solution.py:192
  675.5 5.1 maximum_add_fusion.2
  683.1 8.4 fusion.163
  697.9 3.5 bitcast_add_fusion.3
  701.4 3.6 bitcast_add_fusion.2
  705.0 4.1 copy.230
  709.1 5.6 fusion.159
  716.7 9.8 fusion.146
  727.8 4.6 maximum_add_fusion
  743.0 39.5 %all-reduce = (f32[2,512]{1,0:T(2,128)}, f32[2,512]{1,0:T(2,128)}, f32[3,512]{1,0:T(4,128)}, f32[3,512]{1,0:T(4,128)}) all-reduce(f32[2,512]{1,0:T(2,128)S(1)} %maximum_add_fusion.5, f32[2,512]{1,0:T(2,128)S(1)} %maximum_add_fusion.6, f32[3,512]{1,0:T(4,128)S(1)} %maximum_add_fusion.3, ...), channel_id=1, replica_groups=mesh['group'=4,'seq'=8] {'group','seq'}, use_global_device_ids=true, to_apply=%region_66.67 | all-reduce | flops 5120 | bytes 40960 | tf_op jit(solution)/shard_map/psum | solution.py:520
  788.2 403.8 %all-reduce.4.cloned.1.call-done = (f32[3,512,512]{1,2,0:T(8,128)}, f32[512,512]{1,0:T(8,128)}, f32[512,2048]{1,0:T(8,128)}, f32[2048,512]{1,0:T(8,128)}, f32[3,...) async-done(((f32[3,512,512]{1,2,0:T(8,128)}, ...) | async-done | bytes 29360144 | tf_op jit(solution)/shard_map/psum | solution.py:520
  1192.0 3.5 copy.266
  1195.5 3.6 copy.267
  1200.1 4.8 copy.338
  (890 shorter events, 288.7 us)
Async XLA Ops:
  7.2 91.1 %copy-start = (bf16[512,2048]{1,0:T(8,128)(2,1)S(1)}, bf16[512,2048]{1,0:T(8,128)(2,1)}, u32[]{:S(2)}) copy-start(bf16[512,2048]{1,0:T(8,128)(2,1)} %param.44) | copy-start | bytes 6291460
  7.2 178.5 %all-gather.17.cloned.1.call-start = ((), (), s32[]{:S(2)}) async-start(), calls=%async_computation.2 | async-start | bytes 2359296 | tf_op jit(solution)/shard_map/all_gather | solution.py:136
  9.6 189.1 %all-gather.19.cloned.1.call-start = ((), (), s32[]{:S(2)}) async-start(), calls=%async_computation.3 | async-start | bytes 2359296 | tf_op jit(solution)/shard_map/all_gather | solution.py:137
  11.8 6.5 copy-start.113
  11.8 236.9 %all-gather.13.cloned.1.call-start = ((), (), s32[]{:S(2)}) async-start(), calls=%async_computation | async-start | bytes 2359296 | tf_op jit(solution)/shard_map/all_gather | solution.py:136
  14.0 249.7 %all-gather.15.cloned.1.call-start = ((), (), s32[]{:S(2)}) async-start(), calls=%async_computation.1 | async-start | bytes 2359296 | tf_op jit(solution)/shard_map/all_gather | solution.py:137
  16.1 6.9 copy-start.41
  16.1 333.0 %all-gather.33.cloned.1.call-start = ((), (), s32[]{:S(2)}) async-start(), calls=%async_computation.10 | async-start | bytes 2359296 | tf_op jit(solution)/shard_map/all_gather | solution.py:189
  18.3 341.1 %all-gather.29.cloned.1.call-start = ((), (), s32[]{:S(2)}) async-start(), calls=%async_computation.8 | async-start | bytes 2359296 | tf_op jit(solution)/shard_map/all_gather | solution.py:189
  20.4 7.1 copy-start.44
  20.4 349.3 %all-gather.21.cloned.1.call-start = ((), (), s32[]{:S(2)}) async-start(), calls=%async_computation.4 | async-start | bytes 2359296 | tf_op jit(solution)/shard_map/all_gather | solution.py:136
  33.5 28.2 %copy-start.209 = (f32[1,512]{1,0:T(1,128)}, f32[1,512]{1,0:T(1,128)S(1)}, u32[]{:S(2)}) copy-start(f32[1,512]{1,0:T(1,128)S(1)} %get-tuple-element.124) | copy-start | bytes 6148
  33.5 28.2 %copy-start.256 = (f32[1,512]{1,0:T(1,128)}, f32[1,512]{1,0:T(1,128)S(1)}, u32[]{:S(2)}) copy-start(f32[1,512]{1,0:T(1,128)S(1)} %get-tuple-element.126) | copy-start | bytes 6148
  38.9 6.9 copy-start.69
  63.2 9.6 copy-start.186
  98.0 10.5 copy-start.5
  98.0 10.5 copy-start.230
  98.3 10.2 copy-start.247
  189.7 6.4 copy-start.198
  202.7 6.0 copy-start.52
  202.7 6.0 copy-start.114
  217.7 195.8 %all-gather.23.cloned.1.call-start = ((), (), s32[]{:S(2)}) async-start(), calls=%async_computation.5 | async-start | bytes 2359296 | tf_op jit(solution)/shard_map/all_gather | solution.py:137
  231.8 6.2 copy-start.86
  232.7 9.2 copy-start.90
  233.9 9.4 copy-start.88
  248.6 334.8 %all-gather.25.cloned.1.call-start = ((), (), s32[]{:S(2)}) async-start(), calls=%async_computation.6 | async-start | bytes 2359296 | tf_op jit(solution)/shard_map/all_gather | solution.py:189
  252.7 10.0 copy-start.67
  267.6 6.1 copy-start.3
  267.6 6.1 copy-start.118
  273.7 5.4 copy-start.48
  283.7 307.6 %all-gather.27.cloned.1.call-start = ((), (), s32[]{:S(2)}) async-start(), calls=%async_computation.7 | async-start | bytes 2359296 | tf_op jit(solution)/shard_map/all_gather | solution.py:190
  417.4 5.9 copy-start.39
  436.9 6.9 copy-start.36
  454.8 166.2 %all-gather.35.cloned.1.call-start = ((), (), s32[]{:S(2)}) async-start(), calls=%async_computation.11 | async-start | bytes 2359296 | tf_op jit(solution)/shard_map/all_gather | solution.py:190
  455.1 73.0 %copy-start.32 = (f32[2,128,512]{2,1,0:T(8,128)}, f32[2,128,512]{2,1,0:T(8,128)S(1)}, u32[]{:S(2)}) copy-start(f32[2,128,512]{2,1,0:T(8,128)S(1)} %subtract_multiply_fusion.9) | copy-start | bytes 1572868
  455.1 71.8 %copy-start.55 = (f32[2,128,512]{2,1,0:T(8,128)S(1)}, f32[2,128,512]{2,1,0:T(8,128)}, u32[]{:S(2)}) copy-start(f32[2,128,512]{2,1,0:T(8,128)} %copy-done.54) | copy-start | bytes 1572868
  455.1 71.7 %copy-start.78 = (f32[2,128,8,64]{1,3,2,0:T(8,128)S(1)}, f32[2,128,8,64]{1,3,2,0:T(8,128)}, u32[]{:S(2)}) copy-start(f32[2,128,8,64]{1,3,2,0:T(8,128)} %copy-done.77) | copy-start | bytes 1572868
  459.4 67.5 %copy-start.93 = (f32[512,512]{1,0:T(8,128)S(1)}, f32[512,512]{1,0:T(8,128)}, u32[]{:S(2)}) copy-start(f32[512,512]{1,0:T(8,128)} %convolution_bitcast_fusion.12) | copy-start | bytes 3145732
  536.5 37.5 %copy-start.35 = (bf16[2,1024,512]{1,2,0:T(8,128)(2,1)S(1)}, bf16[2,1024,512]{1,2,0:T(8,128)(2,1)}, u32[]{:S(2)}) copy-start(bf16[2,1024,512]{1,2,0:T(8,128)(2,1)} %copy.175) | copy-start | bytes 6291460
  536.5 37.5 %copy-start.119 = (pred[2,128,1024]{2,1,0:T(8,128)(4,1)S(1)}, pred[2,128,1024]{2,1,0:T(8,128)(4,1)}, u32[]{:S(2)}) copy-start(pred[2,128,1024]{2,1,0:T(8,128)(4,1)} %broadcast_and_fusion.1) | copy-start | bytes 786436
  536.5 37.5 %copy-start.195 = (bf16[2,128,512]{1,2,0:T(8,128)(2,1)S(1)}, bf16[2,128,512]{1,2,0:T(8,128)(2,1)}, u32[]{:S(2)}) copy-start(bf16[2,128,512]{1,2,0:T(8,128)(2,1)} %copy.236) | copy-start | bytes 786436
  536.5 37.5 %copy-start.272 = (f32[2,8,128]{2,1,0:T(8,128)S(1)}, f32[2,8,128]{2,1,0:T(8,128)}, u32[]{:S(2)}) copy-start(f32[2,8,128]{2,1,0:T(8,128)} %log_add_fusion.3) | copy-start | bytes 24580
  540.2 164.8 %all-gather.31.cloned.1.call-start = ((), (), s32[]{:S(2)}) async-start(), calls=%async_computation.9 | async-start | bytes 2359296 | tf_op jit(solution)/shard_map/all_gather | solution.py:190
  594.3 6.6 copy-start.128
  594.3 6.6 copy-start.194
  594.3 6.6 copy-start.222
  600.9 9.6 copy-start.173
  601.0 9.1 copy-start.57
  601.0 9.5 copy-start.31
  601.0 9.5 copy-start.212
  601.0 9.5 copy-start.253
  601.0 9.5 copy-start.260
  620.9 571.1 %all-reduce.4.cloned.1.call-start = ((), (), s32[]{:S(2)}) async-start(), calls=%async_computation.12 | async-start | bytes 58720256 | tf_op jit(solution)/shard_map/psum | solution.py:520
  624.9 7.2 copy-start.193
  624.9 7.2 copy-start.221
  632.1 10.3 copy-start.141
  641.2 34.3 %copy-start.95 = (f32[1,512,512]{2,1,0:T(8,128)S(1)}, f32[1,512,512]{2,1,0:T(8,128)}, u32[]{:S(2)}) copy-start(f32[1,512,512]{2,1,0:T(8,128)} %convolution_bitcast_fusion.14) | copy-start | bytes 3145732
  683.1 8.4 copy-start.115
  683.1 9.7 copy-start.68
  709.1 7.6 copy-start.34
  709.1 7.6 copy-start.192
  726.5 5.9 copy-start.166
  740.9 41.6 %copy-start.59 = (bf16[3,512,512]{2,1,0:T(8,128)(2,1)S(1)}, bf16[3,512,512]{2,1,0:T(8,128)(2,1)}, u32[]{:S(2)}) copy-start(bf16[3,512,512]{2,1,0:T(8,128)(2,1)} %param.40) | copy-start | bytes 4718596
  742.5 43.0 %copy-start.161 = (bf16[2,8,64,128]{3,2,1,0:T(8,128)(2,1)S(1)}, bf16[2,8,64,128]{3,2,1,0:T(8,128)(2,1)}, u32[]{:S(2)}) copy-start(bf16[2,8,64,128]{3,2,1,0:T(8,128)(2,1)} %copy-done.160) | copy-start | bytes 786436
  (253 other events, 621.6 us)
Sparse Core Ops, SparseCore 0:
  10.2 51.9 all-gather.16
  64.4 47.7 all-gather.18
  114.4 47.7 all-gather.12
  164.2 47.7 all-gather.14
  214.1 47.8 all-gather.32
  264.0 48.5 all-gather.28
  314.7 48.1 all-gather.20
  365.7 47.7 all-gather.22
  415.7 47.8 all-gather.24
  465.6 48.4 all-gather.26
  540.3 47.5 all-gather.34
  621.0 47.4 all-gather.30
  732.5 459.3 all-reduce.3
where the time goes:
time: 1240 us; the launch traced here: 1230 us
  waiting for transfers between devices  436 us (35%)
  matrix products  301 us (24%)
  blocking collectives  235 us (19%)
  local copies, waits for them, and re-layouts  176 us (14%)
  other arithmetic  61.8 us (5%)
  between operations  17.2 us (1%)
    psum x1, waiting for transfers between devices, shards(): summed = lax.psum(local_grads, ('group', 'seq'))  404 us
    all_gather x3, blocking collectives, attend_backward(): lax.all_gather(own_rows[2], 'seq', axis=1, tiled=True)  97.8 us
    all_gather x3, blocking collectives, attend_backward(): lax.all_gather(own_rows[3], 'seq', axis=1, tiled=True)  97.6 us
    unnamed x618, local copies, waits for them, and re-layouts  65.1 us
    dot_general x32, matrix products, outer_sum(): jnp.einsum('bsd,bse->de', left_rows, right_rows, preferred_element_type=j...  52.4 us
    dot_general x32, matrix products, rows_times_transposed(): jnp.einsum('bse,de->bsd', rows, matrix, preferred_element_type=jnp.float32)  52.1 us
    dot_general x32, matrix products, rows_times(): jnp.einsum('bsd,de->bse', rows, matrix, preferred_element_type=jnp.float32)  46.9 us
    psum x1, blocking collectives, shards(): summed = lax.psum(local_grads, ('group', 'seq'))  39.5 us
  transfers between devices with their start and end apart: 13, of which 2 were waited for; matrix products, arithmetic and copies ran while one was open for 36% of the time, Pallas kernels for 0%

commit v1 on v0

v1 whole, which is shorter than its diff:
```python
import functools
import random
import jax
import jax.numpy as jnp
from jax import lax
from jax.experimental import pallas as pl
from jax.experimental.pallas import tpu as pltpu
from jax.sharding import Mesh, PartitionSpec as P

HEADS = 8
HEAD_DIM = 64
PAIR = 2 * HEAD_DIM
PAIRS = HEADS // 2
SCALE = HEAD_DIM**-0.5
FLOOR_SCORE = -1e30
EPSILON = 1e-05
KEY_BLOCK = 256
CHUNK = 512
F32 = jnp.float32
BF16 = jnp.bfloat16
CORE, X, INNER, OUTER = "core", "x", "inner", "outer"


def nn(left, right):
    return lax.dot_general(left, right, (((1,), (0,)), ((), ())), preferred_element_type=F32)


def nt(left, right):
    return lax.dot_general(left, right, (((1,), (1,)), ((), ())), preferred_element_type=F32)


def tn(left, right):
    return lax.dot_general(left, right, (((0,), (0,)), ((), ())), preferred_element_type=F32)


def two_heads(rows):
    lane = lax.broadcasted_iota(jnp.int32, rows.shape, 1)
    zero = jnp.zeros_like(rows)
    first = jnp.where(lane < HEAD_DIM, rows, zero)
    second = jnp.where(lane < HEAD_DIM, zero, rows)
    return jnp.concatenate([first, second], axis=0)


def diagonal(product):
    half = product.shape[1] // 2
    return jnp.concatenate([product[:HEAD_DIM, :half], product[HEAD_DIM:, half:]], axis=0)


def delta_rows(grad_out, outputs):
    product = grad_out.astype(F32) * outputs.astype(F32)
    high = product.astype(BF16)
    low = (product - high.astype(F32)).astype(BF16)
    width = product.shape[1]
    head = lax.broadcasted_iota(jnp.int32, (HEADS, width), 0)
    lane = lax.broadcasted_iota(jnp.int32, (HEADS, width), 1)
    pick = jnp.where(lax.div(lane, HEAD_DIM) == head, 1.0, 0.0).astype(BF16)
    return nt(pick, high) + nt(pick, low)


def pair_row(rows, pair):
    return jnp.concatenate([rows[2 * pair : 2 * pair + 1], rows[2 * pair + 1 : 2 * pair + 2]], axis=1)


def pair_lanes(pair):
    return slice(pair * PAIR, (pair + 1) * PAIR)


def norm(residual, gain, bias):
    centred = residual - jnp.mean(residual, axis=1, keepdims=True)
    inverse = lax.rsqrt(jnp.mean(centred * centred, axis=1, keepdims=True) + EPSILON)
    normed = centred * inverse
    return normed * gain + bias, normed, inverse


def norm_back(upstream, normed, inverse, gain):
    normed = normed.astype(F32)
    scaled = upstream * gain
    grad = inverse * (
        scaled
        - jnp.mean(scaled, axis=1, keepdims=True)
        - normed * jnp.mean(scaled * normed, axis=1, keepdims=True)
    )
    return (
        grad,
        jnp.sum(upstream * normed, axis=0, keepdims=True),
        jnp.sum(upstream, axis=0, keepdims=True),
    )


def feed_forward(rows, up_ref, down_ref, act_ref, gate_ref):
    low = rows.astype(BF16)
    total = rows
    for start in range(0, up_ref.shape[1], CHUNK):
        part = slice(start, start + CHUNK)
        hidden = nn(low, up_ref[:, part])
        sigmoid = 0.5 * jnp.tanh(0.5 * hidden) + 0.5
        active = hidden * sigmoid
        gate_ref[:, part] = (sigmoid + active * (1.0 - sigmoid)).astype(BF16)
        active = active.astype(BF16)
        act_ref[:, part] = active
        total = total + nn(active, down_ref[part, :])
    return low, total


def feed_back(grad, gate_ref, up_ref, down_ref, hidden_grad_ref):
    low = grad.astype(BF16)
    total = grad
    for start in range(0, up_ref.shape[1], CHUNK):
        part = slice(start, start + CHUNK)
        hidden = nt(low, down_ref[part, :]) * gate_ref[:, part].astype(F32)
        hidden = hidden.astype(BF16)
        hidden_grad_ref[:, part] = hidden
        total = total + nt(hidden, up_ref[:, part])
    return low, total


def short_allowed(key_segment, query_segment, causal):
    allowed = key_segment == query_segment
    if causal:
        key = lax.broadcasted_iota(jnp.int32, key_segment.shape, 0)
        query = lax.broadcasted_iota(jnp.int32, key_segment.shape, 1)
        allowed = allowed & (key <= query)
    return jnp.concatenate([allowed, allowed], axis=1)


def short_attend(causal, q_ref, k_ref, v_ref, kseg_ref, qseg_ref, o_ref, lse_ref):
    size = kseg_ref.shape[1]
    for block in range(kseg_ref.shape[0]):
        rows = slice(block * size, (block + 1) * size)
        allowed = short_allowed(kseg_ref[block], qseg_ref[block], causal)
        logs = []
        for pair in range(PAIRS):
            lanes = pair_lanes(pair)
            scores = nt(k_ref[rows, lanes], two_heads(q_ref[rows, lanes]))
            scores = jnp.where(allowed, scores, FLOOR_SCORE)
            top = jnp.max(scores, axis=0, keepdims=True)
            weights = jnp.exp(scores - top)
            total = jnp.sum(weights, axis=0, keepdims=True)
            mixed = nn(v_ref[rows, lanes].T, weights.astype(BF16)) / total
            o_ref[rows, lanes] = diagonal(mixed).T.astype(BF16)
            log_total = top + jnp.log(total)
            logs += [log_total[:, :size], log_total[:, size:]]
        lse_ref[block] = jnp.concatenate(logs, axis=0)


def short_attend_back(
    causal, q_ref, k_ref, v_ref, kseg_ref, qseg_ref, o_ref, lse_ref, go_ref, dq_ref, dk_ref, dv_ref
):
    size = kseg_ref.shape[1]
    for block in range(kseg_ref.shape[0]):
        rows = slice(block * size, (block + 1) * size)
        allowed = short_allowed(kseg_ref[block], qseg_ref[block], causal)
        delta = delta_rows(go_ref[rows, :], o_ref[rows, :])
        lse = lse_ref[block]
        for pair in range(PAIRS):
            lanes = pair_lanes(pair)
            queries, grads = two_heads(q_ref[rows, lanes]), two_heads(go_ref[rows, lanes])
            scores = nt(k_ref[rows, lanes], queries)
            weights = jnp.where(allowed, jnp.exp(scores - pair_row(lse, pair)), 0.0)
            grad_weights = nt(v_ref[rows, lanes], grads)
            grad_scores = (weights * (grad_weights - pair_row(delta, pair))).astype(BF16)
            dv_ref[rows, lanes] = nn(weights.astype(BF16), grads).astype(BF16)
            dk_ref[rows, lanes] = nn(grad_scores, queries).astype(BF16)
            turned = diagonal(nn(k_ref[rows, lanes].T, grad_scores)).T
            dq_ref[rows, lanes] = (turned.astype(BF16).astype(F32) * SCALE).astype(BF16)


def load_keys(ref, pair_index, block, lanes):
    pieces = KEY_BLOCK // ref.shape[2]
    rows = ref[pl.ds(block * pieces, pieces), pair_index, :, lanes]
    return rows.reshape(KEY_BLOCK, rows.shape[2])


def store_keys(ref, pair_index, block, lanes, rows):
    pieces = KEY_BLOCK // ref.shape[2]
    ref[pl.ds(block * pieces, pieces), pair_index, :, lanes] = rows.astype(BF16).reshape(
        pieces, ref.shape[2], rows.shape[1]
    )


def store_part(ref, info_ref, pair_index, block, rows):
    partners, _, pairs, size, _ = ref.shape
    for piece in range(KEY_BLOCK // size):
        place = block * (KEY_BLOCK // size) + piece
        inner = lax.rem(place, partners) ^ info_ref[pairs + 1]
        outer = lax.div(place, partners) ^ info_ref[pairs + 3]
        ref[inner, outer, pair_index] = rows[piece * size : (piece + 1) * size]


def long_limit(info_ref, causal, pair_index, size, pairs):
    length = info_ref[pair_index]
    limit = length
    if causal:
        limit = jnp.minimum(length, info_ref[pairs] + size)
    return length, lax.div(limit + KEY_BLOCK - 1, KEY_BLOCK)


def long_allowed(start, causal, length, block, shape):
    key = lax.broadcasted_iota(jnp.int32, shape, 0) + block * KEY_BLOCK
    allowed = key < length
    if causal:
        half = shape[1] // 2
        lane = lax.broadcasted_iota(jnp.int32, shape, 1)
        query = jnp.where(lane < half, lane, lane - half) + start
        allowed = allowed & (key <= query)
    return allowed


def long_attend(
    causal, info_ref, q_ref, x_ref, k_w, v_w, k_ref, v_ref, o_ref, lse_ref, score_ref, sum_ref, mix_ref
):
    places, pairs, size, width = x_ref.shape
    shape = (KEY_BLOCK, 2 * size)
    everything = slice(None)

    def one(pair_index, carry):
        length, count = long_limit(info_ref, causal, pair_index, size, pairs)
        own = pl.ds(pl.multiple_of(pair_index * size, size), size)

        def first(block, tops):
            rows = pl.ds(pl.multiple_of(block * KEY_BLOCK, KEY_BLOCK), KEY_BLOCK)
            allowed = long_allowed(info_ref[pairs], causal, length, block, shape)
            context = load_keys(x_ref, pair_index, block, everything)
            store_keys(k_ref, pair_index, block, everything, nn(context, k_w[...]))
            store_keys(v_ref, pair_index, block, everything, nn(context, v_w[...]))
            after = []
            for pair in range(PAIRS):
                lanes = pair_lanes(pair)
                keys = load_keys(k_ref, pair_index, block, lanes)
                scores = nt(keys, two_heads(q_ref[own, lanes]))
                scores = jnp.where(allowed, scores, FLOOR_SCORE)
                score_ref[pair, rows] = scores
                folded = jnp.max(scores.reshape(KEY_BLOCK // 8, 8, 2 * size), axis=0)
                after.append(jnp.maximum(tops[pair], folded))
            return tuple(after)

        start = tuple(jnp.full((8, 2 * size), FLOOR_SCORE, F32) for _ in range(PAIRS))
        tops = lax.fori_loop(0, count, first, start)
        tops = [jnp.max(top, axis=0, keepdims=True) for top in tops]
        sum_ref[...] = jnp.zeros_like(sum_ref)
        mix_ref[...] = jnp.zeros_like(mix_ref)

        def second(block, carry):
            rows = pl.ds(pl.multiple_of(block * KEY_BLOCK, KEY_BLOCK), KEY_BLOCK)
            for pair in range(PAIRS):
                weights = jnp.exp(score_ref[pair, rows] - tops[pair])
                sum_ref[pair] += jnp.sum(weights.reshape(KEY_BLOCK // 8, 8, 2 * size), axis=0)
                values = load_keys(v_ref, pair_index, block, pair_lanes(pair))
                mix_ref[pair] += nn(values.T, weights.astype(BF16))
            return carry

        lax.fori_loop(0, count, second, 0)
        logs = []
        for pair in range(PAIRS):
            total = jnp.sum(sum_ref[pair], axis=0, keepdims=True)
            mixed = mix_ref[pair] / total
            o_ref[own, pair_lanes(pair)] = diagonal(mixed).T.astype(BF16)
            log_total = tops[pair] + jnp.log(total)
            logs += [log_total[:, :size], log_total[:, size:]]
        lse_ref[pair_index] = jnp.concatenate(logs, axis=0)
        return carry

    lax.fori_loop(0, pairs, one, 0)


def long_attend_back(
    causal,
    info_ref,
    q_ref,
    k_ref,
    v_ref,
    o_ref,
    lse_ref,
    go_ref,
    k_w,
    v_w,
    dq_ref,
    dk_ref,
    dv_ref,
    part_ref,
    mix_ref,
):
    places, pairs, size, width = k_ref.shape
    shape = (KEY_BLOCK, 2 * size)
    everything = slice(None)

    def one(pair_index, carry):
        length, count = long_limit(info_ref, causal, pair_index, size, pairs)
        own = pl.ds(pl.multiple_of(pair_index * size, size), size)
        delta = delta_rows(go_ref[own, :], o_ref[own, :])
        lse = lse_ref[pair_index]
        mix_ref[...] = jnp.zeros_like(mix_ref)

        def step(block, carry):
            allowed = long_allowed(info_ref[pairs], causal, length, block, shape)
            for pair in range(PAIRS):
                lanes = pair_lanes(pair)
                queries, grads = two_heads(q_ref[own, lanes]), two_heads(go_ref[own, lanes])
                keys = load_keys(k_ref, pair_index, block, lanes)
                scores = nt(keys, queries)
                weights = jnp.where(allowed, jnp.exp(scores - pair_row(lse, pair)), 0.0)
                grad_weights = nt(load_keys(v_ref, pair_index, block, lanes), grads)
                grad_scores = (weights * (grad_weights - pair_row(delta, pair))).astype(BF16)
                store_keys(dv_ref, pair_index, block, lanes, nn(weights.astype(BF16), grads))
                store_keys(dk_ref, pair_index, block, lanes, nn(grad_scores, queries))
                mix_ref[pair] += nn(keys.T, grad_scores)
            part = nt(load_keys(dk_ref, pair_index, block, everything), k_w[...])
            part = part + nt(load_keys(dv_ref, pair_index, block, everything), v_w[...])
            store_part(part_ref, info_ref, pair_index, block, part.astype(BF16))
            return carry

        lax.fori_loop(0, count, step, 0)

        def clear(block, carry):
            nothing = jnp.zeros((KEY_BLOCK, width), BF16)
            store_keys(dk_ref, pair_index, block, everything, nothing)
            store_keys(dv_ref, pair_index, block, everything, nothing)
            store_part(part_ref, info_ref, pair_index, block, nothing)
            return carry

        lax.fori_loop(count, places * size // KEY_BLOCK, clear, 0)
        for pair in range(PAIRS):
            turned = diagonal(mix_ref[pair]).T
            dq_ref[own, pair_lanes(pair)] = (turned.astype(BF16).astype(F32) * SCALE).astype(BF16)
        return carry

    lax.fori_loop(0, pairs, one, 0)


class Refs(dict):
    def __init__(self, *args):
        super().__init__(*args)
        self.coming, self.leaving = {}, {}

    def __getattr__(self, name):
        if name in self.coming:
            self.coming.pop(name).wait()
        return self[name]

    def leave(self, *names):
        for name in names:
            self["left"].add(name)
            for copy in self.leaving.get(name, ()):
                copy.start()


def copied(shape, dtype):
    size = dtype.itemsize
    for length in shape:
        size *= length
    return shape[-1] % 128 == 0 and size >= 2**16


def launch(body, arrays, gives, scratch=(), info=None, after=(), pieces=(), plain=False, cost=10):
    memory = pl.BlockSpec(memory_space=pltpu.VMEM)
    far = pl.BlockSpec(memory_space=pl.ANY)
    ins, specs = [], []
    if info is not None:
        ins.append(info)
        specs.append(pl.BlockSpec(memory_space=pltpu.SMEM))
    moved_in = [
        name for name, array in arrays.items() if not plain and copied(array.shape, array.dtype)
    ]
    moved_out = [
        name
        for name, (shape, dtype) in gives.items()
        if name in pieces or not plain and copied(shape, jnp.dtype(dtype))
    ]
    for name, array in arrays.items():
        ins.append(array)
        specs.append(far if name in moved_in else memory)
    for array in after:
        ins.append(array)
        specs.append(far)
    count_out = sum(gives[name][0][0] if name in pieces else 1 for name in moved_out)
    rooms = [pltpu.VMEM(arrays[name].shape, arrays[name].dtype) for name in moved_in]
    rooms += [pltpu.VMEM(*gives[name]) for name in moved_out]
    rooms += [pltpu.SemaphoreType.DMA((max(len(moved_in), 1),))]
    rooms += [pltpu.SemaphoreType.DMA((max(count_out, 1),))]
    names = [name for name, _ in scratch]

    def run(*refs):
        refs = list(refs)
        r = Refs()
        if info is not None:
            r["info"] = refs.pop(0)
        outer = {name: refs.pop(0) for name in arrays}
        del refs[: len(after)]
        outer.update((name, refs.pop(0)) for name in gives)
        room = {name: refs.pop(0) for name in moved_in + moved_out}
        come, go = refs.pop(0), refs.pop(0)
        r.update(outer)
        r.update(room)
        r.update(zip(names, refs))
        for place, name in enumerate(moved_in):
            copy = pltpu.make_async_copy(outer[name], room[name], come.at[place])
            copy.start()
            r.coming[name] = copy
        place = 0
        for name in moved_out:
            copies = []
            if name in pieces:
                for piece in range(gives[name][0][0]):
                    source, target = room[name].at[piece], outer[name].at[piece]
                    copies.append(pltpu.make_async_copy(source, target, go.at[place]))
                    place += 1
            else:
                copies.append(pltpu.make_async_copy(room[name], outer[name], go.at[place]))
                place += 1
            r.leaving[name] = copies
        left = set()
        r["left"] = left
        body(r)
        for name in list(r.coming):
            r.coming.pop(name).wait()
        for name in moved_out:
            if name not in left and name not in pieces:
                r.leave(name)
        for name in moved_out:
            for copy in r.leaving[name]:
                copy.wait()

    out = pl.pallas_call(
        run,
        in_specs=specs,
        out_specs=[far if name in moved_out else memory for name in gives],
        out_shape=[jax.ShapeDtypeStruct(shape, dtype) for shape, dtype in gives.values()],
        scratch_shapes=rooms + [shape for _, shape in scratch],
        compiler_params=pltpu.CompilerParams(vmem_limit_bytes=VMEM_LIMIT),
        cost_estimate=pl.CostEstimate(
            flops=int(cost * 1.1e9), bytes_accessed=int(cost * 3.5e6), transcendentals=0
        ),
    )(*ins)
    return Refs(zip(gives, out))


VMEM_LIMIT = 56 * 2**20


def add_sums(ref, rows):
    ref[...] = jnp.concatenate(rows, axis=0)


def encoder_tail(r, o_ref):
    residual = r.x[...].astype(F32) + nn(o_ref[...], r.w_o[...])
    first, normed, inverse = norm(residual, r.gain[0:1], r.bias[0:1])
    r.n1[...] = normed.astype(BF16)
    r.i1[...] = inverse
    low, total = feed_forward(first, r.up, r.down, r.act, r.gate)
    r.y[...] = low
    r.leave("n1", "act", "gate", "y")
    encoded, normed, inverse = norm(total, r.gain[1:2], r.bias[1:2])
    r.n2[...] = normed.astype(BF16)
    r.i2[...] = inverse
    r.enc[...] = encoded.astype(BF16)


def project_short(r, name, rows, w_q, w_k, w_v, context=None):
    context = rows if context is None else context
    r["q" + name][...] = (nn(rows, w_q) * SCALE).astype(BF16)
    r["k" + name][...] = nn(context, w_k).astype(BF16)
    r["v" + name][...] = nn(context, w_v).astype(BF16)


def short_encoder_forward(r):
    project_short(r, "", r.x[...], r.w_in[0], r.w_in[1], r.w_in[2])
    r.leave("q", "k", "v")
    short_attend(False, r.q, r.k, r.v, r.kseg, r.qseg, r.o, r.lse)
    r.leave("o")
    encoder_tail(r, r.o)


def decoder_middle(r, o_ref):
    residual = r.t[...].astype(F32) + nn(o_ref[...], r.w_o[...])
    upper, normed, inverse = norm(residual, r.gain[0:1], r.bias[0:1])
    r.n3[...] = normed.astype(BF16)
    r.i3[...] = inverse
    r.u[...] = upper.astype(BF16)
    return upper


def decoder_tail(r, upper, o_ref):
    gain, bias = r.gain, r.bias
    residual = upper + nn(o_ref[...], r.w_co[...])
    middle, normed4, inverse4 = norm(residual, gain[1:2], bias[1:2])
    low, total = feed_forward(middle, r.up, r.down, r.act, r.gate)
    r.m[...] = low
    r.leave("m", "act", "gate")
    final, normed5, inverse5 = norm(total, gain[2:3], bias[2:3])
    r.final[...] = final
    r.leave("final")
    grad, gain5, bias5 = norm_back(r.cot[...].astype(F32), normed5, inverse5, gain[2:3])
    low, grad = feed_back(grad, r.gate, r.up, r.down, r.dh)
    r.b5[...] = low
    r.leave("b5", "dh")
    grad, gain4, bias4 = norm_back(grad, normed4, inverse4, gain[1:2])
    low = grad.astype(BF16)
    r.b4[...] = low
    r.d4[...] = grad
    r.go_c[...] = nt(low, r.w_co[...]).astype(BF16)
    add_sums(r.small, [gain4, gain5, bias4, bias5])


def short_decoder_forward(r):
    project_short(r, "", r.t[...], r.w_in[0], r.w_in[1], r.w_in[2])
    r.leave("q", "k", "v")
    short_attend(True, r.q, r.k, r.v, r.tkseg, r.tqseg, r.o, r.lse)
    r.leave("o")
    r.upper[...] = decoder_middle(r, r.o)


def short_cross_forward(r):
    project_short(r, "_c", r.u[...], r.w_cin[0], r.w_cin[1], r.w_cin[2], r.enc[...])
    r.leave("q_c", "k_c", "v_c")
    short_attend(False, r.q_c, r.k_c, r.v_c, r.kseg, r.tqseg, r.o_c, r.lse_c)
    r.leave("o_c")
    decoder_tail(r, r.upper[...], r.o_c)


def decoder_middle_back(r):
    grad = r.d4[...] + nt(r.dq_c[...], r.w_cin[0])
    grad, gain3, bias3 = norm_back(grad, r.n3[...], r.i3[...], r.gain[0:1])
    low = grad.astype(BF16)
    r.b3[...] = low
    r.go[...] = nt(low, r.w_o[...]).astype(BF16)
    add_sums(r.small, [gain3, bias3])
    return grad


def short_decoder_back(r):
    short_attend_back(
        False, r.q_c, r.k_c, r.v_c, r.kseg, r.tqseg, r.o_c, r.lse_c, r.go_c, r.dq_c, r.dk_c, r.dv_c
    )
    r.denc[...] = nt(r.dk_c[...], r.w_cin[1]) + nt(r.dv_c[...], r.w_cin[2])
    r.leave("dq_c", "dk_c", "dv_c", "denc")
    r.d3[...] = decoder_middle_back(r)
    short_attend_back(
        True, r.q, r.k, r.v, r.tkseg, r.tqseg, r.o, r.lse, r.go, r.dq, r.dk, r.dv
    )
    r.leave("dq", "dk", "dv")
    grad = r.d3[...] + nt(r.dq[...], r.w_in[0])
    r.dt[...] = grad + nt(r.dk[...], r.w_in[1]) + nt(r.dv[...], r.w_in[2])


def encoder_tail_back(r, grad):
    grad, gain2, bias2 = norm_back(grad, r.n2[...], r.i2[...], r.gain[1:2])
    low, grad = feed_back(grad, r.gate, r.up, r.down, r.dh)
    r.b2[...] = low
    r.leave("b2", "dh")
    grad, gain1, bias1 = norm_back(grad, r.n1[...], r.i1[...], r.gain[0:1])
    low = grad.astype(BF16)
    r.b1[...] = low
    r.go[...] = nt(low, r.w_o[...]).astype(BF16)
    r.d1[...] = grad
    add_sums(r.small, [gain1, gain2, bias1, bias2])


def short_encoder_back(r):
    encoder_tail_back(r, r.denc[...])
    short_attend_back(
        False, r.q, r.k, r.v, r.kseg, r.qseg, r.o, r.lse, r.go, r.dq, r.dk, r.dv
    )
    r.leave("dq", "dk", "dv")
    grad = r.d1[...] + nt(r.dq[...], r.w_in[0])
    r.dx[...] = grad + nt(r.dk[...], r.w_in[1]) + nt(r.dv[...], r.w_in[2])


def long_encoder_forward(r):
    r.q[...] = (nn(r.x[...], r.w_in[0]) * SCALE).astype(BF16)
    long_attend(
        False, r.info, r.q, r.xg, r.w_in.at[1], r.w_in.at[2], r.k, r.v, r.o, r.lse, r.s, r.a, r.mix
    )
    r.leave("q", "k", "v", "o")
    encoder_tail(r, r.o)


def long_self_forward(r):
    r.q[...] = (nn(r.t[...], r.w_in[0]) * SCALE).astype(BF16)
    long_attend(
        True, r.info, r.q, r.tg, r.w_in.at[1], r.w_in.at[2], r.k, r.v, r.o, r.lse, r.s, r.a, r.mix
    )
    r.leave("q", "k", "v", "o")
    upper = decoder_middle(r, r.o)
    r.upper[...] = upper
    r.q_c[...] = (nn(upper.astype(BF16), r.w_cin[0]) * SCALE).astype(BF16)


def long_cross(r):
    k_w, v_w = r.w_cin.at[1], r.w_cin.at[2]
    long_attend(
        False, r.info, r.q_c, r.eg, k_w, v_w, r.k_c, r.v_c, r.o_c, r.lse_c, r.s, r.a, r.mix
    )
    r.leave("k_c", "v_c", "o_c")
    decoder_tail(r, r.upper[...], r.o_c)


def long_cross_back(r):
    long_attend_back(
        False,
        r.info,
        r.q_c,
        r.k_c,
        r.v_c,
        r.o_c,
        r.lse_c,
        r.go_c,
        r.w_cin.at[1],
        r.w_cin.at[2],
        r.dq_c,
        r.dk_c,
        r.dv_c,
        r.part,
        r.mix,
    )


def long_self_back(r):
    grad = decoder_middle_back(r)
    long_attend_back(
        True,
        r.info,
        r.q,
        r.k,
        r.v,
        r.o,
        r.lse,
        r.go,
        r.w_in.at[1],
        r.w_in.at[2],
        r.dq,
        r.dk,
        r.dv,
        r.part,
        r.mix,
    )
    r.dt[...] = grad + nt(r.dq[...], r.w_in[0])


def long_encoder_tail_back(r):
    grad = r.part0[...].astype(F32) + r.part1[...].astype(F32)
    grad = grad + r.part2[...].astype(F32) + r.part3[...].astype(F32)
    encoder_tail_back(r, grad)


def long_encoder_back(r):
    long_attend_back(
        False,
        r.info,
        r.q,
        r.k,
        r.v,
        r.o,
        r.lse,
        r.go,
        r.w_in.at[1],
        r.w_in.at[2],
        r.dq,
        r.dk,
        r.dv,
        r.part,
        r.mix,
    )
    r.dx[...] = r.d1[...] + nt(r.dq[...], r.w_in[0])


SIDE = 512


class Weights:
    def __init__(self, pairs):
        self.arrays, self.plan, known = {}, [], {}

        def place(rows):
            if isinstance(rows, tuple):
                return rows
            if id(rows) not in known:
                known[id(rows)] = "w%d" % len(known)
                self.arrays[known[id(rows)]] = rows
            return known[id(rows)], rows.shape[1]

        for terms in pairs:
            terms = [(place(a), place(b)) for a, b in terms]
            (_, height), (_, width) = terms[0]
            for row in range(0, height, SIDE):
                for column in range(0, width, SIDE):
                    self.plan.append([(a[0], row, b[0], column) for a, b in terms])
        count = len(self.plan)
        self.gives = {name: ((count, SIDE // 2, SIDE), BF16) for name in ("kept", "sent")}

    def body(self, r, core):
        half = SIDE // 2
        for index, terms in enumerate(self.plan):
            for flip, name in enumerate(("kept", "sent")):
                total = None
                for a, row, b, column in terms:
                    left, right = getattr(r, a), getattr(r, b)
                    begin = pl.multiple_of(row + (core ^ flip) * half, half)
                    across = slice(column, column + SIDE)
                    if len(left.shape) == 4:
                        tall = left.shape[0] * left.shape[1] * left.shape[2]
                        rows = left[:, :, :, pl.ds(begin, half)].reshape(tall, half)
                    else:
                        rows = left[:, pl.ds(begin, half)]
                    if len(right.shape) == 4:
                        tall = right.shape[0] * right.shape[1] * right.shape[2]
                        product = tn(rows, right[:, :, :, across].reshape(tall, SIDE))
                    else:
                        product = tn(rows, right[:, across])
                    total = product if total is None else total + product
                r[name][index] = total.astype(BF16)
                r.leaving[name][index].start()


def weight_tiles(pairs, core_info, after=(), cost=10):
    weights = Weights(pairs)
    out = launch(
        lambda r: weights.body(r, r.info[0]),
        weights.arrays,
        weights.gives,
        info=core_info,
        after=after,
        pieces=("kept", "sent"),
        cost=cost,
    )
    return [out.kept, out.sent]


def send(piece, axis, offset):
    count = lax.axis_size(axis)
    return lax.ppermute(piece, axis, [(i, i ^ offset) for i in range(count)])


def ordered(pieces, place, dim):
    if len(pieces) == 1:
        return pieces[0]
    level = len(pieces) // 2
    inside = lax.rem(place, level)
    low = ordered(pieces[:level], inside, dim)
    high = ordered(pieces[level:], inside, dim)
    return jnp.where(
        place >= level, jnp.concatenate([high, low], dim), jnp.concatenate([low, high], dim)
    )


def hold(value, token):
    return lax.optimization_barrier((value, token))[0]


def gather_first(piece, axis):
    return [piece] + [send(piece, axis, k) for k in range(1, lax.axis_size(axis))]


def gather_last(pieces, axis, dim, token=None):
    if token is not None:
        pieces = hold(pieces, token)
    return ordered(pieces, lax.axis_index(axis), dim)


def added(pieces):
    total = pieces[0].astype(F32)
    for piece in pieces[1:]:
        total = total + piece.astype(F32)
    return total.astype(BF16)


def scatter_step(pending, axis, dim, token=None):
    if token is not None:
        pending = hold(pending, token)
    place, count = lax.axis_index(axis), lax.axis_size(axis)
    size = pending[0].shape[dim] // count
    after = []
    for k in range(count):
        parts = [
            lax.dynamic_slice_in_dim(piece, (place ^ k) * size, size, dim) for piece in pending
        ]
        block = added(parts)
        after.append(send(block, axis, k) if k else block)
    return after


def gather_step(piece, axis, dim):
    return gather_last(gather_first(piece, axis), axis, dim)


def gather_early(rows):
    return lax.all_gather(rows, (OUTER, INNER), axis=0, tiled=False)


SEQ = (OUTER, INNER)


class Chain:
    def __init__(self, halves, order, small=None, doubled=False):
        self.order = (CORE,) + order
        self.doubled = doubled
        self.stage = 0
        self.tiles = halves[0].shape[0]
        self.small, self.carried = None, 0
        if small is not None:
            self.carried = small.shape[0]
            halves = [jnp.concatenate([self.flat(half), small]) for half in halves]
        self.held = [halves[0], send(halves[1], CORE, 1)]

    def flat(self, block):
        return block.reshape(-1, block.shape[-1])

    def parts(self):
        if not self.carried:
            return self.held, None
        body = [piece[: -self.carried] for piece in self.held]
        body = [piece.reshape(self.tiles, -1, piece.shape[-1]) for piece in body]
        return body, added([piece[-self.carried :] for piece in self.held])

    def next_axis(self):
        stage, count = self.stage + 1, len(self.order)
        return self.order[stage] if stage < count else self.order[2 * count - 1 - stage]

    def over(self):
        return self.stage == 2 * len(self.order) - 1

    def go(self):
        axis = self.next_axis()
        self.stage += 1
        count = len(self.order)
        if self.doubled and self.stage in (count - 1, count):
            total = added(self.held)
            self.held = [total, send(total, OUTER, self.stage - count + 2)]
            return
        if self.doubled and self.stage == count + 1:
            pending, self.small = self.parts()
            self.held = gather_first(added(pending), axis)
            return
        if self.stage < count:
            pending, small = self.parts()
            place, members = lax.axis_index(axis), lax.axis_size(axis)
            size = pending[0].shape[1] // members
            self.held = []
            for k in range(members):
                begin = (place ^ k) * size
                block = added([lax.dynamic_slice_in_dim(p, begin, size, 1) for p in pending])
                if small is not None:
                    block = jnp.concatenate([self.flat(block), small])
                self.held.append(send(block, axis, k) if k else block)
            return
        if self.stage == count:
            pending, self.small = self.parts()
            piece = added(pending)
        else:
            piece = gather_last(self.held, self.order[2 * count - self.stage], 1)
        self.held = gather_first(piece, axis)

    def volume(self):
        return self.held[0].size * 2 / 2**20


class Spread:
    def __init__(self, part, straight):
        self.straight, self.stage = straight, 0
        self.held = [send(part[k], INNER, k) if k else part[k] for k in range(part.shape[0])]

    def next_axis(self):
        return OUTER

    def over(self):
        return self.stage == (1 if self.straight else 2)

    def go(self):
        self.stage += 1
        if self.straight:
            blocks = [added([piece[k] for piece in self.held]) for k in range(4)]
            self.held = [send(block, OUTER, k) if k else block for k, block in enumerate(blocks)]
            return
        if self.stage == 1:
            pick, offset = (lambda piece, odd: jnp.stack([piece[odd], piece[2 + odd]])), 1
        else:
            pick, offset = (lambda piece, odd: piece[odd]), 2
        mine, theirs = [added([pick(piece, odd) for piece in self.held]) for odd in (0, 1)]
        self.held = [mine, send(theirs, OUTER, offset)]

    def volume(self):
        return self.held[0].size * 2 / 2**20

    def result(self):
        return added(self.held)


def finish(chains, *tokens):
    held, _ = lax.optimization_barrier(([chain.held for chain in chains], tokens))
    for chain, pieces in zip(chains, held):
        chain.held = pieces


def go(*chains):
    for chain in chains:
        chain.go()


FLOW = {CORE: 3.5, X: 21.0, INNER: 21.0, OUTER: 84.0}


def plan_of(chain):
    if isinstance(chain, Spread):
        return [(INNER, 21.0, 1), (OUTER, 10.5, 1), (OUTER, 10.5, 1)][chain.stage :]
    size, out = chain.tiles * 0.5, []
    for axis in chain.order:
        count = lax.axis_size(axis)
        if axis == OUTER and chain.doubled:
            out += [(OUTER, 21.0 * size, 1), (OUTER, 42.0 * size, 1)]
            continue
        size = size / count
        out.append((axis, FLOW[axis] * size, count - 1))
    back = [entry for entry in reversed(out)]
    if chain.doubled:
        back = [entry for entry in back if entry[0] != OUTER]
    return (out + back)[chain.stage :]


def rehearse(plans, first, gate, weights, slack):
    free = dict.fromkeys(FLOW, 0.0)
    position, queue, order, clock, waiting = [0] * len(plans), [], [], 0.0, []

    def depart(index, when):
        axis, long, _ = plans[index][position[index]]
        begin = max(when, free[axis])
        free[axis] = begin + long
        queue.append((free[axis] + 6.0, index))

    def left(index):
        rest = plans[index][position[index] :]
        return weights[index] * sum(long + 10.0 for _, long, _ in rest)

    for index, since in first:
        depart(index, -since)
    while queue or waiting:
        soon = min(queue)[0] if queue else clock + 99.0
        if waiting and soon > clock + 4.0:
            clock += 6.5
            order.append((waiting.pop(0), True))
            continue
        near = [entry for entry in queue if entry[0] <= max(clock, soon) + slack]
        entry = max(near, key=lambda entry: left(entry[1]))
        queue.remove(entry)
        arrival, index = entry
        clock = max(clock, arrival)
        position[index] += 1
        order.append((index, False))
        if position[index] == len(plans[index]):
            clock += 1.0
            waiting.append(index)
            continue
        axis, long, sends = plans[index][position[index]]
        clock += 2.0 + 1.5 * sends + 0.03 * long
        depart(index, clock)
        if gate[1] == index and position[index] == 1:
            clock += 2.0
            depart(gate[0], clock)
    return clock, order


def run_out(flights, later):
    chains, ends = [chain for chain, _, _ in flights], [end for _, _, end in flights]
    plans = [plan_of(chain) for chain in chains]
    plans.append([(INNER, 21.0, 1), (OUTER, 10.5, 1), (OUTER, 10.5, 1)])
    first = [(index, since) for index, (_, since, _) in enumerate(flights)]
    rng, best = random.Random(7), None
    for trial in range(1500):
        weights = [1.0 if trial < 4 else rng.uniform(0.3, 2.0) for _ in plans]
        slack = (0.0, 2.0, 4.0, 8.0)[trial % 4]
        found = rehearse(plans, first, (len(chains), 0), weights, slack)
        if best is None or found[0] < best[0]:
            best = found
    token, results = (), {}
    for index, is_end in best[1]:
        chain = chains[index]
        if is_end:
            results[index] = ends[index](chain, token)
            token = (results[index][0],)
            continue
        finish([chain], *token)
        if chain.over():
            token = tuple(chain.held)
            continue
        chain.go()
        token = (chain.held[0],)
        if index == 0 and chain.stage == 1:
            chain, _, end = later(token)
            chains.append(chain)
            ends.append(end)
    return [results[index] for index in range(len(chains))]


def assemble(chain, core_info, shapes, after=()):
    tiles, half, side = chain.held[0].shape

    def body(r):
        low = pl.multiple_of(r.info[0] * half, half)
        high = pl.multiple_of((1 - r.info[0]) * half, half)
        tile = 0
        for name, shape in shapes.items():
            out = r[name]
            for start in range(0, shape[-2] * shape[-1] * (shape[0] if len(shape) > 2 else 1), side * side):
                place = start // (side * side)
                for begin, source in ((low, r.mine), (high, r.other)):
                    rows = source[tile].astype(F32)
                    if len(shape) > 2:
                        out[place, pl.ds(begin, half), :] = rows
                    elif shape[1] > shape[0]:
                        out[pl.ds(begin, half), place * side : (place + 1) * side] = rows
                    else:
                        out[pl.ds(begin + place * side, half), :] = rows
                tile += 1
            r.leave(name)

    gives = {name: (shape, F32) for name, shape in shapes.items()}
    arrays = {"mine": chain.held[0], "other": chain.held[1]}
    return list(launch(body, arrays, gives, info=core_info, after=after, cost=5).values())


def shards(
    source_short,
    target_short,
    source_segment,
    target_segment,
    source_long,
    target_long,
    source_length,
    target_length,
    cotangent_short,
    cotangent_long,
    encoder_project,
    encoder_output,
    encoder_up,
    encoder_down,
    encoder_gain,
    encoder_bias,
    decoder_project,
    decoder_output,
    cross_project,
    cross_output,
    decoder_up,
    decoder_down,
    decoder_gain,
    decoder_bias,
):
    blocks, size, width = source_short.shape
    hidden = encoder_up.shape[1]
    rows = blocks * size
    pairs, own, _ = source_long.shape
    rows_long = pairs * own
    flat = lambda a: a.reshape(-1, width)
    start = lax.axis_index((OUTER, INNER)) * own
    core = lax.axis_index(CORE)
    here = [start, lax.axis_index(INNER), core, lax.axis_index(OUTER)]
    here = jnp.stack(here).astype(jnp.int32)
    info_of = lambda lengths: jnp.concatenate([lengths, here])
    core_info = core.astype(jnp.int32)[None]
    source_info, target_info = info_of(source_length), info_of(target_length)

    spread = lambda s: jnp.broadcast_to(s[:, :, None], (blocks, size, size))
    line = lambda s: s[:, None, :]
    encoder_in = {
        "w_in": encoder_project,
        "w_o": encoder_output,
        "up": encoder_up,
        "down": encoder_down,
        "gain": encoder_gain,
        "bias": encoder_bias,
    }
    decoder_in = {
        "w_in": decoder_project,
        "w_o": decoder_output,
        "w_cin": cross_project,
        "w_co": cross_output,
        "up": decoder_up,
        "down": decoder_down,
        "gain": decoder_gain,
        "bias": decoder_bias,
    }

    def pick(table, names):
        return {name: table[name] for name in names}

    def rows_of(n, names):
        return {name: ((n, width), BF16) for name in names}

    def wide_of(n, names):
        return {name: ((n, hidden), BF16) for name in names}

    def floats(n, names):
        return {name: ((n, width), F32) for name in names}

    def column(n, names):
        return {name: ((n, 1), F32) for name in names}

    def logs(n, names):
        return {name: ((n, HEADS, size), F32) for name in names}

    def sums(n):
        return {"small": ((n, width), F32)}

    def keys_of(names):
        shape = (places, pairs, own, width)
        return {name: (shape, BF16) for name in names}

    def parts():
        inner = lax.axis_size(INNER)
        return {"part": ((inner, places // inner, pairs, own, width), BF16)}

    def saved(kernel, names):
        return {name: kernel[name] for name in names}

    whole_source = gather_early(source_long)
    places = lax.axis_size(OUTER) * lax.axis_size(INNER)
    keys = places * own
    work = [
        ("s", pltpu.VMEM((PAIRS, keys, 2 * own), F32)),
        ("a", pltpu.VMEM((PAIRS, 8, 2 * own), F32)),
        ("mix", pltpu.VMEM((PAIRS, PAIR, 2 * own), F32)),
    ]
    mix = work[2:]

    segments = {"kseg": spread(source_segment), "qseg": line(source_segment)}
    turned = {"tkseg": spread(target_segment), "tqseg": line(target_segment)}
    encoder_keeps = lambda n: {
        **rows_of(n, ("n1", "y", "n2", "enc")),
        **wide_of(n, ("act", "gate")),
        **column(n, ("i1", "i2")),
    }
    se = launch(
        short_encoder_forward,
        {"x": flat(source_short), **segments, **encoder_in},
        {**rows_of(rows, ("q", "k", "v", "o")), **logs(blocks, ("lse",)), **encoder_keeps(rows)},
        cost=0.01,
    )
    decoder_keeps = lambda n: {
        **rows_of(n, ("m", "b5", "b4", "go_c")),
        **wide_of(n, ("act", "gate", "dh")),
        **floats(n, ("final", "d4")),
        **sums(4),
    }
    sd = launch(
        short_decoder_forward,
        {
            "t": flat(target_short),
            **turned,
            **pick(decoder_in, ("w_in", "w_o", "gain", "bias")),
        },
        {
            **rows_of(rows, ("q", "k", "v", "o", "n3", "u")),
            **logs(blocks, ("lse",)),
            **column(rows, ("i3",)),
            **floats(rows, ("upper",)),
        },
        after=(se.lse,),
        cost=0.01,
    )
    early_target = gather_first(hold(target_long, sd.lse)[None, None], OUTER)
    sc = launch(
        short_cross_forward,
        {
            "u": sd.u,
            "upper": sd.upper,
            "enc": se.enc,
            "cot": flat(cotangent_short),
            "kseg": segments["kseg"],
            "tqseg": turned["tqseg"],
            **pick(decoder_in, ("w_cin", "w_co", "up", "down", "gain", "bias")),
        },
        {
            **rows_of(rows, ("q_c", "k_c", "v_c", "o_c")),
            **logs(blocks, ("lse_c",)),
            **decoder_keeps(rows),
        },
        after=(sd.lse,),
        cost=0.01,
    )

    sb = launch(
        short_decoder_back,
        {
            **saved(sd, ("q", "k", "v", "o", "lse", "n3", "i3")),
            **saved(sc, ("q_c", "k_c", "v_c", "o_c", "lse_c", "go_c", "d4")),
            "kseg": segments["kseg"],
            **turned,
            **pick(decoder_in, ("w_in", "w_o", "w_cin", "gain")),
        },
        {
            **rows_of(rows, ("dq_c", "dk_c", "dv_c", "dq", "dk", "dv", "b3", "go")),
            **floats(rows, ("denc", "dt")),
            **sums(2),
        },
        scratch=[("d3", pltpu.VMEM((rows, width), F32))],
        after=(sc.small,),
        cost=0.01,
    )

    early_target = gather_last(early_target, OUTER, 0, sb.small)
    late_target = gather_first(early_target, INNER)

    whole_source = hold(whole_source, sb.small)
    x_long, t_long = flat(source_long), flat(target_long)
    le = launch(
        long_encoder_forward,
        {"x": x_long, "xg": whole_source, **encoder_in},
        {
            **rows_of(rows_long, ("q", "o")),
            **keys_of(("k", "v")),
            **logs(pairs, ("lse",)),
            **encoder_keeps(rows_long),
        },
        scratch=work,
        info=source_info,
        after=(sb.small, early_target),
        cost=13,
        plain=True,
    )
    whole_encoded = gather_early(le.enc.reshape(pairs, own, width))

    seb = launch(
        short_encoder_back,
        {
            "denc": sb.denc,
            **saved(se, ("q", "k", "v", "o", "lse", "n1", "i1", "n2", "i2", "gate")),
            **segments,
            **pick(encoder_in, ("w_in", "w_o", "up", "down", "gain")),
        },
        {
            **rows_of(rows, ("dq", "dk", "dv", "b1", "b2", "go")),
            **wide_of(rows, ("dh",)),
            **floats(rows, ("dx",)),
            **sums(4),
        },
        scratch=[("d1", pltpu.VMEM((rows, width), F32))],
        after=(le.lse,),
        cost=16,
    )

    whole_target = gather_last(late_target, INNER, 1, seb.small)
    whole_target = whole_target.reshape(places, pairs, own, width)
    ls = launch(
        long_self_forward,
        {
            "t": t_long,
            "tg": whole_target,
            **pick(decoder_in, ("w_in", "w_o", "w_cin", "gain", "bias")),
        },
        {
            **rows_of(rows_long, ("q", "o", "n3", "u", "q_c")),
            **keys_of(("k", "v")),
            **logs(pairs, ("lse",)),
            **column(rows_long, ("i3",)),
            **floats(rows_long, ("upper",)),
        },
        scratch=work,
        info=target_info,
        after=(seb.small,),
        cost=10,
        plain=True,
    )

    whole_encoded = hold(whole_encoded, ls.lse)
    lc = launch(
        long_cross,
        {
            "eg": whole_encoded,
            "upper": ls.upper,
            "q_c": ls.q_c,
            "cot": flat(cotangent_long),
            **pick(decoder_in, ("w_cin", "w_co", "up", "down", "gain", "bias")),
        },
        {
            **rows_of(rows_long, ("o_c",)),
            **keys_of(("k_c", "v_c")),
            **logs(pairs, ("lse_c",)),
            **decoder_keeps(rows_long),
        },
        scratch=work,
        info=source_info,
        after=(ls.lse,),
        cost=14,
        plain=True,
    )
    lcb = launch(
        long_cross_back,
        {
            "q_c": ls.q_c,
            **saved(lc, ("k_c", "v_c", "o_c", "lse_c", "go_c")),
            **pick(decoder_in, ("w_cin",)),
        },
        {**rows_of(rows_long, ("dq_c",)), **keys_of(("dk_c", "dv_c")), **parts()},
        scratch=mix,
        info=source_info,
        after=(lc.small,),
        cost=14,
        plain=True,
    )
    encoded_back = Spread(lcb.part, True)
    first_weights = Weights(
        [[(sc.m, sc.dh), (lc.m, lc.dh)], [(sc.act, sc.b5), (lc.act, lc.b5)]]
    )

    def self_back_and_weights(r):
        first_weights.body(r, r.info[pairs + 2])
        long_self_back(r)

    lsb = launch(
        self_back_and_weights,
        {
            **first_weights.arrays,
            "d4": lc.d4,
            "dq_c": lcb.dq_c,
            **saved(ls, ("q", "k", "v", "o", "lse", "n3", "i3")),
            **pick(decoder_in, ("w_in", "w_o", "w_cin", "gain")),
        },
        {
            **first_weights.gives,
            **rows_of(rows_long, ("dq", "b3")),
            **keys_of(("dk", "dv")),
            **parts(),
            **floats(rows_long, ("dt",)),
            **sums(2),
        },
        scratch=mix + [("go", pltpu.VMEM((rows_long, width), BF16))],
        info=target_info,
        after=(lcb.dq_c,),
        pieces=("kept", "sent"),
        cost=22,
    )
    decoder_ffn = Chain([lsb.kept, lsb.sent], (X, INNER, OUTER))
    finish([encoded_back], lsb.small)
    go(encoded_back)
    target_back = Spread(lsb.part, False)
    grad_attention = weight_tiles(
        [
            [(sd.u, sb.dq_c), (ls.u, lcb.dq_c)],
            [(se.enc, sb.dk_c), (flat(whole_encoded), flat(lcb.dk_c))],
            [(se.enc, sb.dv_c), (flat(whole_encoded), flat(lcb.dv_c))],
            [(sc.o_c, sc.b4), (lc.o_c, lc.b4)],
            [(flat(target_short), sb.dq), (t_long, lsb.dq)],
            [(flat(target_short), sb.dk), (flat(whole_target), flat(lsb.dk))],
            [(flat(target_short), sb.dv), (flat(whole_target), flat(lsb.dv))],
            [(sd.o, sb.b3), (ls.o, lsb.b3)],
        ],
        core_info,
        after=(lsb.small, encoded_back.held[0]),
        cost=15,
    )
    finish([encoded_back, decoder_ffn], grad_attention[0])
    go(decoder_ffn)
    attention = Chain(grad_attention, (INNER, X, OUTER))
    ffn_weights = Weights(
        [
            [(se.y, seb.dh), (le.y, ("dh", hidden))],
            [(se.act, seb.b2), (le.act, ("b2", width))],
        ]
    )

    def encoder_back_and_weights(r):
        long_encoder_tail_back(r)
        ffn_weights.body(r, r.info[0])

    leb = launch(
        encoder_back_and_weights,
        {
            **{"part%d" % k: flat(piece) for k, piece in enumerate(encoded_back.held)},
            **saved(le, ("n1", "i1", "n2", "i2", "gate")),
            **pick(encoder_in, ("down", "up", "w_o", "gain")),
            **ffn_weights.arrays,
        },
        {
            **ffn_weights.gives,
            **rows_of(rows_long, ("b1", "b2", "go")),
            **wide_of(rows_long, ("dh",)),
            **floats(rows_long, ("d1",)),
            **sums(4),
        },
        info=core_info,
        after=(grad_attention[0], decoder_ffn.held[0]),
        pieces=("kept", "sent"),
        cost=12,
    )
    small = jnp.concatenate([seb.small + leb.small, sb.small + lsb.small, sc.small + lc.small])
    small = jnp.pad(small, ((0, 16 - small.shape[0]), (0, 0))).astype(BF16)
    finish([attention], leb.small)
    go(attention)
    encoder_ffn = Chain([leb.kept, leb.sent], (X, INNER, OUTER))
    attention_weights = Weights(
        [
            [(flat(source_short), seb.dq), (x_long, ("dq", width))],
            [(flat(source_short), seb.dk), (whole_source, ("dk", width))],
            [(flat(source_short), seb.dv), (whole_source, ("dv", width))],
            [(se.o, seb.b1), (le.o, leb.b1)],
        ]
    )

    def attention_back_and_weights(r):
        long_encoder_back(r)
        r.leave("part", "dx")
        attention_weights.body(r, r.info[pairs + 2])

    lea = launch(
        attention_back_and_weights,
        {
            **saved(le, ("q", "k", "v")),
            "o": le.o,
            "lse": le.lse,
            **saved(leb, ("go", "d1")),
            **pick(encoder_in, ("w_in",)),
            **attention_weights.arrays,
        },
        {
            **attention_weights.gives,
            **parts(),
            **floats(rows_long, ("dx",)),
        },
        scratch=mix
        + [
            ("dq", pltpu.VMEM((rows_long, width), BF16)),
            ("dk", pltpu.VMEM((places, pairs, own, width), BF16)),
            ("dv", pltpu.VMEM((places, pairs, own, width), BF16)),
        ],
        info=source_info,
        after=(leb.small, attention.held[0]),
        pieces=("kept", "sent"),
        cost=19,
    )
    done = lea.dx
    finish([decoder_ffn, encoder_ffn, target_back], done)
    encoder = Chain([lea.kept, lea.sent], (INNER, X, OUTER), small, True)
    go(decoder_ffn, encoder_ffn, target_back)
    square = (3, width, width)
    feed = {"up": encoder_up.shape, "down": encoder_down.shape}
    one = {"project": square, "output": square[1:]}
    two = {"cross_in": square, "cross_out": square[1:], "self_in": square, "self_out": square[1:]}

    def out(shapes):
        return lambda chain, token: assemble(chain, core_info, shapes, token)

    rows_out = lambda rows: lambda chain, token: [chain.result().astype(F32) + rows]
    flights = [
        (encoder, 0.0, out(one)),
        (decoder_ffn, 0.0, out(feed)),
        (attention, 20.0, out(two)),
        (encoder_ffn, 0.0, out(feed)),
        (target_back, 0.0, rows_out(lsb.dt.reshape(source_long.shape))),
    ]

    def source_back(token):
        chain = Spread(hold(lea.part, token), False)
        return chain, 0.0, rows_out(lea.dx.reshape(source_long.shape))

    results = run_out(flights, source_back)
    (encoder_in_out, encoder_out_out), (decoder_up_out, decoder_down_out) = results[:2]
    (cross_in, cross_out, self_in, self_out), (encoder_up_out, encoder_down_out) = results[2:4]
    (grad_target,), (grad_source,) = results[4:]
    small = encoder.small.astype(F32)
    return (
        sc.final.reshape(source_short.shape),
        lc.final.reshape(source_long.shape),
        seb.dx.reshape(source_short.shape),
        sb.dt.reshape(source_short.shape),
        grad_source,
        grad_target,
        encoder_in_out,
        encoder_out_out,
        encoder_up_out,
        encoder_down_out,
        small[0:2],
        small[2:4],
        self_in,
        self_out,
        cross_in,
        cross_out,
        decoder_up_out,
        decoder_down_out,
        jnp.stack([small[4], small[6], small[7]]),
        jnp.stack([small[5], small[8], small[9]]),
    )


def solution(mesh):
    group, seq = mesh.devices.shape
    fine = Mesh(
        mesh.devices.reshape(group // 2, 2, 4, seq // 4), (X, CORE, OUTER, INNER)
    )
    groups, positions = (X, CORE), (OUTER, INNER)
    blocks = P(groups + positions, None, None)
    long_rows = P(groups, positions, None)
    in_specs = (
        (blocks, blocks, P(groups + positions, None), P(groups + positions, None))
        + (long_rows, long_rows, P(groups), P(groups), blocks, long_rows)
        + (P(),) * 14
    )
    out_specs = (blocks, long_rows, blocks, blocks, long_rows, long_rows) + (P(),) * 14
    return jax.shard_map(
        shards, mesh=fine, in_specs=in_specs, out_specs=out_specs, check_vma=False
    )
```

time: 1240 us -> 499 us (0.40)
  matrix products: 301 us -> 0 us
  waiting for transfers between devices: 436 us -> 151 us
  blocking collectives: 235 us -> 0 us
  Pallas kernels: 0 us -> 208 us
  local copies, waits for them, and re-layouts: 176 us -> 14.7 us
  starting transfers between devices: 0.72 us -> 73.7 us
  other arithmetic: 61.8 us -> 26 us
    psum x1 -> x0, waiting for transfers between devices: 404 us -> none  [shards(): summed = lax.psum(local_grads, ('group', 'seq'))]
    dot_general x132 -> x0, matrix products: 301 us -> none  [the longest x32 52.4 us: outer_sum(): jnp.einsum('bsd,bse->de', left_rows, right_rows, preferred_element_type=j...]
    pallas_call x0 -> x17, Pallas kernels: none -> 208 us  [launch(): pl.pallas_call(run, in_specs=specs, out_specs=[far if name in moved_out e...]
    all_gather x6 -> x0, blocking collectives: 195 us -> none  [the longest x3 97.8 us: attend_backward(): lax.all_gather(own_rows[2], 'seq', axis=1, tiled=True)]
    ppermute x0 -> x58, waiting for transfers between devices: none -> 138 us  [send(): return lax.ppermute(piece, axis, [(i, i ^ offset) for i in range(count)])]
    ppermute x0 -> x58, starting transfers between devices: none -> 73.6 us  [send(): return lax.ppermute(piece, axis, [(i, i ^ offset) for i in range(count)])]
    convert_element_type x30 -> x0, local copies, waits for them, and re-layouts: 61.6 us -> none  [the longest x3 11.2 us: attend_backward(): piece_queries = pieces[0].astype(jnp.bfloat16)]
    unnamed x618 -> x58, local copies, waits for them, and re-layouts: 65.1 us -> 4.97 us
  transfers between devices with their start and end apart: 13 -> 60, of which waited for: 2 -> 24; matrix products, arithmetic and copies ran while one was open for 36% -> 7% of each run, Pallas kernels for 0% -> 31%
where the time goes in v1:
time: 499 us; the launch traced here: 490 us
  Pallas kernels  208 us (42%)
  waiting for transfers between devices  151 us (30%)
  starting transfers between devices  73.7 us (15%)
  other arithmetic  26 us (5%)
  between operations  15.5 us (3%)
  local copies, waits for them, and re-layouts  14.7 us (3%)
    pallas_call x17, Pallas kernels, launch(): pl.pallas_call(run, in_specs=specs, out_specs=[far if name in moved_out e...  208 us
    ppermute x58, waiting for transfers between devices, send(): return lax.ppermute(piece, axis, [(i, i ^ offset) for i in range(count)])  138 us
    ppermute x58, starting transfers between devices, send(): return lax.ppermute(piece, axis, [(i, i ^ offset) for i in range(count)])  73.6 us
    all_gather x2, waiting for transfers between devices, gather_early(): return lax.all_gather(rows, (OUTER, INNER), axis=0, tiled=False)  13.2 us
    convert_element_type x26, other arithmetic, added(): return total.astype(BF16)  12.5 us
  transfers between devices with their start and end apart: 60, of which 24 were waited for; matrix products, arithmetic and copies ran while one was open for 7% of the time, Pallas kernels for 31%

profile of v1, /device:TPU:0, one launch (start us, length us, event | category | flops | bytes accessed | tf_op | source)
XLA Modules:
  0.0 489.6 jit_solution(15377059156458454207)
XLA Ops:
  9.5 11.3 %shard_map.383 = (bf16[512,512]{1,0:T(8,128)(2,1)}, bf16[512,512]{1,0:T(8,128)(2,1)}, bf16[512,512]{1,0:T(8,128)(2,1)}, bf16[512,512]{1,0:T(8,128)(2,1)}, f32[4,...) custom-call(bf16[512,512]{1,0:T(8,128)(2,1)} %bitcast.99, ...), custom_call_target="tpu_custom_call" | custom-call | flops 11000000 | bytes 35000 | tf_op jit(solution)/shard_map/pallas_call | solution.py:423
  21.7 7.4 %shard_map.384 = (bf16[512,512]{1,0:T(8,128)(2,1)}, bf16[512,512]{1,0:T(8,128)(2,1)}, bf16[512,512]{1,0:T(8,128)(2,1)}, bf16[512,512]{1,0:T(8,128)(2,1)}, bf16[5...) custom-call(bf16[512,512]{1,0:T(8,128)(2,1)} %bitcast.95, ...), custom_call_target="tpu_custom_call" | custom-call | flops 11000000 | bytes 35000 | tf_op jit(solution)/shard_map/pallas_call | solution.py:423
  29.1 5.1 %collective-permute-start.2 = (bf16[1,1,2,128,512]{4,3,2,1,0:T(8,128)(2,1)S(1)}, bf16[1,1,2,128,512]{4,3,2,1,0:T(8,128)(2,1)S(1)}, u32[]{:S(2)}, u32[]{:S(2)}) collective-permute-start(bf16[1,1,2,128,512]{4,3,2,1,0:T(8,128)(2,1)S(1)} %bitcast.107), channel_id=1, source_target_pairs={{0,6},{2,4},{4,2},{6,0},{1,7},{3,5},{5,3},{7,1},{8,14},{10,12},{12... | collective-permute-start | bytes 786440 | tf_op jit(solution)/shard_map/ppermute | solution.py:730
  35.5 14.6 %shard_map.385 = (bf16[512,512]{1,0:T(8,128)(2,1)}, bf16[512,512]{1,0:T(8,128)(2,1)}, bf16[512,512]{1,0:T(8,128)(2,1)}, bf16[512,512]{1,0:T(8,128)(2,1)}, f32[4,...) custom-call(bf16[512,512]{1,0:T(8,128)(2,1)} %get-tuple-element.250., ...), custom_call_target="tpu_custom_call" | custom-call | flops 11000000 | bytes 35000 | tf_op jit(solution)/shard_map/pallas_call | solution.py:423
  50.1 16.3 %shard_map.386 = (bf16[512,512]{1,0:T(8,128)(2,1)}, bf16[512,512]{1,0:T(8,128)(2,1)}, bf16[512,512]{1,0:T(8,128)(2,1)}, bf16[512,512]{1,0:T(8,128)(2,1)}, bf16[5...) custom-call(bf16[512,512]{1,0:T(8,128)(2,1)} %get-tuple-element.255., ...), custom_call_target="tpu_custom_call" | custom-call | flops 11000000 | bytes 35000 | tf_op jit(solution)/shard_map/pallas_call | solution.py:423
  66.4 7.7 %collective-permute-done.1 = bf16[1,1,2,128,512]{4,3,2,1,0:T(8,128)(2,1)S(1)} collective-permute-done((bf16[1,1,2,128,512]{4,3,2,1,0:T(8,128)(2,1)S(1)}, bf16[1,1,2,128,512]{4,3,2,1,0:T(8,128)(2,1)S(1)}, u32[]{:S(2)}, u32[]{:S(2)}) %collective-permute-start.1) | collective-permute-done | bytes 262176 | tf_op jit(solution)/shard_map/ppermute | solution.py:730
  75.3 15.1 %shard_map.387 = (bf16[256,512]{1,0:T(8,128)(2,1)}, bf16[256,512]{1,0:T(8,128)(2,1)}, bf16[8,2,128,512]{3,2,1,0:T(8,128)(2,1)}, bf16[8,2,128,512]{3,2,1,0:T(8,12...) custom-call(s32[6]{0:T(128)} %concatenate.236.refs_0_, ...), custom_call_target="tpu_custom_call" | custom-call | flops 14300000256 | bytes 45500000 | tf_op jit(solution)/shard_map/pallas_call | solution.py:423
  92.3 15.9 %shard_map.388 = (bf16[512,512]{1,0:T(8,128)(2,1)}, bf16[512,512]{1,0:T(8,128)(2,1)}, bf16[512,512]{1,0:T(8,128)(2,1)}, bf16[512,512]{1,0:T(8,128)(2,1)}, bf16[5...) custom-call(f32[512,512]{1,0:T(8,128)} %get-tuple-element.277.refs_0, ...), custom_call_target="tpu_custom_call" | custom-call | flops 17600000000 | bytes 56000000 | tf_op jit(solution)/shard_map/pallas_call | solution.py:423
  108.3 10.3 %collective-permute-done.3 = bf16[4,1,2,128,512]{4,3,2,1,0:T(8,128)(2,1)S(1)} collective-permute-done((bf16[4,1,2,128,512]{4,3,2,1,0:T(8,128)(2,1)S(1)}, bf16[4,1,2,128,512]{4,3,2,1,0:T(8,128)(2,1)S(1)}, u32[]{:S(2)}, u32[]{:S(2)}) %collective-permute-start.3) | collective-permute-done | bytes 1048608 | tf_op jit(solution)/shard_map/ppermute | solution.py:730
  118.6 1.6 maximum_select_fusion
  120.2 7.8 %shard_map.389 = (bf16[256,512]{1,0:T(8,128)(2,1)}, bf16[256,512]{1,0:T(8,128)(2,1)}, bf16[256,512]{1,0:T(8,128)(2,1)}, bf16[256,512]{1,0:T(8,128)(2,1)}, bf16[2...) custom-call(s32[6]{0:T(128)} %concatenate.249.refs_0_, ...), custom_call_target="tpu_custom_call" | custom-call | flops 11000000512 | bytes 35000000 | tf_op jit(solution)/shard_map/pallas_call | solution.py:423
  128.0 13.2 %all-gather.4.cloned.1.call-done.refs_1_ = bf16[8,2,128,512]{3,2,1,0:T(8,128)(2,1)} async-done(((bf16[1,2,128,512]{3,2,1,0:T(8,128)(2,1)}), bf16[8,2,128,512]{3,2,1,0:T(8,128)(2,1)}) %all-gather.4.cloned.1.call-update) | async-done | bytes 2097168 | tf_op jit(solution)/shard_map/all_gather | solution.py:786
  141.1 16.5 %shard_map.390 = (bf16[256,512]{1,0:T(8,128)(2,1)}, bf16[8,2,128,512]{3,2,1,0:T(8,128)(2,1)}, bf16[8,2,128,512]{3,2,1,0:T(8,128)(2,1)}, f32[2,8,128]{2,1,0:T(8,1...) custom-call(s32[6]{0:T(128)} %concatenate.236.refs_0_, ...), custom_call_target="tpu_custom_call" | custom-call | flops 15399999488 | bytes 49000000 | tf_op jit(solution)/shard_map/pallas_call | solution.py:423
  157.7 16.5 %shard_map.391 = (bf16[256,512]{1,0:T(8,128)(2,1)}, bf16[8,2,128,512]{3,2,1,0:T(8,128)(2,1)}, bf16[8,2,128,512]{3,2,1,0:T(8,128)(2,1)}, bf16[2,4,2,128,512]{4,3,2,1,0:T(8,128)(2,1)}) custom-call(s32[6]{0:T(128)} %concatenate.236.refs_0_, bf16[256,512]{1,0:T(8,128)(2,1)} %get-tuple-element.294.refs_3_.refs_1_, ...), custom_call_target="tpu_custom_call" | custom-call | flops 15399999488 | bytes 49000000 | tf_op jit(solution)/shard_map/pallas_call | solution.py:423
  174.2 1.7 slice_bitcast_fusion.4
  176.6 17.6 %shard_map.392 = (bf16[8,256,512]{2,1,0:T(8,128)(2,1)}, bf16[8,256,512]{2,1,0:T(8,128)(2,1)}, bf16[256,512]{1,0:T(8,128)(2,1)}, bf16[256,512]{1,0:T(8,128)(2,1)}...) custom-call(s32[6]{0:T(128)} %concatenate.249.refs_0_, ...), custom_call_target="tpu_custom_call" | custom-call | flops 24199999488 | bytes 77000000 | tf_op jit(solution)/shard_map/pallas_call | solution.py:423
  194.2 2.7 slice_bitcast_fusion
  197.0 2.9 collective-permute-done.4
  200.8 5.5 %collective-permute-start.7 = (bf16[2,128,512]{2,1,0:T(8,128)(2,1)S(1)}, bf16[2,128,512]{2,1,0:T(8,128)(2,1)S(1)}, u32[]{:S(2)}, u32[]{:S(2)}) collective-permute-start(bf16[2,128,512]{2,1,0:T(8,128)(2,1)S(1)} %get-tuple-element.496), channel_id=1, source_target_pairs={{0,6},{2,4},{4,2},{6,0},{1,7},{3,5},{5,3},{7,1},{8,14},{10,12},{12... | collective-permute-start | bytes 786440 | tf_op jit(solution)/shard_map/ppermute | solution.py:730
  206.9 14.4 %shard_map.393 = (bf16[8,256,512]{2,1,0:T(8,128)(2,1)}, bf16[8,256,512]{2,1,0:T(8,128)(2,1)}) custom-call(s32[1]{0:T(128)} %bitcast.8.refs_0_, bf16[512,512]{1,0:T(8,128)(2,1)} %get-tuple-element.250.refs_0_.refs_1_, bf16[512,512]{1,0:T(8,128)(2,1)} %get-tuple-element.330.refs_2_, bf16[256,512]{1,0:T(8,128)(2,1)} %get-tuple-element.331.refs_3_, ...), custom_call_target="tpu_custom_call" | custom-call | flops 16499999744 | bytes 52500000 | tf_op jit(solution)/shard_map/pallas_call | solution.py:423
  221.4 1.6 collective-permute-start.15
  223.0 4.8 collective-permute-done.6
  227.8 2.0 add_convert_fusion.2
  230.0 12.5 %shard_map.394 = (bf16[8,256,512]{2,1,0:T(8,128)(2,1)}, bf16[8,256,512]{2,1,0:T(8,128)(2,1)}, bf16[256,512]{1,0:T(8,128)(2,1)}, bf16[256,512]{1,0:T(8,128)(2,1)}...) custom-call(s32[1]{0:T(128)} %bitcast.8.refs_0_, ...), custom_call_target="tpu_custom_call" | custom-call | flops 13200000000 | bytes 42000000 | tf_op jit(solution)/shard_map/pallas_call | solution.py:423
  243.3 3.5 add_convert_fusion.3
  248.3 20.5 %shard_map.395 = (bf16[4,256,512]{2,1,0:T(8,128)(2,1)}, bf16[4,256,512]{2,1,0:T(8,128)(2,1)}, bf16[2,4,2,128,512]{4,3,2,1,0:T(8,128)(2,1)}, f32[256,512]{1,0:T(8,128)}) custom-call(s32[6]{0:T(128)} %concatenate.236.refs_0_, bf16[256,512]{1,0:T(8,128)(2,1)} %get-tuple-element.298.refs_1_, bf16[8,2,128,512]{3,2,1,0:T(8,128)(2,1)} %get-tuple-element.299.refs_2_, ...), custom_call_target="tpu_custom_call" | custom-call | flops 20899999744 | bytes 66500000 | tf_op jit(solution)/shard_map/pallas_call | solution.py:423
  268.8 1.8 pad_maximum_fusion
  273.6 1.5 add_convert_fusion.13
  278.0 12.0 %collective-permute-done.18 = bf16[8,64,512]{2,1,0:T(8,128)(2,1)S(1)} collective-permute-done((bf16[8,64,512]{2,1,0:T(8,128)(2,1)S(1)}, bf16[8,64,512]{2,1,0:T(8,128)(2,1)S(1)}, u32[]{:S(2)}, u32[]{:S(2)}) %collective-permute-start.18) | collective-permute-done | bytes 524320 | tf_op jit(solution)/shard_map/ppermute | solution.py:730
  290.2 2.7 collective-permute-start.23
  292.9 4.2 collective-permute-done.17
  297.4 3.3 collective-permute-start.21
  301.2 4.5 collective-permute-done.22
  307.2 1.5 collective-permute-start.19
  309.0 2.0 collective-permute-start.33
  311.0 1.7 collective-permute-start.32
  312.7 12.1 %collective-permute-done.25 = bf16[2,128,512]{2,1,0:T(8,128)(2,1)S(1)} collective-permute-done((bf16[2,128,512]{2,1,0:T(8,128)(2,1)S(1)}, bf16[2,128,512]{2,1,0:T(8,128)(2,1)S(1)}, u32[]{:S(2)}, u32[]{:S(2)}) %collective-permute-start.25) | collective-permute-done | bytes 262176 | tf_op jit(solution)/shard_map/ppermute | solution.py:730
  326.3 2.1 collective-permute-start.30
  328.6 1.8 collective-permute-done.32
  330.4 2.8 collective-permute-done.31
  333.2 2.7 collective-permute-start.28
  335.9 1.7 collective-permute-start.26
  338.0 4.8 collective-permute-done.30
  343.9 1.5 collective-permute-start.11
  346.5 8.0 %collective-permute-start.41 = (bf16[8,16,512]{2,1,0:T(8,128)(2,1)S(1)}, bf16[8,16,512]{2,1,0:T(8,128)(2,1)S(1)}, u32[]{:S(2)}, u32[]{:S(2)}) collective-permute-start(bf16[8,16,512]{2,1,0:T(8,128)(2,1)S(1)} %get-tuple-element.512), channel_id=1, source_target_pairs={{0,6},{2,4},{4,2},{6,0},{1,7},{3,5},{5,3},{7,1},{8,14},{10,12},{12... | collective-permute-start | bytes 393224 | tf_op jit(solution)/shard_map/ppermute | solution.py:730
  354.5 8.8 %collective-permute-done.37 = bf16[272,512]{1,0:T(8,128)(2,1)S(1)} collective-permute-done((bf16[272,512]{1,0:T(8,128)(2,1)S(1)}, bf16[272,512]{1,0:T(8,128)(2,1)S(1)}, u32[]{:S(2)}, u32[]{:S(2)}) %collective-permute-start.37) | collective-permute-done | bytes 278560 | tf_op jit(solution)/shard_map/ppermute | solution.py:730
  364.5 2.8 collective-permute-start.36
  367.2 2.3 collective-permute-done.40
  369.6 4.6 collective-permute-done.39
  374.1 3.8 collective-permute-start.34
  379.8 3.2 collective-permute-start.44
  383.0 4.0 collective-permute-start.49
  389.2 2.7 collective-permute-done.45
  392.3 6.7 %collective-permute-done.50 = bf16[4,128,512]{2,1,0:T(8,128)(2,1)S(1)} collective-permute-done((bf16[4,128,512]{2,1,0:T(8,128)(2,1)S(1)}, bf16[4,128,512]{2,1,0:T(8,128)(2,1)S(1)}, u32[]{:S(2)}, u32[]{:S(2)}) %collective-permute-start.50) | collective-permute-done | bytes 524320 | tf_op jit(solution)/shard_map/ppermute | solution.py:730
  399.5 8.9 %collective-permute-done.49 = bf16[8,128,512]{2,1,0:T(8,128)(2,1)S(1)} collective-permute-done((bf16[8,128,512]{2,1,0:T(8,128)(2,1)S(1)}, bf16[8,128,512]{2,1,0:T(8,128)(2,1)S(1)}, u32[]{:S(2)}, u32[]{:S(2)}) %collective-permute-start.49) | collective-permute-done | bytes 1048608 | tf_op jit(solution)/shard_map/ppermute | solution.py:730
  409.2 1.8 collective-permute-start.48
  411.6 11.9 %collective-permute-done.48 = bf16[8,64,512]{2,1,0:T(8,128)(2,1)S(1)} collective-permute-done((bf16[8,64,512]{2,1,0:T(8,128)(2,1)S(1)}, bf16[8,64,512]{2,1,0:T(8,128)(2,1)S(1)}, u32[]{:S(2)}, u32[]{:S(2)}) %collective-permute-start.48) | collective-permute-done | bytes 524320 | tf_op jit(solution)/shard_map/ppermute | solution.py:730
  429.7 3.8 shard_map.396
  433.5 6.1 %shard_map.397 = (f32[512,2048]{1,0:T(8,128)}, f32[2048,512]{1,0:T(8,128)}) custom-call(s32[1]{0:T(128)} %bitcast.8.refs_0_, bf16[8,256,512]{2,1,0:T(8,128)(2,1)} %copy-done.7, bf16[8,256,512]{2,1,0:T(8,128)(2,1)} %copy-done.23, f32[3,512,512]{2,1,0:T(8,128)} %get-tuple-element.235.refs_3_), custom_call_target="tpu_custom_call" | custom-call | flops 5500000256 | bytes 17500000 | tf_op jit(solution)/shard_map/pallas_call | solution.py:423
  439.7 9.1 %collective-permute-done.52 = bf16[8,128,512]{2,1,0:T(8,128)(2,1)S(1)} collective-permute-done((bf16[8,128,512]{2,1,0:T(8,128)(2,1)S(1)}, bf16[8,128,512]{2,1,0:T(8,128)(2,1)S(1)}, u32[]{:S(2)}, u32[]{:S(2)}) %collective-permute-start.52) | collective-permute-done | bytes 1048608 | tf_op jit(solution)/shard_map/ppermute | solution.py:730
  449.7 3.5 collective-permute-start.51
  453.2 12.1 %collective-permute-done.51 = bf16[2,128,512]{2,1,0:T(8,128)(2,1)S(1)} collective-permute-done((bf16[2,128,512]{2,1,0:T(8,128)(2,1)S(1)}, bf16[2,128,512]{2,1,0:T(8,128)(2,1)S(1)}, u32[]{:S(2)}, u32[]{:S(2)}) %collective-permute-start.51) | collective-permute-done | bytes 262176 | tf_op jit(solution)/shard_map/ppermute | solution.py:730
  470.3 5.9 %shard_map.398 = (f32[3,512,512]{2,1,0:T(8,128)}, f32[512,512]{1,0:T(8,128)}, f32[3,512,512]{2,1,0:T(8,128)}, f32[512,512]{1,0:T(8,128)}) custom-call(s32[1]{0:T(128)} %bitcast.8.refs_0_, bf16[8,256,512]{2,1,0:T(8,128)(2,1)} %copy-done.8, bf16[8,256,512]{2,1,0:T(8,128)(2,1)} %copy-done.24, bf16[8,256,512]{2,1,0:T(8,128)(2,1)} %copy-done.8, ...), custom_call_target="tpu_custom_call" | custom-call | flops 5500000256 | bytes 17500000 | tf_op jit(solution)/shard_map/pallas_call | solution.py:423
  476.2 6.1 %shard_map.399 = (f32[512,2048]{1,0:T(8,128)}, f32[2048,512]{1,0:T(8,128)}) custom-call(s32[1]{0:T(128)} %bitcast.8.refs_0_, bf16[8,256,512]{2,1,0:T(8,128)(2,1)} %copy-done.9, bf16[8,256,512]{2,1,0:T(8,128)(2,1)} %collective-permute-done.56.refs_2_.refs_4_, bf16[8,256,512]{2,1,0:T(8,128)(2,1)} %copy-done.9, ...), custom_call_target="tpu_custom_call" | custom-call | flops 5500000256 | bytes 17500000 | tf_op jit(solution)/shard_map/pallas_call | solution.py:423
  (208 shorter events, 44.5 us)
Async XLA Ops:
  7.2 68.1 %all-gather.6.cloned.1.call-start = ((), (), s32[]{:S(2)}) async-start(), calls=%async_computation.1 | async-start | bytes 2359296 | tf_op jit(solution)/shard_map/all_gather | solution.py:786
  7.9 133.2 %all-gather.4.cloned.1.call-start = ((), (), s32[]{:S(2)}) async-start(), calls=%async_computation | async-start | bytes 2359296 | tf_op jit(solution)/shard_map/all_gather | solution.py:786
  29.1 37.3 %collective-permute-start.2 = (bf16[1,1,2,128,512]{4,3,2,1,0:T(8,128)(2,1)S(1)}, bf16[1,1,2,128,512]{4,3,2,1,0:T(8,128)(2,1)S(1)}, u32[]{:S(2)}, u32[]{:S(2)}) collective-permute-start(bf16[1,1,2,128,512]{4,3,2,1,0:T(8,128)(2,1)S(1)} %bitcast.107), channel_id=1, source_target_pairs={{0,6},{2,4},{4,2},{6,0},{1,7},{3,5},{5,3},{7,1},{8,14},{10,12},{12... | collective-permute-start | bytes 786440 | tf_op jit(solution)/shard_map/ppermute | solution.py:730
  34.2 39.8 %collective-permute-start.1 = (bf16[1,1,2,128,512]{4,3,2,1,0:T(8,128)(2,1)S(1)}, bf16[1,1,2,128,512]{4,3,2,1,0:T(8,128)(2,1)S(1)}, u32[]{:S(2)}, u32[]{:S(2)}) collective-permute-start(bf16[1,1,2,128,512]{4,3,2,1,0:T(8,128)(2,1)S(1)} %bitcast.108), channel_id=1, source_target_pairs={{0,4},{2,6},{4,0},{6,2},{1,5},{3,7},{5,1},{7,3},{8,12},{10,14},{12... | collective-permute-start | bytes 786440 | tf_op jit(solution)/shard_map/ppermute | solution.py:730
  34.2 39.8 %collective-permute-start = (bf16[1,1,2,128,512]{4,3,2,1,0:T(8,128)(2,1)S(1)}, bf16[1,1,2,128,512]{4,3,2,1,0:T(8,128)(2,1)S(1)}, u32[]{:S(2)}, u32[]{:S(2)}) collective-permute-start(bf16[1,1,2,128,512]{4,3,2,1,0:T(8,128)(2,1)S(1)} %bitcast.109), channel_id=1, source_target_pairs={{0,2},{2,0},{4,6},{6,4},{1,3},{3,1},{5,7},{7,5},{8,10},{10,8},{12,... | collective-permute-start | bytes 786440 | tf_op jit(solution)/shard_map/ppermute | solution.py:730
  91.1 27.5 %collective-permute-start.3 = (bf16[4,1,2,128,512]{4,3,2,1,0:T(8,128)(2,1)S(1)}, bf16[4,1,2,128,512]{4,3,2,1,0:T(8,128)(2,1)S(1)}, u32[]{:S(2)}, u32[]{:S(2)}) collective-permute-start(bf16[4,1,2,128,512]{4,3,2,1,0:T(8,128)(2,1)S(1)} %copy-done), channel_id=1, source_target_pairs={{0,1},{1,0},{2,3},{3,2},{4,5},{5,4},{6,7},{7,6},{8,9},{9,8},{10,11... | collective-permute-start | bytes 3145736 | tf_op jit(solution)/shard_map/ppermute | solution.py:730
  176.0 23.9 %collective-permute-start.4 = (bf16[4,2,128,512]{3,2,1,0:T(8,128)(2,1)S(1)}, bf16[4,2,128,512]{3,2,1,0:T(8,128)(2,1)S(1)}, u32[]{:S(2)}, u32[]{:S(2)}) collective-permute-start(bf16[4,2,128,512]{3,2,1,0:T(8,128)(2,1)S(1)} %get-tuple-element.500), channel_id=1, source_target_pairs={{0,1},{1,0},{2,3},{3,2},{4,5},{5,4},{6,7},{7,6},{8,9},{9,8},{10,11... | collective-permute-start | bytes 3145736 | tf_op jit(solution)/shard_map/ppermute | solution.py:730
  194.2 33.7 %collective-permute-start.8 = (bf16[8,256,512]{2,1,0:T(8,128)(2,1)}, bf16[8,256,512]{2,1,0:T(8,128)(2,1)S(1)}, u32[]{:S(2)}, u32[]{:S(2)}) collective-permute-start(bf16[8,256,512]{2,1,0:T(8,128)(2,1)} %get-tuple-element.329), channel_id=1, source_target_pairs={{0,8},{8,0},{1,9},{9,1},{2,10},{10,2},{3,11},{11,3},{4,12},{12,4},... | collective-permute-start | bytes 6291464 | tf_op jit(solution)/shard_map/ppermute | solution.py:730
  200.8 20.6 %collective-permute-start.7 = (bf16[2,128,512]{2,1,0:T(8,128)(2,1)S(1)}, bf16[2,128,512]{2,1,0:T(8,128)(2,1)S(1)}, u32[]{:S(2)}, u32[]{:S(2)}) collective-permute-start(bf16[2,128,512]{2,1,0:T(8,128)(2,1)S(1)} %get-tuple-element.496), channel_id=1, source_target_pairs={{0,6},{2,4},{4,2},{6,0},{1,7},{3,5},{5,3},{7,1},{8,14},{10,12},{12... | collective-permute-start | bytes 786440 | tf_op jit(solution)/shard_map/ppermute | solution.py:730
  206.3 21.5 %collective-permute-start.6 = (bf16[2,128,512]{2,1,0:T(8,128)(2,1)S(1)}, bf16[2,128,512]{2,1,0:T(8,128)(2,1)S(1)}, u32[]{:S(2)}, u32[]{:S(2)}) collective-permute-start(bf16[2,128,512]{2,1,0:T(8,128)(2,1)S(1)} %get-tuple-element.497), channel_id=1, source_target_pairs={{0,4},{2,6},{4,0},{6,2},{1,5},{3,7},{5,1},{7,3},{8,12},{10,14},{12... | collective-permute-start | bytes 786440 | tf_op jit(solution)/shard_map/ppermute | solution.py:730
  206.3 21.5 %collective-permute-start.5 = (bf16[2,128,512]{2,1,0:T(8,128)(2,1)S(1)}, bf16[2,128,512]{2,1,0:T(8,128)(2,1)S(1)}, u32[]{:S(2)}, u32[]{:S(2)}) collective-permute-start(bf16[2,128,512]{2,1,0:T(8,128)(2,1)S(1)} %get-tuple-element.498), channel_id=1, source_target_pairs={{0,2},{2,0},{4,6},{6,4},{1,3},{3,1},{5,7},{7,5},{8,10},{10,8},{12,... | collective-permute-start | bytes 786440 | tf_op jit(solution)/shard_map/ppermute | solution.py:730
  206.9 21.0 %copy-start.4 = (bf16[8,256,512]{2,1,0:T(8,128)(2,1)S(1)}, bf16[8,256,512]{2,1,0:T(8,128)(2,1)}, u32[]{:S(2)}) copy-start(bf16[8,256,512]{2,1,0:T(8,128)(2,1)} %get-tuple-element.362) | copy-start | bytes 6291460
  221.2 22.1 %collective-permute-start.9 = (bf16[8,256,512]{2,1,0:T(8,128)(2,1)}, bf16[8,256,512]{2,1,0:T(8,128)(2,1)}, u32[]{:S(2)}, u32[]{:S(2)}) collective-permute-start(bf16[8,256,512]{2,1,0:T(8,128)(2,1)} %get-tuple-element.372), channel_id=1, source_target_pairs={{0,8},{8,0},{1,9},{9,1},{2,10},{10,2},{3,11},{11,3},{4,12},{12,4},... | collective-permute-start | bytes 6291464 | tf_op jit(solution)/shard_map/ppermute | solution.py:730
  221.4 49.5 %collective-permute-start.15 = (bf16[4,2,128,512]{3,2,1,0:T(8,128)(2,1)}, bf16[4,2,128,512]{3,2,1,0:T(8,128)(2,1)S(1)}, u32[]{:S(2)}, u32[]{:S(2)}) collective-permute-start(bf16[4,2,128,512]{3,2,1,0:T(8,128)(2,1)} %get-tuple-element.492), channel_id=1, source_target_pairs={{0,1},{1,0},{2,3},{3,2},{4,5},{5,4},{6,7},{7,6},{8,9},{9,8},{10,11... | collective-permute-start | bytes 3145736 | tf_op jit(solution)/shard_map/ppermute | solution.py:730
  229.9 41.1 %collective-permute-start.13 = (bf16[8,128,512]{2,1,0:T(8,128)(2,1)}, bf16[8,128,512]{2,1,0:T(8,128)(2,1)}, u32[]{:S(2)}, u32[]{:S(2)}) collective-permute-start(bf16[8,128,512]{2,1,0:T(8,128)(2,1)} %get-tuple-element.480), channel_id=1, source_target_pairs={{0,16},{16,0},{1,17},{17,1},{2,18},{18,2},{3,19},{19,3},{4,20},{20... | collective-permute-start | bytes 3145736 | tf_op jit(solution)/shard_map/ppermute | solution.py:730
  242.5 28.4 %collective-permute-start.14 = (bf16[8,256,512]{2,1,0:T(8,128)(2,1)}, bf16[8,256,512]{2,1,0:T(8,128)(2,1)S(1)}, u32[]{:S(2)}, u32[]{:S(2)}) collective-permute-start(bf16[8,256,512]{2,1,0:T(8,128)(2,1)} %get-tuple-element.382), channel_id=1, source_target_pairs={{0,8},{8,0},{1,9},{9,1},{2,10},{10,2},{3,11},{11,3},{4,12},{12,4},... | collective-permute-start | bytes 6291464 | tf_op jit(solution)/shard_map/ppermute | solution.py:730
  246.8 54.0 %collective-permute-start.12 = (bf16[8,128,512]{2,1,0:T(8,128)(2,1)}, bf16[8,128,512]{2,1,0:T(8,128)(2,1)S(1)}, u32[]{:S(2)}, u32[]{:S(2)}) collective-permute-start(bf16[8,128,512]{2,1,0:T(8,128)(2,1)} %get-tuple-element.482), channel_id=1, source_target_pairs={{0,1},{1,0},{2,3},{3,2},{4,5},{5,4},{6,7},{7,6},{8,9},{9,8},{10,11... | collective-permute-start | bytes 3145736 | tf_op jit(solution)/shard_map/ppermute | solution.py:730
  270.6 5.2 %collective-permute-start.10 = (bf16[1040,512]{1,0:T(8,128)(2,1)S(1)}, bf16[1040,512]{1,0:T(8,128)(2,1)S(1)}, u32[]{:S(2)}, u32[]{:S(2)}) collective-permute-start(bf16[1040,512]{1,0:T(8,128)(2,1)S(1)} %get-tuple-element.546), channel_id=1, source_target_pairs={{0,8},{8,0},{1,9},{9,1},{2,10},{10,2},{3,11},{11,3},{4,12},{12,4},... | collective-permute-start | bytes 3194888 | tf_op jit(solution)/shard_map/ppermute | solution.py:730
  271.7 25.4 %collective-permute-start.17 = (bf16[8,128,512]{2,1,0:T(8,128)(2,1)S(1)}, bf16[8,128,512]{2,1,0:T(8,128)(2,1)S(1)}, u32[]{:S(2)}, u32[]{:S(2)}) collective-permute-start(bf16[8,128,512]{2,1,0:T(8,128)(2,1)S(1)} %get-tuple-element.478), channel_id=1, source_target_pairs={{0,16},{16,0},{1,17},{17,1},{2,18},{18,2},{3,19},{19,3},{4,20},{20... | collective-permute-start | bytes 3145736 | tf_op jit(solution)/shard_map/ppermute | solution.py:730
  272.6 24.8 %collective-permute-start.16 = (bf16[2,2,128,512]{3,2,1,0:T(8,128)(2,1)S(1)}, bf16[2,2,128,512]{3,2,1,0:T(8,128)(2,1)S(1)}, u32[]{:S(2)}, u32[]{:S(2)}) collective-permute-start(bf16[2,2,128,512]{3,2,1,0:T(8,128)(2,1)S(1)} %add_convert_fusion.15), channel_id=1, source_target_pairs={{0,2},{2,0},{4,6},{6,4},{1,3},{3,1},{5,7},{7,5},{8,10},{10,8},{12,... | collective-permute-start | bytes 1572872 | tf_op jit(solution)/shard_map/ppermute | solution.py:730
  275.1 14.9 %collective-permute-start.18 = (bf16[8,64,512]{2,1,0:T(8,128)(2,1)S(1)}, bf16[8,64,512]{2,1,0:T(8,128)(2,1)S(1)}, u32[]{:S(2)}, u32[]{:S(2)}) collective-permute-start(bf16[8,64,512]{2,1,0:T(8,128)(2,1)S(1)} %get-tuple-element.490), channel_id=1, source_target_pairs={{0,1},{1,0},{2,3},{3,2},{4,5},{5,4},{6,7},{7,6},{8,9},{9,8},{10,11... | collective-permute-start | bytes 1572872 | tf_op jit(solution)/shard_map/ppermute | solution.py:730
  276.5 29.8 %collective-permute-start.20 = (bf16[528,512]{1,0:T(8,128)(2,1)S(1)}, bf16[528,512]{1,0:T(8,128)(2,1)S(1)}, u32[]{:S(2)}, u32[]{:S(2)}) collective-permute-start(bf16[528,512]{1,0:T(8,128)(2,1)S(1)} %get-tuple-element.544), channel_id=1, source_target_pairs={{0,1},{1,0},{2,3},{3,2},{4,5},{5,4},{6,7},{7,6},{8,9},{9,8},{10,11... | collective-permute-start | bytes 1622024 | tf_op jit(solution)/shard_map/ppermute | solution.py:730
  290.2 11.0 %collective-permute-start.23 = (bf16[8,16,512]{2,1,0:T(8,128)(2,1)S(1)}, bf16[8,16,512]{2,1,0:T(8,128)(2,1)S(1)}, u32[]{:S(2)}, u32[]{:S(2)}) collective-permute-start(bf16[8,16,512]{2,1,0:T(8,128)(2,1)S(1)} %get-tuple-element.524), channel_id=1, source_target_pairs={{0,6},{2,4},{4,2},{6,0},{1,7},{3,5},{5,3},{7,1},{8,14},{10,12},{12... | collective-permute-start | bytes 393224 | tf_op jit(solution)/shard_map/ppermute | solution.py:730
  297.1 8.6 %collective-permute-start.22 = (bf16[8,16,512]{2,1,0:T(8,128)(2,1)S(1)}, bf16[8,16,512]{2,1,0:T(8,128)(2,1)S(1)}, u32[]{:S(2)}, u32[]{:S(2)}) collective-permute-start(bf16[8,16,512]{2,1,0:T(8,128)(2,1)S(1)} %get-tuple-element.525), channel_id=1, source_target_pairs={{0,4},{2,6},{4,0},{6,2},{1,5},{3,7},{5,1},{7,3},{8,12},{10,14},{12... | collective-permute-start | bytes 393224 | tf_op jit(solution)/shard_map/ppermute | solution.py:730
  297.4 8.8 %collective-permute-start.21 = (bf16[8,16,512]{2,1,0:T(8,128)(2,1)S(1)}, bf16[8,16,512]{2,1,0:T(8,128)(2,1)S(1)}, u32[]{:S(2)}, u32[]{:S(2)}) collective-permute-start(bf16[8,16,512]{2,1,0:T(8,128)(2,1)S(1)} %get-tuple-element.526), channel_id=1, source_target_pairs={{0,2},{2,0},{4,6},{6,4},{1,3},{3,1},{5,7},{7,5},{8,10},{10,8},{12,... | collective-permute-start | bytes 393224 | tf_op jit(solution)/shard_map/ppermute | solution.py:730
  306.4 18.4 %collective-permute-start.25 = (bf16[2,128,512]{2,1,0:T(8,128)(2,1)S(1)}, bf16[2,128,512]{2,1,0:T(8,128)(2,1)S(1)}, u32[]{:S(2)}, u32[]{:S(2)}) collective-permute-start(bf16[2,128,512]{2,1,0:T(8,128)(2,1)S(1)} %get-tuple-element.520), channel_id=1, source_target_pairs={{0,4},{2,6},{4,0},{6,2},{1,5},{3,7},{5,1},{7,3},{8,12},{10,14},{12... | collective-permute-start | bytes 786440 | tf_op jit(solution)/shard_map/ppermute | solution.py:730
  306.7 19.0 %collective-permute-start.24 = (bf16[272,512]{1,0:T(8,128)(2,1)S(1)}, bf16[272,512]{1,0:T(8,128)(2,1)S(1)}, u32[]{:S(2)}, u32[]{:S(2)}) collective-permute-start(bf16[272,512]{1,0:T(8,128)(2,1)S(1)} %get-tuple-element.542), channel_id=1, source_target_pairs={{0,16},{16,0},{1,17},{17,1},{2,18},{18,2},{3,19},{19,3},{4,20},{20... | collective-permute-start | bytes 835592 | tf_op jit(solution)/shard_map/ppermute | solution.py:730
  307.2 17.6 %copy-start.12 = (f32[256,512]{1,0:T(8,128)S(1)}, f32[256,512]{1,0:T(8,128)}, u32[]{:S(2)}) copy-start(f32[256,512]{1,0:T(8,128)} %get-tuple-element.407) | copy-start | bytes 1572868
  307.2 19.1 %collective-permute-start.19 = (bf16[8,64,512]{2,1,0:T(8,128)(2,1)S(1)}, bf16[8,64,512]{2,1,0:T(8,128)(2,1)S(1)}, u32[]{:S(2)}, u32[]{:S(2)}) collective-permute-start(bf16[8,64,512]{2,1,0:T(8,128)(2,1)S(1)} %get-tuple-element.488), channel_id=1, source_target_pairs={{0,16},{16,0},{1,17},{17,1},{2,18},{18,2},{3,19},{19,3},{4,20},{20... | collective-permute-start | bytes 1572872 | tf_op jit(solution)/shard_map/ppermute | solution.py:730
  309.0 19.6 %collective-permute-start.33 = (bf16[8,16,512]{2,1,0:T(8,128)(2,1)S(1)}, bf16[8,16,512]{2,1,0:T(8,128)(2,1)S(1)}, u32[]{:S(2)}, u32[]{:S(2)}) collective-permute-start(bf16[8,16,512]{2,1,0:T(8,128)(2,1)S(1)} %add_convert_fusion.43), channel_id=1, source_target_pairs={{0,6},{2,4},{4,2},{6,0},{1,7},{3,5},{5,3},{7,1},{8,14},{10,12},{12... | collective-permute-start | bytes 393224 | tf_op jit(solution)/shard_map/ppermute | solution.py:730
  311.0 19.4 %collective-permute-start.32 = (bf16[8,16,512]{2,1,0:T(8,128)(2,1)S(1)}, bf16[8,16,512]{2,1,0:T(8,128)(2,1)S(1)}, u32[]{:S(2)}, u32[]{:S(2)}) collective-permute-start(bf16[8,16,512]{2,1,0:T(8,128)(2,1)S(1)} %add_convert_fusion.43), channel_id=1, source_target_pairs={{0,4},{2,6},{4,0},{6,2},{1,5},{3,7},{5,1},{7,3},{8,12},{10,14},{12... | collective-permute-start | bytes 393224 | tf_op jit(solution)/shard_map/ppermute | solution.py:730
  324.8 8.4 %collective-permute-start.31 = (bf16[8,16,512]{2,1,0:T(8,128)(2,1)S(1)}, bf16[8,16,512]{2,1,0:T(8,128)(2,1)S(1)}, u32[]{:S(2)}, u32[]{:S(2)}) collective-permute-start(bf16[8,16,512]{2,1,0:T(8,128)(2,1)S(1)} %add_convert_fusion.43), channel_id=1, source_target_pairs={{0,2},{2,0},{4,6},{6,4},{1,3},{3,1},{5,7},{7,5},{8,10},{10,8},{12,... | collective-permute-start | bytes 393224 | tf_op jit(solution)/shard_map/ppermute | solution.py:730
  325.7 17.1 %collective-permute-start.29 = (bf16[8,64,512]{2,1,0:T(8,128)(2,1)S(1)}, bf16[8,64,512]{2,1,0:T(8,128)(2,1)S(1)}, u32[]{:S(2)}, u32[]{:S(2)}) collective-permute-start(bf16[8,64,512]{2,1,0:T(8,128)(2,1)S(1)} %get-tuple-element.484), channel_id=1, source_target_pairs={{0,1},{1,0},{2,3},{3,2},{4,5},{5,4},{6,7},{7,6},{8,9},{9,8},{10,11... | collective-permute-start | bytes 1572872 | tf_op jit(solution)/shard_map/ppermute | solution.py:730
  326.3 16.4 %collective-permute-start.30 = (bf16[272,512]{1,0:T(8,128)(2,1)S(1)}, bf16[272,512]{1,0:T(8,128)(2,1)S(1)}, u32[]{:S(2)}, u32[]{:S(2)}) collective-permute-start(bf16[272,512]{1,0:T(8,128)(2,1)S(1)} %add_convert_fusion.19), channel_id=1, source_target_pairs={{0,2},{2,0},{4,6},{6,4},{1,3},{3,1},{5,7},{7,5},{8,10},{10,8},{12,... | collective-permute-start | bytes 835592 | tf_op jit(solution)/shard_map/ppermute | solution.py:730
  333.2 10.6 %collective-permute-start.28 = (bf16[8,16,512]{2,1,0:T(8,128)(2,1)S(1)}, bf16[8,16,512]{2,1,0:T(8,128)(2,1)S(1)}, u32[]{:S(2)}, u32[]{:S(2)}) collective-permute-start(bf16[8,16,512]{2,1,0:T(8,128)(2,1)S(1)} %get-tuple-element.516), channel_id=1, source_target_pairs={{0,6},{2,4},{4,2},{6,0},{1,7},{3,5},{5,3},{7,1},{8,14},{10,12},{12... | collective-permute-start | bytes 393224 | tf_op jit(solution)/shard_map/ppermute | solution.py:730
  335.9 10.6 %collective-permute-start.27 = (bf16[8,16,512]{2,1,0:T(8,128)(2,1)S(1)}, bf16[8,16,512]{2,1,0:T(8,128)(2,1)S(1)}, u32[]{:S(2)}, u32[]{:S(2)}) collective-permute-start(bf16[8,16,512]{2,1,0:T(8,128)(2,1)S(1)} %get-tuple-element.517), channel_id=1, source_target_pairs={{0,4},{2,6},{4,0},{6,2},{1,5},{3,7},{5,1},{7,3},{8,12},{10,14},{12... | collective-permute-start | bytes 393224 | tf_op jit(solution)/shard_map/ppermute | solution.py:730
  335.9 18.5 %collective-permute-start.26 = (bf16[8,16,512]{2,1,0:T(8,128)(2,1)S(1)}, bf16[8,16,512]{2,1,0:T(8,128)(2,1)S(1)}, u32[]{:S(2)}, u32[]{:S(2)}) collective-permute-start(bf16[8,16,512]{2,1,0:T(8,128)(2,1)S(1)} %get-tuple-element.518), channel_id=1, source_target_pairs={{0,2},{2,0},{4,6},{6,4},{1,3},{3,1},{5,7},{7,5},{8,10},{10,8},{12,... | collective-permute-start | bytes 393224 | tf_op jit(solution)/shard_map/ppermute | solution.py:730
  342.7 20.7 %collective-permute-start.42 = (bf16[8,64,512]{2,1,0:T(8,128)(2,1)S(1)}, bf16[8,64,512]{2,1,0:T(8,128)(2,1)S(1)}, u32[]{:S(2)}, u32[]{:S(2)}) collective-permute-start(bf16[8,64,512]{2,1,0:T(8,128)(2,1)S(1)} %maximum_select_fusion.11), channel_id=1, source_target_pairs={{0,1},{1,0},{2,3},{3,2},{4,5},{5,4},{6,7},{7,6},{8,9},{9,8},{10,11... | collective-permute-start | bytes 1572872 | tf_op jit(solution)/shard_map/ppermute | solution.py:730
  342.8 20.5 %collective-permute-start.37 = (bf16[272,512]{1,0:T(8,128)(2,1)S(1)}, bf16[272,512]{1,0:T(8,128)(2,1)S(1)}, u32[]{:S(2)}, u32[]{:S(2)}) collective-permute-start(bf16[272,512]{1,0:T(8,128)(2,1)S(1)} %add_convert_fusion.18), channel_id=1, source_target_pairs={{0,4},{2,6},{4,0},{6,2},{1,5},{3,7},{5,1},{7,3},{8,12},{10,14},{12... | collective-permute-start | bytes 835592 | tf_op jit(solution)/shard_map/ppermute | solution.py:730
  343.9 43.5 %collective-permute-start.11 = (bf16[4,2,128,512]{3,2,1,0:T(8,128)(2,1)S(1)}, bf16[4,2,128,512]{3,2,1,0:T(8,128)(2,1)S(1)}, u32[]{:S(2)}, u32[]{:S(2)}) collective-permute-start(bf16[4,2,128,512]{3,2,1,0:T(8,128)(2,1)S(1)} %get-tuple-element.494), channel_id=1, source_target_pairs={{0,1},{1,0},{2,3},{3,2},{4,5},{5,4},{6,7},{7,6},{8,9},{9,8},{10,11... | collective-permute-start | bytes 3145736 | tf_op jit(solution)/shard_map/ppermute | solution.py:730
  346.5 18.0 %collective-permute-start.41 = (bf16[8,16,512]{2,1,0:T(8,128)(2,1)S(1)}, bf16[8,16,512]{2,1,0:T(8,128)(2,1)S(1)}, u32[]{:S(2)}, u32[]{:S(2)}) collective-permute-start(bf16[8,16,512]{2,1,0:T(8,128)(2,1)S(1)} %get-tuple-element.512), channel_id=1, source_target_pairs={{0,6},{2,4},{4,2},{6,0},{1,7},{3,5},{5,3},{7,1},{8,14},{10,12},{12... | collective-permute-start | bytes 393224 | tf_op jit(solution)/shard_map/ppermute | solution.py:730
  354.5 15.1 %collective-permute-start.40 = (bf16[8,16,512]{2,1,0:T(8,128)(2,1)S(1)}, bf16[8,16,512]{2,1,0:T(8,128)(2,1)S(1)}, u32[]{:S(2)}, u32[]{:S(2)}) collective-permute-start(bf16[8,16,512]{2,1,0:T(8,128)(2,1)S(1)} %get-tuple-element.513), channel_id=1, source_target_pairs={{0,4},{2,6},{4,0},{6,2},{1,5},{3,7},{5,1},{7,3},{8,12},{10,14},{12... | collective-permute-start | bytes 393224 | tf_op jit(solution)/shard_map/ppermute | solution.py:730
  363.3 10.8 %collective-permute-start.39 = (bf16[8,16,512]{2,1,0:T(8,128)(2,1)S(1)}, bf16[8,16,512]{2,1,0:T(8,128)(2,1)S(1)}, u32[]{:S(2)}, u32[]{:S(2)}) collective-permute-start(bf16[8,16,512]{2,1,0:T(8,128)(2,1)S(1)} %get-tuple-element.514), channel_id=1, source_target_pairs={{0,2},{2,0},{4,6},{6,4},{1,3},{3,1},{5,7},{7,5},{8,10},{10,8},{12,... | collective-permute-start | bytes 393224 | tf_op jit(solution)/shard_map/ppermute | solution.py:730
  363.4 14.6 %collective-permute-start.38 = (bf16[4,64,512]{2,1,0:T(8,128)(2,1)S(1)}, bf16[4,64,512]{2,1,0:T(8,128)(2,1)S(1)}, u32[]{:S(2)}, u32[]{:S(2)}) collective-permute-start(bf16[4,64,512]{2,1,0:T(8,128)(2,1)S(1)} %bitcast.88), channel_id=1, source_target_pairs={{0,16},{16,0},{1,17},{17,1},{2,18},{18,2},{3,19},{19,3},{4,20},{20... | collective-permute-start | bytes 786440 | tf_op jit(solution)/shard_map/ppermute | solution.py:730
  364.5 13.8 %collective-permute-start.36 = (bf16[8,16,512]{2,1,0:T(8,128)(2,1)S(1)}, bf16[8,16,512]{2,1,0:T(8,128)(2,1)S(1)}, u32[]{:S(2)}, u32[]{:S(2)}) collective-permute-start(bf16[8,16,512]{2,1,0:T(8,128)(2,1)S(1)} %add_convert_fusion.37), channel_id=1, source_target_pairs={{0,6},{2,4},{4,2},{6,0},{1,7},{3,5},{5,3},{7,1},{8,14},{10,12},{12... | collective-permute-start | bytes 393224 | tf_op jit(solution)/shard_map/ppermute | solution.py:730
  369.6 10.2 %collective-permute-start.35 = (bf16[8,16,512]{2,1,0:T(8,128)(2,1)S(1)}, bf16[8,16,512]{2,1,0:T(8,128)(2,1)S(1)}, u32[]{:S(2)}, u32[]{:S(2)}) collective-permute-start(bf16[8,16,512]{2,1,0:T(8,128)(2,1)S(1)} %add_convert_fusion.37), channel_id=1, source_target_pairs={{0,4},{2,6},{4,0},{6,2},{1,5},{3,7},{5,1},{7,3},{8,12},{10,14},{12... | collective-permute-start | bytes 393224 | tf_op jit(solution)/shard_map/ppermute | solution.py:730
  374.1 8.9 %collective-permute-start.34 = (bf16[8,16,512]{2,1,0:T(8,128)(2,1)S(1)}, bf16[8,16,512]{2,1,0:T(8,128)(2,1)S(1)}, u32[]{:S(2)}, u32[]{:S(2)}) collective-permute-start(bf16[8,16,512]{2,1,0:T(8,128)(2,1)S(1)} %add_convert_fusion.37), channel_id=1, source_target_pairs={{0,2},{2,0},{4,6},{6,4},{1,3},{3,1},{5,7},{7,5},{8,10},{10,8},{12,... | collective-permute-start | bytes 393224 | tf_op jit(solution)/shard_map/ppermute | solution.py:730
  378.0 11.2 %collective-permute-start.46 = (bf16[8,16,512]{2,1,0:T(8,128)(2,1)S(1)}, bf16[8,16,512]{2,1,0:T(8,128)(2,1)S(1)}, u32[]{:S(2)}, u32[]{:S(2)}) collective-permute-start(bf16[8,16,512]{2,1,0:T(8,128)(2,1)S(1)} %add_convert_fusion.33), channel_id=1, source_target_pairs={{0,6},{2,4},{4,2},{6,0},{1,7},{3,5},{5,3},{7,1},{8,14},{10,12},{12... | collective-permute-start | bytes 393224 | tf_op jit(solution)/shard_map/ppermute | solution.py:730
  378.3 13.6 %collective-permute-start.45 = (bf16[8,16,512]{2,1,0:T(8,128)(2,1)S(1)}, bf16[8,16,512]{2,1,0:T(8,128)(2,1)S(1)}, u32[]{:S(2)}, u32[]{:S(2)}) collective-permute-start(bf16[8,16,512]{2,1,0:T(8,128)(2,1)S(1)} %add_convert_fusion.33), channel_id=1, source_target_pairs={{0,4},{2,6},{4,0},{6,2},{1,5},{3,7},{5,1},{7,3},{8,12},{10,14},{12... | collective-permute-start | bytes 393224 | tf_op jit(solution)/shard_map/ppermute | solution.py:730
  379.8 12.1 %collective-permute-start.44 = (bf16[8,16,512]{2,1,0:T(8,128)(2,1)S(1)}, bf16[8,16,512]{2,1,0:T(8,128)(2,1)S(1)}, u32[]{:S(2)}, u32[]{:S(2)}) collective-permute-start(bf16[8,16,512]{2,1,0:T(8,128)(2,1)S(1)} %add_convert_fusion.33), channel_id=1, source_target_pairs={{0,2},{2,0},{4,6},{6,4},{1,3},{3,1},{5,7},{7,5},{8,10},{10,8},{12,... | collective-permute-start | bytes 393224 | tf_op jit(solution)/shard_map/ppermute | solution.py:730
  383.0 25.3 %collective-permute-start.49 = (bf16[8,128,512]{2,1,0:T(8,128)(2,1)S(1)}, bf16[8,128,512]{2,1,0:T(8,128)(2,1)S(1)}, u32[]{:S(2)}, u32[]{:S(2)}) collective-permute-start(bf16[8,128,512]{2,1,0:T(8,128)(2,1)S(1)} %maximum_select_fusion.5), channel_id=1, source_target_pairs={{0,16},{16,0},{1,17},{17,1},{2,18},{18,2},{3,19},{19,3},{4,20},{20... | collective-permute-start | bytes 3145736 | tf_op jit(solution)/shard_map/ppermute | solution.py:730
  387.4 11.7 %collective-permute-start.50 = (bf16[4,128,512]{2,1,0:T(8,128)(2,1)S(1)}, bf16[4,128,512]{2,1,0:T(8,128)(2,1)S(1)}, u32[]{:S(2)}, u32[]{:S(2)}) collective-permute-start(bf16[4,128,512]{2,1,0:T(8,128)(2,1)S(1)} %maximum_select_fusion.12), channel_id=1, source_target_pairs={{0,1},{1,0},{2,3},{3,2},{4,5},{5,4},{6,7},{7,6},{8,9},{9,8},{10,11... | collective-permute-start | bytes 1572872 | tf_op jit(solution)/shard_map/ppermute | solution.py:730
  409.1 16.7 %copy-start.7 = (bf16[8,256,512]{2,1,0:T(8,128)(2,1)}, bf16[8,256,512]{2,1,0:T(8,128)(2,1)S(1)}, u32[]{:S(2)}) copy-start(bf16[8,256,512]{2,1,0:T(8,128)(2,1)S(1)} %maximum_select_fusion.1.refs_3_.refs_1_) | copy-start | bytes 6291460
  409.1 18.4 %collective-permute-start.53 = (bf16[8,256,512]{2,1,0:T(8,128)(2,1)S(1)}, bf16[8,256,512]{2,1,0:T(8,128)(2,1)S(1)}, u32[]{:S(2)}, u32[]{:S(2)}) collective-permute-start(bf16[8,256,512]{2,1,0:T(8,128)(2,1)S(1)} %maximum_select_fusion.1.refs_3_.refs_1_), channel_id=1, source_target_pairs={{0,8},{8,0},{1,9},{9,1},{2,10},{10,2},{3,11},{11,3},{4,12},{12,4},... | collective-permute-start | bytes 6291464 | tf_op jit(solution)/shard_map/ppermute | solution.py:730
  409.2 14.3 %collective-permute-start.48 = (bf16[8,64,512]{2,1,0:T(8,128)(2,1)S(1)}, bf16[8,64,512]{2,1,0:T(8,128)(2,1)S(1)}, u32[]{:S(2)}, u32[]{:S(2)}) collective-permute-start(bf16[8,64,512]{2,1,0:T(8,128)(2,1)S(1)} %maximum_select_fusion.13), channel_id=1, source_target_pairs={{0,16},{16,0},{1,17},{17,1},{2,18},{18,2},{3,19},{19,3},{4,20},{20... | collective-permute-start | bytes 1572872 | tf_op jit(solution)/shard_map/ppermute | solution.py:730
  411.0 16.5 %collective-permute-start.54 = (bf16[4,256,512]{2,1,0:T(8,128)(2,1)S(1)}, bf16[4,256,512]{2,1,0:T(8,128)(2,1)S(1)}, u32[]{:S(2)}, u32[]{:S(2)}) collective-permute-start(bf16[4,256,512]{2,1,0:T(8,128)(2,1)S(1)} %maximum_select_fusion.6.refs_1_), channel_id=1, source_target_pairs={{0,8},{8,0},{1,9},{9,1},{2,10},{10,2},{3,11},{11,3},{4,12},{12,4},... | collective-permute-start | bytes 3145736 | tf_op jit(solution)/shard_map/ppermute | solution.py:730
  411.1 14.2 %collective-permute-start.47 = (bf16[8,64,512]{2,1,0:T(8,128)(2,1)S(1)}, bf16[8,64,512]{2,1,0:T(8,128)(2,1)S(1)}, u32[]{:S(2)}, u32[]{:S(2)}) collective-permute-start(bf16[8,64,512]{2,1,0:T(8,128)(2,1)S(1)} %maximum_select_fusion.14), channel_id=1, source_target_pairs={{0,1},{1,0},{2,3},{3,2},{4,5},{5,4},{6,7},{7,6},{8,9},{9,8},{10,11... | collective-permute-start | bytes 1572872 | tf_op jit(solution)/shard_map/ppermute | solution.py:730
  411.5 15.1 %collective-permute-start.43 = (bf16[2,2,128,512]{3,2,1,0:T(8,128)(2,1)S(1)}, bf16[2,2,128,512]{3,2,1,0:T(8,128)(2,1)S(1)}, u32[]{:S(2)}, u32[]{:S(2)}) collective-permute-start(bf16[2,2,128,512]{3,2,1,0:T(8,128)(2,1)S(1)} %add_convert_fusion.6), channel_id=1, source_target_pairs={{0,2},{2,0},{4,6},{6,4},{1,3},{3,1},{5,7},{7,5},{8,10},{10,8},{12,... | collective-permute-start | bytes 1572872 | tf_op jit(solution)/shard_map/ppermute | solution.py:730
  424.0 24.8 %collective-permute-start.52 = (bf16[8,128,512]{2,1,0:T(8,128)(2,1)S(1)}, bf16[8,128,512]{2,1,0:T(8,128)(2,1)S(1)}, u32[]{:S(2)}, u32[]{:S(2)}) collective-permute-start(bf16[8,128,512]{2,1,0:T(8,128)(2,1)S(1)} %maximum_select_fusion.7), channel_id=1, source_target_pairs={{0,1},{1,0},{2,3},{3,2},{4,5},{5,4},{6,7},{7,6},{8,9},{9,8},{10,11... | collective-permute-start | bytes 3145736 | tf_op jit(solution)/shard_map/ppermute | solution.py:730
  425.8 39.5 %collective-permute-start.55 = (bf16[8,128,512]{2,1,0:T(8,128)(2,1)S(1)}, bf16[8,128,512]{2,1,0:T(8,128)(2,1)S(1)}, u32[]{:S(2)}, u32[]{:S(2)}) collective-permute-start(bf16[8,128,512]{2,1,0:T(8,128)(2,1)S(1)} %maximum_select_fusion.8), channel_id=1, source_target_pairs={{0,16},{16,0},{1,17},{17,1},{2,18},{18,2},{3,19},{19,3},{4,20},{20... | collective-permute-start | bytes 3145736 | tf_op jit(solution)/shard_map/ppermute | solution.py:730
  449.4 19.6 %collective-permute-start.57 = (bf16[8,256,512]{2,1,0:T(8,128)(2,1)S(1)}, bf16[8,256,512]{2,1,0:T(8,128)(2,1)S(1)}, u32[]{:S(2)}, u32[]{:S(2)}) collective-permute-start(bf16[8,256,512]{2,1,0:T(8,128)(2,1)S(1)} %maximum_select_fusion.2.refs_1_.refs_3_), channel_id=1, source_target_pairs={{0,8},{8,0},{1,9},{9,1},{2,10},{10,2},{3,11},{11,3},{4,12},{12,4},... | collective-permute-start | bytes 6291464 | tf_op jit(solution)/shard_map/ppermute | solution.py:730
  449.7 18.4 %copy-start.11 = (f32[256,512]{1,0:T(8,128)S(1)}, f32[256,512]{1,0:T(8,128)}, u32[]{:S(2)}) copy-start(f32[256,512]{1,0:T(8,128)} %get-tuple-element.384) | copy-start | bytes 1572868
  449.7 15.6 %collective-permute-start.51 = (bf16[2,128,512]{2,1,0:T(8,128)(2,1)S(1)}, bf16[2,128,512]{2,1,0:T(8,128)(2,1)S(1)}, u32[]{:S(2)}, u32[]{:S(2)}) collective-permute-start(bf16[2,128,512]{2,1,0:T(8,128)(2,1)S(1)} %copy-done.14), channel_id=1, source_target_pairs={{0,4},{2,6},{4,0},{6,2},{1,5},{3,7},{5,1},{7,3},{8,12},{10,14},{12... | collective-permute-start | bytes 786440 | tf_op jit(solution)/shard_map/ppermute | solution.py:730
  466.0 10.3 %collective-permute-start.56 = (bf16[8,256,512]{2,1,0:T(8,128)(2,1)S(1)}, bf16[8,256,512]{2,1,0:T(8,128)(2,1)}, u32[]{:S(2)}, u32[]{:S(2)}) collective-permute-start(bf16[8,256,512]{2,1,0:T(8,128)(2,1)S(1)} %maximum_select_fusion.3.refs_1_.refs_3_), channel_id=1, source_target_pairs={{0,8},{8,0},{1,9},{9,1},{2,10},{10,2},{3,11},{11,3},{4,12},{12,4},... | collective-permute-start | bytes 6291464 | tf_op jit(solution)/shard_map/ppermute | solution.py:730
  (25 other events, 213.7 us)
Sparse Core Ops, SparseCore 0:
  10.1 62.3 all-gather.5
  90.5 50.5 all-gather.3

commit v2 on v1

--- a/solution.py
+++ b/solution.py
@@ -667,7 +667,7 @@
 
 
 class Weights:
-    def __init__(self, pairs):
+    def __init__(self, pairs, base=None):
         self.arrays, self.plan, known = {}, [], {}
 
         def place(rows):
@@ -686,12 +686,17 @@
                     self.plan.append([(a[0], row, b[0], column) for a, b in terms])
         count = len(self.plan)
         self.gives = {name: ((count, SIDE // 2, SIDE), BF16) for name in ("kept", "sent")}
+        if base is not None:
+            self.arrays["base"] = base
 
     def body(self, r, core):
         half = SIDE // 2
         for index, terms in enumerate(self.plan):
             for flip, name in enumerate(("kept", "sent")):
                 total = None
+                if "base" in self.arrays:
+                    begin = pl.multiple_of((core ^ flip) * half, half)
+                    total = r.base[index, pl.ds(begin, half), :].astype(F32)
                 for a, row, b, column in terms:
                     left, right = getattr(r, a), getattr(r, b)
                     begin = pl.multiple_of(row + (core ^ flip) * half, half)
@@ -711,8 +716,28 @@
                 r.leaving[name][index].start()
 
 
-def weight_tiles(pairs, core_info, after=(), cost=10):
-    weights = Weights(pairs)
+def whole_tiles(chunks, after=(), cost=10):
+    weights = [Weights([[pair] for pair in chunk]) for chunk in chunks]
+    arrays, gives = {}, {}
+    for number, part in enumerate(weights):
+        gives["c%d" % number] = ((len(part.plan), SIDE, SIDE), BF16)
+        arrays.update((name + "c%d" % number, array) for name, array in part.arrays.items())
+
+    def body(r):
+        for number, part in enumerate(weights):
+            tag = "c%d" % number
+            for index, ((a, row, b, column),) in enumerate(part.plan):
+                left, right = getattr(r, a + tag), getattr(r, b + tag)
+                product = tn(left[:, row : row + SIDE], right[:, column : column + SIDE])
+                r[tag][index] = product.astype(BF16)
+                r.leaving[tag][index].start()
+
+    out = launch(body, arrays, gives, after=after, pieces=tuple(gives), cost=cost)
+    return list(out.values())
+
+
+def weight_tiles(pairs, core_info, after=(), cost=10, base=None):
+    weights = Weights(pairs, base)
     out = launch(
         lambda r: weights.body(r, r.info[0]),
         weights.arrays,
@@ -992,28 +1017,54 @@
 def assemble(chain, core_info, shapes, after=()):
     tiles, half, side = chain.held[0].shape
 
-    def body(r):
-        low = pl.multiple_of(r.info[0] * half, half)
-        high = pl.multiple_of((1 - r.info[0]) * half, half)
-        tile = 0
-        for name, shape in shapes.items():
-            out = r[name]
-            for start in range(0, shape[-2] * shape[-1] * (shape[0] if len(shape) > 2 else 1), side * side):
-                place = start // (side * side)
-                for begin, source in ((low, r.mine), (high, r.other)):
-                    rows = source[tile].astype(F32)
-                    if len(shape) > 2:
-                        out[place, pl.ds(begin, half), :] = rows
-                    elif shape[1] > shape[0]:
-                        out[pl.ds(begin, half), place * side : (place + 1) * side] = rows
-                    else:
-                        out[pl.ds(begin + place * side, half), :] = rows
-                tile += 1
-            r.leave(name)
-
-    gives = {name: (shape, F32) for name, shape in shapes.items()}
-    arrays = {"mine": chain.held[0], "other": chain.held[1]}
-    return list(launch(body, arrays, gives, info=core_info, after=after, cost=5).values())
+    places = []
+    for name, shape in shapes.items():
+        blocks = shape[0] if len(shape) > 2 else shape[0] * shape[1] // (side * side)
+        for block in range(blocks):
+            if len(shape) > 2:
+                places.append((name, lambda rows, b=block: (b, rows, slice(None))))
+            elif shape[1] > shape[0]:
+                lanes = slice(block * side, (block + 1) * side)
+                places.append((name, lambda rows, l=lanes: (rows, l)))
+            else:
+                places.append((name, lambda rows, b=block: (pl.ds(rows.start + b * side, half), slice(None))))
+
+    def body(info, mine, other, *refs):
+        outs = dict(zip(shapes, refs))
+        room, full, come, go = refs[len(shapes) :]
+        starts = [pl.multiple_of((info[0] ^ flip) * half, half) for flip in (0, 1)]
+        arrive, leave = [], []
+        for tile in range(tiles):
+            for flip, source in enumerate((mine, other)):
+                index = 2 * tile + flip
+                arrive.append(pltpu.make_async_copy(source.at[tile], room.at[index], come.at[index]))
+                arrive[-1].start()
+        for tile, (name, where) in enumerate(places):
+            for flip in (0, 1):
+                index = 2 * tile + flip
+                arrive[index].wait()
+                full[index] = room[index].astype(F32)
+                target = outs[name].at[where(pl.ds(starts[flip], half))]
+                leave.append(pltpu.make_async_copy(full.at[index], target, go.at[index]))
+                leave[-1].start()
+        for copy in leave:
+            copy.wait()
+
+    far = pl.BlockSpec(memory_space=pl.ANY)
+    return pl.pallas_call(
+        lambda info, mine, other, *refs: body(info, mine, other, *refs[len(after) :]),
+        in_specs=[pl.BlockSpec(memory_space=pltpu.SMEM)] + [far] * (2 + len(after)),
+        out_specs=[far] * len(shapes),
+        out_shape=[jax.ShapeDtypeStruct(shape, F32) for shape in shapes.values()],
+        scratch_shapes=[
+            pltpu.VMEM((2 * tiles, half, side), BF16),
+            pltpu.VMEM((2 * tiles, half, side), F32),
+            pltpu.SemaphoreType.DMA((2 * tiles,)),
+            pltpu.SemaphoreType.DMA((2 * tiles,)),
+        ],
+        compiler_params=pltpu.CompilerParams(vmem_limit_bytes=VMEM_LIMIT),
+        cost_estimate=pl.CostEstimate(flops=5 * 10**9, bytes_accessed=2 * 10**7, transcendentals=0),
+    )(core_info, chain.held[0], chain.held[1], *after)
 
 
 def shards(
@@ -1235,7 +1286,27 @@
         cost=16,
     )
 
-    whole_target = gather_last(late_target, INNER, 1, seb.small)
+    t_short, x_short = flat(target_short), flat(source_short)
+    short_weights = whole_tiles(
+        [
+            [(sc.m, sc.dh), (sc.act, sc.b5)],
+            [
+                (sd.u, sb.dq_c),
+                (se.enc, sb.dk_c),
+                (se.enc, sb.dv_c),
+                (sc.o_c, sc.b4),
+                (t_short, sb.dq),
+                (t_short, sb.dk),
+                (t_short, sb.dv),
+                (sd.o, sb.b3),
+            ],
+            [(se.y, seb.dh), (se.act, seb.b2)],
+            [(x_short, seb.dq), (x_short, seb.dk), (x_short, seb.dv), (se.o, seb.b1)],
+        ],
+        after=(seb.small,),
+        cost=15,
+    )
+    whole_target = gather_last(late_target, INNER, 1, short_weights[0])
     whole_target = whole_target.reshape(places, pairs, own, width)
     ls = launch(
         long_self_forward,
@@ -1253,7 +1324,7 @@
         },
         scratch=work,
         info=target_info,
-        after=(seb.small,),
+        after=(short_weights[0],),
         cost=10,
         plain=True,
     )
@@ -1296,7 +1367,7 @@
     )
     encoded_back = Spread(lcb.part, True)
     first_weights = Weights(
-        [[(sc.m, sc.dh), (lc.m, lc.dh)], [(sc.act, sc.b5), (lc.act, lc.b5)]]
+        [[(lc.m, lc.dh)], [(lc.act, lc.b5)]], short_weights[0]
     )
 
     def self_back_and_weights(r):
@@ -1332,17 +1403,18 @@
     target_back = Spread(lsb.part, False)
     grad_attention = weight_tiles(
         [
-            [(sd.u, sb.dq_c), (ls.u, lcb.dq_c)],
-            [(se.enc, sb.dk_c), (flat(whole_encoded), flat(lcb.dk_c))],
-            [(se.enc, sb.dv_c), (flat(whole_encoded), flat(lcb.dv_c))],
-            [(sc.o_c, sc.b4), (lc.o_c, lc.b4)],
-            [(flat(target_short), sb.dq), (t_long, lsb.dq)],
-            [(flat(target_short), sb.dk), (flat(whole_target), flat(lsb.dk))],
-            [(flat(target_short), sb.dv), (flat(whole_target), flat(lsb.dv))],
-            [(sd.o, sb.b3), (ls.o, lsb.b3)],
+            [(ls.u, lcb.dq_c)],
+            [(flat(whole_encoded), flat(lcb.dk_c))],
+            [(flat(whole_encoded), flat(lcb.dv_c))],
+            [(lc.o_c, lc.b4)],
+            [(t_long, lsb.dq)],
+            [(flat(whole_target), flat(lsb.dk))],
+            [(flat(whole_target), flat(lsb.dv))],
+            [(ls.o, lsb.b3)],
         ],
         core_info,
         after=(lsb.small, encoded_back.held[0]),
+        base=short_weights[1],
         cost=15,
     )
     finish([encoded_back, decoder_ffn], grad_attention[0])
@@ -1350,9 +1422,10 @@
     attention = Chain(grad_attention, (INNER, X, OUTER))
     ffn_weights = Weights(
         [
-            [(se.y, seb.dh), (le.y, ("dh", hidden))],
-            [(se.act, seb.b2), (le.act, ("b2", width))],
-        ]
+            [(le.y, ("dh", hidden))],
+            [(le.act, ("b2", width))],
+        ],
+        short_weights[2],
     )
 
     def encoder_back_and_weights(r):
@@ -1386,11 +1459,12 @@
     encoder_ffn = Chain([leb.kept, leb.sent], (X, INNER, OUTER))
     attention_weights = Weights(
         [
-            [(flat(source_short), seb.dq), (x_long, ("dq", width))],
-            [(flat(source_short), seb.dk), (whole_source, ("dk", width))],
-            [(flat(source_short), seb.dv), (whole_source, ("dv", width))],
-            [(se.o, seb.b1), (le.o, leb.b1)],
-        ]
+            [(x_long, ("dq", width))],
+            [(whole_source, ("dk", width))],
+            [(whole_source, ("dv", width))],
+            [(le.o, leb.b1)],
+        ],
+        short_weights[3],
     )
 
     def attention_back_and_weights(r):

time: 499 us -> 483 us (0.968)
  waiting for transfers between devices: 151 us -> 125 us
  starting transfers between devices: 73.7 us -> 83 us
  Pallas kernels: 208 us -> 214 us
    ppermute x58, waiting for transfers between devices: 138 us -> 116 us  [send(): return lax.ppermute(piece, axis, [(i, i ^ offset) for i in range(count)])]
    pallas_call x0 -> x4, Pallas kernels: none -> 16.8 us  [assemble(): pl.pallas_call(lambda info, mine, other, *refs: body(info, mine, other, *...]
    pallas_call x17 -> x14, Pallas kernels: 208 us -> 197 us  [launch(): pl.pallas_call(run, in_specs=specs, out_specs=[far if name in moved_out e...]
    ppermute x58, starting transfers between devices: 73.6 us -> 82.9 us  [send(): return lax.ppermute(piece, axis, [(i, i ^ offset) for i in range(count)])]
  transfers between devices with their start and end apart: 60 -> 60, of which waited for: 24 -> 24; matrix products, arithmetic and copies ran while one was open for 7% -> 7% of each run, Pallas kernels for 31% -> 37%
where the time goes in v2:
time: 483 us; the launch traced here: 479 us
  Pallas kernels  214 us (44%)
  waiting for transfers between devices  125 us (26%)
  starting transfers between devices  83 us (17%)
  other arithmetic  26.2 us (5%)
  between operations  15.6 us (3%)
  local copies, waits for them, and re-layouts  14.7 us (3%)
    pallas_call x14, Pallas kernels, launch(): pl.pallas_call(run, in_specs=specs, out_specs=[far if name in moved_out e...  197 us
    ppermute x58, waiting for transfers between devices, send(): return lax.ppermute(piece, axis, [(i, i ^ offset) for i in range(count)])  116 us
    ppermute x58, starting transfers between devices, send(): return lax.ppermute(piece, axis, [(i, i ^ offset) for i in range(count)])  82.9 us
    pallas_call x4, Pallas kernels, assemble(): pl.pallas_call(lambda info, mine, other, *refs: body(info, mine, other, *...  16.8 us
    convert_element_type x26, other arithmetic, added(): return total.astype(BF16)  12.4 us
  transfers between devices with their start and end apart: 60, of which 24 were waited for; matrix products, arithmetic and copies ran while one was open for 7% of the time, Pallas kernels for 37%

profile of v2, /device:TPU:0, one launch (start us, length us, event | category | flops | bytes accessed | tf_op | source)
XLA Modules:
  0.0 478.6 jit_solution(9183816006806838052)
XLA Ops:
  8.0 1.5 broadcast_in_dim.24.refs_1_.refs_4_.refs_14_.refs_11_
  9.5 11.3 %shard_map.383 = (bf16[512,512]{1,0:T(8,128)(2,1)}, bf16[512,512]{1,0:T(8,128)(2,1)}, bf16[512,512]{1,0:T(8,128)(2,1)}, bf16[512,512]{1,0:T(8,128)(2,1)}, f32[4,...) custom-call(bf16[512,512]{1,0:T(8,128)(2,1)} %bitcast.97, ...), custom_call_target="tpu_custom_call" | custom-call | flops 11000000 | bytes 35000 | tf_op jit(solution)/shard_map/pallas_call | solution.py:423
  21.7 7.4 %shard_map.384 = (bf16[512,512]{1,0:T(8,128)(2,1)}, bf16[512,512]{1,0:T(8,128)(2,1)}, bf16[512,512]{1,0:T(8,128)(2,1)}, bf16[512,512]{1,0:T(8,128)(2,1)}, bf16[5...) custom-call(bf16[512,512]{1,0:T(8,128)(2,1)} %bitcast.95, ...), custom_call_target="tpu_custom_call" | custom-call | flops 11000000 | bytes 35000 | tf_op jit(solution)/shard_map/pallas_call | solution.py:423
  29.1 5.1 %collective-permute-start.2 = (bf16[1,1,2,128,512]{4,3,2,1,0:T(8,128)(2,1)S(1)}, bf16[1,1,2,128,512]{4,3,2,1,0:T(8,128)(2,1)S(1)}, u32[]{:S(2)}, u32[]{:S(2)}) collective-permute-start(bf16[1,1,2,128,512]{4,3,2,1,0:T(8,128)(2,1)S(1)} %bitcast.103), channel_id=1, source_target_pairs={{0,6},{2,4},{4,2},{6,0},{1,7},{3,5},{5,3},{7,1},{8,14},{10,12},{12... | collective-permute-start | bytes 786440 | tf_op jit(solution)/shard_map/ppermute | solution.py:755
  36.1 14.7 %shard_map.385 = (bf16[512,512]{1,0:T(8,128)(2,1)}, bf16[512,512]{1,0:T(8,128)(2,1)}, bf16[512,512]{1,0:T(8,128)(2,1)}, bf16[512,512]{1,0:T(8,128)(2,1)}, f32[4,...) custom-call(bf16[512,512]{1,0:T(8,128)(2,1)} %get-tuple-element.254., ...), custom_call_target="tpu_custom_call" | custom-call | flops 11000000 | bytes 35000 | tf_op jit(solution)/shard_map/pallas_call | solution.py:423
  50.8 16.3 %shard_map.386 = (bf16[512,512]{1,0:T(8,128)(2,1)}, bf16[512,512]{1,0:T(8,128)(2,1)}, bf16[512,512]{1,0:T(8,128)(2,1)}, bf16[512,512]{1,0:T(8,128)(2,1)}, bf16[5...) custom-call(bf16[512,512]{1,0:T(8,128)(2,1)} %get-tuple-element.259., ...), custom_call_target="tpu_custom_call" | custom-call | flops 11000000 | bytes 35000 | tf_op jit(solution)/shard_map/pallas_call | solution.py:423
  67.1 7.0 %collective-permute-done.1 = bf16[1,1,2,128,512]{4,3,2,1,0:T(8,128)(2,1)S(1)} collective-permute-done((bf16[1,1,2,128,512]{4,3,2,1,0:T(8,128)(2,1)S(1)}, bf16[1,1,2,128,512]{4,3,2,1,0:T(8,128)(2,1)S(1)}, u32[]{:S(2)}, u32[]{:S(2)}) %collective-permute-start.1) | collective-permute-done | bytes 262176 | tf_op jit(solution)/shard_map/ppermute | solution.py:755
  74.4 10.6 %collective-permute-start.3 = (bf16[4,1,2,128,512]{4,3,2,1,0:T(8,128)(2,1)S(1)}, bf16[4,1,2,128,512]{4,3,2,1,0:T(8,128)(2,1)S(1)}, u32[]{:S(2)}, u32[]{:S(2)}) collective-permute-start(bf16[4,1,2,128,512]{4,3,2,1,0:T(8,128)(2,1)S(1)} %maximum_select_fusion.4.refs_10_), channel_id=1, source_target_pairs={{0,1},{1,0},{2,3},{3,2},{4,5},{5,4},{6,7},{7,6},{8,9},{9,8},{10,11... | collective-permute-start | bytes 3145736 | tf_op jit(solution)/shard_map/ppermute | solution.py:755
  85.0 14.6 %shard_map.387 = (bf16[256,512]{1,0:T(8,128)(2,1)}, bf16[256,512]{1,0:T(8,128)(2,1)}, bf16[8,2,128,512]{3,2,1,0:T(8,128)(2,1)}, bf16[8,2,128,512]{3,2,1,0:T(8,12...) custom-call(s32[6]{0:T(128)} %concatenate.236.refs_0_, ...), custom_call_target="tpu_custom_call" | custom-call | flops 14300000256 | bytes 45500000 | tf_op jit(solution)/shard_map/pallas_call | solution.py:423
  99.6 15.8 %shard_map.388 = (bf16[512,512]{1,0:T(8,128)(2,1)}, bf16[512,512]{1,0:T(8,128)(2,1)}, bf16[512,512]{1,0:T(8,128)(2,1)}, bf16[512,512]{1,0:T(8,128)(2,1)}, bf16[5...) custom-call(f32[512,512]{1,0:T(8,128)} %get-tuple-element.294.refs_0, ...), custom_call_target="tpu_custom_call" | custom-call | flops 17600000000 | bytes 56000000 | tf_op jit(solution)/shard_map/pallas_call | solution.py:423
  115.4 14.3 %shard_map.389 = (bf16[8,512,512]{2,1,0:T(8,128)(2,1)}, bf16[8,512,512]{2,1,0:T(8,128)(2,1)}, bf16[8,512,512]{2,1,0:T(8,128)(2,1)}, bf16[4,512,512]{2,1,0:T(8,128)(2,1)}) custom-call(bf16[512,512]{1,0:T(8,128)(2,1)} %get-tuple-element.281.refs_0_, bf16[512,2048]{1,0:T(8,128)(2,1)} %get-tuple-element.282.refs_1_, ...), custom_call_target="tpu_custom_call" | custom-call | flops 16499999744 | bytes 52500000 | tf_op jit(solution)/shard_map/pallas_call | solution.py:423
  129.8 1.6 maximum_select_fusion
  131.4 7.8 %shard_map.390 = (bf16[256,512]{1,0:T(8,128)(2,1)}, bf16[256,512]{1,0:T(8,128)(2,1)}, bf16[256,512]{1,0:T(8,128)(2,1)}, bf16[256,512]{1,0:T(8,128)(2,1)}, bf16[2...) custom-call(s32[6]{0:T(128)} %concatenate.249.refs_0_, ...), custom_call_target="tpu_custom_call" | custom-call | flops 11000000512 | bytes 35000000 | tf_op jit(solution)/shard_map/pallas_call | solution.py:423
  139.2 9.1 %all-gather.4.cloned.1.call-done.refs_1_ = bf16[8,2,128,512]{3,2,1,0:T(8,128)(2,1)} async-done(((bf16[1,2,128,512]{3,2,1,0:T(8,128)(2,1)}), bf16[8,2,128,512]{3,2,1,0:T(8,128)(2,1)}) %all-gather.4.cloned.1.call-update) | async-done | bytes 2097168 | tf_op jit(solution)/shard_map/all_gather | solution.py:811
  148.2 16.4 %shard_map.391 = (bf16[256,512]{1,0:T(8,128)(2,1)}, bf16[8,2,128,512]{3,2,1,0:T(8,128)(2,1)}, bf16[8,2,128,512]{3,2,1,0:T(8,128)(2,1)}, f32[2,8,128]{2,1,0:T(8,1...) custom-call(s32[6]{0:T(128)} %concatenate.236.refs_0_, ...), custom_call_target="tpu_custom_call" | custom-call | flops 15399999488 | bytes 49000000 | tf_op jit(solution)/shard_map/pallas_call | solution.py:423
  164.6 16.5 %shard_map.392 = (bf16[256,512]{1,0:T(8,128)(2,1)}, bf16[8,2,128,512]{3,2,1,0:T(8,128)(2,1)}, bf16[8,2,128,512]{3,2,1,0:T(8,128)(2,1)}, bf16[2,4,2,128,512]{4,3,2,1,0:T(8,128)(2,1)}) custom-call(s32[6]{0:T(128)} %concatenate.236.refs_0_, bf16[256,512]{1,0:T(8,128)(2,1)} %get-tuple-element.319.refs_3_.refs_1_, ...), custom_call_target="tpu_custom_call" | custom-call | flops 15399999488 | bytes 49000000 | tf_op jit(solution)/shard_map/pallas_call | solution.py:423
  181.1 1.7 slice_bitcast_fusion.4
  183.0 17.0 %shard_map.393 = (bf16[8,256,512]{2,1,0:T(8,128)(2,1)}, bf16[8,256,512]{2,1,0:T(8,128)(2,1)}, bf16[256,512]{1,0:T(8,128)(2,1)}, bf16[256,512]{1,0:T(8,128)(2,1)}...) custom-call(s32[6]{0:T(128)} %concatenate.249.refs_0_, ...), custom_call_target="tpu_custom_call" | custom-call | flops 24199999488 | bytes 77000000 | tf_op jit(solution)/shard_map/pallas_call | solution.py:423
  200.1 2.7 slice_bitcast_fusion
  202.7 1.6 collective-permute-done.4
  205.4 9.0 %collective-permute-start.7 = (bf16[2,128,512]{2,1,0:T(8,128)(2,1)S(1)}, bf16[2,128,512]{2,1,0:T(8,128)(2,1)S(1)}, u32[]{:S(2)}, u32[]{:S(2)}) collective-permute-start(bf16[2,128,512]{2,1,0:T(8,128)(2,1)S(1)} %get-tuple-element.504), channel_id=1, source_target_pairs={{0,6},{2,4},{4,2},{6,0},{1,7},{3,5},{5,3},{7,1},{8,14},{10,12},{12... | collective-permute-start | bytes 786440 | tf_op jit(solution)/shard_map/ppermute | solution.py:755
  215.0 15.5 %shard_map.394 = (bf16[8,256,512]{2,1,0:T(8,128)(2,1)}, bf16[8,256,512]{2,1,0:T(8,128)(2,1)}) custom-call(s32[1]{0:T(128)} %bitcast.8.refs_0_.info, bf16[256,512]{1,0:T(8,128)(2,1)} %get-tuple-element.351.refs_1_, bf16[256,512]{1,0:T(8,128)(2,1)} %get-tuple-element.339.refs_7_.refs_19_.refs_2_, bf16[2048,512]{1,0:T(8,128)(2,1)} %bitcast.121, ...), custom_call_target="tpu_custom_call" | custom-call | flops 16499999744 | bytes 52500000 | tf_op jit(solution)/shard_map/pallas_call | solution.py:423
  230.7 1.7 collective-permute-start.15
  232.3 3.6 collective-permute-done.6
  235.9 2.0 add_convert_fusion.2
  238.1 10.1 %shard_map.395 = (bf16[8,256,512]{2,1,0:T(8,128)(2,1)}, bf16[8,256,512]{2,1,0:T(8,128)(2,1)}, bf16[256,512]{1,0:T(8,128)(2,1)}, bf16[256,512]{1,0:T(8,128)(2,1)}...) custom-call(s32[1]{0:T(128)} %bitcast.8.refs_0_.info, ...), custom_call_target="tpu_custom_call" | custom-call | flops 13200000000 | bytes 42000000 | tf_op jit(solution)/shard_map/pallas_call | solution.py:423
  249.0 3.5 add_convert_fusion.3
  253.7 19.4 %shard_map.396 = (bf16[4,256,512]{2,1,0:T(8,128)(2,1)}, bf16[4,256,512]{2,1,0:T(8,128)(2,1)}, bf16[2,4,2,128,512]{4,3,2,1,0:T(8,128)(2,1)}, f32[256,512]{1,0:T(8,128)}) custom-call(s32[6]{0:T(128)} %concatenate.236.refs_0_, bf16[256,512]{1,0:T(8,128)(2,1)} %get-tuple-element.323.refs_1_, bf16[8,2,128,512]{3,2,1,0:T(8,128)(2,1)} %get-tuple-element.324.refs_2_, ...), custom_call_target="tpu_custom_call" | custom-call | flops 20899999744 | bytes 66500000 | tf_op jit(solution)/shard_map/pallas_call | solution.py:423
  273.1 1.8 pad_maximum_fusion
  275.9 2.0 collective-permute-start.17
  279.3 1.5 add_convert_fusion.13
  283.7 12.0 %collective-permute-done.18 = bf16[8,64,512]{2,1,0:T(8,128)(2,1)S(1)} collective-permute-done((bf16[8,64,512]{2,1,0:T(8,128)(2,1)S(1)}, bf16[8,64,512]{2,1,0:T(8,128)(2,1)S(1)}, u32[]{:S(2)}, u32[]{:S(2)}) %collective-permute-start.18) | collective-permute-done | bytes 524320 | tf_op jit(solution)/shard_map/ppermute | solution.py:755
  295.9 2.7 collective-permute-start.23
  298.6 2.9 collective-permute-done.17
  301.9 3.3 collective-permute-start.21
  305.6 4.7 collective-permute-done.22
  311.4 1.6 collective-permute-start.24
  313.7 2.0 collective-permute-start.33
  315.6 1.7 collective-permute-start.32
  317.3 12.4 %collective-permute-done.25 = bf16[2,128,512]{2,1,0:T(8,128)(2,1)S(1)} collective-permute-done((bf16[2,128,512]{2,1,0:T(8,128)(2,1)S(1)}, bf16[2,128,512]{2,1,0:T(8,128)(2,1)S(1)}, u32[]{:S(2)}, u32[]{:S(2)}) %collective-permute-start.25) | collective-permute-done | bytes 262176 | tf_op jit(solution)/shard_map/ppermute | solution.py:755
  331.6 2.1 collective-permute-start.30
  333.9 1.4 collective-permute-done.32
  335.3 2.8 collective-permute-done.31
  338.1 2.5 collective-permute-start.28
  340.7 1.8 collective-permute-start.26
  342.9 4.6 collective-permute-done.30
  350.7 11.2 %collective-permute-start.41 = (bf16[8,16,512]{2,1,0:T(8,128)(2,1)S(1)}, bf16[8,16,512]{2,1,0:T(8,128)(2,1)S(1)}, u32[]{:S(2)}, u32[]{:S(2)}) collective-permute-start(bf16[8,16,512]{2,1,0:T(8,128)(2,1)S(1)} %get-tuple-element.520), channel_id=1, source_target_pairs={{0,6},{2,4},{4,2},{6,0},{1,7},{3,5},{5,3},{7,1},{8,14},{10,12},{12... | collective-permute-start | bytes 393224 | tf_op jit(solution)/shard_map/ppermute | solution.py:755
  362.0 6.3 %collective-permute-done.37 = bf16[272,512]{1,0:T(8,128)(2,1)S(1)} collective-permute-done((bf16[272,512]{1,0:T(8,128)(2,1)S(1)}, bf16[272,512]{1,0:T(8,128)(2,1)S(1)}, u32[]{:S(2)}, u32[]{:S(2)}) %collective-permute-start.37) | collective-permute-done | bytes 278560 | tf_op jit(solution)/shard_map/ppermute | solution.py:755
  370.2 2.7 collective-permute-start.36
  374.0 5.3 %collective-permute-done.39 = bf16[8,16,512]{2,1,0:T(8,128)(2,1)S(1)} collective-permute-done((bf16[8,16,512]{2,1,0:T(8,128)(2,1)S(1)}, bf16[8,16,512]{2,1,0:T(8,128)(2,1)S(1)}, u32[]{:S(2)}, u32[]{:S(2)}) %collective-permute-start.39) | collective-permute-done | bytes 131104 | tf_op jit(solution)/shard_map/ppermute | solution.py:755
  379.3 2.5 collective-permute-start.46
  382.1 2.3 collective-permute-start.45
  384.4 7.0 %collective-permute-done.35 = bf16[8,16,512]{2,1,0:T(8,128)(2,1)S(1)} collective-permute-done((bf16[8,16,512]{2,1,0:T(8,128)(2,1)S(1)}, bf16[8,16,512]{2,1,0:T(8,128)(2,1)S(1)}, u32[]{:S(2)}, u32[]{:S(2)}) %collective-permute-start.35) | collective-permute-done | bytes 131104 | tf_op jit(solution)/shard_map/ppermute | solution.py:755
  393.0 3.5 collective-permute-done.45
  398.1 5.6 %collective-permute-done.50 = bf16[4,128,512]{2,1,0:T(8,128)(2,1)S(1)} collective-permute-done((bf16[4,128,512]{2,1,0:T(8,128)(2,1)S(1)}, bf16[4,128,512]{2,1,0:T(8,128)(2,1)S(1)}, u32[]{:S(2)}, u32[]{:S(2)}) %collective-permute-start.50) | collective-permute-done | bytes 524320 | tf_op jit(solution)/shard_map/ppermute | solution.py:755
  404.4 10.1 %collective-permute-done.49 = bf16[8,128,512]{2,1,0:T(8,128)(2,1)S(1)} collective-permute-done((bf16[8,128,512]{2,1,0:T(8,128)(2,1)S(1)}, bf16[8,128,512]{2,1,0:T(8,128)(2,1)S(1)}, u32[]{:S(2)}, u32[]{:S(2)}) %collective-permute-start.49) | collective-permute-done | bytes 1048608 | tf_op jit(solution)/shard_map/ppermute | solution.py:755
  416.8 12.8 %collective-permute-done.48 = bf16[8,64,512]{2,1,0:T(8,128)(2,1)S(1)} collective-permute-done((bf16[8,64,512]{2,1,0:T(8,128)(2,1)S(1)}, bf16[8,64,512]{2,1,0:T(8,128)(2,1)S(1)}, u32[]{:S(2)}, u32[]{:S(2)}) %collective-permute-start.48) | collective-permute-done | bytes 524320 | tf_op jit(solution)/shard_map/ppermute | solution.py:755
  433.1 3.5 collective-permute-start.51
  438.9 3.1 shard_map.397
  442.1 4.5 shard_map.398
  446.6 8.3 %collective-permute-done.52 = bf16[8,128,512]{2,1,0:T(8,128)(2,1)S(1)} collective-permute-done((bf16[8,128,512]{2,1,0:T(8,128)(2,1)S(1)}, bf16[8,128,512]{2,1,0:T(8,128)(2,1)S(1)}, u32[]{:S(2)}, u32[]{:S(2)}) %collective-permute-start.52) | collective-permute-done | bytes 1048608 | tf_op jit(solution)/shard_map/ppermute | solution.py:755
  459.0 1.8 convert_add_fusion
  462.2 4.5 shard_map.399
  466.7 4.5 shard_map.400
  (209 shorter events, 41.7 us)
Async XLA Ops:
  7.2 77.8 %all-gather.6.cloned.1.call-start = ((), (), s32[]{:S(2)}) async-start(), calls=%async_computation.1 | async-start | bytes 2359296 | tf_op jit(solution)/shard_map/all_gather | solution.py:811
  7.9 140.3 %all-gather.4.cloned.1.call-start = ((), (), s32[]{:S(2)}) async-start(), calls=%async_computation | async-start | bytes 2359296 | tf_op jit(solution)/shard_map/all_gather | solution.py:811
  29.1 38.0 %collective-permute-start.2 = (bf16[1,1,2,128,512]{4,3,2,1,0:T(8,128)(2,1)S(1)}, bf16[1,1,2,128,512]{4,3,2,1,0:T(8,128)(2,1)S(1)}, u32[]{:S(2)}, u32[]{:S(2)}) collective-permute-start(bf16[1,1,2,128,512]{4,3,2,1,0:T(8,128)(2,1)S(1)} %bitcast.103), channel_id=1, source_target_pairs={{0,6},{2,4},{4,2},{6,0},{1,7},{3,5},{5,3},{7,1},{8,14},{10,12},{12... | collective-permute-start | bytes 786440 | tf_op jit(solution)/shard_map/ppermute | solution.py:755
  34.2 39.8 %collective-permute-start.1 = (bf16[1,1,2,128,512]{4,3,2,1,0:T(8,128)(2,1)S(1)}, bf16[1,1,2,128,512]{4,3,2,1,0:T(8,128)(2,1)S(1)}, u32[]{:S(2)}, u32[]{:S(2)}) collective-permute-start(bf16[1,1,2,128,512]{4,3,2,1,0:T(8,128)(2,1)S(1)} %bitcast.104), channel_id=1, source_target_pairs={{0,4},{2,6},{4,0},{6,2},{1,5},{3,7},{5,1},{7,3},{8,12},{10,14},{12... | collective-permute-start | bytes 786440 | tf_op jit(solution)/shard_map/ppermute | solution.py:755
  34.2 39.8 %collective-permute-start = (bf16[1,1,2,128,512]{4,3,2,1,0:T(8,128)(2,1)S(1)}, bf16[1,1,2,128,512]{4,3,2,1,0:T(8,128)(2,1)S(1)}, u32[]{:S(2)}, u32[]{:S(2)}) collective-permute-start(bf16[1,1,2,128,512]{4,3,2,1,0:T(8,128)(2,1)S(1)} %bitcast.105), channel_id=1, source_target_pairs={{0,2},{2,0},{4,6},{6,4},{1,3},{3,1},{5,7},{7,5},{8,10},{10,8},{12,... | collective-permute-start | bytes 786440 | tf_op jit(solution)/shard_map/ppermute | solution.py:755
  74.4 55.4 %collective-permute-start.3 = (bf16[4,1,2,128,512]{4,3,2,1,0:T(8,128)(2,1)S(1)}, bf16[4,1,2,128,512]{4,3,2,1,0:T(8,128)(2,1)S(1)}, u32[]{:S(2)}, u32[]{:S(2)}) collective-permute-start(bf16[4,1,2,128,512]{4,3,2,1,0:T(8,128)(2,1)S(1)} %maximum_select_fusion.4.refs_10_), channel_id=1, source_target_pairs={{0,1},{1,0},{2,3},{3,2},{4,5},{5,4},{6,7},{7,6},{8,9},{9,8},{10,11... | collective-permute-start | bytes 3145736 | tf_op jit(solution)/shard_map/ppermute | solution.py:755
  182.9 21.5 %collective-permute-start.4 = (bf16[4,2,128,512]{3,2,1,0:T(8,128)(2,1)S(1)}, bf16[4,2,128,512]{3,2,1,0:T(8,128)(2,1)S(1)}, u32[]{:S(2)}, u32[]{:S(2)}) collective-permute-start(bf16[4,2,128,512]{3,2,1,0:T(8,128)(2,1)S(1)} %get-tuple-element.508), channel_id=1, source_target_pairs={{0,1},{1,0},{2,3},{3,2},{4,5},{5,4},{6,7},{7,6},{8,9},{9,8},{10,11... | collective-permute-start | bytes 3145736 | tf_op jit(solution)/shard_map/ppermute | solution.py:755
  200.0 35.9 %collective-permute-start.8 = (bf16[8,256,512]{2,1,0:T(8,128)(2,1)}, bf16[8,256,512]{2,1,0:T(8,128)(2,1)S(1)}, u32[]{:S(2)}, u32[]{:S(2)}) collective-permute-start(bf16[8,256,512]{2,1,0:T(8,128)(2,1)} %get-tuple-element.350), channel_id=1, source_target_pairs={{0,8},{8,0},{1,9},{9,1},{2,10},{10,2},{3,11},{11,3},{4,12},{12,4},... | collective-permute-start | bytes 6291464 | tf_op jit(solution)/shard_map/ppermute | solution.py:755
  205.4 25.3 %collective-permute-start.7 = (bf16[2,128,512]{2,1,0:T(8,128)(2,1)S(1)}, bf16[2,128,512]{2,1,0:T(8,128)(2,1)S(1)}, u32[]{:S(2)}, u32[]{:S(2)}) collective-permute-start(bf16[2,128,512]{2,1,0:T(8,128)(2,1)S(1)} %get-tuple-element.504), channel_id=1, source_target_pairs={{0,6},{2,4},{4,2},{6,0},{1,7},{3,5},{5,3},{7,1},{8,14},{10,12},{12... | collective-permute-start | bytes 786440 | tf_op jit(solution)/shard_map/ppermute | solution.py:755
  214.4 21.5 %collective-permute-start.6 = (bf16[2,128,512]{2,1,0:T(8,128)(2,1)S(1)}, bf16[2,128,512]{2,1,0:T(8,128)(2,1)S(1)}, u32[]{:S(2)}, u32[]{:S(2)}) collective-permute-start(bf16[2,128,512]{2,1,0:T(8,128)(2,1)S(1)} %get-tuple-element.505), channel_id=1, source_target_pairs={{0,4},{2,6},{4,0},{6,2},{1,5},{3,7},{5,1},{7,3},{8,12},{10,14},{12... | collective-permute-start | bytes 786440 | tf_op jit(solution)/shard_map/ppermute | solution.py:755
  214.4 21.5 %collective-permute-start.5 = (bf16[2,128,512]{2,1,0:T(8,128)(2,1)S(1)}, bf16[2,128,512]{2,1,0:T(8,128)(2,1)S(1)}, u32[]{:S(2)}, u32[]{:S(2)}) collective-permute-start(bf16[2,128,512]{2,1,0:T(8,128)(2,1)S(1)} %get-tuple-element.506), channel_id=1, source_target_pairs={{0,2},{2,0},{4,6},{6,4},{1,3},{3,1},{5,7},{7,5},{8,10},{10,8},{12,... | collective-permute-start | bytes 786440 | tf_op jit(solution)/shard_map/ppermute | solution.py:755
  215.0 15.6 %copy-start.18 = (f32[4,512]{1,0:T(4,128)S(1)}, f32[4,512]{1,0:T(4,128)}, u32[]{:S(2)}) copy-start(f32[4,512]{1,0:T(4,128)} %get-tuple-element.332.refs_8_) | copy-start | bytes 24580
  215.0 20.9 %copy-start.5 = (bf16[8,256,512]{2,1,0:T(8,128)(2,1)S(1)}, bf16[8,256,512]{2,1,0:T(8,128)(2,1)}, u32[]{:S(2)}) copy-start(bf16[8,256,512]{2,1,0:T(8,128)(2,1)} %get-tuple-element.373) | copy-start | bytes 6291460
  230.5 18.5 %collective-permute-start.9 = (bf16[8,256,512]{2,1,0:T(8,128)(2,1)}, bf16[8,256,512]{2,1,0:T(8,128)(2,1)}, u32[]{:S(2)}, u32[]{:S(2)}) collective-permute-start(bf16[8,256,512]{2,1,0:T(8,128)(2,1)} %get-tuple-element.380), channel_id=1, source_target_pairs={{0,8},{8,0},{1,9},{9,1},{2,10},{10,2},{3,11},{11,3},{4,12},{12,4},... | collective-permute-start | bytes 6291464 | tf_op jit(solution)/shard_map/ppermute | solution.py:755
  230.7 44.3 %collective-permute-start.15 = (bf16[4,2,128,512]{3,2,1,0:T(8,128)(2,1)}, bf16[4,2,128,512]{3,2,1,0:T(8,128)(2,1)S(1)}, u32[]{:S(2)}, u32[]{:S(2)}) collective-permute-start(bf16[4,2,128,512]{3,2,1,0:T(8,128)(2,1)} %get-tuple-element.500), channel_id=1, source_target_pairs={{0,1},{1,0},{2,3},{3,2},{4,5},{5,4},{6,7},{7,6},{8,9},{9,8},{10,11... | collective-permute-start | bytes 3145736 | tf_op jit(solution)/shard_map/ppermute | solution.py:755
  238.0 37.0 %collective-permute-start.13 = (bf16[8,128,512]{2,1,0:T(8,128)(2,1)}, bf16[8,128,512]{2,1,0:T(8,128)(2,1)}, u32[]{:S(2)}, u32[]{:S(2)}) collective-permute-start(bf16[8,128,512]{2,1,0:T(8,128)(2,1)} %get-tuple-element.488), channel_id=1, source_target_pairs={{0,16},{16,0},{1,17},{17,1},{2,18},{18,2},{3,19},{19,3},{4,20},{20... | collective-permute-start | bytes 3145736 | tf_op jit(solution)/shard_map/ppermute | solution.py:755
  248.2 26.8 %collective-permute-start.14 = (bf16[8,256,512]{2,1,0:T(8,128)(2,1)}, bf16[8,256,512]{2,1,0:T(8,128)(2,1)S(1)}, u32[]{:S(2)}, u32[]{:S(2)}) collective-permute-start(bf16[8,256,512]{2,1,0:T(8,128)(2,1)} %get-tuple-element.390), channel_id=1, source_target_pairs={{0,8},{8,0},{1,9},{9,1},{2,10},{10,2},{3,11},{11,3},{4,12},{12,4},... | collective-permute-start | bytes 6291464 | tf_op jit(solution)/shard_map/ppermute | solution.py:755
  252.5 52.8 %collective-permute-start.12 = (bf16[8,128,512]{2,1,0:T(8,128)(2,1)}, bf16[8,128,512]{2,1,0:T(8,128)(2,1)S(1)}, u32[]{:S(2)}, u32[]{:S(2)}) collective-permute-start(bf16[8,128,512]{2,1,0:T(8,128)(2,1)} %get-tuple-element.490), channel_id=1, source_target_pairs={{0,1},{1,0},{2,3},{3,2},{4,5},{5,4},{6,7},{7,6},{8,9},{9,8},{10,11... | collective-permute-start | bytes 3145736 | tf_op jit(solution)/shard_map/ppermute | solution.py:755
  274.9 7.0 %collective-permute-start.10 = (bf16[1040,512]{1,0:T(8,128)(2,1)S(1)}, bf16[1040,512]{1,0:T(8,128)(2,1)S(1)}, u32[]{:S(2)}, u32[]{:S(2)}) collective-permute-start(bf16[1040,512]{1,0:T(8,128)(2,1)S(1)} %get-tuple-element.554), channel_id=1, source_target_pairs={{0,8},{8,0},{1,9},{9,1},{2,10},{10,2},{3,11},{11,3},{4,12},{12,4},... | collective-permute-start | bytes 3194888 | tf_op jit(solution)/shard_map/ppermute | solution.py:755
  275.9 25.6 %collective-permute-start.17 = (bf16[8,128,512]{2,1,0:T(8,128)(2,1)S(1)}, bf16[8,128,512]{2,1,0:T(8,128)(2,1)S(1)}, u32[]{:S(2)}, u32[]{:S(2)}) collective-permute-start(bf16[8,128,512]{2,1,0:T(8,128)(2,1)S(1)} %get-tuple-element.486), channel_id=1, source_target_pairs={{0,16},{16,0},{1,17},{17,1},{2,18},{18,2},{3,19},{19,3},{4,20},{20... | collective-permute-start | bytes 3145736 | tf_op jit(solution)/shard_map/ppermute | solution.py:755
  278.3 23.6 %collective-permute-start.16 = (bf16[2,2,128,512]{3,2,1,0:T(8,128)(2,1)S(1)}, bf16[2,2,128,512]{3,2,1,0:T(8,128)(2,1)S(1)}, u32[]{:S(2)}, u32[]{:S(2)}) collective-permute-start(bf16[2,2,128,512]{3,2,1,0:T(8,128)(2,1)S(1)} %add_convert_fusion.15), channel_id=1, source_target_pairs={{0,2},{2,0},{4,6},{6,4},{1,3},{3,1},{5,7},{7,5},{8,10},{10,8},{12,... | collective-permute-start | bytes 1572872 | tf_op jit(solution)/shard_map/ppermute | solution.py:755
  280.8 14.9 %collective-permute-start.18 = (bf16[8,64,512]{2,1,0:T(8,128)(2,1)S(1)}, bf16[8,64,512]{2,1,0:T(8,128)(2,1)S(1)}, u32[]{:S(2)}, u32[]{:S(2)}) collective-permute-start(bf16[8,64,512]{2,1,0:T(8,128)(2,1)S(1)} %get-tuple-element.498), channel_id=1, source_target_pairs={{0,1},{1,0},{2,3},{3,2},{4,5},{5,4},{6,7},{7,6},{8,9},{9,8},{10,11... | collective-permute-start | bytes 1572872 | tf_op jit(solution)/shard_map/ppermute | solution.py:755
  282.5 28.4 %collective-permute-start.20 = (bf16[528,512]{1,0:T(8,128)(2,1)S(1)}, bf16[528,512]{1,0:T(8,128)(2,1)S(1)}, u32[]{:S(2)}, u32[]{:S(2)}) collective-permute-start(bf16[528,512]{1,0:T(8,128)(2,1)S(1)} %get-tuple-element.552), channel_id=1, source_target_pairs={{0,1},{1,0},{2,3},{3,2},{4,5},{5,4},{6,7},{7,6},{8,9},{9,8},{10,11... | collective-permute-start | bytes 1622024 | tf_op jit(solution)/shard_map/ppermute | solution.py:755
  295.9 9.8 %collective-permute-start.23 = (bf16[8,16,512]{2,1,0:T(8,128)(2,1)S(1)}, bf16[8,16,512]{2,1,0:T(8,128)(2,1)S(1)}, u32[]{:S(2)}, u32[]{:S(2)}) collective-permute-start(bf16[8,16,512]{2,1,0:T(8,128)(2,1)S(1)} %get-tuple-element.532), channel_id=1, source_target_pairs={{0,6},{2,4},{4,2},{6,0},{1,7},{3,5},{5,3},{7,1},{8,14},{10,12},{12... | collective-permute-start | bytes 393224 | tf_op jit(solution)/shard_map/ppermute | solution.py:755
  301.5 8.9 %collective-permute-start.22 = (bf16[8,16,512]{2,1,0:T(8,128)(2,1)S(1)}, bf16[8,16,512]{2,1,0:T(8,128)(2,1)S(1)}, u32[]{:S(2)}, u32[]{:S(2)}) collective-permute-start(bf16[8,16,512]{2,1,0:T(8,128)(2,1)S(1)} %get-tuple-element.533), channel_id=1, source_target_pairs={{0,4},{2,6},{4,0},{6,2},{1,5},{3,7},{5,1},{7,3},{8,12},{10,14},{12... | collective-permute-start | bytes 393224 | tf_op jit(solution)/shard_map/ppermute | solution.py:755
  301.9 9.0 %collective-permute-start.21 = (bf16[8,16,512]{2,1,0:T(8,128)(2,1)S(1)}, bf16[8,16,512]{2,1,0:T(8,128)(2,1)S(1)}, u32[]{:S(2)}, u32[]{:S(2)}) collective-permute-start(bf16[8,16,512]{2,1,0:T(8,128)(2,1)S(1)} %get-tuple-element.534), channel_id=1, source_target_pairs={{0,2},{2,0},{4,6},{6,4},{1,3},{3,1},{5,7},{7,5},{8,10},{10,8},{12,... | collective-permute-start | bytes 393224 | tf_op jit(solution)/shard_map/ppermute | solution.py:755
  311.1 18.6 %collective-permute-start.25 = (bf16[2,128,512]{2,1,0:T(8,128)(2,1)S(1)}, bf16[2,128,512]{2,1,0:T(8,128)(2,1)S(1)}, u32[]{:S(2)}, u32[]{:S(2)}) collective-permute-start(bf16[2,128,512]{2,1,0:T(8,128)(2,1)S(1)} %get-tuple-element.528), channel_id=1, source_target_pairs={{0,4},{2,6},{4,0},{6,2},{1,5},{3,7},{5,1},{7,3},{8,12},{10,14},{12... | collective-permute-start | bytes 786440 | tf_op jit(solution)/shard_map/ppermute | solution.py:755
  311.4 19.2 %collective-permute-start.24 = (bf16[272,512]{1,0:T(8,128)(2,1)S(1)}, bf16[272,512]{1,0:T(8,128)(2,1)S(1)}, u32[]{:S(2)}, u32[]{:S(2)}) collective-permute-start(bf16[272,512]{1,0:T(8,128)(2,1)S(1)} %get-tuple-element.550), channel_id=1, source_target_pairs={{0,16},{16,0},{1,17},{17,1},{2,18},{18,2},{3,19},{19,3},{4,20},{20... | collective-permute-start | bytes 835592 | tf_op jit(solution)/shard_map/ppermute | solution.py:755
  312.9 16.8 %copy-start.13 = (f32[256,512]{1,0:T(8,128)S(1)}, f32[256,512]{1,0:T(8,128)}, u32[]{:S(2)}) copy-start(f32[256,512]{1,0:T(8,128)} %get-tuple-element.415) | copy-start | bytes 1572868
  312.9 18.7 %collective-permute-start.19 = (bf16[8,64,512]{2,1,0:T(8,128)(2,1)S(1)}, bf16[8,64,512]{2,1,0:T(8,128)(2,1)S(1)}, u32[]{:S(2)}, u32[]{:S(2)}) collective-permute-start(bf16[8,64,512]{2,1,0:T(8,128)(2,1)S(1)} %get-tuple-element.496), channel_id=1, source_target_pairs={{0,16},{16,0},{1,17},{17,1},{2,18},{18,2},{3,19},{19,3},{4,20},{20... | collective-permute-start | bytes 1572872 | tf_op jit(solution)/shard_map/ppermute | solution.py:755
  313.7 20.2 %collective-permute-start.33 = (bf16[8,16,512]{2,1,0:T(8,128)(2,1)S(1)}, bf16[8,16,512]{2,1,0:T(8,128)(2,1)S(1)}, u32[]{:S(2)}, u32[]{:S(2)}) collective-permute-start(bf16[8,16,512]{2,1,0:T(8,128)(2,1)S(1)} %add_convert_fusion.43), channel_id=1, source_target_pairs={{0,6},{2,4},{4,2},{6,0},{1,7},{3,5},{5,3},{7,1},{8,14},{10,12},{12... | collective-permute-start | bytes 393224 | tf_op jit(solution)/shard_map/ppermute | solution.py:755
  315.6 19.7 %collective-permute-start.32 = (bf16[8,16,512]{2,1,0:T(8,128)(2,1)S(1)}, bf16[8,16,512]{2,1,0:T(8,128)(2,1)S(1)}, u32[]{:S(2)}, u32[]{:S(2)}) collective-permute-start(bf16[8,16,512]{2,1,0:T(8,128)(2,1)S(1)} %add_convert_fusion.43), channel_id=1, source_target_pairs={{0,4},{2,6},{4,0},{6,2},{1,5},{3,7},{5,1},{7,3},{8,12},{10,14},{12... | collective-permute-start | bytes 393224 | tf_op jit(solution)/shard_map/ppermute | solution.py:755
  329.7 8.4 %collective-permute-start.31 = (bf16[8,16,512]{2,1,0:T(8,128)(2,1)S(1)}, bf16[8,16,512]{2,1,0:T(8,128)(2,1)S(1)}, u32[]{:S(2)}, u32[]{:S(2)}) collective-permute-start(bf16[8,16,512]{2,1,0:T(8,128)(2,1)S(1)} %add_convert_fusion.43), channel_id=1, source_target_pairs={{0,2},{2,0},{4,6},{6,4},{1,3},{3,1},{5,7},{7,5},{8,10},{10,8},{12,... | collective-permute-start | bytes 393224 | tf_op jit(solution)/shard_map/ppermute | solution.py:755
  330.6 17.6 %collective-permute-start.29 = (bf16[8,64,512]{2,1,0:T(8,128)(2,1)S(1)}, bf16[8,64,512]{2,1,0:T(8,128)(2,1)S(1)}, u32[]{:S(2)}, u32[]{:S(2)}) collective-permute-start(bf16[8,64,512]{2,1,0:T(8,128)(2,1)S(1)} %get-tuple-element.492), channel_id=1, source_target_pairs={{0,1},{1,0},{2,3},{3,2},{4,5},{5,4},{6,7},{7,6},{8,9},{9,8},{10,11... | collective-permute-start | bytes 1572872 | tf_op jit(solution)/shard_map/ppermute | solution.py:755
  331.6 15.8 %collective-permute-start.30 = (bf16[272,512]{1,0:T(8,128)(2,1)S(1)}, bf16[272,512]{1,0:T(8,128)(2,1)S(1)}, u32[]{:S(2)}, u32[]{:S(2)}) collective-permute-start(bf16[272,512]{1,0:T(8,128)(2,1)S(1)} %add_convert_fusion.19), channel_id=1, source_target_pairs={{0,2},{2,0},{4,6},{6,4},{1,3},{3,1},{5,7},{7,5},{8,10},{10,8},{12,... | collective-permute-start | bytes 835592 | tf_op jit(solution)/shard_map/ppermute | solution.py:755
  338.1 10.9 %collective-permute-start.28 = (bf16[8,16,512]{2,1,0:T(8,128)(2,1)S(1)}, bf16[8,16,512]{2,1,0:T(8,128)(2,1)S(1)}, u32[]{:S(2)}, u32[]{:S(2)}) collective-permute-start(bf16[8,16,512]{2,1,0:T(8,128)(2,1)S(1)} %get-tuple-element.524), channel_id=1, source_target_pairs={{0,6},{2,4},{4,2},{6,0},{1,7},{3,5},{5,3},{7,1},{8,14},{10,12},{12... | collective-permute-start | bytes 393224 | tf_op jit(solution)/shard_map/ppermute | solution.py:755
  340.7 10.0 %collective-permute-start.27 = (bf16[8,16,512]{2,1,0:T(8,128)(2,1)S(1)}, bf16[8,16,512]{2,1,0:T(8,128)(2,1)S(1)}, u32[]{:S(2)}, u32[]{:S(2)}) collective-permute-start(bf16[8,16,512]{2,1,0:T(8,128)(2,1)S(1)} %get-tuple-element.525), channel_id=1, source_target_pairs={{0,4},{2,6},{4,0},{6,2},{1,5},{3,7},{5,1},{7,3},{8,12},{10,14},{12... | collective-permute-start | bytes 393224 | tf_op jit(solution)/shard_map/ppermute | solution.py:755
  340.7 21.2 %collective-permute-start.26 = (bf16[8,16,512]{2,1,0:T(8,128)(2,1)S(1)}, bf16[8,16,512]{2,1,0:T(8,128)(2,1)S(1)}, u32[]{:S(2)}, u32[]{:S(2)}) collective-permute-start(bf16[8,16,512]{2,1,0:T(8,128)(2,1)S(1)} %get-tuple-element.526), channel_id=1, source_target_pairs={{0,2},{2,0},{4,6},{6,4},{1,3},{3,1},{5,7},{7,5},{8,10},{10,8},{12,... | collective-permute-start | bytes 393224 | tf_op jit(solution)/shard_map/ppermute | solution.py:755
  347.5 20.9 %collective-permute-start.42 = (bf16[8,64,512]{2,1,0:T(8,128)(2,1)S(1)}, bf16[8,64,512]{2,1,0:T(8,128)(2,1)S(1)}, u32[]{:S(2)}, u32[]{:S(2)}) collective-permute-start(bf16[8,64,512]{2,1,0:T(8,128)(2,1)S(1)} %maximum_select_fusion.11), channel_id=1, source_target_pairs={{0,1},{1,0},{2,3},{3,2},{4,5},{5,4},{6,7},{7,6},{8,9},{9,8},{10,11... | collective-permute-start | bytes 1572872 | tf_op jit(solution)/shard_map/ppermute | solution.py:755
  348.2 20.1 %collective-permute-start.37 = (bf16[272,512]{1,0:T(8,128)(2,1)S(1)}, bf16[272,512]{1,0:T(8,128)(2,1)S(1)}, u32[]{:S(2)}, u32[]{:S(2)}) collective-permute-start(bf16[272,512]{1,0:T(8,128)(2,1)S(1)} %add_convert_fusion.18), channel_id=1, source_target_pairs={{0,4},{2,6},{4,0},{6,2},{1,5},{3,7},{5,1},{7,3},{8,12},{10,14},{12... | collective-permute-start | bytes 835592 | tf_op jit(solution)/shard_map/ppermute | solution.py:755
  349.0 42.8 %collective-permute-start.11 = (bf16[4,2,128,512]{3,2,1,0:T(8,128)(2,1)S(1)}, bf16[4,2,128,512]{3,2,1,0:T(8,128)(2,1)S(1)}, u32[]{:S(2)}, u32[]{:S(2)}) collective-permute-start(bf16[4,2,128,512]{3,2,1,0:T(8,128)(2,1)S(1)} %get-tuple-element.502), channel_id=1, source_target_pairs={{0,1},{1,0},{2,3},{3,2},{4,5},{5,4},{6,7},{7,6},{8,9},{9,8},{10,11... | collective-permute-start | bytes 3145736 | tf_op jit(solution)/shard_map/ppermute | solution.py:755
  350.7 19.5 %collective-permute-start.41 = (bf16[8,16,512]{2,1,0:T(8,128)(2,1)S(1)}, bf16[8,16,512]{2,1,0:T(8,128)(2,1)S(1)}, u32[]{:S(2)}, u32[]{:S(2)}) collective-permute-start(bf16[8,16,512]{2,1,0:T(8,128)(2,1)S(1)} %get-tuple-element.520), channel_id=1, source_target_pairs={{0,6},{2,4},{4,2},{6,0},{1,7},{3,5},{5,3},{7,1},{8,14},{10,12},{12... | collective-permute-start | bytes 393224 | tf_op jit(solution)/shard_map/ppermute | solution.py:755
  361.9 12.1 %collective-permute-start.40 = (bf16[8,16,512]{2,1,0:T(8,128)(2,1)S(1)}, bf16[8,16,512]{2,1,0:T(8,128)(2,1)S(1)}, u32[]{:S(2)}, u32[]{:S(2)}) collective-permute-start(bf16[8,16,512]{2,1,0:T(8,128)(2,1)S(1)} %get-tuple-element.521), channel_id=1, source_target_pairs={{0,4},{2,6},{4,0},{6,2},{1,5},{3,7},{5,1},{7,3},{8,12},{10,14},{12... | collective-permute-start | bytes 393224 | tf_op jit(solution)/shard_map/ppermute | solution.py:755
  368.3 10.9 %collective-permute-start.39 = (bf16[8,16,512]{2,1,0:T(8,128)(2,1)S(1)}, bf16[8,16,512]{2,1,0:T(8,128)(2,1)S(1)}, u32[]{:S(2)}, u32[]{:S(2)}) collective-permute-start(bf16[8,16,512]{2,1,0:T(8,128)(2,1)S(1)} %get-tuple-element.522), channel_id=1, source_target_pairs={{0,2},{2,0},{4,6},{6,4},{1,3},{3,1},{5,7},{7,5},{8,10},{10,8},{12,... | collective-permute-start | bytes 393224 | tf_op jit(solution)/shard_map/ppermute | solution.py:755
  368.4 10.9 %collective-permute-start.38 = (bf16[4,64,512]{2,1,0:T(8,128)(2,1)S(1)}, bf16[4,64,512]{2,1,0:T(8,128)(2,1)S(1)}, u32[]{:S(2)}, u32[]{:S(2)}) collective-permute-start(bf16[4,64,512]{2,1,0:T(8,128)(2,1)S(1)} %bitcast.88), channel_id=1, source_target_pairs={{0,16},{16,0},{1,17},{17,1},{2,18},{18,2},{3,19},{19,3},{4,20},{20... | collective-permute-start | bytes 786440 | tf_op jit(solution)/shard_map/ppermute | solution.py:755
  370.2 11.8 %collective-permute-start.36 = (bf16[8,16,512]{2,1,0:T(8,128)(2,1)S(1)}, bf16[8,16,512]{2,1,0:T(8,128)(2,1)S(1)}, u32[]{:S(2)}, u32[]{:S(2)}) collective-permute-start(bf16[8,16,512]{2,1,0:T(8,128)(2,1)S(1)} %add_convert_fusion.37), channel_id=1, source_target_pairs={{0,6},{2,4},{4,2},{6,0},{1,7},{3,5},{5,3},{7,1},{8,14},{10,12},{12... | collective-permute-start | bytes 393224 | tf_op jit(solution)/shard_map/ppermute | solution.py:755
  374.0 17.4 %collective-permute-start.35 = (bf16[8,16,512]{2,1,0:T(8,128)(2,1)S(1)}, bf16[8,16,512]{2,1,0:T(8,128)(2,1)S(1)}, u32[]{:S(2)}, u32[]{:S(2)}) collective-permute-start(bf16[8,16,512]{2,1,0:T(8,128)(2,1)S(1)} %add_convert_fusion.37), channel_id=1, source_target_pairs={{0,4},{2,6},{4,0},{6,2},{1,5},{3,7},{5,1},{7,3},{8,12},{10,14},{12... | collective-permute-start | bytes 393224 | tf_op jit(solution)/shard_map/ppermute | solution.py:755
  379.2 12.2 %collective-permute-start.34 = (bf16[8,16,512]{2,1,0:T(8,128)(2,1)S(1)}, bf16[8,16,512]{2,1,0:T(8,128)(2,1)S(1)}, u32[]{:S(2)}, u32[]{:S(2)}) collective-permute-start(bf16[8,16,512]{2,1,0:T(8,128)(2,1)S(1)} %add_convert_fusion.37), channel_id=1, source_target_pairs={{0,2},{2,0},{4,6},{6,4},{1,3},{3,1},{5,7},{7,5},{8,10},{10,8},{12,... | collective-permute-start | bytes 393224 | tf_op jit(solution)/shard_map/ppermute | solution.py:755
  379.3 13.7 %collective-permute-start.46 = (bf16[8,16,512]{2,1,0:T(8,128)(2,1)S(1)}, bf16[8,16,512]{2,1,0:T(8,128)(2,1)S(1)}, u32[]{:S(2)}, u32[]{:S(2)}) collective-permute-start(bf16[8,16,512]{2,1,0:T(8,128)(2,1)S(1)} %add_convert_fusion.33), channel_id=1, source_target_pairs={{0,6},{2,4},{4,2},{6,0},{1,7},{3,5},{5,3},{7,1},{8,14},{10,12},{12... | collective-permute-start | bytes 393224 | tf_op jit(solution)/shard_map/ppermute | solution.py:755
  382.1 14.4 %collective-permute-start.45 = (bf16[8,16,512]{2,1,0:T(8,128)(2,1)S(1)}, bf16[8,16,512]{2,1,0:T(8,128)(2,1)S(1)}, u32[]{:S(2)}, u32[]{:S(2)}) collective-permute-start(bf16[8,16,512]{2,1,0:T(8,128)(2,1)S(1)} %add_convert_fusion.33), channel_id=1, source_target_pairs={{0,4},{2,6},{4,0},{6,2},{1,5},{3,7},{5,1},{7,3},{8,12},{10,14},{12... | collective-permute-start | bytes 393224 | tf_op jit(solution)/shard_map/ppermute | solution.py:755
  391.4 6.4 %collective-permute-start.44 = (bf16[8,16,512]{2,1,0:T(8,128)(2,1)S(1)}, bf16[8,16,512]{2,1,0:T(8,128)(2,1)S(1)}, u32[]{:S(2)}, u32[]{:S(2)}) collective-permute-start(bf16[8,16,512]{2,1,0:T(8,128)(2,1)S(1)} %add_convert_fusion.33), channel_id=1, source_target_pairs={{0,2},{2,0},{4,6},{6,4},{1,3},{3,1},{5,7},{7,5},{8,10},{10,8},{12,... | collective-permute-start | bytes 393224 | tf_op jit(solution)/shard_map/ppermute | solution.py:755
  391.4 23.1 %collective-permute-start.49 = (bf16[8,128,512]{2,1,0:T(8,128)(2,1)S(1)}, bf16[8,128,512]{2,1,0:T(8,128)(2,1)S(1)}, u32[]{:S(2)}, u32[]{:S(2)}) collective-permute-start(bf16[8,128,512]{2,1,0:T(8,128)(2,1)S(1)} %maximum_select_fusion.5), channel_id=1, source_target_pairs={{0,16},{16,0},{1,17},{17,1},{2,18},{18,2},{3,19},{19,3},{4,20},{20... | collective-permute-start | bytes 3145736 | tf_op jit(solution)/shard_map/ppermute | solution.py:755
  391.8 11.9 %collective-permute-start.50 = (bf16[4,128,512]{2,1,0:T(8,128)(2,1)S(1)}, bf16[4,128,512]{2,1,0:T(8,128)(2,1)S(1)}, u32[]{:S(2)}, u32[]{:S(2)}) collective-permute-start(bf16[4,128,512]{2,1,0:T(8,128)(2,1)S(1)} %maximum_select_fusion.12), channel_id=1, source_target_pairs={{0,1},{1,0},{2,3},{3,2},{4,5},{5,4},{6,7},{7,6},{8,9},{9,8},{10,11... | collective-permute-start | bytes 1572872 | tf_op jit(solution)/shard_map/ppermute | solution.py:755
  415.2 16.2 %copy-start.8 = (bf16[8,256,512]{2,1,0:T(8,128)(2,1)}, bf16[8,256,512]{2,1,0:T(8,128)(2,1)S(1)}, u32[]{:S(2)}) copy-start(bf16[8,256,512]{2,1,0:T(8,128)(2,1)S(1)} %maximum_select_fusion.1.refs_0_.mine) | copy-start | bytes 6291460
  415.2 21.4 %collective-permute-start.53 = (bf16[8,256,512]{2,1,0:T(8,128)(2,1)S(1)}, bf16[8,256,512]{2,1,0:T(8,128)(2,1)S(1)}, u32[]{:S(2)}, u32[]{:S(2)}) collective-permute-start(bf16[8,256,512]{2,1,0:T(8,128)(2,1)S(1)} %maximum_select_fusion.1.refs_0_.mine), channel_id=1, source_target_pairs={{0,8},{8,0},{1,9},{9,1},{2,10},{10,2},{3,11},{11,3},{4,12},{12,4},... | collective-permute-start | bytes 6291464 | tf_op jit(solution)/shard_map/ppermute | solution.py:755
  415.3 14.3 %collective-permute-start.48 = (bf16[8,64,512]{2,1,0:T(8,128)(2,1)S(1)}, bf16[8,64,512]{2,1,0:T(8,128)(2,1)S(1)}, u32[]{:S(2)}, u32[]{:S(2)}) collective-permute-start(bf16[8,64,512]{2,1,0:T(8,128)(2,1)S(1)} %maximum_select_fusion.13), channel_id=1, source_target_pairs={{0,16},{16,0},{1,17},{17,1},{2,18},{18,2},{3,19},{19,3},{4,20},{20... | collective-permute-start | bytes 1572872 | tf_op jit(solution)/shard_map/ppermute | solution.py:755
  415.6 21.0 %collective-permute-start.54 = (bf16[4,256,512]{2,1,0:T(8,128)(2,1)S(1)}, bf16[4,256,512]{2,1,0:T(8,128)(2,1)S(1)}, u32[]{:S(2)}, u32[]{:S(2)}) collective-permute-start(bf16[4,256,512]{2,1,0:T(8,128)(2,1)S(1)} %maximum_select_fusion.6.mine), channel_id=1, source_target_pairs={{0,8},{8,0},{1,9},{9,1},{2,10},{10,2},{3,11},{11,3},{4,12},{12,4},... | collective-permute-start | bytes 3145736 | tf_op jit(solution)/shard_map/ppermute | solution.py:755
  415.8 15.1 %collective-permute-start.47 = (bf16[8,64,512]{2,1,0:T(8,128)(2,1)S(1)}, bf16[8,64,512]{2,1,0:T(8,128)(2,1)S(1)}, u32[]{:S(2)}, u32[]{:S(2)}) collective-permute-start(bf16[8,64,512]{2,1,0:T(8,128)(2,1)S(1)} %maximum_select_fusion.14), channel_id=1, source_target_pairs={{0,1},{1,0},{2,3},{3,2},{4,5},{5,4},{6,7},{7,6},{8,9},{9,8},{10,11... | collective-permute-start | bytes 1572872 | tf_op jit(solution)/shard_map/ppermute | solution.py:755
  416.7 15.6 %collective-permute-start.43 = (bf16[2,2,128,512]{3,2,1,0:T(8,128)(2,1)S(1)}, bf16[2,2,128,512]{3,2,1,0:T(8,128)(2,1)S(1)}, u32[]{:S(2)}, u32[]{:S(2)}) collective-permute-start(bf16[2,2,128,512]{3,2,1,0:T(8,128)(2,1)S(1)} %add_convert_fusion.6), channel_id=1, source_target_pairs={{0,2},{2,0},{4,6},{6,4},{1,3},{3,1},{5,7},{7,5},{8,10},{10,8},{12,... | collective-permute-start | bytes 1572872 | tf_op jit(solution)/shard_map/ppermute | solution.py:755
  430.1 24.8 %collective-permute-start.52 = (bf16[8,128,512]{2,1,0:T(8,128)(2,1)S(1)}, bf16[8,128,512]{2,1,0:T(8,128)(2,1)S(1)}, u32[]{:S(2)}, u32[]{:S(2)}) collective-permute-start(bf16[8,128,512]{2,1,0:T(8,128)(2,1)S(1)} %maximum_select_fusion.7), channel_id=1, source_target_pairs={{0,1},{1,0},{2,3},{3,2},{4,5},{5,4},{6,7},{7,6},{8,9},{9,8},{10,11... | collective-permute-start | bytes 3145736 | tf_op jit(solution)/shard_map/ppermute | solution.py:755
  431.4 24.5 %collective-permute-start.55 = (bf16[8,128,512]{2,1,0:T(8,128)(2,1)S(1)}, bf16[8,128,512]{2,1,0:T(8,128)(2,1)S(1)}, u32[]{:S(2)}, u32[]{:S(2)}) collective-permute-start(bf16[8,128,512]{2,1,0:T(8,128)(2,1)S(1)} %maximum_select_fusion.8), channel_id=1, source_target_pairs={{0,16},{16,0},{1,17},{17,1},{2,18},{18,2},{3,19},{19,3},{4,20},{20... | collective-permute-start | bytes 3145736 | tf_op jit(solution)/shard_map/ppermute | solution.py:755
  433.1 22.5 %collective-permute-start.51 = (bf16[2,128,512]{2,1,0:T(8,128)(2,1)}, bf16[2,128,512]{2,1,0:T(8,128)(2,1)}, u32[]{:S(2)}, u32[]{:S(2)}) collective-permute-start(bf16[2,128,512]{2,1,0:T(8,128)(2,1)} %get-tuple-element.510), channel_id=1, source_target_pairs={{0,4},{2,6},{4,0},{6,2},{1,5},{3,7},{5,1},{7,3},{8,12},{10,14},{12... | collective-permute-start | bytes 786440 | tf_op jit(solution)/shard_map/ppermute | solution.py:755
  455.5 5.3 %collective-permute-start.57 = (bf16[8,256,512]{2,1,0:T(8,128)(2,1)S(1)}, bf16[8,256,512]{2,1,0:T(8,128)(2,1)S(1)}, u32[]{:S(2)}, u32[]{:S(2)}) collective-permute-start(bf16[8,256,512]{2,1,0:T(8,128)(2,1)S(1)} %maximum_select_fusion.2.mine.refs_0_), channel_id=1, source_target_pairs={{0,8},{8,0},{1,9},{9,1},{2,10},{10,2},{3,11},{11,3},{4,12},{12,4},... | collective-permute-start | bytes 6291464 | tf_op jit(solution)/shard_map/ppermute | solution.py:755
  457.1 9.6 %collective-permute-start.56 = (bf16[8,256,512]{2,1,0:T(8,128)(2,1)S(1)}, bf16[8,256,512]{2,1,0:T(8,128)(2,1)}, u32[]{:S(2)}, u32[]{:S(2)}) collective-permute-start(bf16[8,256,512]{2,1,0:T(8,128)(2,1)S(1)} %maximum_select_fusion.3.mine.refs_0_), channel_id=1, source_target_pairs={{0,8},{8,0},{1,9},{9,1},{2,10},{10,2},{3,11},{11,3},{4,12},{12,4},... | collective-permute-start | bytes 6291464 | tf_op jit(solution)/shard_map/ppermute | solution.py:755
  (25 other events, 191.9 us)
Sparse Core Ops, SparseCore 0:
  10.1 62.2 all-gather.5
  99.8 48.4 all-gather.3

commit v3 on v2

--- a/solution.py
+++ b/solution.py
@@ -178,13 +178,25 @@
     )
 
 
-def store_part(ref, info_ref, pair_index, block, rows):
-    partners, _, pairs, size, _ = ref.shape
+def store_part(refs, info_ref, pair_index, block, rows):
+    partners, (_, pairs, size, _) = len(refs), refs[0].shape
+    if partners == 2 and KEY_BLOCK == 2 * size:
+        outer = block ^ info_ref[pairs + 3]
+        swap = info_ref[pairs + 1] == 1
+        first, second = rows[:size], rows[size:]
+        refs[0][outer, pair_index] = jnp.where(swap, second, first)
+        refs[1][outer, pair_index] = jnp.where(swap, first, second)
+        return
     for piece in range(KEY_BLOCK // size):
         place = block * (KEY_BLOCK // size) + piece
         inner = lax.rem(place, partners) ^ info_ref[pairs + 1]
         outer = lax.div(place, partners) ^ info_ref[pairs + 3]
-        ref[inner, outer, pair_index] = rows[piece * size : (piece + 1) * size]
+        part = rows[piece * size : (piece + 1) * size]
+        for partner, ref in enumerate(refs):
+
+            @pl.when(inner == partner)
+            def _(ref=ref):
+                ref[outer, pair_index] = part
 
 
 def long_limit(info_ref, causal, pair_index, size, pairs):
@@ -351,21 +363,18 @@
     return shape[-1] % 128 == 0 and size >= 2**16
 
 
-def launch(body, arrays, gives, scratch=(), info=None, after=(), pieces=(), plain=False, cost=10):
+def launch(body, arrays, gives, scratch=(), info=None, after=(), pieces=(), moved=None, cost=10):
     memory = pl.BlockSpec(memory_space=pltpu.VMEM)
     far = pl.BlockSpec(memory_space=pl.ANY)
     ins, specs = [], []
     if info is not None:
         ins.append(info)
         specs.append(pl.BlockSpec(memory_space=pltpu.SMEM))
-    moved_in = [
-        name for name, array in arrays.items() if not plain and copied(array.shape, array.dtype)
-    ]
-    moved_out = [
-        name
-        for name, (shape, dtype) in gives.items()
-        if name in pieces or not plain and copied(shape, jnp.dtype(dtype))
-    ]
+    by_itself = lambda name, shape, dtype: (
+        copied(shape, jnp.dtype(dtype)) if moved is None else name in moved
+    )
+    moved_in = [name for name, a in arrays.items() if by_itself(name, a.shape, a.dtype)]
+    moved_out = [name for name, give in gives.items() if name in pieces or by_itself(name, *give)]
     for name, array in arrays.items():
         ins.append(array)
         specs.append(far if name in moved_in else memory)
@@ -594,6 +603,10 @@
     decoder_tail(r, r.upper[...], r.o_c)
 
 
+def part_refs(r):
+    return [r[name] for name in r if name[0] == "p" and name[1:].isdigit()]
+
+
 def long_cross_back(r):
     long_attend_back(
         False,
@@ -609,7 +622,7 @@
         r.dq_c,
         r.dk_c,
         r.dv_c,
-        r.part,
+        part_refs(r),
         r.mix,
     )
 
@@ -630,7 +643,7 @@
         r.dq,
         r.dk,
         r.dv,
-        r.part,
+        part_refs(r),
         r.mix,
     )
     r.dt[...] = grad + nt(r.dq[...], r.w_in[0])
@@ -657,7 +670,7 @@
         r.dq,
         r.dk,
         r.dv,
-        r.part,
+        part_refs(r),
         r.mix,
     )
     r.dx[...] = r.d1[...] + nt(r.dq[...], r.w_in[0])
@@ -881,7 +894,7 @@
 class Spread:
     def __init__(self, part, straight):
         self.straight, self.stage = straight, 0
-        self.held = [send(part[k], INNER, k) if k else part[k] for k in range(part.shape[0])]
+        self.held = [send(rows, INNER, k) if k else rows for k, rows in enumerate(part)]
 
     def next_axis(self):
         return OUTER
@@ -1155,7 +1168,7 @@
 
     def parts():
         inner = lax.axis_size(INNER)
-        return {"part": ((inner, places // inner, pairs, own, width), BF16)}
+        return {"p%d" % k: ((places // inner, pairs, own, width), BF16) for k in range(inner)}
 
     def saved(kernel, names):
         return {name: kernel[name] for name in names}
@@ -1246,7 +1259,6 @@
     )
 
     early_target = gather_last(early_target, OUTER, 0, sb.small)
-    late_target = gather_first(early_target, INNER)
 
     whole_source = hold(whole_source, sb.small)
     x_long, t_long = flat(source_long), flat(target_long)
@@ -1263,8 +1275,9 @@
         info=source_info,
         after=(sb.small, early_target),
         cost=13,
-        plain=True,
-    )
+        moved=(),
+    )
+    late_target = gather_first(hold(early_target, le.lse), INNER)
     whole_encoded = gather_early(le.enc.reshape(pairs, own, width))
 
     seb = launch(
@@ -1326,7 +1339,7 @@
         info=target_info,
         after=(short_weights[0],),
         cost=10,
-        plain=True,
+        moved=(),
     )
 
     whole_encoded = hold(whole_encoded, ls.lse)
@@ -1349,7 +1362,7 @@
         info=source_info,
         after=(ls.lse,),
         cost=14,
-        plain=True,
+        moved=("k_c", "v_c", "up", "down", "w_co", "act", "gate", "dh", "final"),
     )
     lcb = launch(
         long_cross_back,
@@ -1363,25 +1376,25 @@
         info=source_info,
         after=(lc.small,),
         cost=14,
-        plain=True,
-    )
-    encoded_back = Spread(lcb.part, True)
+        moved=(),
+    )
+    encoded_back = Spread(part_refs(lcb), True)
     first_weights = Weights(
         [[(lc.m, lc.dh)], [(lc.act, lc.b5)]], short_weights[0]
     )
 
     def self_back_and_weights(r):
+        long_self_back(r)
         first_weights.body(r, r.info[pairs + 2])
-        long_self_back(r)
 
     lsb = launch(
         self_back_and_weights,
         {
-            **first_weights.arrays,
             "d4": lc.d4,
             "dq_c": lcb.dq_c,
             **saved(ls, ("q", "k", "v", "o", "lse", "n3", "i3")),
             **pick(decoder_in, ("w_in", "w_o", "w_cin", "gain")),
+            **first_weights.arrays,
         },
         {
             **first_weights.gives,
@@ -1400,7 +1413,7 @@
     decoder_ffn = Chain([lsb.kept, lsb.sent], (X, INNER, OUTER))
     finish([encoded_back], lsb.small)
     go(encoded_back)
-    target_back = Spread(lsb.part, False)
+    target_back = Spread(part_refs(lsb), False)
     grad_attention = weight_tiles(
         [
             [(ls.u, lcb.dq_c)],
@@ -1469,7 +1482,7 @@
 
     def attention_back_and_weights(r):
         long_encoder_back(r)
-        r.leave("part", "dx")
+        r.leave("dx", *[name for name in r if name[0] == "p" and name[1:].isdigit()])
         attention_weights.body(r, r.info[pairs + 2])
 
     lea = launch(
@@ -1520,7 +1533,7 @@
     ]
 
     def source_back(token):
-        chain = Spread(hold(lea.part, token), False)
+        chain = Spread(hold(part_refs(lea), token), False)
         return chain, 0.0, rows_out(lea.dx.reshape(source_long.shape))
 
     results = run_out(flights, source_back)

time: 483 us -> 477 us (0.988)
  starting transfers between devices: 83 us -> 73 us
  waiting for transfers between devices: 125 us -> 134 us
  local copies, waits for them, and re-layouts: 14.7 us -> 7.27 us
  Pallas kernels: 214 us -> 209 us
    ppermute x58, starting transfers between devices: 82.9 us -> 72.9 us  [send(): return lax.ppermute(piece, axis, [(i, i ^ offset) for i in range(count)])]
    ppermute x58, waiting for transfers between devices: 116 us -> 122 us  [send(): return lax.ppermute(piece, axis, [(i, i ^ offset) for i in range(count)])]
    pallas_call x14, Pallas kernels: 197 us -> 192 us  [launch(): pl.pallas_call(run, in_specs=specs, out_specs=[far if name in moved_out e...]
  transfers between devices with their start and end apart: 60 -> 60, of which waited for: 24 -> 23; matrix products, arithmetic and copies ran while one was open for 7% -> 7% of each run, Pallas kernels for 37% -> 34%
where the time goes in v3:
time: 477 us; the launch traced here: 468 us
  Pallas kernels  209 us (44%)
  waiting for transfers between devices  134 us (28%)
  starting transfers between devices  73 us (15%)
  other arithmetic  29.7 us (6%)
  between operations  15.5 us (3%)
  local copies, waits for them, and re-layouts  7.27 us (2%)
    pallas_call x14, Pallas kernels, launch(): pl.pallas_call(run, in_specs=specs, out_specs=[far if name in moved_out e...  192 us
    ppermute x58, waiting for transfers between devices, send(): return lax.ppermute(piece, axis, [(i, i ^ offset) for i in range(count)])  122 us
    ppermute x58, starting transfers between devices, send(): return lax.ppermute(piece, axis, [(i, i ^ offset) for i in range(count)])  72.9 us
    pallas_call x4, Pallas kernels, assemble(): pl.pallas_call(lambda info, mine, other, *refs: body(info, mine, other, *...  16.8 us
    convert_element_type x26, other arithmetic, added(): return total.astype(BF16)  13.4 us
    all_gather x2, waiting for transfers between devices, gather_early(): return lax.all_gather(rows, (OUTER, INNER), axis=0, tiled=False)  12.1 us
  transfers between devices with their start and end apart: 60, of which 23 were waited for; matrix products, arithmetic and copies ran while one was open for 7% of the time, Pallas kernels for 34%

profile of v3, /device:TPU:0, one launch (start us, length us, event | category | flops | bytes accessed | tf_op | source)
XLA Modules:
  0.0 468.3 jit_solution(15730173045338479264)
XLA Ops:
  8.0 1.5 broadcast_in_dim.24.refs_1_.refs_4_.refs_14_.refs_11_
  9.5 11.3 %shard_map.383 = (bf16[512,512]{1,0:T(8,128)(2,1)}, bf16[512,512]{1,0:T(8,128)(2,1)}, bf16[512,512]{1,0:T(8,128)(2,1)}, bf16[512,512]{1,0:T(8,128)(2,1)}, f32[4,...) custom-call(bf16[512,512]{1,0:T(8,128)(2,1)} %bitcast.85, ...), custom_call_target="tpu_custom_call" | custom-call | flops 11000000 | bytes 35000 | tf_op jit(solution)/shard_map/pallas_call | solution.py:432
  21.7 7.4 %shard_map.384 = (bf16[512,512]{1,0:T(8,128)(2,1)}, bf16[512,512]{1,0:T(8,128)(2,1)}, bf16[512,512]{1,0:T(8,128)(2,1)}, bf16[512,512]{1,0:T(8,128)(2,1)}, bf16[5...) custom-call(bf16[512,512]{1,0:T(8,128)(2,1)} %bitcast.83, ...), custom_call_target="tpu_custom_call" | custom-call | flops 11000000 | bytes 35000 | tf_op jit(solution)/shard_map/pallas_call | solution.py:432
  29.1 5.1 %collective-permute-start.2 = (bf16[1,1,2,128,512]{4,3,2,1,0:T(8,128)(2,1)S(1)}, bf16[1,1,2,128,512]{4,3,2,1,0:T(8,128)(2,1)S(1)}, u32[]{:S(2)}, u32[]{:S(2)}) collective-permute-start(bf16[1,1,2,128,512]{4,3,2,1,0:T(8,128)(2,1)S(1)} %bitcast.91), channel_id=1, source_target_pairs={{0,6},{2,4},{4,2},{6,0},{1,7},{3,5},{5,3},{7,1},{8,14},{10,12},{12... | collective-permute-start | bytes 786440 | tf_op jit(solution)/shard_map/ppermute | solution.py:768
  36.1 14.7 %shard_map.385 = (bf16[512,512]{1,0:T(8,128)(2,1)}, bf16[512,512]{1,0:T(8,128)(2,1)}, bf16[512,512]{1,0:T(8,128)(2,1)}, bf16[512,512]{1,0:T(8,128)(2,1)}, f32[4,...) custom-call(bf16[512,512]{1,0:T(8,128)(2,1)} %get-tuple-element.259., ...), custom_call_target="tpu_custom_call" | custom-call | flops 11000000 | bytes 35000 | tf_op jit(solution)/shard_map/pallas_call | solution.py:432
  50.8 16.3 %shard_map.386 = (bf16[512,512]{1,0:T(8,128)(2,1)}, bf16[512,512]{1,0:T(8,128)(2,1)}, bf16[512,512]{1,0:T(8,128)(2,1)}, bf16[512,512]{1,0:T(8,128)(2,1)}, bf16[5...) custom-call(bf16[512,512]{1,0:T(8,128)(2,1)} %get-tuple-element.264., ...), custom_call_target="tpu_custom_call" | custom-call | flops 11000000 | bytes 35000 | tf_op jit(solution)/shard_map/pallas_call | solution.py:432
  67.1 7.0 %collective-permute-done.1 = bf16[1,1,2,128,512]{4,3,2,1,0:T(8,128)(2,1)S(1)} collective-permute-done((bf16[1,1,2,128,512]{4,3,2,1,0:T(8,128)(2,1)S(1)}, bf16[1,1,2,128,512]{4,3,2,1,0:T(8,128)(2,1)S(1)}, u32[]{:S(2)}, u32[]{:S(2)}) %collective-permute-start.1) | collective-permute-done | bytes 262176 | tf_op jit(solution)/shard_map/ppermute | solution.py:768
  75.3 19.3 %shard_map.387 = (bf16[256,512]{1,0:T(8,128)(2,1)}, bf16[256,512]{1,0:T(8,128)(2,1)}, bf16[8,2,128,512]{3,2,1,0:T(8,128)(2,1)}, bf16[8,2,128,512]{3,2,1,0:T(8,12...) custom-call(s32[6]{0:T(128)} %concatenate.236.refs_0_, ...), custom_call_target="tpu_custom_call" | custom-call | flops 14300000256 | bytes 45500000 | tf_op jit(solution)/shard_map/pallas_call | solution.py:432
  95.9 15.7 %shard_map.388 = (bf16[512,512]{1,0:T(8,128)(2,1)}, bf16[512,512]{1,0:T(8,128)(2,1)}, bf16[512,512]{1,0:T(8,128)(2,1)}, bf16[512,512]{1,0:T(8,128)(2,1)}, bf16[5...) custom-call(f32[512,512]{1,0:T(8,128)} %get-tuple-element.301.refs_0, ...), custom_call_target="tpu_custom_call" | custom-call | flops 17600000000 | bytes 56000000 | tf_op jit(solution)/shard_map/pallas_call | solution.py:432
  111.6 14.3 %shard_map.389 = (bf16[8,512,512]{2,1,0:T(8,128)(2,1)}, bf16[8,512,512]{2,1,0:T(8,128)(2,1)}, bf16[8,512,512]{2,1,0:T(8,128)(2,1)}, bf16[4,512,512]{2,1,0:T(8,128)(2,1)}) custom-call(bf16[512,512]{1,0:T(8,128)(2,1)} %get-tuple-element.288.refs_0_, bf16[512,2048]{1,0:T(8,128)(2,1)} %get-tuple-element.289.refs_1_, ...), custom_call_target="tpu_custom_call" | custom-call | flops 16499999744 | bytes 52500000 | tf_op jit(solution)/shard_map/pallas_call | solution.py:432
  125.9 1.6 maximum_select_fusion
  127.5 7.8 %shard_map.390 = (bf16[256,512]{1,0:T(8,128)(2,1)}, bf16[256,512]{1,0:T(8,128)(2,1)}, bf16[256,512]{1,0:T(8,128)(2,1)}, bf16[256,512]{1,0:T(8,128)(2,1)}, bf16[2...) custom-call(s32[6]{0:T(128)} %concatenate.249.refs_0_, ...), custom_call_target="tpu_custom_call" | custom-call | flops 11000000512 | bytes 35000000 | tf_op jit(solution)/shard_map/pallas_call | solution.py:432
  135.3 12.1 %all-gather.4.cloned.1.call-done.refs_1_ = bf16[8,2,128,512]{3,2,1,0:T(8,128)(2,1)} async-done(((bf16[1,2,128,512]{3,2,1,0:T(8,128)(2,1)}), bf16[8,2,128,512]{3,2,1,0:T(8,128)(2,1)}) %all-gather.4.cloned.1.call-update) | async-done | bytes 2097168 | tf_op jit(solution)/shard_map/all_gather | solution.py:824
  147.4 13.7 %shard_map.391 = (bf16[256,512]{1,0:T(8,128)(2,1)}, bf16[8,2,128,512]{3,2,1,0:T(8,128)(2,1)}, bf16[8,2,128,512]{3,2,1,0:T(8,128)(2,1)}, f32[2,8,128]{2,1,0:T(8,1...) custom-call(s32[6]{0:T(128)} %concatenate.236.refs_0_, ...), custom_call_target="tpu_custom_call" | custom-call | flops 15399999488 | bytes 49000000 | tf_op jit(solution)/shard_map/pallas_call | solution.py:432
  161.1 13.7 %shard_map.392 = (bf16[256,512]{1,0:T(8,128)(2,1)}, bf16[8,2,128,512]{3,2,1,0:T(8,128)(2,1)}, bf16[8,2,128,512]{3,2,1,0:T(8,128)(2,1)}, bf16[4,2,128,512]{3,2,1,0:T(8,128)(2,1)}, bf16[4,2,128,512]{3,2,1,0:T(8,128)(2,1)}) custom-call(s32[6]{0:T(128)} %concatenate.236.refs_0_, bf16[256,512]{1,0:T(8,128)(2,1)} %get-tuple-element.325.refs_3_.refs_1_, ...), custom_call_target="tpu_custom_call" | custom-call | flops 15399999488 | bytes 49000000 | tf_op jit(solution)/shard_map/pallas_call | solution.py:432
  175.4 15.7 %shard_map.393 = (bf16[8,256,512]{2,1,0:T(8,128)(2,1)}, bf16[8,256,512]{2,1,0:T(8,128)(2,1)}, bf16[256,512]{1,0:T(8,128)(2,1)}, bf16[256,512]{1,0:T(8,128)(2,1)}...) custom-call(s32[6]{0:T(128)} %concatenate.249.refs_0_, ...), custom_call_target="tpu_custom_call" | custom-call | flops 24199999488 | bytes 77000000 | tf_op jit(solution)/shard_map/pallas_call | solution.py:432
  191.1 5.6 %collective-permute-start.8 = (bf16[8,256,512]{2,1,0:T(8,128)(2,1)}, bf16[8,256,512]{2,1,0:T(8,128)(2,1)S(1)}, u32[]{:S(2)}, u32[]{:S(2)}) collective-permute-start(bf16[8,256,512]{2,1,0:T(8,128)(2,1)} %get-tuple-element.357), channel_id=1, source_target_pairs={{0,8},{8,0},{1,9},{9,1},{2,10},{10,2},{3,11},{11,3},{4,12},{12,4},... | collective-permute-start | bytes 6291464 | tf_op jit(solution)/shard_map/ppermute | solution.py:768
  197.8 7.0 %collective-permute-start.7 = (bf16[2,128,512]{2,1,0:T(8,128)(2,1)S(1)}, bf16[2,128,512]{2,1,0:T(8,128)(2,1)S(1)}, u32[]{:S(2)}, u32[]{:S(2)}) collective-permute-start(bf16[2,128,512]{2,1,0:T(8,128)(2,1)S(1)} %get-tuple-element.510), channel_id=1, source_target_pairs={{0,6},{2,4},{4,2},{6,0},{1,7},{3,5},{5,3},{7,1},{8,14},{10,12},{12... | collective-permute-start | bytes 786440 | tf_op jit(solution)/shard_map/ppermute | solution.py:768
  205.4 15.5 %shard_map.394 = (bf16[8,256,512]{2,1,0:T(8,128)(2,1)}, bf16[8,256,512]{2,1,0:T(8,128)(2,1)}) custom-call(s32[1]{0:T(128)} %bitcast.8.refs_0_.info, bf16[256,512]{1,0:T(8,128)(2,1)} %get-tuple-element.358.refs_1_, bf16[256,512]{1,0:T(8,128)(2,1)} %get-tuple-element.342.refs_2_.refs_19_, bf16[2048,512]{1,0:T(8,128)(2,1)} %bitcast.109, ...), custom_call_target="tpu_custom_call" | custom-call | flops 16499999744 | bytes 52500000 | tf_op jit(solution)/shard_map/pallas_call | solution.py:432
  221.2 1.5 collective-permute-start.15
  222.6 3.5 collective-permute-done.6
  226.2 2.0 add_convert_fusion.2
  229.5 10.1 %shard_map.395 = (bf16[8,256,512]{2,1,0:T(8,128)(2,1)}, bf16[8,256,512]{2,1,0:T(8,128)(2,1)}, bf16[256,512]{1,0:T(8,128)(2,1)}, bf16[256,512]{1,0:T(8,128)(2,1)}...) custom-call(s32[1]{0:T(128)} %bitcast.8.refs_0_.info, ...), custom_call_target="tpu_custom_call" | custom-call | flops 13200000000 | bytes 42000000 | tf_op jit(solution)/shard_map/pallas_call | solution.py:432
  240.6 2.0 add_convert_fusion.3
  242.6 1.5 collective-permute-start.12
  244.1 16.4 %shard_map.396 = (bf16[4,256,512]{2,1,0:T(8,128)(2,1)}, bf16[4,256,512]{2,1,0:T(8,128)(2,1)}, bf16[4,2,128,512]{3,2,1,0:T(8,128)(2,1)}, bf16[4,2,128,512]{3,2,1,0:T(8,128)(2,1)}, f32[256,512]{1,0:T(8,128)}) custom-call(s32[6]{0:T(128)} %concatenate.236.refs_0_, bf16[256,512]{1,0:T(8,128)(2,1)} %get-tuple-element.329.refs_1_, ...), custom_call_target="tpu_custom_call" | custom-call | flops 20899999744 | bytes 66500000 | tf_op jit(solution)/shard_map/pallas_call | solution.py:432
  260.5 1.8 pad_maximum_fusion
  262.3 4.5 collective-permute-start.10
  269.4 1.5 add_convert_fusion.13
  272.2 1.6 collective-permute-start.20
  273.8 11.9 %collective-permute-done.18 = bf16[8,64,512]{2,1,0:T(8,128)(2,1)S(1)} collective-permute-done((bf16[8,64,512]{2,1,0:T(8,128)(2,1)S(1)}, bf16[8,64,512]{2,1,0:T(8,128)(2,1)S(1)}, u32[]{:S(2)}, u32[]{:S(2)}) %collective-permute-start.18) | collective-permute-done | bytes 524320 | tf_op jit(solution)/shard_map/ppermute | solution.py:768
  285.9 2.7 collective-permute-start.23
  288.6 4.3 collective-permute-done.17
  293.3 3.3 collective-permute-start.21
  298.5 3.1 collective-permute-done.22
  305.4 1.9 collective-permute-start.33
  307.3 1.6 collective-permute-start.32
  308.9 12.2 %collective-permute-done.25 = bf16[2,128,512]{2,1,0:T(8,128)(2,1)} collective-permute-done((bf16[2,128,512]{2,1,0:T(8,128)(2,1)}, bf16[2,128,512]{2,1,0:T(8,128)(2,1)}, u32[]{:S(2)}, u32[]{:S(2)}) %collective-permute-start.25) | collective-permute-done | bytes 262176 | tf_op jit(solution)/shard_map/ppermute | solution.py:768
  321.1 1.8 convert_add_fusion.1
  324.5 2.1 collective-permute-start.30
  326.8 2.6 collective-permute-done.31
  329.4 2.6 collective-permute-start.28
  332.0 1.7 collective-permute-start.26
  334.1 4.4 collective-permute-done.30
  341.4 2.5 collective-permute-done.27
  345.7 15.2 %collective-permute-done.37 = bf16[272,512]{1,0:T(8,128)(2,1)S(1)} collective-permute-done((bf16[272,512]{1,0:T(8,128)(2,1)S(1)}, bf16[272,512]{1,0:T(8,128)(2,1)S(1)}, u32[]{:S(2)}, u32[]{:S(2)}) %collective-permute-start.37) | collective-permute-done | bytes 278560 | tf_op jit(solution)/shard_map/ppermute | solution.py:768
  362.3 1.5 collective-permute-start.36
  363.8 7.0 %collective-permute-done.40 = bf16[8,16,512]{2,1,0:T(8,128)(2,1)S(1)} collective-permute-done((bf16[8,16,512]{2,1,0:T(8,128)(2,1)S(1)}, bf16[8,16,512]{2,1,0:T(8,128)(2,1)S(1)}, u32[]{:S(2)}, u32[]{:S(2)}) %collective-permute-start.40) | collective-permute-done | bytes 131104 | tf_op jit(solution)/shard_map/ppermute | solution.py:768
  370.8 2.1 collective-permute-start.34
  373.0 2.4 collective-permute-start.46
  375.7 8.0 %collective-permute-done.35 = bf16[8,16,512]{2,1,0:T(8,128)(2,1)S(1)} collective-permute-done((bf16[8,16,512]{2,1,0:T(8,128)(2,1)S(1)}, bf16[8,16,512]{2,1,0:T(8,128)(2,1)S(1)}, u32[]{:S(2)}, u32[]{:S(2)}) %collective-permute-start.35) | collective-permute-done | bytes 131104 | tf_op jit(solution)/shard_map/ppermute | solution.py:768
  385.9 2.5 collective-permute-done.45
  390.1 5.9 %collective-permute-done.50 = bf16[4,128,512]{2,1,0:T(8,128)(2,1)S(1)} collective-permute-done((bf16[4,128,512]{2,1,0:T(8,128)(2,1)S(1)}, bf16[4,128,512]{2,1,0:T(8,128)(2,1)S(1)}, u32[]{:S(2)}, u32[]{:S(2)}) %collective-permute-start.50) | collective-permute-done | bytes 524320 | tf_op jit(solution)/shard_map/ppermute | solution.py:768
  396.7 8.6 %collective-permute-done.49 = bf16[8,128,512]{2,1,0:T(8,128)(2,1)S(1)} collective-permute-done((bf16[8,128,512]{2,1,0:T(8,128)(2,1)S(1)}, bf16[8,128,512]{2,1,0:T(8,128)(2,1)S(1)}, u32[]{:S(2)}, u32[]{:S(2)}) %collective-permute-start.49) | collective-permute-done | bytes 1048608 | tf_op jit(solution)/shard_map/ppermute | solution.py:768
  406.1 1.8 collective-permute-start.48
  408.5 1.8 collective-permute-start.43
  410.3 10.2 %collective-permute-done.48 = bf16[8,64,512]{2,1,0:T(8,128)(2,1)S(1)} collective-permute-done((bf16[8,64,512]{2,1,0:T(8,128)(2,1)S(1)}, bf16[8,64,512]{2,1,0:T(8,128)(2,1)S(1)}, u32[]{:S(2)}, u32[]{:S(2)}) %collective-permute-start.48) | collective-permute-done | bytes 524320 | tf_op jit(solution)/shard_map/ppermute | solution.py:768
  424.4 3.1 collective-permute-start.51
  428.5 3.1 shard_map.397
  431.6 4.5 shard_map.398
  436.2 9.5 %collective-permute-done.52 = bf16[8,128,512]{2,1,0:T(8,128)(2,1)S(1)} collective-permute-done((bf16[8,128,512]{2,1,0:T(8,128)(2,1)S(1)}, bf16[8,128,512]{2,1,0:T(8,128)(2,1)S(1)}, u32[]{:S(2)}, u32[]{:S(2)}) %collective-permute-start.52) | collective-permute-done | bytes 1048608 | tf_op jit(solution)/shard_map/ppermute | solution.py:768
  450.1 1.8 convert_add_fusion
  451.9 4.5 shard_map.399
  456.5 4.5 shard_map.400
  (202 shorter events, 44.3 us)
Async XLA Ops:
  7.2 68.1 %all-gather.6.cloned.1.call-start = ((), (), s32[]{:S(2)}) async-start(), calls=%async_computation.1 | async-start | bytes 2359296 | tf_op jit(solution)/shard_map/all_gather | solution.py:824
  7.9 139.4 %all-gather.4.cloned.1.call-start = ((), (), s32[]{:S(2)}) async-start(), calls=%async_computation | async-start | bytes 2359296 | tf_op jit(solution)/shard_map/all_gather | solution.py:824
  29.1 37.9 %collective-permute-start.2 = (bf16[1,1,2,128,512]{4,3,2,1,0:T(8,128)(2,1)S(1)}, bf16[1,1,2,128,512]{4,3,2,1,0:T(8,128)(2,1)S(1)}, u32[]{:S(2)}, u32[]{:S(2)}) collective-permute-start(bf16[1,1,2,128,512]{4,3,2,1,0:T(8,128)(2,1)S(1)} %bitcast.91), channel_id=1, source_target_pairs={{0,6},{2,4},{4,2},{6,0},{1,7},{3,5},{5,3},{7,1},{8,14},{10,12},{12... | collective-permute-start | bytes 786440 | tf_op jit(solution)/shard_map/ppermute | solution.py:768
  34.2 39.8 %collective-permute-start.1 = (bf16[1,1,2,128,512]{4,3,2,1,0:T(8,128)(2,1)S(1)}, bf16[1,1,2,128,512]{4,3,2,1,0:T(8,128)(2,1)S(1)}, u32[]{:S(2)}, u32[]{:S(2)}) collective-permute-start(bf16[1,1,2,128,512]{4,3,2,1,0:T(8,128)(2,1)S(1)} %bitcast.92), channel_id=1, source_target_pairs={{0,4},{2,6},{4,0},{6,2},{1,5},{3,7},{5,1},{7,3},{8,12},{10,14},{12... | collective-permute-start | bytes 786440 | tf_op jit(solution)/shard_map/ppermute | solution.py:768
  34.2 39.8 %collective-permute-start = (bf16[1,1,2,128,512]{4,3,2,1,0:T(8,128)(2,1)S(1)}, bf16[1,1,2,128,512]{4,3,2,1,0:T(8,128)(2,1)S(1)}, u32[]{:S(2)}, u32[]{:S(2)}) collective-permute-start(bf16[1,1,2,128,512]{4,3,2,1,0:T(8,128)(2,1)S(1)} %bitcast.93), channel_id=1, source_target_pairs={{0,2},{2,0},{4,6},{6,4},{1,3},{3,1},{5,7},{7,5},{8,10},{10,8},{12,... | collective-permute-start | bytes 786440 | tf_op jit(solution)/shard_map/ppermute | solution.py:768
  75.3 19.3 %copy-start = (bf16[4,1,2,128,512]{4,3,2,1,0:T(8,128)(2,1)S(1)}, bf16[4,1,2,128,512]{4,3,2,1,0:T(8,128)(2,1)}, u32[]{:S(2)}) copy-start(bf16[4,1,2,128,512]{4,3,2,1,0:T(8,128)(2,1)} %maximum_select_fusion.4.refs_10_) | copy-start | bytes 3145732
  94.6 31.3 %collective-permute-start.3 = (bf16[4,1,2,128,512]{4,3,2,1,0:T(8,128)(2,1)S(1)}, bf16[4,1,2,128,512]{4,3,2,1,0:T(8,128)(2,1)S(1)}, u32[]{:S(2)}, u32[]{:S(2)}) collective-permute-start(bf16[4,1,2,128,512]{4,3,2,1,0:T(8,128)(2,1)S(1)} %copy-done), channel_id=1, source_target_pairs={{0,1},{1,0},{2,3},{3,2},{4,5},{5,4},{6,7},{7,6},{8,9},{9,8},{10,11... | collective-permute-start | bytes 3145736 | tf_op jit(solution)/shard_map/ppermute | solution.py:768
  174.8 21.9 %collective-permute-start.4 = (bf16[4,2,128,512]{3,2,1,0:T(8,128)(2,1)}, bf16[4,2,128,512]{3,2,1,0:T(8,128)(2,1)S(1)}, u32[]{:S(2)}, u32[]{:S(2)}) collective-permute-start(bf16[4,2,128,512]{3,2,1,0:T(8,128)(2,1)} %get-tuple-element.340), channel_id=1, source_target_pairs={{0,1},{1,0},{2,3},{3,2},{4,5},{5,4},{6,7},{7,6},{8,9},{9,8},{10,11... | collective-permute-start | bytes 3145736 | tf_op jit(solution)/shard_map/ppermute | solution.py:768
  175.4 21.3 %copy-start.9 = (bf16[4,2,128,512]{3,2,1,0:T(8,128)(2,1)S(1)}, bf16[4,2,128,512]{3,2,1,0:T(8,128)(2,1)}, u32[]{:S(2)}) copy-start(bf16[4,2,128,512]{3,2,1,0:T(8,128)(2,1)} %get-tuple-element.354) | copy-start | bytes 3145732
  191.1 35.1 %collective-permute-start.8 = (bf16[8,256,512]{2,1,0:T(8,128)(2,1)}, bf16[8,256,512]{2,1,0:T(8,128)(2,1)S(1)}, u32[]{:S(2)}, u32[]{:S(2)}) collective-permute-start(bf16[8,256,512]{2,1,0:T(8,128)(2,1)} %get-tuple-element.357), channel_id=1, source_target_pairs={{0,8},{8,0},{1,9},{9,1},{2,10},{10,2},{3,11},{11,3},{4,12},{12,4},... | collective-permute-start | bytes 6291464 | tf_op jit(solution)/shard_map/ppermute | solution.py:768
  197.8 23.4 %collective-permute-start.7 = (bf16[2,128,512]{2,1,0:T(8,128)(2,1)S(1)}, bf16[2,128,512]{2,1,0:T(8,128)(2,1)S(1)}, u32[]{:S(2)}, u32[]{:S(2)}) collective-permute-start(bf16[2,128,512]{2,1,0:T(8,128)(2,1)S(1)} %get-tuple-element.510), channel_id=1, source_target_pairs={{0,6},{2,4},{4,2},{6,0},{1,7},{3,5},{5,3},{7,1},{8,14},{10,12},{12... | collective-permute-start | bytes 786440 | tf_op jit(solution)/shard_map/ppermute | solution.py:768
  204.8 21.4 %collective-permute-start.6 = (bf16[2,128,512]{2,1,0:T(8,128)(2,1)S(1)}, bf16[2,128,512]{2,1,0:T(8,128)(2,1)}, u32[]{:S(2)}, u32[]{:S(2)}) collective-permute-start(bf16[2,128,512]{2,1,0:T(8,128)(2,1)S(1)} %get-tuple-element.511), channel_id=1, source_target_pairs={{0,4},{2,6},{4,0},{6,2},{1,5},{3,7},{5,1},{7,3},{8,12},{10,14},{12... | collective-permute-start | bytes 786440 | tf_op jit(solution)/shard_map/ppermute | solution.py:768
  204.8 21.4 %collective-permute-start.5 = (bf16[2,128,512]{2,1,0:T(8,128)(2,1)S(1)}, bf16[2,128,512]{2,1,0:T(8,128)(2,1)}, u32[]{:S(2)}, u32[]{:S(2)}) collective-permute-start(bf16[2,128,512]{2,1,0:T(8,128)(2,1)S(1)} %get-tuple-element.512), channel_id=1, source_target_pairs={{0,2},{2,0},{4,6},{6,4},{1,3},{3,1},{5,7},{7,5},{8,10},{10,8},{12,... | collective-permute-start | bytes 786440 | tf_op jit(solution)/shard_map/ppermute | solution.py:768
  205.4 20.8 %copy-start.3 = (bf16[8,256,512]{2,1,0:T(8,128)(2,1)S(1)}, bf16[8,256,512]{2,1,0:T(8,128)(2,1)}, u32[]{:S(2)}) copy-start(bf16[8,256,512]{2,1,0:T(8,128)(2,1)} %get-tuple-element.380) | copy-start | bytes 6291460
  220.9 19.7 %collective-permute-start.9 = (bf16[8,256,512]{2,1,0:T(8,128)(2,1)}, bf16[8,256,512]{2,1,0:T(8,128)(2,1)S(1)}, u32[]{:S(2)}, u32[]{:S(2)}) collective-permute-start(bf16[8,256,512]{2,1,0:T(8,128)(2,1)} %get-tuple-element.387), channel_id=1, source_target_pairs={{0,8},{8,0},{1,9},{9,1},{2,10},{10,2},{3,11},{11,3},{4,12},{12,4},... | collective-permute-start | bytes 6291464 | tf_op jit(solution)/shard_map/ppermute | solution.py:768
  221.2 45.6 %collective-permute-start.15 = (bf16[4,2,128,512]{3,2,1,0:T(8,128)(2,1)}, bf16[4,2,128,512]{3,2,1,0:T(8,128)(2,1)S(1)}, u32[]{:S(2)}, u32[]{:S(2)}) collective-permute-start(bf16[4,2,128,512]{3,2,1,0:T(8,128)(2,1)} %get-tuple-element.401), channel_id=1, source_target_pairs={{0,1},{1,0},{2,3},{3,2},{4,5},{5,4},{6,7},{7,6},{8,9},{9,8},{10,11... | collective-permute-start | bytes 3145736 | tf_op jit(solution)/shard_map/ppermute | solution.py:768
  228.2 38.6 %collective-permute-start.13 = (bf16[8,128,512]{2,1,0:T(8,128)(2,1)}, bf16[8,128,512]{2,1,0:T(8,128)(2,1)}, u32[]{:S(2)}, u32[]{:S(2)}) collective-permute-start(bf16[8,128,512]{2,1,0:T(8,128)(2,1)} %get-tuple-element.498), channel_id=1, source_target_pairs={{0,16},{16,0},{1,17},{17,1},{2,18},{18,2},{3,19},{19,3},{4,20},{20... | collective-permute-start | bytes 3145736 | tf_op jit(solution)/shard_map/ppermute | solution.py:768
  239.6 27.2 %collective-permute-start.14 = (bf16[8,256,512]{2,1,0:T(8,128)(2,1)}, bf16[8,256,512]{2,1,0:T(8,128)(2,1)S(1)}, u32[]{:S(2)}, u32[]{:S(2)}) collective-permute-start(bf16[8,256,512]{2,1,0:T(8,128)(2,1)} %get-tuple-element.399), channel_id=1, source_target_pairs={{0,8},{8,0},{1,9},{9,1},{2,10},{10,2},{3,11},{11,3},{4,12},{12,4},... | collective-permute-start | bytes 6291464 | tf_op jit(solution)/shard_map/ppermute | solution.py:768
  242.6 54.8 %collective-permute-start.12 = (bf16[8,128,512]{2,1,0:T(8,128)(2,1)}, bf16[8,128,512]{2,1,0:T(8,128)(2,1)S(1)}, u32[]{:S(2)}, u32[]{:S(2)}) collective-permute-start(bf16[8,128,512]{2,1,0:T(8,128)(2,1)} %get-tuple-element.500), channel_id=1, source_target_pairs={{0,1},{1,0},{2,3},{3,2},{4,5},{5,4},{6,7},{7,6},{8,9},{9,8},{10,11... | collective-permute-start | bytes 3145736 | tf_op jit(solution)/shard_map/ppermute | solution.py:768
  262.3 9.3 %collective-permute-start.10 = (bf16[1040,512]{1,0:T(8,128)(2,1)S(1)}, bf16[1040,512]{1,0:T(8,128)(2,1)S(1)}, u32[]{:S(2)}, u32[]{:S(2)}) collective-permute-start(bf16[1040,512]{1,0:T(8,128)(2,1)S(1)} %get-tuple-element.558), channel_id=1, source_target_pairs={{0,8},{8,0},{1,9},{9,1},{2,10},{10,2},{3,11},{11,3},{4,12},{12,4},... | collective-permute-start | bytes 3194888 | tf_op jit(solution)/shard_map/ppermute | solution.py:768
  267.5 25.4 %collective-permute-start.17 = (bf16[8,128,512]{2,1,0:T(8,128)(2,1)S(1)}, bf16[8,128,512]{2,1,0:T(8,128)(2,1)S(1)}, u32[]{:S(2)}, u32[]{:S(2)}) collective-permute-start(bf16[8,128,512]{2,1,0:T(8,128)(2,1)S(1)} %get-tuple-element.496), channel_id=1, source_target_pairs={{0,16},{16,0},{1,17},{17,1},{2,18},{18,2},{3,19},{19,3},{4,20},{20... | collective-permute-start | bytes 3145736 | tf_op jit(solution)/shard_map/ppermute | solution.py:768
  268.4 24.9 %collective-permute-start.16 = (bf16[2,2,128,512]{3,2,1,0:T(8,128)(2,1)S(1)}, bf16[2,2,128,512]{3,2,1,0:T(8,128)(2,1)S(1)}, u32[]{:S(2)}, u32[]{:S(2)}) collective-permute-start(bf16[2,2,128,512]{3,2,1,0:T(8,128)(2,1)S(1)} %add_convert_fusion.15), channel_id=1, source_target_pairs={{0,2},{2,0},{4,6},{6,4},{1,3},{3,1},{5,7},{7,5},{8,10},{10,8},{12,... | collective-permute-start | bytes 1572872 | tf_op jit(solution)/shard_map/ppermute | solution.py:768
  270.9 14.8 %collective-permute-start.18 = (bf16[8,64,512]{2,1,0:T(8,128)(2,1)S(1)}, bf16[8,64,512]{2,1,0:T(8,128)(2,1)S(1)}, u32[]{:S(2)}, u32[]{:S(2)}) collective-permute-start(bf16[8,64,512]{2,1,0:T(8,128)(2,1)S(1)} %get-tuple-element.508), channel_id=1, source_target_pairs={{0,1},{1,0},{2,3},{3,2},{4,5},{5,4},{6,7},{7,6},{8,9},{9,8},{10,11... | collective-permute-start | bytes 1572872 | tf_op jit(solution)/shard_map/ppermute | solution.py:768
  272.2 30.0 %collective-permute-start.20 = (bf16[528,512]{1,0:T(8,128)(2,1)S(1)}, bf16[528,512]{1,0:T(8,128)(2,1)S(1)}, u32[]{:S(2)}, u32[]{:S(2)}) collective-permute-start(bf16[528,512]{1,0:T(8,128)(2,1)S(1)} %get-tuple-element.556), channel_id=1, source_target_pairs={{0,1},{1,0},{2,3},{3,2},{4,5},{5,4},{6,7},{7,6},{8,9},{9,8},{10,11... | collective-permute-start | bytes 1622024 | tf_op jit(solution)/shard_map/ppermute | solution.py:768
  285.9 12.6 %collective-permute-start.23 = (bf16[8,16,512]{2,1,0:T(8,128)(2,1)S(1)}, bf16[8,16,512]{2,1,0:T(8,128)(2,1)S(1)}, u32[]{:S(2)}, u32[]{:S(2)}) collective-permute-start(bf16[8,16,512]{2,1,0:T(8,128)(2,1)S(1)} %get-tuple-element.536), channel_id=1, source_target_pairs={{0,6},{2,4},{4,2},{6,0},{1,7},{3,5},{5,3},{7,1},{8,14},{10,12},{12... | collective-permute-start | bytes 393224 | tf_op jit(solution)/shard_map/ppermute | solution.py:768
  292.9 8.7 %collective-permute-start.22 = (bf16[8,16,512]{2,1,0:T(8,128)(2,1)S(1)}, bf16[8,16,512]{2,1,0:T(8,128)(2,1)S(1)}, u32[]{:S(2)}, u32[]{:S(2)}) collective-permute-start(bf16[8,16,512]{2,1,0:T(8,128)(2,1)S(1)} %get-tuple-element.537), channel_id=1, source_target_pairs={{0,4},{2,6},{4,0},{6,2},{1,5},{3,7},{5,1},{7,3},{8,12},{10,14},{12... | collective-permute-start | bytes 393224 | tf_op jit(solution)/shard_map/ppermute | solution.py:768
  293.3 8.8 %collective-permute-start.21 = (bf16[8,16,512]{2,1,0:T(8,128)(2,1)S(1)}, bf16[8,16,512]{2,1,0:T(8,128)(2,1)S(1)}, u32[]{:S(2)}, u32[]{:S(2)}) collective-permute-start(bf16[8,16,512]{2,1,0:T(8,128)(2,1)S(1)} %get-tuple-element.538), channel_id=1, source_target_pairs={{0,2},{2,0},{4,6},{6,4},{1,3},{3,1},{5,7},{7,5},{8,10},{10,8},{12,... | collective-permute-start | bytes 393224 | tf_op jit(solution)/shard_map/ppermute | solution.py:768
  302.3 18.7 %collective-permute-start.25 = (bf16[2,128,512]{2,1,0:T(8,128)(2,1)}, bf16[2,128,512]{2,1,0:T(8,128)(2,1)}, u32[]{:S(2)}, u32[]{:S(2)}) collective-permute-start(bf16[2,128,512]{2,1,0:T(8,128)(2,1)} %get-tuple-element.532), channel_id=1, source_target_pairs={{0,4},{2,6},{4,0},{6,2},{1,5},{3,7},{5,1},{7,3},{8,12},{10,14},{12... | collective-permute-start | bytes 786440 | tf_op jit(solution)/shard_map/ppermute | solution.py:768
  302.4 22.0 %collective-permute-start.19 = (bf16[8,64,512]{2,1,0:T(8,128)(2,1)}, bf16[8,64,512]{2,1,0:T(8,128)(2,1)S(1)}, u32[]{:S(2)}, u32[]{:S(2)}) collective-permute-start(bf16[8,64,512]{2,1,0:T(8,128)(2,1)} %get-tuple-element.506), channel_id=1, source_target_pairs={{0,16},{16,0},{1,17},{17,1},{2,18},{18,2},{3,19},{19,3},{4,20},{20... | collective-permute-start | bytes 1572872 | tf_op jit(solution)/shard_map/ppermute | solution.py:768
  304.0 18.9 %collective-permute-start.24 = (bf16[272,512]{1,0:T(8,128)(2,1)}, bf16[272,512]{1,0:T(8,128)(2,1)}, u32[]{:S(2)}, u32[]{:S(2)}) collective-permute-start(bf16[272,512]{1,0:T(8,128)(2,1)} %get-tuple-element.554), channel_id=1, source_target_pairs={{0,16},{16,0},{1,17},{17,1},{2,18},{18,2},{3,19},{19,3},{4,20},{20... | collective-permute-start | bytes 835592 | tf_op jit(solution)/shard_map/ppermute | solution.py:768
  305.4 21.3 %collective-permute-start.33 = (bf16[8,16,512]{2,1,0:T(8,128)(2,1)S(1)}, bf16[8,16,512]{2,1,0:T(8,128)(2,1)S(1)}, u32[]{:S(2)}, u32[]{:S(2)}) collective-permute-start(bf16[8,16,512]{2,1,0:T(8,128)(2,1)S(1)} %add_convert_fusion.43), channel_id=1, source_target_pairs={{0,6},{2,4},{4,2},{6,0},{1,7},{3,5},{5,3},{7,1},{8,14},{10,12},{12... | collective-permute-start | bytes 393224 | tf_op jit(solution)/shard_map/ppermute | solution.py:768
  307.3 19.5 %collective-permute-start.32 = (bf16[8,16,512]{2,1,0:T(8,128)(2,1)S(1)}, bf16[8,16,512]{2,1,0:T(8,128)(2,1)S(1)}, u32[]{:S(2)}, u32[]{:S(2)}) collective-permute-start(bf16[8,16,512]{2,1,0:T(8,128)(2,1)S(1)} %add_convert_fusion.43), channel_id=1, source_target_pairs={{0,4},{2,6},{4,0},{6,2},{1,5},{3,7},{5,1},{7,3},{8,12},{10,14},{12... | collective-permute-start | bytes 393224 | tf_op jit(solution)/shard_map/ppermute | solution.py:768
  321.1 8.3 %collective-permute-start.31 = (bf16[8,16,512]{2,1,0:T(8,128)(2,1)S(1)}, bf16[8,16,512]{2,1,0:T(8,128)(2,1)S(1)}, u32[]{:S(2)}, u32[]{:S(2)}) collective-permute-start(bf16[8,16,512]{2,1,0:T(8,128)(2,1)S(1)} %add_convert_fusion.43), channel_id=1, source_target_pairs={{0,2},{2,0},{4,6},{6,4},{1,3},{3,1},{5,7},{7,5},{8,10},{10,8},{12,... | collective-permute-start | bytes 393224 | tf_op jit(solution)/shard_map/ppermute | solution.py:768
  322.9 16.3 %collective-permute-start.29 = (bf16[8,64,512]{2,1,0:T(8,128)(2,1)S(1)}, bf16[8,64,512]{2,1,0:T(8,128)(2,1)S(1)}, u32[]{:S(2)}, u32[]{:S(2)}) collective-permute-start(bf16[8,64,512]{2,1,0:T(8,128)(2,1)S(1)} %get-tuple-element.502), channel_id=1, source_target_pairs={{0,1},{1,0},{2,3},{3,2},{4,5},{5,4},{6,7},{7,6},{8,9},{9,8},{10,11... | collective-permute-start | bytes 1572872 | tf_op jit(solution)/shard_map/ppermute | solution.py:768
  324.5 14.1 %collective-permute-start.30 = (bf16[272,512]{1,0:T(8,128)(2,1)S(1)}, bf16[272,512]{1,0:T(8,128)(2,1)S(1)}, u32[]{:S(2)}, u32[]{:S(2)}) collective-permute-start(bf16[272,512]{1,0:T(8,128)(2,1)S(1)} %add_convert_fusion.19), channel_id=1, source_target_pairs={{0,2},{2,0},{4,6},{6,4},{1,3},{3,1},{5,7},{7,5},{8,10},{10,8},{12,... | collective-permute-start | bytes 835592 | tf_op jit(solution)/shard_map/ppermute | solution.py:768
  329.4 11.3 %collective-permute-start.28 = (bf16[8,16,512]{2,1,0:T(8,128)(2,1)S(1)}, bf16[8,16,512]{2,1,0:T(8,128)(2,1)S(1)}, u32[]{:S(2)}, u32[]{:S(2)}) collective-permute-start(bf16[8,16,512]{2,1,0:T(8,128)(2,1)S(1)} %get-tuple-element.528), channel_id=1, source_target_pairs={{0,6},{2,4},{4,2},{6,0},{1,7},{3,5},{5,3},{7,1},{8,14},{10,12},{12... | collective-permute-start | bytes 393224 | tf_op jit(solution)/shard_map/ppermute | solution.py:768
  332.0 11.9 %collective-permute-start.27 = (bf16[8,16,512]{2,1,0:T(8,128)(2,1)S(1)}, bf16[8,16,512]{2,1,0:T(8,128)(2,1)S(1)}, u32[]{:S(2)}, u32[]{:S(2)}) collective-permute-start(bf16[8,16,512]{2,1,0:T(8,128)(2,1)S(1)} %get-tuple-element.529), channel_id=1, source_target_pairs={{0,4},{2,6},{4,0},{6,2},{1,5},{3,7},{5,1},{7,3},{8,12},{10,14},{12... | collective-permute-start | bytes 393224 | tf_op jit(solution)/shard_map/ppermute | solution.py:768
  332.0 13.1 %collective-permute-start.26 = (bf16[8,16,512]{2,1,0:T(8,128)(2,1)S(1)}, bf16[8,16,512]{2,1,0:T(8,128)(2,1)S(1)}, u32[]{:S(2)}, u32[]{:S(2)}) collective-permute-start(bf16[8,16,512]{2,1,0:T(8,128)(2,1)S(1)} %get-tuple-element.530), channel_id=1, source_target_pairs={{0,2},{2,0},{4,6},{6,4},{1,3},{3,1},{5,7},{7,5},{8,10},{10,8},{12,... | collective-permute-start | bytes 393224 | tf_op jit(solution)/shard_map/ppermute | solution.py:768
  338.6 22.4 %collective-permute-start.42 = (bf16[8,64,512]{2,1,0:T(8,128)(2,1)S(1)}, bf16[8,64,512]{2,1,0:T(8,128)(2,1)S(1)}, u32[]{:S(2)}, u32[]{:S(2)}) collective-permute-start(bf16[8,64,512]{2,1,0:T(8,128)(2,1)S(1)} %maximum_select_fusion.11), channel_id=1, source_target_pairs={{0,1},{1,0},{2,3},{3,2},{4,5},{5,4},{6,7},{7,6},{8,9},{9,8},{10,11... | collective-permute-start | bytes 1572872 | tf_op jit(solution)/shard_map/ppermute | solution.py:768
  339.2 21.7 %collective-permute-start.37 = (bf16[272,512]{1,0:T(8,128)(2,1)S(1)}, bf16[272,512]{1,0:T(8,128)(2,1)S(1)}, u32[]{:S(2)}, u32[]{:S(2)}) collective-permute-start(bf16[272,512]{1,0:T(8,128)(2,1)S(1)} %add_convert_fusion.18), channel_id=1, source_target_pairs={{0,4},{2,6},{4,0},{6,2},{1,5},{3,7},{5,1},{7,3},{8,12},{10,14},{12... | collective-permute-start | bytes 835592 | tf_op jit(solution)/shard_map/ppermute | solution.py:768
  340.7 43.9 %collective-permute-start.11 = (bf16[4,2,128,512]{3,2,1,0:T(8,128)(2,1)S(1)}, bf16[4,2,128,512]{3,2,1,0:T(8,128)(2,1)S(1)}, u32[]{:S(2)}, u32[]{:S(2)}) collective-permute-start(bf16[4,2,128,512]{3,2,1,0:T(8,128)(2,1)S(1)} %copy-done.24), channel_id=1, source_target_pairs={{0,1},{1,0},{2,3},{3,2},{4,5},{5,4},{6,7},{7,6},{8,9},{9,8},{10,11... | collective-permute-start | bytes 3145736 | tf_op jit(solution)/shard_map/ppermute | solution.py:768
  343.9 18.4 %collective-permute-start.41 = (bf16[8,16,512]{2,1,0:T(8,128)(2,1)S(1)}, bf16[8,16,512]{2,1,0:T(8,128)(2,1)S(1)}, u32[]{:S(2)}, u32[]{:S(2)}) collective-permute-start(bf16[8,16,512]{2,1,0:T(8,128)(2,1)S(1)} %get-tuple-element.524), channel_id=1, source_target_pairs={{0,6},{2,4},{4,2},{6,0},{1,7},{3,5},{5,3},{7,1},{8,14},{10,12},{12... | collective-permute-start | bytes 393224 | tf_op jit(solution)/shard_map/ppermute | solution.py:768
  345.1 25.6 %collective-permute-start.40 = (bf16[8,16,512]{2,1,0:T(8,128)(2,1)S(1)}, bf16[8,16,512]{2,1,0:T(8,128)(2,1)S(1)}, u32[]{:S(2)}, u32[]{:S(2)}) collective-permute-start(bf16[8,16,512]{2,1,0:T(8,128)(2,1)S(1)} %get-tuple-element.525), channel_id=1, source_target_pairs={{0,4},{2,6},{4,0},{6,2},{1,5},{3,7},{5,1},{7,3},{8,12},{10,14},{12... | collective-permute-start | bytes 393224 | tf_op jit(solution)/shard_map/ppermute | solution.py:768
  360.9 9.9 %collective-permute-start.39 = (bf16[8,16,512]{2,1,0:T(8,128)(2,1)S(1)}, bf16[8,16,512]{2,1,0:T(8,128)(2,1)S(1)}, u32[]{:S(2)}, u32[]{:S(2)}) collective-permute-start(bf16[8,16,512]{2,1,0:T(8,128)(2,1)S(1)} %get-tuple-element.526), channel_id=1, source_target_pairs={{0,2},{2,0},{4,6},{6,4},{1,3},{3,1},{5,7},{7,5},{8,10},{10,8},{12,... | collective-permute-start | bytes 393224 | tf_op jit(solution)/shard_map/ppermute | solution.py:768
  361.0 12.0 %collective-permute-start.38 = (bf16[4,64,512]{2,1,0:T(8,128)(2,1)S(1)}, bf16[4,64,512]{2,1,0:T(8,128)(2,1)S(1)}, u32[]{:S(2)}, u32[]{:S(2)}) collective-permute-start(bf16[4,64,512]{2,1,0:T(8,128)(2,1)S(1)} %bitcast.76), channel_id=1, source_target_pairs={{0,16},{16,0},{1,17},{17,1},{2,18},{18,2},{3,19},{19,3},{4,20},{20... | collective-permute-start | bytes 786440 | tf_op jit(solution)/shard_map/ppermute | solution.py:768
  362.3 23.4 %copy-start.11 = (bf16[4,2,128,512]{3,2,1,0:T(8,128)(2,1)S(1)}, bf16[4,2,128,512]{3,2,1,0:T(8,128)(2,1)}, u32[]{:S(2)}) copy-start(bf16[4,2,128,512]{3,2,1,0:T(8,128)(2,1)} %get-tuple-element.456) | copy-start | bytes 3145732
  362.3 13.3 %collective-permute-start.36 = (bf16[8,16,512]{2,1,0:T(8,128)(2,1)S(1)}, bf16[8,16,512]{2,1,0:T(8,128)(2,1)S(1)}, u32[]{:S(2)}, u32[]{:S(2)}) collective-permute-start(bf16[8,16,512]{2,1,0:T(8,128)(2,1)S(1)} %add_convert_fusion.37), channel_id=1, source_target_pairs={{0,6},{2,4},{4,2},{6,0},{1,7},{3,5},{5,3},{7,1},{8,14},{10,12},{12... | collective-permute-start | bytes 393224 | tf_op jit(solution)/shard_map/ppermute | solution.py:768
  370.8 12.9 %collective-permute-start.35 = (bf16[8,16,512]{2,1,0:T(8,128)(2,1)S(1)}, bf16[8,16,512]{2,1,0:T(8,128)(2,1)S(1)}, u32[]{:S(2)}, u32[]{:S(2)}) collective-permute-start(bf16[8,16,512]{2,1,0:T(8,128)(2,1)S(1)} %add_convert_fusion.37), channel_id=1, source_target_pairs={{0,4},{2,6},{4,0},{6,2},{1,5},{3,7},{5,1},{7,3},{8,12},{10,14},{12... | collective-permute-start | bytes 393224 | tf_op jit(solution)/shard_map/ppermute | solution.py:768
  370.8 12.9 %collective-permute-start.34 = (bf16[8,16,512]{2,1,0:T(8,128)(2,1)S(1)}, bf16[8,16,512]{2,1,0:T(8,128)(2,1)S(1)}, u32[]{:S(2)}, u32[]{:S(2)}) collective-permute-start(bf16[8,16,512]{2,1,0:T(8,128)(2,1)S(1)} %add_convert_fusion.37), channel_id=1, source_target_pairs={{0,2},{2,0},{4,6},{6,4},{1,3},{3,1},{5,7},{7,5},{8,10},{10,8},{12,... | collective-permute-start | bytes 393224 | tf_op jit(solution)/shard_map/ppermute | solution.py:768
  373.0 13.0 %collective-permute-start.46 = (bf16[8,16,512]{2,1,0:T(8,128)(2,1)S(1)}, bf16[8,16,512]{2,1,0:T(8,128)(2,1)S(1)}, u32[]{:S(2)}, u32[]{:S(2)}) collective-permute-start(bf16[8,16,512]{2,1,0:T(8,128)(2,1)S(1)} %add_convert_fusion.33), channel_id=1, source_target_pairs={{0,6},{2,4},{4,2},{6,0},{1,7},{3,5},{5,3},{7,1},{8,14},{10,12},{12... | collective-permute-start | bytes 393224 | tf_op jit(solution)/shard_map/ppermute | solution.py:768
  375.6 12.9 %collective-permute-start.45 = (bf16[8,16,512]{2,1,0:T(8,128)(2,1)S(1)}, bf16[8,16,512]{2,1,0:T(8,128)(2,1)S(1)}, u32[]{:S(2)}, u32[]{:S(2)}) collective-permute-start(bf16[8,16,512]{2,1,0:T(8,128)(2,1)S(1)} %add_convert_fusion.33), channel_id=1, source_target_pairs={{0,4},{2,6},{4,0},{6,2},{1,5},{3,7},{5,1},{7,3},{8,12},{10,14},{12... | collective-permute-start | bytes 393224 | tf_op jit(solution)/shard_map/ppermute | solution.py:768
  383.7 6.1 %collective-permute-start.44 = (bf16[8,16,512]{2,1,0:T(8,128)(2,1)S(1)}, bf16[8,16,512]{2,1,0:T(8,128)(2,1)S(1)}, u32[]{:S(2)}, u32[]{:S(2)}) collective-permute-start(bf16[8,16,512]{2,1,0:T(8,128)(2,1)S(1)} %add_convert_fusion.33), channel_id=1, source_target_pairs={{0,2},{2,0},{4,6},{6,4},{1,3},{3,1},{5,7},{7,5},{8,10},{10,8},{12,... | collective-permute-start | bytes 393224 | tf_op jit(solution)/shard_map/ppermute | solution.py:768
  383.7 21.7 %collective-permute-start.49 = (bf16[8,128,512]{2,1,0:T(8,128)(2,1)S(1)}, bf16[8,128,512]{2,1,0:T(8,128)(2,1)S(1)}, u32[]{:S(2)}, u32[]{:S(2)}) collective-permute-start(bf16[8,128,512]{2,1,0:T(8,128)(2,1)S(1)} %maximum_select_fusion.5), channel_id=1, source_target_pairs={{0,16},{16,0},{1,17},{17,1},{2,18},{18,2},{3,19},{19,3},{4,20},{20... | collective-permute-start | bytes 3145736 | tf_op jit(solution)/shard_map/ppermute | solution.py:768
  384.6 11.4 %collective-permute-start.50 = (bf16[4,128,512]{2,1,0:T(8,128)(2,1)S(1)}, bf16[4,128,512]{2,1,0:T(8,128)(2,1)S(1)}, u32[]{:S(2)}, u32[]{:S(2)}) collective-permute-start(bf16[4,128,512]{2,1,0:T(8,128)(2,1)S(1)} %maximum_select_fusion.12), channel_id=1, source_target_pairs={{0,1},{1,0},{2,3},{3,2},{4,5},{5,4},{6,7},{7,6},{8,9},{9,8},{10,11... | collective-permute-start | bytes 1572872 | tf_op jit(solution)/shard_map/ppermute | solution.py:768
  406.0 22.5 %collective-permute-start.53 = (bf16[8,256,512]{2,1,0:T(8,128)(2,1)S(1)}, bf16[8,256,512]{2,1,0:T(8,128)(2,1)}, u32[]{:S(2)}, u32[]{:S(2)}) collective-permute-start(bf16[8,256,512]{2,1,0:T(8,128)(2,1)S(1)} %maximum_select_fusion.1.refs_0_.mine), channel_id=1, source_target_pairs={{0,8},{8,0},{1,9},{9,1},{2,10},{10,2},{3,11},{11,3},{4,12},{12,4},... | collective-permute-start | bytes 6291464 | tf_op jit(solution)/shard_map/ppermute | solution.py:768
  406.1 14.3 %collective-permute-start.48 = (bf16[8,64,512]{2,1,0:T(8,128)(2,1)S(1)}, bf16[8,64,512]{2,1,0:T(8,128)(2,1)S(1)}, u32[]{:S(2)}, u32[]{:S(2)}) collective-permute-start(bf16[8,64,512]{2,1,0:T(8,128)(2,1)S(1)} %maximum_select_fusion.13), channel_id=1, source_target_pairs={{0,16},{16,0},{1,17},{17,1},{2,18},{18,2},{3,19},{19,3},{4,20},{20... | collective-permute-start | bytes 1572872 | tf_op jit(solution)/shard_map/ppermute | solution.py:768
  407.9 19.6 %collective-permute-start.54 = (bf16[4,256,512]{2,1,0:T(8,128)(2,1)S(1)}, bf16[4,256,512]{2,1,0:T(8,128)(2,1)S(1)}, u32[]{:S(2)}, u32[]{:S(2)}) collective-permute-start(bf16[4,256,512]{2,1,0:T(8,128)(2,1)S(1)} %maximum_select_fusion.6.mine), channel_id=1, source_target_pairs={{0,8},{8,0},{1,9},{9,1},{2,10},{10,2},{3,11},{11,3},{4,12},{12,4},... | collective-permute-start | bytes 3145736 | tf_op jit(solution)/shard_map/ppermute | solution.py:768
  408.1 14.2 %collective-permute-start.47 = (bf16[8,64,512]{2,1,0:T(8,128)(2,1)S(1)}, bf16[8,64,512]{2,1,0:T(8,128)(2,1)S(1)}, u32[]{:S(2)}, u32[]{:S(2)}) collective-permute-start(bf16[8,64,512]{2,1,0:T(8,128)(2,1)S(1)} %maximum_select_fusion.14), channel_id=1, source_target_pairs={{0,1},{1,0},{2,3},{3,2},{4,5},{5,4},{6,7},{7,6},{8,9},{9,8},{10,11... | collective-permute-start | bytes 1572872 | tf_op jit(solution)/shard_map/ppermute | solution.py:768
  408.5 15.0 %collective-permute-start.43 = (bf16[2,2,128,512]{3,2,1,0:T(8,128)(2,1)S(1)}, bf16[2,2,128,512]{3,2,1,0:T(8,128)(2,1)S(1)}, u32[]{:S(2)}, u32[]{:S(2)}) collective-permute-start(bf16[2,2,128,512]{3,2,1,0:T(8,128)(2,1)S(1)} %add_convert_fusion.6), channel_id=1, source_target_pairs={{0,2},{2,0},{4,6},{6,4},{1,3},{3,1},{5,7},{7,5},{8,10},{10,8},{12,... | collective-permute-start | bytes 1572872 | tf_op jit(solution)/shard_map/ppermute | solution.py:768
  420.9 24.8 %collective-permute-start.52 = (bf16[8,128,512]{2,1,0:T(8,128)(2,1)S(1)}, bf16[8,128,512]{2,1,0:T(8,128)(2,1)S(1)}, u32[]{:S(2)}, u32[]{:S(2)}) collective-permute-start(bf16[8,128,512]{2,1,0:T(8,128)(2,1)S(1)} %maximum_select_fusion.7), channel_id=1, source_target_pairs={{0,1},{1,0},{2,3},{3,2},{4,5},{5,4},{6,7},{7,6},{8,9},{9,8},{10,11... | collective-permute-start | bytes 3145736 | tf_op jit(solution)/shard_map/ppermute | solution.py:768
  422.7 24.7 %collective-permute-start.55 = (bf16[8,128,512]{2,1,0:T(8,128)(2,1)S(1)}, bf16[8,128,512]{2,1,0:T(8,128)(2,1)S(1)}, u32[]{:S(2)}, u32[]{:S(2)}) collective-permute-start(bf16[8,128,512]{2,1,0:T(8,128)(2,1)S(1)} %maximum_select_fusion.8), channel_id=1, source_target_pairs={{0,16},{16,0},{1,17},{17,1},{2,18},{18,2},{3,19},{19,3},{4,20},{20... | collective-permute-start | bytes 3145736 | tf_op jit(solution)/shard_map/ppermute | solution.py:768
  424.4 22.1 %collective-permute-start.51 = (bf16[2,128,512]{2,1,0:T(8,128)(2,1)}, bf16[2,128,512]{2,1,0:T(8,128)(2,1)}, u32[]{:S(2)}, u32[]{:S(2)}) collective-permute-start(bf16[2,128,512]{2,1,0:T(8,128)(2,1)} %get-tuple-element.514), channel_id=1, source_target_pairs={{0,4},{2,6},{4,0},{6,2},{1,5},{3,7},{5,1},{7,3},{8,12},{10,14},{12... | collective-permute-start | bytes 786440 | tf_op jit(solution)/shard_map/ppermute | solution.py:768
  446.3 5.6 %collective-permute-start.57 = (bf16[8,256,512]{2,1,0:T(8,128)(2,1)S(1)}, bf16[8,256,512]{2,1,0:T(8,128)(2,1)}, u32[]{:S(2)}, u32[]{:S(2)}) collective-permute-start(bf16[8,256,512]{2,1,0:T(8,128)(2,1)S(1)} %maximum_select_fusion.2.mine.refs_0_), channel_id=1, source_target_pairs={{0,8},{8,0},{1,9},{9,1},{2,10},{10,2},{3,11},{11,3},{4,12},{12,4},... | collective-permute-start | bytes 6291464 | tf_op jit(solution)/shard_map/ppermute | solution.py:768
  448.0 8.5 %collective-permute-start.56 = (bf16[8,256,512]{2,1,0:T(8,128)(2,1)S(1)}, bf16[8,256,512]{2,1,0:T(8,128)(2,1)}, u32[]{:S(2)}, u32[]{:S(2)}) collective-permute-start(bf16[8,256,512]{2,1,0:T(8,128)(2,1)S(1)} %maximum_select_fusion.3.mine.refs_0_), channel_id=1, source_target_pairs={{0,8},{8,0},{1,9},{9,1},{2,10},{10,2},{3,11},{11,3},{4,12},{12,4},... | collective-permute-start | bytes 6291464 | tf_op jit(solution)/shard_map/ppermute | solution.py:768
  (23 other events, 221.4 us)
Sparse Core Ops, SparseCore 0:
  10.1 62.3 all-gather.5
  94.7 52.5 all-gather.3

commit v4 on v3

--- a/solution.py
+++ b/solution.py
@@ -87,31 +87,43 @@
     )
 
 
-def feed_forward(rows, up_ref, down_ref, act_ref, gate_ref):
-    low = rows.astype(BF16)
-    total = rows
-    for start in range(0, up_ref.shape[1], CHUNK):
-        part = slice(start, start + CHUNK)
-        hidden = nn(low, up_ref[:, part])
+def chunks(ref, axis, step):
+    def body(index, carry):
+        step(pl.ds(pl.multiple_of(index * CHUNK, CHUNK), CHUNK))
+        return carry
+
+    lax.fori_loop(0, ref.shape[axis] // CHUNK, body, 0)
+
+
+def feed_forward(rows, up_ref, down_ref, act_ref, gate_ref, low_ref, total_ref):
+    low_ref[...] = rows.astype(BF16)
+    total_ref[...] = rows
+
+    def step(part):
+        hidden = nn(low_ref[...], up_ref[:, part])
         sigmoid = 0.5 * jnp.tanh(0.5 * hidden) + 0.5
         active = hidden * sigmoid
         gate_ref[:, part] = (sigmoid + active * (1.0 - sigmoid)).astype(BF16)
         active = active.astype(BF16)
         act_ref[:, part] = active
-        total = total + nn(active, down_ref[part, :])
-    return low, total
-
-
-def feed_back(grad, gate_ref, up_ref, down_ref, hidden_grad_ref):
-    low = grad.astype(BF16)
-    total = grad
-    for start in range(0, up_ref.shape[1], CHUNK):
-        part = slice(start, start + CHUNK)
-        hidden = nt(low, down_ref[part, :]) * gate_ref[:, part].astype(F32)
+        total_ref[...] += nn(active, down_ref[part, :])
+
+    chunks(up_ref, 1, step)
+    return total_ref[...]
+
+
+def feed_back(grad, gate_ref, up_ref, down_ref, hidden_grad_ref, low_ref, total_ref):
+    low_ref[...] = grad.astype(BF16)
+    total_ref[...] = grad
+
+    def step(part):
+        hidden = nt(low_ref[...], down_ref[part, :]) * gate_ref[:, part].astype(F32)
         hidden = hidden.astype(BF16)
         hidden_grad_ref[:, part] = hidden
-        total = total + nt(hidden, up_ref[:, part])
-    return low, total
+        total_ref[...] += nt(hidden, up_ref[:, part])
+
+    chunks(up_ref, 1, step)
+    return total_ref[...]
 
 
 def short_allowed(key_segment, query_segment, causal):
@@ -125,8 +137,9 @@
 
 def short_attend(causal, q_ref, k_ref, v_ref, kseg_ref, qseg_ref, o_ref, lse_ref):
     size = kseg_ref.shape[1]
-    for block in range(kseg_ref.shape[0]):
-        rows = slice(block * size, (block + 1) * size)
+
+    def one(block, carry):
+        rows = pl.ds(pl.multiple_of(block * size, size), size)
         allowed = short_allowed(kseg_ref[block], qseg_ref[block], causal)
         logs = []
         for pair in range(PAIRS):
@@ -141,14 +154,18 @@
             log_total = top + jnp.log(total)
             logs += [log_total[:, :size], log_total[:, size:]]
         lse_ref[block] = jnp.concatenate(logs, axis=0)
+        return carry
+
+    lax.fori_loop(0, kseg_ref.shape[0], one, 0)
 
 
 def short_attend_back(
     causal, q_ref, k_ref, v_ref, kseg_ref, qseg_ref, o_ref, lse_ref, go_ref, dq_ref, dk_ref, dv_ref
 ):
     size = kseg_ref.shape[1]
-    for block in range(kseg_ref.shape[0]):
-        rows = slice(block * size, (block + 1) * size)
+
+    def one(block, carry):
+        rows = pl.ds(pl.multiple_of(block * size, size), size)
         allowed = short_allowed(kseg_ref[block], qseg_ref[block], causal)
         delta = delta_rows(go_ref[rows, :], o_ref[rows, :])
         lse = lse_ref[block]
@@ -163,6 +180,9 @@
             dk_ref[rows, lanes] = nn(grad_scores, queries).astype(BF16)
             turned = diagonal(nn(k_ref[rows, lanes].T, grad_scores)).T
             dq_ref[rows, lanes] = (turned.astype(BF16).astype(F32) * SCALE).astype(BF16)
+        return carry
+
+    lax.fori_loop(0, kseg_ref.shape[0], one, 0)
 
 
 def load_keys(ref, pair_index, block, lanes):
@@ -342,12 +362,16 @@
 class Refs(dict):
     def __init__(self, *args):
         super().__init__(*args)
-        self.coming, self.leaving = {}, {}
+        self.coming, self.leaving, self.pieced = {}, {}, {}
 
     def __getattr__(self, name):
         if name in self.coming:
             self.coming.pop(name).wait()
         return self[name]
+
+    def leave_piece(self, name, piece):
+        source, target, signals, first = self.pieced[name]
+        pltpu.make_async_copy(source.at[piece], target.at[piece], signals.at[first + piece]).start()
 
     def leave(self, *names):
         for name in names:
@@ -409,6 +433,7 @@
         for name in moved_out:
             copies = []
             if name in pieces:
+                r.pieced[name] = (room[name], outer[name], go, place)
                 for piece in range(gives[name][0][0]):
                     source, target = room[name].at[piece], outer[name].at[piece]
                     copies.append(pltpu.make_async_copy(source, target, go.at[place]))
@@ -455,8 +480,7 @@
     first, normed, inverse = norm(residual, r.gain[0:1], r.bias[0:1])
     r.n1[...] = normed.astype(BF16)
     r.i1[...] = inverse
-    low, total = feed_forward(first, r.up, r.down, r.act, r.gate)
-    r.y[...] = low
+    total = feed_forward(first, r.up, r.down, r.act, r.gate, r.y, r.acc)
     r.leave("n1", "act", "gate", "y")
     encoded, normed, inverse = norm(total, r.gain[1:2], r.bias[1:2])
     r.n2[...] = normed.astype(BF16)
@@ -492,15 +516,13 @@
     gain, bias = r.gain, r.bias
     residual = upper + nn(o_ref[...], r.w_co[...])
     middle, normed4, inverse4 = norm(residual, gain[1:2], bias[1:2])
-    low, total = feed_forward(middle, r.up, r.down, r.act, r.gate)
-    r.m[...] = low
+    total = feed_forward(middle, r.up, r.down, r.act, r.gate, r.m, r.acc)
     r.leave("m", "act", "gate")
     final, normed5, inverse5 = norm(total, gain[2:3], bias[2:3])
     r.final[...] = final
     r.leave("final")
     grad, gain5, bias5 = norm_back(r.cot[...].astype(F32), normed5, inverse5, gain[2:3])
-    low, grad = feed_back(grad, r.gate, r.up, r.down, r.dh)
-    r.b5[...] = low
+    grad = feed_back(grad, r.gate, r.up, r.down, r.dh, r.b5, r.acc)
     r.leave("b5", "dh")
     grad, gain4, bias4 = norm_back(grad, normed4, inverse4, gain[1:2])
     low = grad.astype(BF16)
@@ -553,8 +575,7 @@
 
 def encoder_tail_back(r, grad):
     grad, gain2, bias2 = norm_back(grad, r.n2[...], r.i2[...], r.gain[1:2])
-    low, grad = feed_back(grad, r.gate, r.up, r.down, r.dh)
-    r.b2[...] = low
+    grad = feed_back(grad, r.gate, r.up, r.down, r.dh, r.b2, r.acc)
     r.leave("b2", "dh")
     grad, gain1, bias1 = norm_back(grad, r.n1[...], r.i1[...], r.gain[0:1])
     low = grad.astype(BF16)
@@ -689,61 +710,88 @@
             if id(rows) not in known:
                 known[id(rows)] = "w%d" % len(known)
                 self.arrays[known[id(rows)]] = rows
-            return known[id(rows)], rows.shape[1]
-
+            return known[id(rows)], rows.shape[-1]
+
+        self.count = 0
         for terms in pairs:
             terms = [(place(a), place(b)) for a, b in terms]
             (_, height), (_, width) = terms[0]
-            for row in range(0, height, SIDE):
-                for column in range(0, width, SIDE):
-                    self.plan.append([(a[0], row, b[0], column) for a, b in terms])
-        count = len(self.plan)
-        self.gives = {name: ((count, SIDE // 2, SIDE), BF16) for name in ("kept", "sent")}
+            self.plan.append((self.count, width // SIDE, [(a[0], b[0]) for a, b in terms]))
+            self.count += height // SIDE * (width // SIDE)
+        self.gives = {name: ((self.count, SIDE // 2, SIDE), BF16) for name in ("kept", "sent")}
         if base is not None:
             self.arrays["base"] = base
 
+    def each(self, r, step):
+        ends = [first for first, _, _ in self.plan[1:]] + [self.count]
+        for (first, across, terms), end in zip(self.plan, ends):
+            terms = [(getattr(r, a), getattr(r, b)) for a, b in terms]
+
+            def body(tile, carry, first=first, across=across, terms=terms):
+                row = pl.multiple_of(lax.div(tile - first, across) * SIDE, SIDE)
+                column = pl.multiple_of(lax.rem(tile - first, across) * SIDE, SIDE)
+                step(tile, row, column, terms)
+                return carry
+
+            lax.fori_loop(first, end, body, 0)
+
     def body(self, r, core):
         half = SIDE // 2
-        for index, terms in enumerate(self.plan):
+        if "base" in self.arrays:
+            r.base
+
+        def step(tile, row, column, terms):
             for flip, name in enumerate(("kept", "sent")):
+                inside = pl.multiple_of((core ^ flip) * half, half)
                 total = None
                 if "base" in self.arrays:
-                    begin = pl.multiple_of((core ^ flip) * half, half)
-                    total = r.base[index, pl.ds(begin, half), :].astype(F32)
-                for a, row, b, column in terms:
-                    left, right = getattr(r, a), getattr(r, b)
-                    begin = pl.multiple_of(row + (core ^ flip) * half, half)
-                    across = slice(column, column + SIDE)
+                    total = r["base"][tile, pl.ds(inside, half), :].astype(F32)
+                for left, right in terms:
+                    rows = pl.ds(pl.multiple_of(row + inside, half), half)
+                    across = pl.ds(column, SIDE)
                     if len(left.shape) == 4:
                         tall = left.shape[0] * left.shape[1] * left.shape[2]
-                        rows = left[:, :, :, pl.ds(begin, half)].reshape(tall, half)
+                        first = left[:, :, :, rows].reshape(tall, half)
                     else:
-                        rows = left[:, pl.ds(begin, half)]
+                        first = left[:, rows]
                     if len(right.shape) == 4:
                         tall = right.shape[0] * right.shape[1] * right.shape[2]
-                        product = tn(rows, right[:, :, :, across].reshape(tall, SIDE))
+                        product = tn(first, right[:, :, :, across].reshape(tall, SIDE))
                     else:
-                        product = tn(rows, right[:, across])
+                        product = tn(first, right[:, across])
                     total = product if total is None else total + product
-                r[name][index] = total.astype(BF16)
-                r.leaving[name][index].start()
+                r[name][tile] = total.astype(BF16)
+                r.leave_piece(name, tile)
+
+        self.each(r, step)
+
+
+class Tagged:
+    def __init__(self, r, tag):
+        self.r, self.tag = r, tag
+
+    def __getattr__(self, name):
+        return getattr(self.r, name + self.tag)
 
 
 def whole_tiles(chunks, after=(), cost=10):
     weights = [Weights([[pair] for pair in chunk]) for chunk in chunks]
     arrays, gives = {}, {}
     for number, part in enumerate(weights):
-        gives["c%d" % number] = ((len(part.plan), SIDE, SIDE), BF16)
+        gives["c%d" % number] = ((part.count, SIDE, SIDE), BF16)
         arrays.update((name + "c%d" % number, array) for name, array in part.arrays.items())
 
     def body(r):
         for number, part in enumerate(weights):
             tag = "c%d" % number
-            for index, ((a, row, b, column),) in enumerate(part.plan):
-                left, right = getattr(r, a + tag), getattr(r, b + tag)
-                product = tn(left[:, row : row + SIDE], right[:, column : column + SIDE])
-                r[tag][index] = product.astype(BF16)
-                r.leaving[tag][index].start()
+
+            def step(tile, row, column, terms, tag=tag):
+                ((left, right),) = terms
+                product = tn(left[:, pl.ds(row, SIDE)], right[:, pl.ds(column, SIDE)])
+                r[tag][tile] = product.astype(BF16)
+                r.leave_piece(tag, tile)
+
+            part.each(Tagged(r, tag), step)
 
     out = launch(body, arrays, gives, after=after, pieces=tuple(gives), cost=cost)
     return list(out.values())
@@ -1195,6 +1243,7 @@
         {"x": flat(source_short), **segments, **encoder_in},
         {**rows_of(rows, ("q", "k", "v", "o")), **logs(blocks, ("lse",)), **encoder_keeps(rows)},
         cost=0.01,
+        scratch=[("acc", pltpu.VMEM((rows, width), F32))],
     )
     decoder_keeps = lambda n: {
         **rows_of(n, ("m", "b5", "b4", "go_c")),
@@ -1237,6 +1286,7 @@
         },
         after=(sd.lse,),
         cost=0.01,
+        scratch=[("acc", pltpu.VMEM((rows, width), F32))],
     )
 
     sb = launch(
@@ -1271,7 +1321,7 @@
             **logs(pairs, ("lse",)),
             **encoder_keeps(rows_long),
         },
-        scratch=work,
+        scratch=work + [("acc", pltpu.VMEM((rows_long, width), F32))],
         info=source_info,
         after=(sb.small, early_target),
         cost=13,
@@ -1294,7 +1344,7 @@
             **floats(rows, ("dx",)),
             **sums(4),
         },
-        scratch=[("d1", pltpu.VMEM((rows, width), F32))],
+        scratch=[("acc", pltpu.VMEM((rows, width), F32)), ("d1", pltpu.VMEM((rows, width), F32))],
         after=(le.lse,),
         cost=16,
     )
@@ -1358,7 +1408,7 @@
             **logs(pairs, ("lse_c",)),
             **decoder_keeps(rows_long),
         },
-        scratch=work,
+        scratch=work + [("acc", pltpu.VMEM((rows_long, width), F32))],
         info=source_info,
         after=(ls.lse,),
         cost=14,
@@ -1464,6 +1514,7 @@
         after=(grad_attention[0], decoder_ffn.held[0]),
         pieces=("kept", "sent"),
         cost=12,
+        scratch=[("acc", pltpu.VMEM((rows_long, width), F32))],
     )
     small = jnp.concatenate([seb.small + leb.small, sb.small + lsb.small, sc.small + lc.small])
     small = jnp.pad(small, ((0, 16 - small.shape[0]), (0, 0))).astype(BF16)

time: 477 us -> 480 us (level)
  Pallas kernels: 209 us -> 231 us
  waiting for transfers between devices: 134 us -> 120 us
  starting transfers between devices: 73 us -> 68.1 us
    pallas_call x14, Pallas kernels: 192 us -> 215 us  [launch(): pl.pallas_call(run, in_specs=specs, out_specs=[far if name in moved_out e...]
    ppermute x58, waiting for transfers between devices: 122 us -> 113 us  [send(): return lax.ppermute(piece, axis, [(i, i ^ offset) for i in range(count)])]
    all_gather x2, waiting for transfers between devices: 12.1 us -> 6.14 us  [gather_early(): return lax.all_gather(rows, (OUTER, INNER), axis=0, tiled=False)]
    ppermute x58, starting transfers between devices: 72.9 us -> 68 us  [send(): return lax.ppermute(piece, axis, [(i, i ^ offset) for i in range(count)])]
  transfers between devices with their start and end apart: 60 -> 60, of which waited for: 23 -> 22; matrix products, arithmetic and copies ran while one was open for 7% -> 7% of each run, Pallas kernels for 34% -> 37%
where the time goes in v4:
time: 480 us; the launch traced here: 472 us
  Pallas kernels  231 us (48%)
  waiting for transfers between devices  120 us (25%)
  starting transfers between devices  68.1 us (14%)
  other arithmetic  29.7 us (6%)
  between operations  15.5 us (3%)
  local copies, waits for them, and re-layouts  7.55 us (2%)
    pallas_call x14, Pallas kernels, launch(): pl.pallas_call(run, in_specs=specs, out_specs=[far if name in moved_out e...  215 us
    ppermute x58, waiting for transfers between devices, send(): return lax.ppermute(piece, axis, [(i, i ^ offset) for i in range(count)])  113 us
    ppermute x58, starting transfers between devices, send(): return lax.ppermute(piece, axis, [(i, i ^ offset) for i in range(count)])  68 us
    pallas_call x4, Pallas kernels, assemble(): pl.pallas_call(lambda info, mine, other, *refs: body(info, mine, other, *...  16.8 us
    convert_element_type x26, other arithmetic, added(): return total.astype(BF16)  13.4 us
  transfers between devices with their start and end apart: 60, of which 22 were waited for; matrix products, arithmetic and copies ran while one was open for 7% of the time, Pallas kernels for 37%

profile of v4, /device:TPU:0, one launch (start us, length us, event | category | flops | bytes accessed | tf_op | source)
XLA Modules:
  0.0 471.8 jit_solution(4649358479364465588)
XLA Ops:
  9.5 14.1 %shard_map.383 = (bf16[512,512]{1,0:T(8,128)(2,1)}, bf16[512,512]{1,0:T(8,128)(2,1)}, bf16[512,512]{1,0:T(8,128)(2,1)}, bf16[512,512]{1,0:T(8,128)(2,1)}, f32[4,...) custom-call(bf16[512,512]{1,0:T(8,128)(2,1)} %bitcast.85, ...), custom_call_target="tpu_custom_call" | custom-call | flops 11000000 | bytes 35000 | tf_op jit(solution)/shard_map/pallas_call | solution.py:457
  24.5 9.3 %shard_map.384 = (bf16[512,512]{1,0:T(8,128)(2,1)}, bf16[512,512]{1,0:T(8,128)(2,1)}, bf16[512,512]{1,0:T(8,128)(2,1)}, bf16[512,512]{1,0:T(8,128)(2,1)}, bf16[5...) custom-call(bf16[512,512]{1,0:T(8,128)(2,1)} %bitcast.83, ...), custom_call_target="tpu_custom_call" | custom-call | flops 11000000 | bytes 35000 | tf_op jit(solution)/shard_map/pallas_call | solution.py:457
  33.8 5.1 %collective-permute-start.2 = (bf16[1,1,2,128,512]{4,3,2,1,0:T(8,128)(2,1)S(1)}, bf16[1,1,2,128,512]{4,3,2,1,0:T(8,128)(2,1)S(1)}, u32[]{:S(2)}, u32[]{:S(2)}) collective-permute-start(bf16[1,1,2,128,512]{4,3,2,1,0:T(8,128)(2,1)S(1)} %bitcast.91), channel_id=1, source_target_pairs={{0,6},{2,4},{4,2},{6,0},{1,7},{3,5},{5,3},{7,1},{8,14},{10,12},{12... | collective-permute-start | bytes 786440 | tf_op jit(solution)/shard_map/ppermute | solution.py:816
  40.7 18.1 %shard_map.385 = (bf16[512,512]{1,0:T(8,128)(2,1)}, bf16[512,512]{1,0:T(8,128)(2,1)}, bf16[512,512]{1,0:T(8,128)(2,1)}, bf16[512,512]{1,0:T(8,128)(2,1)}, f32[4,...) custom-call(bf16[512,512]{1,0:T(8,128)(2,1)} %get-tuple-element.259., ...), custom_call_target="tpu_custom_call" | custom-call | flops 11000000 | bytes 35000 | tf_op jit(solution)/shard_map/pallas_call | solution.py:457
  58.9 18.2 %shard_map.386 = (bf16[512,512]{1,0:T(8,128)(2,1)}, bf16[512,512]{1,0:T(8,128)(2,1)}, bf16[512,512]{1,0:T(8,128)(2,1)}, bf16[512,512]{1,0:T(8,128)(2,1)}, bf16[5...) custom-call(bf16[512,512]{1,0:T(8,128)(2,1)} %get-tuple-element.264., ...), custom_call_target="tpu_custom_call" | custom-call | flops 11000000 | bytes 35000 | tf_op jit(solution)/shard_map/pallas_call | solution.py:457
  79.4 16.5 %shard_map.387 = (bf16[256,512]{1,0:T(8,128)(2,1)}, bf16[256,512]{1,0:T(8,128)(2,1)}, bf16[8,2,128,512]{3,2,1,0:T(8,128)(2,1)}, bf16[8,2,128,512]{3,2,1,0:T(8,12...) custom-call(s32[6]{0:T(128)} %concatenate.236.refs_0_, ...), custom_call_target="tpu_custom_call" | custom-call | flops 14300000256 | bytes 45500000 | tf_op jit(solution)/shard_map/pallas_call | solution.py:457
  95.9 1.6 collective-permute-start.3
  97.5 17.5 %shard_map.388 = (bf16[512,512]{1,0:T(8,128)(2,1)}, bf16[512,512]{1,0:T(8,128)(2,1)}, bf16[512,512]{1,0:T(8,128)(2,1)}, bf16[512,512]{1,0:T(8,128)(2,1)}, bf16[5...) custom-call(f32[512,512]{1,0:T(8,128)} %get-tuple-element.301.refs_0, ...), custom_call_target="tpu_custom_call" | custom-call | flops 17600000000 | bytes 56000000 | tf_op jit(solution)/shard_map/pallas_call | solution.py:457
  115.0 16.7 %shard_map.389 = (bf16[8,512,512]{2,1,0:T(8,128)(2,1)}, bf16[8,512,512]{2,1,0:T(8,128)(2,1)}, bf16[8,512,512]{2,1,0:T(8,128)(2,1)}, bf16[4,512,512]{2,1,0:T(8,128)(2,1)}) custom-call(bf16[512,512]{1,0:T(8,128)(2,1)} %get-tuple-element.288.refs_0_, bf16[512,2048]{1,0:T(8,128)(2,1)} %get-tuple-element.289.refs_1_, ...), custom_call_target="tpu_custom_call" | custom-call | flops 16499999744 | bytes 52500000 | tf_op jit(solution)/shard_map/pallas_call | solution.py:457
  131.8 1.6 maximum_select_fusion
  133.4 7.8 %shard_map.390 = (bf16[256,512]{1,0:T(8,128)(2,1)}, bf16[256,512]{1,0:T(8,128)(2,1)}, bf16[256,512]{1,0:T(8,128)(2,1)}, bf16[256,512]{1,0:T(8,128)(2,1)}, bf16[2...) custom-call(s32[6]{0:T(128)} %concatenate.249.refs_0_, ...), custom_call_target="tpu_custom_call" | custom-call | flops 11000000512 | bytes 35000000 | tf_op jit(solution)/shard_map/pallas_call | solution.py:457
  141.1 6.1 %all-gather.4.cloned.1.call-done.refs_1_ = bf16[8,2,128,512]{3,2,1,0:T(8,128)(2,1)} async-done(((bf16[1,2,128,512]{3,2,1,0:T(8,128)(2,1)}), bf16[8,2,128,512]{3,2,1,0:T(8,128)(2,1)}) %all-gather.4.cloned.1.call-update) | async-done | bytes 2097168 | tf_op jit(solution)/shard_map/all_gather | solution.py:872
  147.3 17.1 %shard_map.391 = (bf16[256,512]{1,0:T(8,128)(2,1)}, bf16[8,2,128,512]{3,2,1,0:T(8,128)(2,1)}, bf16[8,2,128,512]{3,2,1,0:T(8,128)(2,1)}, f32[2,8,128]{2,1,0:T(8,1...) custom-call(s32[6]{0:T(128)} %concatenate.236.refs_0_, ...), custom_call_target="tpu_custom_call" | custom-call | flops 15399999488 | bytes 49000000 | tf_op jit(solution)/shard_map/pallas_call | solution.py:457
  164.4 16.6 %shard_map.392 = (bf16[256,512]{1,0:T(8,128)(2,1)}, bf16[8,2,128,512]{3,2,1,0:T(8,128)(2,1)}, bf16[8,2,128,512]{3,2,1,0:T(8,128)(2,1)}, bf16[4,2,128,512]{3,2,1,0:T(8,128)(2,1)}, bf16[4,2,128,512]{3,2,1,0:T(8,128)(2,1)}) custom-call(s32[6]{0:T(128)} %concatenate.236.refs_0_, bf16[256,512]{1,0:T(8,128)(2,1)} %get-tuple-element.325.refs_3_.refs_1_, ...), custom_call_target="tpu_custom_call" | custom-call | flops 15399999488 | bytes 49000000 | tf_op jit(solution)/shard_map/pallas_call | solution.py:457
  181.6 16.6 %shard_map.393 = (bf16[8,256,512]{2,1,0:T(8,128)(2,1)}, bf16[8,256,512]{2,1,0:T(8,128)(2,1)}, bf16[256,512]{1,0:T(8,128)(2,1)}, bf16[256,512]{1,0:T(8,128)(2,1)}...) custom-call(s32[6]{0:T(128)} %concatenate.249.refs_0_, ...), custom_call_target="tpu_custom_call" | custom-call | flops 24199999488 | bytes 77000000 | tf_op jit(solution)/shard_map/pallas_call | solution.py:457
  198.2 2.1 collective-permute-done.4
  201.3 3.9 collective-permute-start.7
  205.9 15.3 %shard_map.394 = (bf16[8,256,512]{2,1,0:T(8,128)(2,1)}, bf16[8,256,512]{2,1,0:T(8,128)(2,1)}) custom-call(s32[1]{0:T(128)} %bitcast.8.refs_0_.info, bf16[256,512]{1,0:T(8,128)(2,1)} %get-tuple-element.358.refs_1_, bf16[256,512]{1,0:T(8,128)(2,1)} %get-tuple-element.342.refs_2_.refs_19_, bf16[2048,512]{1,0:T(8,128)(2,1)} %bitcast.109, ...), custom_call_target="tpu_custom_call" | custom-call | flops 16499999744 | bytes 52500000 | tf_op jit(solution)/shard_map/pallas_call | solution.py:457
  221.3 1.6 collective-permute-start.15
  222.9 5.0 %collective-permute-done.6 = bf16[2,128,512]{2,1,0:T(8,128)(2,1)} collective-permute-done((bf16[2,128,512]{2,1,0:T(8,128)(2,1)S(1)}, bf16[2,128,512]{2,1,0:T(8,128)(2,1)}, u32[]{:S(2)}, u32[]{:S(2)}) %collective-permute-start.6) | collective-permute-done | bytes 262176 | tf_op jit(solution)/shard_map/ppermute | solution.py:816
  227.9 2.0 add_convert_fusion.2
  229.9 3.2 collective-permute-start.13
  233.1 11.7 %shard_map.395 = (bf16[8,256,512]{2,1,0:T(8,128)(2,1)}, bf16[8,256,512]{2,1,0:T(8,128)(2,1)}, bf16[256,512]{1,0:T(8,128)(2,1)}, bf16[256,512]{1,0:T(8,128)(2,1)}...) custom-call(s32[1]{0:T(128)} %bitcast.8.refs_0_.info, ...), custom_call_target="tpu_custom_call" | custom-call | flops 13200000000 | bytes 42000000 | tf_op jit(solution)/shard_map/pallas_call | solution.py:457
  245.6 2.0 add_convert_fusion.3
  248.2 19.2 %shard_map.396 = (bf16[4,256,512]{2,1,0:T(8,128)(2,1)}, bf16[4,256,512]{2,1,0:T(8,128)(2,1)}, bf16[4,2,128,512]{3,2,1,0:T(8,128)(2,1)}, bf16[4,2,128,512]{3,2,1,0:T(8,128)(2,1)}, f32[256,512]{1,0:T(8,128)}) custom-call(s32[6]{0:T(128)} %concatenate.236.refs_0_, bf16[256,512]{1,0:T(8,128)(2,1)} %get-tuple-element.329.refs_1_, ...), custom_call_target="tpu_custom_call" | custom-call | flops 20899999744 | bytes 66500000 | tf_op jit(solution)/shard_map/pallas_call | solution.py:457
  267.4 1.8 pad_maximum_fusion
  276.6 11.9 %collective-permute-done.18 = bf16[8,64,512]{2,1,0:T(8,128)(2,1)S(1)} collective-permute-done((bf16[8,64,512]{2,1,0:T(8,128)(2,1)S(1)}, bf16[8,64,512]{2,1,0:T(8,128)(2,1)S(1)}, u32[]{:S(2)}, u32[]{:S(2)}) %collective-permute-start.18) | collective-permute-done | bytes 524320 | tf_op jit(solution)/shard_map/ppermute | solution.py:816
  288.7 1.9 collective-permute-start.23
  290.6 5.1 %collective-permute-done.17 = bf16[8,128,512]{2,1,0:T(8,128)(2,1)S(1)} collective-permute-done((bf16[8,128,512]{2,1,0:T(8,128)(2,1)S(1)}, bf16[8,128,512]{2,1,0:T(8,128)(2,1)S(1)}, u32[]{:S(2)}, u32[]{:S(2)}) %collective-permute-start.17) | collective-permute-done | bytes 1048608 | tf_op jit(solution)/shard_map/ppermute | solution.py:816
  296.1 2.4 collective-permute-start.21
  300.4 3.0 collective-permute-done.22
  307.4 2.0 collective-permute-start.33
  309.4 1.9 collective-permute-start.32
  311.4 12.5 %collective-permute-done.25 = bf16[2,128,512]{2,1,0:T(8,128)(2,1)} collective-permute-done((bf16[2,128,512]{2,1,0:T(8,128)(2,1)}, bf16[2,128,512]{2,1,0:T(8,128)(2,1)}, u32[]{:S(2)}, u32[]{:S(2)}) %collective-permute-start.25) | collective-permute-done | bytes 262176 | tf_op jit(solution)/shard_map/ppermute | solution.py:816
  323.9 1.8 convert_add_fusion.1
  328.2 2.1 collective-permute-start.30
  330.5 1.6 collective-permute-done.31
  332.2 1.8 collective-permute-start.28
  334.0 2.6 collective-permute-start.26
  336.9 5.6 %collective-permute-done.30 = bf16[272,512]{1,0:T(8,128)(2,1)S(1)} collective-permute-done((bf16[272,512]{1,0:T(8,128)(2,1)S(1)}, bf16[272,512]{1,0:T(8,128)(2,1)S(1)}, u32[]{:S(2)}, u32[]{:S(2)}) %collective-permute-start.30) | collective-permute-done | bytes 278560 | tf_op jit(solution)/shard_map/ppermute | solution.py:816
  343.3 1.7 collective-permute-start.11
  345.1 2.0 collective-permute-start.41
  348.2 15.9 %collective-permute-done.37 = bf16[272,512]{1,0:T(8,128)(2,1)S(1)} collective-permute-done((bf16[272,512]{1,0:T(8,128)(2,1)S(1)}, bf16[272,512]{1,0:T(8,128)(2,1)S(1)}, u32[]{:S(2)}, u32[]{:S(2)}) %collective-permute-start.37) | collective-permute-done | bytes 278560 | tf_op jit(solution)/shard_map/ppermute | solution.py:816
  365.3 2.0 collective-permute-start.36
  367.3 6.6 %collective-permute-done.40 = bf16[8,16,512]{2,1,0:T(8,128)(2,1)S(1)} collective-permute-done((bf16[8,16,512]{2,1,0:T(8,128)(2,1)S(1)}, bf16[8,16,512]{2,1,0:T(8,128)(2,1)S(1)}, u32[]{:S(2)}, u32[]{:S(2)}) %collective-permute-start.40) | collective-permute-done | bytes 131104 | tf_op jit(solution)/shard_map/ppermute | solution.py:816
  374.0 2.5 collective-permute-start.34
  376.5 2.0 collective-permute-start.46
  378.7 3.3 collective-permute-start.45
  382.0 3.2 collective-permute-done.35
  385.2 2.0 collective-permute-start.49
  388.8 2.7 collective-permute-done.45
  392.8 6.2 %collective-permute-done.50 = bf16[4,128,512]{2,1,0:T(8,128)(2,1)S(1)} collective-permute-done((bf16[4,128,512]{2,1,0:T(8,128)(2,1)S(1)}, bf16[4,128,512]{2,1,0:T(8,128)(2,1)S(1)}, u32[]{:S(2)}, u32[]{:S(2)}) %collective-permute-start.50) | collective-permute-done | bytes 524320 | tf_op jit(solution)/shard_map/ppermute | solution.py:816
  399.4 9.3 %collective-permute-done.49 = bf16[8,128,512]{2,1,0:T(8,128)(2,1)S(1)} collective-permute-done((bf16[8,128,512]{2,1,0:T(8,128)(2,1)S(1)}, bf16[8,128,512]{2,1,0:T(8,128)(2,1)S(1)}, u32[]{:S(2)}, u32[]{:S(2)}) %collective-permute-start.49) | collective-permute-done | bytes 1048608 | tf_op jit(solution)/shard_map/ppermute | solution.py:816
  410.6 2.5 collective-permute-start.47
  413.2 1.8 collective-permute-start.43
  415.0 9.1 %collective-permute-done.48 = bf16[8,64,512]{2,1,0:T(8,128)(2,1)S(1)} collective-permute-done((bf16[8,64,512]{2,1,0:T(8,128)(2,1)S(1)}, bf16[8,64,512]{2,1,0:T(8,128)(2,1)S(1)}, u32[]{:S(2)}, u32[]{:S(2)}) %collective-permute-start.48) | collective-permute-done | bytes 524320 | tf_op jit(solution)/shard_map/ppermute | solution.py:816
  426.4 1.8 collective-permute-start.55
  429.1 2.2 collective-permute-start.51
  432.2 3.1 shard_map.397
  435.4 4.5 shard_map.398
  439.9 9.4 %collective-permute-done.52 = bf16[8,128,512]{2,1,0:T(8,128)(2,1)S(1)} collective-permute-done((bf16[8,128,512]{2,1,0:T(8,128)(2,1)S(1)}, bf16[8,128,512]{2,1,0:T(8,128)(2,1)S(1)}, u32[]{:S(2)}, u32[]{:S(2)}) %collective-permute-start.52) | collective-permute-done | bytes 1048608 | tf_op jit(solution)/shard_map/ppermute | solution.py:816
  453.6 1.8 convert_add_fusion
  455.4 4.5 shard_map.399
  460.0 4.5 shard_map.400
  (202 shorter events, 44.8 us)
Async XLA Ops:
  7.2 72.2 %all-gather.6.cloned.1.call-start = ((), (), s32[]{:S(2)}) async-start(), calls=%async_computation.1 | async-start | bytes 2359296 | tf_op jit(solution)/shard_map/all_gather | solution.py:872
  7.9 139.4 %all-gather.4.cloned.1.call-start = ((), (), s32[]{:S(2)}) async-start(), calls=%async_computation | async-start | bytes 2359296 | tf_op jit(solution)/shard_map/all_gather | solution.py:872
  33.8 43.3 %collective-permute-start.2 = (bf16[1,1,2,128,512]{4,3,2,1,0:T(8,128)(2,1)S(1)}, bf16[1,1,2,128,512]{4,3,2,1,0:T(8,128)(2,1)S(1)}, u32[]{:S(2)}, u32[]{:S(2)}) collective-permute-start(bf16[1,1,2,128,512]{4,3,2,1,0:T(8,128)(2,1)S(1)} %bitcast.91), channel_id=1, source_target_pairs={{0,6},{2,4},{4,2},{6,0},{1,7},{3,5},{5,3},{7,1},{8,14},{10,12},{12... | collective-permute-start | bytes 786440 | tf_op jit(solution)/shard_map/ppermute | solution.py:816
  38.9 39.2 %collective-permute-start.1 = (bf16[1,1,2,128,512]{4,3,2,1,0:T(8,128)(2,1)S(1)}, bf16[1,1,2,128,512]{4,3,2,1,0:T(8,128)(2,1)S(1)}, u32[]{:S(2)}, u32[]{:S(2)}) collective-permute-start(bf16[1,1,2,128,512]{4,3,2,1,0:T(8,128)(2,1)S(1)} %bitcast.92), channel_id=1, source_target_pairs={{0,4},{2,6},{4,0},{6,2},{1,5},{3,7},{5,1},{7,3},{8,12},{10,14},{12... | collective-permute-start | bytes 786440 | tf_op jit(solution)/shard_map/ppermute | solution.py:816
  38.9 39.2 %collective-permute-start = (bf16[1,1,2,128,512]{4,3,2,1,0:T(8,128)(2,1)S(1)}, bf16[1,1,2,128,512]{4,3,2,1,0:T(8,128)(2,1)S(1)}, u32[]{:S(2)}, u32[]{:S(2)}) collective-permute-start(bf16[1,1,2,128,512]{4,3,2,1,0:T(8,128)(2,1)S(1)} %bitcast.93), channel_id=1, source_target_pairs={{0,2},{2,0},{4,6},{6,4},{1,3},{3,1},{5,7},{7,5},{8,10},{10,8},{12,... | collective-permute-start | bytes 786440 | tf_op jit(solution)/shard_map/ppermute | solution.py:816
  95.9 35.8 %collective-permute-start.3 = (bf16[4,1,2,128,512]{4,3,2,1,0:T(8,128)(2,1)S(1)}, bf16[4,1,2,128,512]{4,3,2,1,0:T(8,128)(2,1)S(1)}, u32[]{:S(2)}, u32[]{:S(2)}) collective-permute-start(bf16[4,1,2,128,512]{4,3,2,1,0:T(8,128)(2,1)S(1)} %copy-done), channel_id=1, source_target_pairs={{0,1},{1,0},{2,3},{3,2},{4,5},{5,4},{6,7},{7,6},{8,9},{9,8},{10,11... | collective-permute-start | bytes 3145736 | tf_op jit(solution)/shard_map/ppermute | solution.py:816
  180.9 19.4 %collective-permute-start.4 = (bf16[4,2,128,512]{3,2,1,0:T(8,128)(2,1)}, bf16[4,2,128,512]{3,2,1,0:T(8,128)(2,1)S(1)}, u32[]{:S(2)}, u32[]{:S(2)}) collective-permute-start(bf16[4,2,128,512]{3,2,1,0:T(8,128)(2,1)} %get-tuple-element.340), channel_id=1, source_target_pairs={{0,1},{1,0},{2,3},{3,2},{4,5},{5,4},{6,7},{7,6},{8,9},{9,8},{10,11... | collective-permute-start | bytes 3145736 | tf_op jit(solution)/shard_map/ppermute | solution.py:816
  181.6 18.7 %copy-start.9 = (bf16[4,2,128,512]{3,2,1,0:T(8,128)(2,1)S(1)}, bf16[4,2,128,512]{3,2,1,0:T(8,128)(2,1)}, u32[]{:S(2)}) copy-start(bf16[4,2,128,512]{3,2,1,0:T(8,128)(2,1)} %get-tuple-element.354) | copy-start | bytes 3145732
  198.1 29.7 %collective-permute-start.8 = (bf16[8,256,512]{2,1,0:T(8,128)(2,1)}, bf16[8,256,512]{2,1,0:T(8,128)(2,1)S(1)}, u32[]{:S(2)}, u32[]{:S(2)}) collective-permute-start(bf16[8,256,512]{2,1,0:T(8,128)(2,1)} %get-tuple-element.357), channel_id=1, source_target_pairs={{0,8},{8,0},{1,9},{9,1},{2,10},{10,2},{3,11},{11,3},{4,12},{12,4},... | collective-permute-start | bytes 6291464 | tf_op jit(solution)/shard_map/ppermute | solution.py:816
  201.3 19.9 %collective-permute-start.7 = (bf16[2,128,512]{2,1,0:T(8,128)(2,1)S(1)}, bf16[2,128,512]{2,1,0:T(8,128)(2,1)S(1)}, u32[]{:S(2)}, u32[]{:S(2)}) collective-permute-start(bf16[2,128,512]{2,1,0:T(8,128)(2,1)S(1)} %get-tuple-element.510), channel_id=1, source_target_pairs={{0,6},{2,4},{4,2},{6,0},{1,7},{3,5},{5,3},{7,1},{8,14},{10,12},{12... | collective-permute-start | bytes 786440 | tf_op jit(solution)/shard_map/ppermute | solution.py:816
  205.3 22.6 %collective-permute-start.6 = (bf16[2,128,512]{2,1,0:T(8,128)(2,1)S(1)}, bf16[2,128,512]{2,1,0:T(8,128)(2,1)}, u32[]{:S(2)}, u32[]{:S(2)}) collective-permute-start(bf16[2,128,512]{2,1,0:T(8,128)(2,1)S(1)} %get-tuple-element.511), channel_id=1, source_target_pairs={{0,4},{2,6},{4,0},{6,2},{1,5},{3,7},{5,1},{7,3},{8,12},{10,14},{12... | collective-permute-start | bytes 786440 | tf_op jit(solution)/shard_map/ppermute | solution.py:816
  205.3 22.6 %collective-permute-start.5 = (bf16[2,128,512]{2,1,0:T(8,128)(2,1)S(1)}, bf16[2,128,512]{2,1,0:T(8,128)(2,1)}, u32[]{:S(2)}, u32[]{:S(2)}) collective-permute-start(bf16[2,128,512]{2,1,0:T(8,128)(2,1)S(1)} %get-tuple-element.512), channel_id=1, source_target_pairs={{0,2},{2,0},{4,6},{6,4},{1,3},{3,1},{5,7},{7,5},{8,10},{10,8},{12,... | collective-permute-start | bytes 786440 | tf_op jit(solution)/shard_map/ppermute | solution.py:816
  205.8 22.0 %copy-start.3 = (bf16[8,256,512]{2,1,0:T(8,128)(2,1)S(1)}, bf16[8,256,512]{2,1,0:T(8,128)(2,1)}, u32[]{:S(2)}) copy-start(bf16[8,256,512]{2,1,0:T(8,128)(2,1)} %get-tuple-element.380) | copy-start | bytes 6291460
  221.1 24.5 %collective-permute-start.9 = (bf16[8,256,512]{2,1,0:T(8,128)(2,1)}, bf16[8,256,512]{2,1,0:T(8,128)(2,1)S(1)}, u32[]{:S(2)}, u32[]{:S(2)}) collective-permute-start(bf16[8,256,512]{2,1,0:T(8,128)(2,1)} %get-tuple-element.387), channel_id=1, source_target_pairs={{0,8},{8,0},{1,9},{9,1},{2,10},{10,2},{3,11},{11,3},{4,12},{12,4},... | collective-permute-start | bytes 6291464 | tf_op jit(solution)/shard_map/ppermute | solution.py:816
  221.3 48.0 %collective-permute-start.15 = (bf16[4,2,128,512]{3,2,1,0:T(8,128)(2,1)}, bf16[4,2,128,512]{3,2,1,0:T(8,128)(2,1)S(1)}, u32[]{:S(2)}, u32[]{:S(2)}) collective-permute-start(bf16[4,2,128,512]{3,2,1,0:T(8,128)(2,1)} %get-tuple-element.401), channel_id=1, source_target_pairs={{0,1},{1,0},{2,3},{3,2},{4,5},{5,4},{6,7},{7,6},{8,9},{9,8},{10,11... | collective-permute-start | bytes 3145736 | tf_op jit(solution)/shard_map/ppermute | solution.py:816
  229.9 39.5 %collective-permute-start.13 = (bf16[8,128,512]{2,1,0:T(8,128)(2,1)}, bf16[8,128,512]{2,1,0:T(8,128)(2,1)}, u32[]{:S(2)}, u32[]{:S(2)}) collective-permute-start(bf16[8,128,512]{2,1,0:T(8,128)(2,1)} %get-tuple-element.498), channel_id=1, source_target_pairs={{0,16},{16,0},{1,17},{17,1},{2,18},{18,2},{3,19},{19,3},{4,20},{20... | collective-permute-start | bytes 3145736 | tf_op jit(solution)/shard_map/ppermute | solution.py:816
  244.8 24.6 %collective-permute-start.14 = (bf16[8,256,512]{2,1,0:T(8,128)(2,1)}, bf16[8,256,512]{2,1,0:T(8,128)(2,1)S(1)}, u32[]{:S(2)}, u32[]{:S(2)}) collective-permute-start(bf16[8,256,512]{2,1,0:T(8,128)(2,1)} %get-tuple-element.399), channel_id=1, source_target_pairs={{0,8},{8,0},{1,9},{9,1},{2,10},{10,2},{3,11},{11,3},{4,12},{12,4},... | collective-permute-start | bytes 6291464 | tf_op jit(solution)/shard_map/ppermute | solution.py:816
  247.6 51.7 %collective-permute-start.12 = (bf16[8,128,512]{2,1,0:T(8,128)(2,1)}, bf16[8,128,512]{2,1,0:T(8,128)(2,1)S(1)}, u32[]{:S(2)}, u32[]{:S(2)}) collective-permute-start(bf16[8,128,512]{2,1,0:T(8,128)(2,1)} %get-tuple-element.500), channel_id=1, source_target_pairs={{0,1},{1,0},{2,3},{3,2},{4,5},{5,4},{6,7},{7,6},{8,9},{9,8},{10,11... | collective-permute-start | bytes 3145736 | tf_op jit(solution)/shard_map/ppermute | solution.py:816
  269.3 6.2 %collective-permute-start.10 = (bf16[1040,512]{1,0:T(8,128)(2,1)S(1)}, bf16[1040,512]{1,0:T(8,128)(2,1)S(1)}, u32[]{:S(2)}, u32[]{:S(2)}) collective-permute-start(bf16[1040,512]{1,0:T(8,128)(2,1)S(1)} %get-tuple-element.558), channel_id=1, source_target_pairs={{0,8},{8,0},{1,9},{9,1},{2,10},{10,2},{3,11},{11,3},{4,12},{12,4},... | collective-permute-start | bytes 3194888 | tf_op jit(solution)/shard_map/ppermute | solution.py:816
  270.3 25.4 %collective-permute-start.17 = (bf16[8,128,512]{2,1,0:T(8,128)(2,1)S(1)}, bf16[8,128,512]{2,1,0:T(8,128)(2,1)S(1)}, u32[]{:S(2)}, u32[]{:S(2)}) collective-permute-start(bf16[8,128,512]{2,1,0:T(8,128)(2,1)S(1)} %get-tuple-element.496), channel_id=1, source_target_pairs={{0,16},{16,0},{1,17},{17,1},{2,18},{18,2},{3,19},{19,3},{4,20},{20... | collective-permute-start | bytes 3145736 | tf_op jit(solution)/shard_map/ppermute | solution.py:816
  271.2 24.8 %collective-permute-start.16 = (bf16[2,2,128,512]{3,2,1,0:T(8,128)(2,1)S(1)}, bf16[2,2,128,512]{3,2,1,0:T(8,128)(2,1)S(1)}, u32[]{:S(2)}, u32[]{:S(2)}) collective-permute-start(bf16[2,2,128,512]{3,2,1,0:T(8,128)(2,1)S(1)} %add_convert_fusion.15), channel_id=1, source_target_pairs={{0,2},{2,0},{4,6},{6,4},{1,3},{3,1},{5,7},{7,5},{8,10},{10,8},{12,... | collective-permute-start | bytes 1572872 | tf_op jit(solution)/shard_map/ppermute | solution.py:816
  273.7 14.8 %collective-permute-start.18 = (bf16[8,64,512]{2,1,0:T(8,128)(2,1)S(1)}, bf16[8,64,512]{2,1,0:T(8,128)(2,1)S(1)}, u32[]{:S(2)}, u32[]{:S(2)}) collective-permute-start(bf16[8,64,512]{2,1,0:T(8,128)(2,1)S(1)} %get-tuple-element.508), channel_id=1, source_target_pairs={{0,1},{1,0},{2,3},{3,2},{4,5},{5,4},{6,7},{7,6},{8,9},{9,8},{10,11... | collective-permute-start | bytes 1572872 | tf_op jit(solution)/shard_map/ppermute | solution.py:816
  276.0 28.2 %collective-permute-start.20 = (bf16[528,512]{1,0:T(8,128)(2,1)S(1)}, bf16[528,512]{1,0:T(8,128)(2,1)S(1)}, u32[]{:S(2)}, u32[]{:S(2)}) collective-permute-start(bf16[528,512]{1,0:T(8,128)(2,1)S(1)} %get-tuple-element.556), channel_id=1, source_target_pairs={{0,1},{1,0},{2,3},{3,2},{4,5},{5,4},{6,7},{7,6},{8,9},{9,8},{10,11... | collective-permute-start | bytes 1622024 | tf_op jit(solution)/shard_map/ppermute | solution.py:816
  288.7 11.7 %collective-permute-start.23 = (bf16[8,16,512]{2,1,0:T(8,128)(2,1)S(1)}, bf16[8,16,512]{2,1,0:T(8,128)(2,1)S(1)}, u32[]{:S(2)}, u32[]{:S(2)}) collective-permute-start(bf16[8,16,512]{2,1,0:T(8,128)(2,1)S(1)} %get-tuple-element.536), channel_id=1, source_target_pairs={{0,6},{2,4},{4,2},{6,0},{1,7},{3,5},{5,3},{7,1},{8,14},{10,12},{12... | collective-permute-start | bytes 393224 | tf_op jit(solution)/shard_map/ppermute | solution.py:816
  295.7 7.8 %collective-permute-start.22 = (bf16[8,16,512]{2,1,0:T(8,128)(2,1)S(1)}, bf16[8,16,512]{2,1,0:T(8,128)(2,1)S(1)}, u32[]{:S(2)}, u32[]{:S(2)}) collective-permute-start(bf16[8,16,512]{2,1,0:T(8,128)(2,1)S(1)} %get-tuple-element.537), channel_id=1, source_target_pairs={{0,4},{2,6},{4,0},{6,2},{1,5},{3,7},{5,1},{7,3},{8,12},{10,14},{12... | collective-permute-start | bytes 393224 | tf_op jit(solution)/shard_map/ppermute | solution.py:816
  296.1 8.1 %collective-permute-start.21 = (bf16[8,16,512]{2,1,0:T(8,128)(2,1)S(1)}, bf16[8,16,512]{2,1,0:T(8,128)(2,1)S(1)}, u32[]{:S(2)}, u32[]{:S(2)}) collective-permute-start(bf16[8,16,512]{2,1,0:T(8,128)(2,1)S(1)} %get-tuple-element.538), channel_id=1, source_target_pairs={{0,2},{2,0},{4,6},{6,4},{1,3},{3,1},{5,7},{7,5},{8,10},{10,8},{12,... | collective-permute-start | bytes 393224 | tf_op jit(solution)/shard_map/ppermute | solution.py:816
  304.3 19.6 %copy-start.14 = (f32[256,512]{1,0:T(8,128)S(1)}, f32[256,512]{1,0:T(8,128)}, u32[]{:S(2)}) copy-start(f32[256,512]{1,0:T(8,128)} %get-tuple-element.425) | copy-start | bytes 1572868
  304.3 19.5 %collective-permute-start.25 = (bf16[2,128,512]{2,1,0:T(8,128)(2,1)}, bf16[2,128,512]{2,1,0:T(8,128)(2,1)}, u32[]{:S(2)}, u32[]{:S(2)}) collective-permute-start(bf16[2,128,512]{2,1,0:T(8,128)(2,1)} %get-tuple-element.532), channel_id=1, source_target_pairs={{0,4},{2,6},{4,0},{6,2},{1,5},{3,7},{5,1},{7,3},{8,12},{10,14},{12... | collective-permute-start | bytes 786440 | tf_op jit(solution)/shard_map/ppermute | solution.py:816
  304.5 23.7 %collective-permute-start.19 = (bf16[8,64,512]{2,1,0:T(8,128)(2,1)}, bf16[8,64,512]{2,1,0:T(8,128)(2,1)S(1)}, u32[]{:S(2)}, u32[]{:S(2)}) collective-permute-start(bf16[8,64,512]{2,1,0:T(8,128)(2,1)} %get-tuple-element.506), channel_id=1, source_target_pairs={{0,16},{16,0},{1,17},{17,1},{2,18},{18,2},{3,19},{19,3},{4,20},{20... | collective-permute-start | bytes 1572872 | tf_op jit(solution)/shard_map/ppermute | solution.py:816
  306.0 19.7 %collective-permute-start.24 = (bf16[272,512]{1,0:T(8,128)(2,1)}, bf16[272,512]{1,0:T(8,128)(2,1)}, u32[]{:S(2)}, u32[]{:S(2)}) collective-permute-start(bf16[272,512]{1,0:T(8,128)(2,1)} %get-tuple-element.554), channel_id=1, source_target_pairs={{0,16},{16,0},{1,17},{17,1},{2,18},{18,2},{3,19},{19,3},{4,20},{20... | collective-permute-start | bytes 835592 | tf_op jit(solution)/shard_map/ppermute | solution.py:816
  307.4 23.1 %collective-permute-start.33 = (bf16[8,16,512]{2,1,0:T(8,128)(2,1)S(1)}, bf16[8,16,512]{2,1,0:T(8,128)(2,1)S(1)}, u32[]{:S(2)}, u32[]{:S(2)}) collective-permute-start(bf16[8,16,512]{2,1,0:T(8,128)(2,1)S(1)} %add_convert_fusion.43), channel_id=1, source_target_pairs={{0,6},{2,4},{4,2},{6,0},{1,7},{3,5},{5,3},{7,1},{8,14},{10,12},{12... | collective-permute-start | bytes 393224 | tf_op jit(solution)/shard_map/ppermute | solution.py:816
  309.4 21.1 %collective-permute-start.32 = (bf16[8,16,512]{2,1,0:T(8,128)(2,1)S(1)}, bf16[8,16,512]{2,1,0:T(8,128)(2,1)S(1)}, u32[]{:S(2)}, u32[]{:S(2)}) collective-permute-start(bf16[8,16,512]{2,1,0:T(8,128)(2,1)S(1)} %add_convert_fusion.43), channel_id=1, source_target_pairs={{0,4},{2,6},{4,0},{6,2},{1,5},{3,7},{5,1},{7,3},{8,12},{10,14},{12... | collective-permute-start | bytes 393224 | tf_op jit(solution)/shard_map/ppermute | solution.py:816
  323.9 8.3 %collective-permute-start.31 = (bf16[8,16,512]{2,1,0:T(8,128)(2,1)S(1)}, bf16[8,16,512]{2,1,0:T(8,128)(2,1)S(1)}, u32[]{:S(2)}, u32[]{:S(2)}) collective-permute-start(bf16[8,16,512]{2,1,0:T(8,128)(2,1)S(1)} %add_convert_fusion.43), channel_id=1, source_target_pairs={{0,2},{2,0},{4,6},{6,4},{1,3},{3,1},{5,7},{7,5},{8,10},{10,8},{12,... | collective-permute-start | bytes 393224 | tf_op jit(solution)/shard_map/ppermute | solution.py:816
  325.7 17.3 %collective-permute-start.29 = (bf16[8,64,512]{2,1,0:T(8,128)(2,1)S(1)}, bf16[8,64,512]{2,1,0:T(8,128)(2,1)S(1)}, u32[]{:S(2)}, u32[]{:S(2)}) collective-permute-start(bf16[8,64,512]{2,1,0:T(8,128)(2,1)S(1)} %get-tuple-element.502), channel_id=1, source_target_pairs={{0,1},{1,0},{2,3},{3,2},{4,5},{5,4},{6,7},{7,6},{8,9},{9,8},{10,11... | collective-permute-start | bytes 1572872 | tf_op jit(solution)/shard_map/ppermute | solution.py:816
  328.2 14.3 %collective-permute-start.30 = (bf16[272,512]{1,0:T(8,128)(2,1)S(1)}, bf16[272,512]{1,0:T(8,128)(2,1)S(1)}, u32[]{:S(2)}, u32[]{:S(2)}) collective-permute-start(bf16[272,512]{1,0:T(8,128)(2,1)S(1)} %add_convert_fusion.19), channel_id=1, source_target_pairs={{0,2},{2,0},{4,6},{6,4},{1,3},{3,1},{5,7},{7,5},{8,10},{10,8},{12,... | collective-permute-start | bytes 835592 | tf_op jit(solution)/shard_map/ppermute | solution.py:816
  332.2 11.1 %collective-permute-start.28 = (bf16[8,16,512]{2,1,0:T(8,128)(2,1)S(1)}, bf16[8,16,512]{2,1,0:T(8,128)(2,1)S(1)}, u32[]{:S(2)}, u32[]{:S(2)}) collective-permute-start(bf16[8,16,512]{2,1,0:T(8,128)(2,1)S(1)} %get-tuple-element.528), channel_id=1, source_target_pairs={{0,6},{2,4},{4,2},{6,0},{1,7},{3,5},{5,3},{7,1},{8,14},{10,12},{12... | collective-permute-start | bytes 393224 | tf_op jit(solution)/shard_map/ppermute | solution.py:816
  334.0 11.1 %collective-permute-start.27 = (bf16[8,16,512]{2,1,0:T(8,128)(2,1)S(1)}, bf16[8,16,512]{2,1,0:T(8,128)(2,1)S(1)}, u32[]{:S(2)}, u32[]{:S(2)}) collective-permute-start(bf16[8,16,512]{2,1,0:T(8,128)(2,1)S(1)} %get-tuple-element.529), channel_id=1, source_target_pairs={{0,4},{2,6},{4,0},{6,2},{1,5},{3,7},{5,1},{7,3},{8,12},{10,14},{12... | collective-permute-start | bytes 393224 | tf_op jit(solution)/shard_map/ppermute | solution.py:816
  334.0 13.2 %collective-permute-start.26 = (bf16[8,16,512]{2,1,0:T(8,128)(2,1)S(1)}, bf16[8,16,512]{2,1,0:T(8,128)(2,1)S(1)}, u32[]{:S(2)}, u32[]{:S(2)}) collective-permute-start(bf16[8,16,512]{2,1,0:T(8,128)(2,1)S(1)} %get-tuple-element.530), channel_id=1, source_target_pairs={{0,2},{2,0},{4,6},{6,4},{1,3},{3,1},{5,7},{7,5},{8,10},{10,8},{12,... | collective-permute-start | bytes 393224 | tf_op jit(solution)/shard_map/ppermute | solution.py:816
  342.6 21.6 %collective-permute-start.42 = (bf16[8,64,512]{2,1,0:T(8,128)(2,1)S(1)}, bf16[8,64,512]{2,1,0:T(8,128)(2,1)S(1)}, u32[]{:S(2)}, u32[]{:S(2)}) collective-permute-start(bf16[8,64,512]{2,1,0:T(8,128)(2,1)S(1)} %maximum_select_fusion.11), channel_id=1, source_target_pairs={{0,1},{1,0},{2,3},{3,2},{4,5},{5,4},{6,7},{7,6},{8,9},{9,8},{10,11... | collective-permute-start | bytes 1572872 | tf_op jit(solution)/shard_map/ppermute | solution.py:816
  343.0 21.0 %collective-permute-start.37 = (bf16[272,512]{1,0:T(8,128)(2,1)S(1)}, bf16[272,512]{1,0:T(8,128)(2,1)S(1)}, u32[]{:S(2)}, u32[]{:S(2)}) collective-permute-start(bf16[272,512]{1,0:T(8,128)(2,1)S(1)} %add_convert_fusion.18), channel_id=1, source_target_pairs={{0,4},{2,6},{4,0},{6,2},{1,5},{3,7},{5,1},{7,3},{8,12},{10,14},{12... | collective-permute-start | bytes 835592 | tf_op jit(solution)/shard_map/ppermute | solution.py:816
  343.3 44.2 %collective-permute-start.11 = (bf16[4,2,128,512]{3,2,1,0:T(8,128)(2,1)S(1)}, bf16[4,2,128,512]{3,2,1,0:T(8,128)(2,1)S(1)}, u32[]{:S(2)}, u32[]{:S(2)}) collective-permute-start(bf16[4,2,128,512]{3,2,1,0:T(8,128)(2,1)S(1)} %copy-done.24), channel_id=1, source_target_pairs={{0,1},{1,0},{2,3},{3,2},{4,5},{5,4},{6,7},{7,6},{8,9},{9,8},{10,11... | collective-permute-start | bytes 3145736 | tf_op jit(solution)/shard_map/ppermute | solution.py:816
  345.1 20.2 %collective-permute-start.41 = (bf16[8,16,512]{2,1,0:T(8,128)(2,1)S(1)}, bf16[8,16,512]{2,1,0:T(8,128)(2,1)S(1)}, u32[]{:S(2)}, u32[]{:S(2)}) collective-permute-start(bf16[8,16,512]{2,1,0:T(8,128)(2,1)S(1)} %get-tuple-element.524), channel_id=1, source_target_pairs={{0,6},{2,4},{4,2},{6,0},{1,7},{3,5},{5,3},{7,1},{8,14},{10,12},{12... | collective-permute-start | bytes 393224 | tf_op jit(solution)/shard_map/ppermute | solution.py:816
  347.1 26.8 %collective-permute-start.40 = (bf16[8,16,512]{2,1,0:T(8,128)(2,1)S(1)}, bf16[8,16,512]{2,1,0:T(8,128)(2,1)S(1)}, u32[]{:S(2)}, u32[]{:S(2)}) collective-permute-start(bf16[8,16,512]{2,1,0:T(8,128)(2,1)S(1)} %get-tuple-element.525), channel_id=1, source_target_pairs={{0,4},{2,6},{4,0},{6,2},{1,5},{3,7},{5,1},{7,3},{8,12},{10,14},{12... | collective-permute-start | bytes 393224 | tf_op jit(solution)/shard_map/ppermute | solution.py:816
  364.1 9.9 %collective-permute-start.39 = (bf16[8,16,512]{2,1,0:T(8,128)(2,1)S(1)}, bf16[8,16,512]{2,1,0:T(8,128)(2,1)S(1)}, u32[]{:S(2)}, u32[]{:S(2)}) collective-permute-start(bf16[8,16,512]{2,1,0:T(8,128)(2,1)S(1)} %get-tuple-element.526), channel_id=1, source_target_pairs={{0,2},{2,0},{4,6},{6,4},{1,3},{3,1},{5,7},{7,5},{8,10},{10,8},{12,... | collective-permute-start | bytes 393224 | tf_op jit(solution)/shard_map/ppermute | solution.py:816
  364.2 12.4 %collective-permute-start.38 = (bf16[4,64,512]{2,1,0:T(8,128)(2,1)S(1)}, bf16[4,64,512]{2,1,0:T(8,128)(2,1)S(1)}, u32[]{:S(2)}, u32[]{:S(2)}) collective-permute-start(bf16[4,64,512]{2,1,0:T(8,128)(2,1)S(1)} %bitcast.76), channel_id=1, source_target_pairs={{0,16},{16,0},{1,17},{17,1},{2,18},{18,2},{3,19},{19,3},{4,20},{20... | collective-permute-start | bytes 786440 | tf_op jit(solution)/shard_map/ppermute | solution.py:816
  365.3 23.2 %copy-start.11 = (bf16[4,2,128,512]{3,2,1,0:T(8,128)(2,1)S(1)}, bf16[4,2,128,512]{3,2,1,0:T(8,128)(2,1)}, u32[]{:S(2)}) copy-start(bf16[4,2,128,512]{3,2,1,0:T(8,128)(2,1)} %get-tuple-element.456) | copy-start | bytes 3145732
  365.3 13.4 %collective-permute-start.36 = (bf16[8,16,512]{2,1,0:T(8,128)(2,1)S(1)}, bf16[8,16,512]{2,1,0:T(8,128)(2,1)S(1)}, u32[]{:S(2)}, u32[]{:S(2)}) collective-permute-start(bf16[8,16,512]{2,1,0:T(8,128)(2,1)S(1)} %add_convert_fusion.37), channel_id=1, source_target_pairs={{0,6},{2,4},{4,2},{6,0},{1,7},{3,5},{5,3},{7,1},{8,14},{10,12},{12... | collective-permute-start | bytes 393224 | tf_op jit(solution)/shard_map/ppermute | solution.py:816
  373.9 11.2 %collective-permute-start.35 = (bf16[8,16,512]{2,1,0:T(8,128)(2,1)S(1)}, bf16[8,16,512]{2,1,0:T(8,128)(2,1)S(1)}, u32[]{:S(2)}, u32[]{:S(2)}) collective-permute-start(bf16[8,16,512]{2,1,0:T(8,128)(2,1)S(1)} %add_convert_fusion.37), channel_id=1, source_target_pairs={{0,4},{2,6},{4,0},{6,2},{1,5},{3,7},{5,1},{7,3},{8,12},{10,14},{12... | collective-permute-start | bytes 393224 | tf_op jit(solution)/shard_map/ppermute | solution.py:816
  374.0 11.2 %collective-permute-start.34 = (bf16[8,16,512]{2,1,0:T(8,128)(2,1)S(1)}, bf16[8,16,512]{2,1,0:T(8,128)(2,1)S(1)}, u32[]{:S(2)}, u32[]{:S(2)}) collective-permute-start(bf16[8,16,512]{2,1,0:T(8,128)(2,1)S(1)} %add_convert_fusion.37), channel_id=1, source_target_pairs={{0,2},{2,0},{4,6},{6,4},{1,3},{3,1},{5,7},{7,5},{8,10},{10,8},{12,... | collective-permute-start | bytes 393224 | tf_op jit(solution)/shard_map/ppermute | solution.py:816
  376.5 12.3 %collective-permute-start.46 = (bf16[8,16,512]{2,1,0:T(8,128)(2,1)S(1)}, bf16[8,16,512]{2,1,0:T(8,128)(2,1)S(1)}, u32[]{:S(2)}, u32[]{:S(2)}) collective-permute-start(bf16[8,16,512]{2,1,0:T(8,128)(2,1)S(1)} %add_convert_fusion.33), channel_id=1, source_target_pairs={{0,6},{2,4},{4,2},{6,0},{1,7},{3,5},{5,3},{7,1},{8,14},{10,12},{12... | collective-permute-start | bytes 393224 | tf_op jit(solution)/shard_map/ppermute | solution.py:816
  378.7 12.8 %collective-permute-start.45 = (bf16[8,16,512]{2,1,0:T(8,128)(2,1)S(1)}, bf16[8,16,512]{2,1,0:T(8,128)(2,1)S(1)}, u32[]{:S(2)}, u32[]{:S(2)}) collective-permute-start(bf16[8,16,512]{2,1,0:T(8,128)(2,1)S(1)} %add_convert_fusion.33), channel_id=1, source_target_pairs={{0,4},{2,6},{4,0},{6,2},{1,5},{3,7},{5,1},{7,3},{8,12},{10,14},{12... | collective-permute-start | bytes 393224 | tf_op jit(solution)/shard_map/ppermute | solution.py:816
  385.2 7.3 %collective-permute-start.44 = (bf16[8,16,512]{2,1,0:T(8,128)(2,1)S(1)}, bf16[8,16,512]{2,1,0:T(8,128)(2,1)S(1)}, u32[]{:S(2)}, u32[]{:S(2)}) collective-permute-start(bf16[8,16,512]{2,1,0:T(8,128)(2,1)S(1)} %add_convert_fusion.33), channel_id=1, source_target_pairs={{0,2},{2,0},{4,6},{6,4},{1,3},{3,1},{5,7},{7,5},{8,10},{10,8},{12,... | collective-permute-start | bytes 393224 | tf_op jit(solution)/shard_map/ppermute | solution.py:816
  385.2 23.6 %collective-permute-start.49 = (bf16[8,128,512]{2,1,0:T(8,128)(2,1)S(1)}, bf16[8,128,512]{2,1,0:T(8,128)(2,1)S(1)}, u32[]{:S(2)}, u32[]{:S(2)}) collective-permute-start(bf16[8,128,512]{2,1,0:T(8,128)(2,1)S(1)} %maximum_select_fusion.5), channel_id=1, source_target_pairs={{0,16},{16,0},{1,17},{17,1},{2,18},{18,2},{3,19},{19,3},{4,20},{20... | collective-permute-start | bytes 3145736 | tf_op jit(solution)/shard_map/ppermute | solution.py:816
  387.6 11.4 %collective-permute-start.50 = (bf16[4,128,512]{2,1,0:T(8,128)(2,1)S(1)}, bf16[4,128,512]{2,1,0:T(8,128)(2,1)S(1)}, u32[]{:S(2)}, u32[]{:S(2)}) collective-permute-start(bf16[4,128,512]{2,1,0:T(8,128)(2,1)S(1)} %maximum_select_fusion.12), channel_id=1, source_target_pairs={{0,1},{1,0},{2,3},{3,2},{4,5},{5,4},{6,7},{7,6},{8,9},{9,8},{10,11... | collective-permute-start | bytes 1572872 | tf_op jit(solution)/shard_map/ppermute | solution.py:816
  409.6 22.6 %collective-permute-start.53 = (bf16[8,256,512]{2,1,0:T(8,128)(2,1)S(1)}, bf16[8,256,512]{2,1,0:T(8,128)(2,1)}, u32[]{:S(2)}, u32[]{:S(2)}) collective-permute-start(bf16[8,256,512]{2,1,0:T(8,128)(2,1)S(1)} %maximum_select_fusion.1.refs_0_.mine), channel_id=1, source_target_pairs={{0,8},{8,0},{1,9},{9,1},{2,10},{10,2},{3,11},{11,3},{4,12},{12,4},... | collective-permute-start | bytes 6291464 | tf_op jit(solution)/shard_map/ppermute | solution.py:816
  409.7 14.3 %collective-permute-start.48 = (bf16[8,64,512]{2,1,0:T(8,128)(2,1)S(1)}, bf16[8,64,512]{2,1,0:T(8,128)(2,1)S(1)}, u32[]{:S(2)}, u32[]{:S(2)}) collective-permute-start(bf16[8,64,512]{2,1,0:T(8,128)(2,1)S(1)} %maximum_select_fusion.13), channel_id=1, source_target_pairs={{0,16},{16,0},{1,17},{17,1},{2,18},{18,2},{3,19},{19,3},{4,20},{20... | collective-permute-start | bytes 1572872 | tf_op jit(solution)/shard_map/ppermute | solution.py:816
  410.4 20.8 %collective-permute-start.54 = (bf16[4,256,512]{2,1,0:T(8,128)(2,1)S(1)}, bf16[4,256,512]{2,1,0:T(8,128)(2,1)S(1)}, u32[]{:S(2)}, u32[]{:S(2)}) collective-permute-start(bf16[4,256,512]{2,1,0:T(8,128)(2,1)S(1)} %maximum_select_fusion.6.mine), channel_id=1, source_target_pairs={{0,8},{8,0},{1,9},{9,1},{2,10},{10,2},{3,11},{11,3},{4,12},{12,4},... | collective-permute-start | bytes 3145736 | tf_op jit(solution)/shard_map/ppermute | solution.py:816
  410.6 15.4 %collective-permute-start.47 = (bf16[8,64,512]{2,1,0:T(8,128)(2,1)S(1)}, bf16[8,64,512]{2,1,0:T(8,128)(2,1)S(1)}, u32[]{:S(2)}, u32[]{:S(2)}) collective-permute-start(bf16[8,64,512]{2,1,0:T(8,128)(2,1)S(1)} %maximum_select_fusion.14), channel_id=1, source_target_pairs={{0,1},{1,0},{2,3},{3,2},{4,5},{5,4},{6,7},{7,6},{8,9},{9,8},{10,11... | collective-permute-start | bytes 1572872 | tf_op jit(solution)/shard_map/ppermute | solution.py:816
  413.2 15.0 %collective-permute-start.43 = (bf16[2,2,128,512]{3,2,1,0:T(8,128)(2,1)S(1)}, bf16[2,2,128,512]{3,2,1,0:T(8,128)(2,1)S(1)}, u32[]{:S(2)}, u32[]{:S(2)}) collective-permute-start(bf16[2,2,128,512]{3,2,1,0:T(8,128)(2,1)S(1)} %add_convert_fusion.6), channel_id=1, source_target_pairs={{0,2},{2,0},{4,6},{6,4},{1,3},{3,1},{5,7},{7,5},{8,10},{10,8},{12,... | collective-permute-start | bytes 1572872 | tf_op jit(solution)/shard_map/ppermute | solution.py:816
  424.5 24.8 %collective-permute-start.52 = (bf16[8,128,512]{2,1,0:T(8,128)(2,1)S(1)}, bf16[8,128,512]{2,1,0:T(8,128)(2,1)S(1)}, u32[]{:S(2)}, u32[]{:S(2)}) collective-permute-start(bf16[8,128,512]{2,1,0:T(8,128)(2,1)S(1)} %maximum_select_fusion.7), channel_id=1, source_target_pairs={{0,1},{1,0},{2,3},{3,2},{4,5},{5,4},{6,7},{7,6},{8,9},{9,8},{10,11... | collective-permute-start | bytes 3145736 | tf_op jit(solution)/shard_map/ppermute | solution.py:816
  426.4 24.5 %collective-permute-start.55 = (bf16[8,128,512]{2,1,0:T(8,128)(2,1)S(1)}, bf16[8,128,512]{2,1,0:T(8,128)(2,1)S(1)}, u32[]{:S(2)}, u32[]{:S(2)}) collective-permute-start(bf16[8,128,512]{2,1,0:T(8,128)(2,1)S(1)} %maximum_select_fusion.8), channel_id=1, source_target_pairs={{0,16},{16,0},{1,17},{17,1},{2,18},{18,2},{3,19},{19,3},{4,20},{20... | collective-permute-start | bytes 3145736 | tf_op jit(solution)/shard_map/ppermute | solution.py:816
  429.1 21.0 %collective-permute-start.51 = (bf16[2,128,512]{2,1,0:T(8,128)(2,1)}, bf16[2,128,512]{2,1,0:T(8,128)(2,1)}, u32[]{:S(2)}, u32[]{:S(2)}) collective-permute-start(bf16[2,128,512]{2,1,0:T(8,128)(2,1)} %get-tuple-element.514), channel_id=1, source_target_pairs={{0,4},{2,6},{4,0},{6,2},{1,5},{3,7},{5,1},{7,3},{8,12},{10,14},{12... | collective-permute-start | bytes 786440 | tf_op jit(solution)/shard_map/ppermute | solution.py:816
  450.0 5.5 %collective-permute-start.57 = (bf16[8,256,512]{2,1,0:T(8,128)(2,1)S(1)}, bf16[8,256,512]{2,1,0:T(8,128)(2,1)}, u32[]{:S(2)}, u32[]{:S(2)}) collective-permute-start(bf16[8,256,512]{2,1,0:T(8,128)(2,1)S(1)} %maximum_select_fusion.2.mine.refs_0_), channel_id=1, source_target_pairs={{0,8},{8,0},{1,9},{9,1},{2,10},{10,2},{3,11},{11,3},{4,12},{12,4},... | collective-permute-start | bytes 6291464 | tf_op jit(solution)/shard_map/ppermute | solution.py:816
  451.5 8.5 %collective-permute-start.56 = (bf16[8,256,512]{2,1,0:T(8,128)(2,1)S(1)}, bf16[8,256,512]{2,1,0:T(8,128)(2,1)}, u32[]{:S(2)}, u32[]{:S(2)}) collective-permute-start(bf16[8,256,512]{2,1,0:T(8,128)(2,1)S(1)} %maximum_select_fusion.3.mine.refs_0_), channel_id=1, source_target_pairs={{0,8},{8,0},{1,9},{9,1},{2,10},{10,2},{3,11},{11,3},{4,12},{12,4},... | collective-permute-start | bytes 6291464 | tf_op jit(solution)/shard_map/ppermute | solution.py:816
  (23 other events, 225.2 us)
Sparse Core Ops, SparseCore 0:
  10.1 66.5 all-gather.5
  96.0 51.2 all-gather.3

commit v5 on v4

--- a/solution.py
+++ b/solution.py
@@ -95,7 +95,7 @@
     lax.fori_loop(0, ref.shape[axis] // CHUNK, body, 0)
 
 
-def feed_forward(rows, up_ref, down_ref, act_ref, gate_ref, low_ref, total_ref):
+def feed_forward_in_loop(rows, up_ref, down_ref, act_ref, gate_ref, low_ref, total_ref):
     low_ref[...] = rows.astype(BF16)
     total_ref[...] = rows
 
@@ -112,18 +112,31 @@
     return total_ref[...]
 
 
-def feed_back(grad, gate_ref, up_ref, down_ref, hidden_grad_ref, low_ref, total_ref):
-    low_ref[...] = grad.astype(BF16)
-    total_ref[...] = grad
-
-    def step(part):
-        hidden = nt(low_ref[...], down_ref[part, :]) * gate_ref[:, part].astype(F32)
+def feed_forward(rows, up_ref, down_ref, act_ref, gate_ref):
+    low = rows.astype(BF16)
+    total = rows
+    for start in range(0, up_ref.shape[1], CHUNK):
+        part = slice(start, start + CHUNK)
+        hidden = nn(low, up_ref[:, part])
+        sigmoid = 0.5 * jnp.tanh(0.5 * hidden) + 0.5
+        active = hidden * sigmoid
+        gate_ref[:, part] = (sigmoid + active * (1.0 - sigmoid)).astype(BF16)
+        active = active.astype(BF16)
+        act_ref[:, part] = active
+        total = total + nn(active, down_ref[part, :])
+    return low, total
+
+
+def feed_back(grad, gate_ref, up_ref, down_ref, hidden_grad_ref):
+    low = grad.astype(BF16)
+    total = grad
+    for start in range(0, up_ref.shape[1], CHUNK):
+        part = slice(start, start + CHUNK)
+        hidden = nt(low, down_ref[part, :]) * gate_ref[:, part].astype(F32)
         hidden = hidden.astype(BF16)
         hidden_grad_ref[:, part] = hidden
-        total_ref[...] += nt(hidden, up_ref[:, part])
-
-    chunks(up_ref, 1, step)
-    return total_ref[...]
+        total = total + nt(hidden, up_ref[:, part])
+    return low, total
 
 
 def short_allowed(key_segment, query_segment, causal):
@@ -137,9 +150,8 @@
 
 def short_attend(causal, q_ref, k_ref, v_ref, kseg_ref, qseg_ref, o_ref, lse_ref):
     size = kseg_ref.shape[1]
-
-    def one(block, carry):
-        rows = pl.ds(pl.multiple_of(block * size, size), size)
+    for block in range(kseg_ref.shape[0]):
+        rows = slice(block * size, (block + 1) * size)
         allowed = short_allowed(kseg_ref[block], qseg_ref[block], causal)
         logs = []
         for pair in range(PAIRS):
@@ -154,18 +166,14 @@
             log_total = top + jnp.log(total)
             logs += [log_total[:, :size], log_total[:, size:]]
         lse_ref[block] = jnp.concatenate(logs, axis=0)
-        return carry
-
-    lax.fori_loop(0, kseg_ref.shape[0], one, 0)
 
 
 def short_attend_back(
     causal, q_ref, k_ref, v_ref, kseg_ref, qseg_ref, o_ref, lse_ref, go_ref, dq_ref, dk_ref, dv_ref
 ):
     size = kseg_ref.shape[1]
-
-    def one(block, carry):
-        rows = pl.ds(pl.multiple_of(block * size, size), size)
+    for block in range(kseg_ref.shape[0]):
+        rows = slice(block * size, (block + 1) * size)
         allowed = short_allowed(kseg_ref[block], qseg_ref[block], causal)
         delta = delta_rows(go_ref[rows, :], o_ref[rows, :])
         lse = lse_ref[block]
@@ -180,9 +188,6 @@
             dk_ref[rows, lanes] = nn(grad_scores, queries).astype(BF16)
             turned = diagonal(nn(k_ref[rows, lanes].T, grad_scores)).T
             dq_ref[rows, lanes] = (turned.astype(BF16).astype(F32) * SCALE).astype(BF16)
-        return carry
-
-    lax.fori_loop(0, kseg_ref.shape[0], one, 0)
 
 
 def load_keys(ref, pair_index, block, lanes):
@@ -480,7 +485,10 @@
     first, normed, inverse = norm(residual, r.gain[0:1], r.bias[0:1])
     r.n1[...] = normed.astype(BF16)
     r.i1[...] = inverse
-    total = feed_forward(first, r.up, r.down, r.act, r.gate, r.y, r.acc)
+    if "acc" in r:
+        total = feed_forward_in_loop(first, r.up, r.down, r.act, r.gate, r.y, r.acc)
+    else:
+        r.y[...], total = feed_forward(first, r.up, r.down, r.act, r.gate)
     r.leave("n1", "act", "gate", "y")
     encoded, normed, inverse = norm(total, r.gain[1:2], r.bias[1:2])
     r.n2[...] = normed.astype(BF16)
@@ -516,13 +524,13 @@
     gain, bias = r.gain, r.bias
     residual = upper + nn(o_ref[...], r.w_co[...])
     middle, normed4, inverse4 = norm(residual, gain[1:2], bias[1:2])
-    total = feed_forward(middle, r.up, r.down, r.act, r.gate, r.m, r.acc)
+    r.m[...], total = feed_forward(middle, r.up, r.down, r.act, r.gate)
     r.leave("m", "act", "gate")
     final, normed5, inverse5 = norm(total, gain[2:3], bias[2:3])
     r.final[...] = final
     r.leave("final")
     grad, gain5, bias5 = norm_back(r.cot[...].astype(F32), normed5, inverse5, gain[2:3])
-    grad = feed_back(grad, r.gate, r.up, r.down, r.dh, r.b5, r.acc)
+    r.b5[...], grad = feed_back(grad, r.gate, r.up, r.down, r.dh)
     r.leave("b5", "dh")
     grad, gain4, bias4 = norm_back(grad, normed4, inverse4, gain[1:2])
     low = grad.astype(BF16)
@@ -575,7 +583,7 @@
 
 def encoder_tail_back(r, grad):
     grad, gain2, bias2 = norm_back(grad, r.n2[...], r.i2[...], r.gain[1:2])
-    grad = feed_back(grad, r.gate, r.up, r.down, r.dh, r.b2, r.acc)
+    r.b2[...], grad = feed_back(grad, r.gate, r.up, r.down, r.dh)
     r.leave("b2", "dh")
     grad, gain1, bias1 = norm_back(grad, r.n1[...], r.i1[...], r.gain[0:1])
     low = grad.astype(BF16)
@@ -1243,7 +1251,6 @@
         {"x": flat(source_short), **segments, **encoder_in},
         {**rows_of(rows, ("q", "k", "v", "o")), **logs(blocks, ("lse",)), **encoder_keeps(rows)},
         cost=0.01,
-        scratch=[("acc", pltpu.VMEM((rows, width), F32))],
     )
     decoder_keeps = lambda n: {
         **rows_of(n, ("m", "b5", "b4", "go_c")),
@@ -1286,7 +1293,6 @@
         },
         after=(sd.lse,),
         cost=0.01,
-        scratch=[("acc", pltpu.VMEM((rows, width), F32))],
     )
 
     sb = launch(
@@ -1344,7 +1350,7 @@
             **floats(rows, ("dx",)),
             **sums(4),
         },
-        scratch=[("acc", pltpu.VMEM((rows, width), F32)), ("d1", pltpu.VMEM((rows, width), F32))],
+        scratch=[("d1", pltpu.VMEM((rows, width), F32))],
         after=(le.lse,),
         cost=16,
     )
@@ -1408,7 +1414,7 @@
             **logs(pairs, ("lse_c",)),
             **decoder_keeps(rows_long),
         },
-        scratch=work + [("acc", pltpu.VMEM((rows_long, width), F32))],
+        scratch=work,
         info=source_info,
         after=(ls.lse,),
         cost=14,
@@ -1514,7 +1520,6 @@
         after=(grad_attention[0], decoder_ffn.held[0]),
         pieces=("kept", "sent"),
         cost=12,
-        scratch=[("acc", pltpu.VMEM((rows_long, width), F32))],
     )
     small = jnp.concatenate([seb.small + leb.small, sb.small + lsb.small, sc.small + lc.small])
     small = jnp.pad(small, ((0, 16 - small.shape[0]), (0, 0))).astype(BF16)

time: 480 us -> 478 us (level)
  waiting for transfers between devices: 120 us -> 132 us
  Pallas kernels: 231 us -> 222 us
  starting transfers between devices: 68.1 us -> 63.2 us
    ppermute x58, waiting for transfers between devices: 113 us -> 124 us  [send(): return lax.ppermute(piece, axis, [(i, i ^ offset) for i in range(count)])]
    pallas_call x14, Pallas kernels: 215 us -> 206 us  [launch(): pl.pallas_call(run, in_specs=specs, out_specs=[far if name in moved_out e...]
    ppermute x58, starting transfers between devices: 68 us -> 63.2 us  [send(): return lax.ppermute(piece, axis, [(i, i ^ offset) for i in range(count)])]
  transfers between devices with their start and end apart: 60 -> 60, of which waited for: 22 -> 22; matrix products, arithmetic and copies ran while one was open for 7% -> 7% of each run, Pallas kernels for 37% -> 35%
where the time goes in v5:
time: 478 us; the launch traced here: 470 us
  Pallas kernels  222 us (46%)
  waiting for transfers between devices  132 us (28%)
  starting transfers between devices  63.2 us (13%)
  other arithmetic  29.7 us (6%)
  between operations  15.3 us (3%)
  local copies, waits for them, and re-layouts  7.55 us (2%)
    pallas_call x14, Pallas kernels, launch(): pl.pallas_call(run, in_specs=specs, out_specs=[far if name in moved_out e...  206 us
    ppermute x58, waiting for transfers between devices, send(): return lax.ppermute(piece, axis, [(i, i ^ offset) for i in range(count)])  124 us
    ppermute x58, starting transfers between devices, send(): return lax.ppermute(piece, axis, [(i, i ^ offset) for i in range(count)])  63.2 us
    pallas_call x4, Pallas kernels, assemble(): pl.pallas_call(lambda info, mine, other, *refs: body(info, mine, other, *...  16.8 us
    convert_element_type x26, other arithmetic, added(): return total.astype(BF16)  13.4 us
  transfers between devices with their start and end apart: 60, of which 22 were waited for; matrix products, arithmetic and copies ran while one was open for 7% of the time, Pallas kernels for 35%

profile of v5, /device:TPU:0, one launch (start us, length us, event | category | flops | bytes accessed | tf_op | source)
XLA Modules:
  0.0 470.2 jit_solution(16411634835970771558)
XLA Ops:
  8.0 1.5 broadcast_in_dim.24.refs_1_.refs_4_.refs_14_.refs_11_
  9.5 11.3 %shard_map.383 = (bf16[512,512]{1,0:T(8,128)(2,1)}, bf16[512,512]{1,0:T(8,128)(2,1)}, bf16[512,512]{1,0:T(8,128)(2,1)}, bf16[512,512]{1,0:T(8,128)(2,1)}, f32[4,...) custom-call(bf16[512,512]{1,0:T(8,128)(2,1)} %bitcast.85, ...), custom_call_target="tpu_custom_call" | custom-call | flops 11000000 | bytes 35000 | tf_op jit(solution)/shard_map/pallas_call | solution.py:462
  21.7 7.4 %shard_map.384 = (bf16[512,512]{1,0:T(8,128)(2,1)}, bf16[512,512]{1,0:T(8,128)(2,1)}, bf16[512,512]{1,0:T(8,128)(2,1)}, bf16[512,512]{1,0:T(8,128)(2,1)}, bf16[5...) custom-call(bf16[512,512]{1,0:T(8,128)(2,1)} %bitcast.83, ...), custom_call_target="tpu_custom_call" | custom-call | flops 11000000 | bytes 35000 | tf_op jit(solution)/shard_map/pallas_call | solution.py:462
  29.1 5.1 %collective-permute-start.2 = (bf16[1,1,2,128,512]{4,3,2,1,0:T(8,128)(2,1)S(1)}, bf16[1,1,2,128,512]{4,3,2,1,0:T(8,128)(2,1)S(1)}, u32[]{:S(2)}, u32[]{:S(2)}) collective-permute-start(bf16[1,1,2,128,512]{4,3,2,1,0:T(8,128)(2,1)S(1)} %bitcast.91), channel_id=1, source_target_pairs={{0,6},{2,4},{4,2},{6,0},{1,7},{3,5},{5,3},{7,1},{8,14},{10,12},{12... | collective-permute-start | bytes 786440 | tf_op jit(solution)/shard_map/ppermute | solution.py:824
  36.1 14.8 %shard_map.385 = (bf16[512,512]{1,0:T(8,128)(2,1)}, bf16[512,512]{1,0:T(8,128)(2,1)}, bf16[512,512]{1,0:T(8,128)(2,1)}, bf16[512,512]{1,0:T(8,128)(2,1)}, f32[4,...) custom-call(bf16[512,512]{1,0:T(8,128)(2,1)} %get-tuple-element.259., ...), custom_call_target="tpu_custom_call" | custom-call | flops 11000000 | bytes 35000 | tf_op jit(solution)/shard_map/pallas_call | solution.py:462
  50.9 16.3 %shard_map.386 = (bf16[512,512]{1,0:T(8,128)(2,1)}, bf16[512,512]{1,0:T(8,128)(2,1)}, bf16[512,512]{1,0:T(8,128)(2,1)}, bf16[512,512]{1,0:T(8,128)(2,1)}, bf16[5...) custom-call(bf16[512,512]{1,0:T(8,128)(2,1)} %get-tuple-element.264., ...), custom_call_target="tpu_custom_call" | custom-call | flops 11000000 | bytes 35000 | tf_op jit(solution)/shard_map/pallas_call | solution.py:462
  67.2 6.9 %collective-permute-done.1 = bf16[1,1,2,128,512]{4,3,2,1,0:T(8,128)(2,1)S(1)} collective-permute-done((bf16[1,1,2,128,512]{4,3,2,1,0:T(8,128)(2,1)S(1)}, bf16[1,1,2,128,512]{4,3,2,1,0:T(8,128)(2,1)S(1)}, u32[]{:S(2)}, u32[]{:S(2)}) %collective-permute-start.1) | collective-permute-done | bytes 262176 | tf_op jit(solution)/shard_map/ppermute | solution.py:824
  75.3 17.4 %shard_map.387 = (bf16[256,512]{1,0:T(8,128)(2,1)}, bf16[256,512]{1,0:T(8,128)(2,1)}, bf16[8,2,128,512]{3,2,1,0:T(8,128)(2,1)}, bf16[8,2,128,512]{3,2,1,0:T(8,12...) custom-call(s32[6]{0:T(128)} %concatenate.236.refs_0_, ...), custom_call_target="tpu_custom_call" | custom-call | flops 14300000256 | bytes 45500000 | tf_op jit(solution)/shard_map/pallas_call | solution.py:462
  94.0 15.9 %shard_map.388 = (bf16[512,512]{1,0:T(8,128)(2,1)}, bf16[512,512]{1,0:T(8,128)(2,1)}, bf16[512,512]{1,0:T(8,128)(2,1)}, bf16[512,512]{1,0:T(8,128)(2,1)}, bf16[5...) custom-call(f32[512,512]{1,0:T(8,128)} %get-tuple-element.301.refs_0, ...), custom_call_target="tpu_custom_call" | custom-call | flops 17600000000 | bytes 56000000 | tf_op jit(solution)/shard_map/pallas_call | solution.py:462
  109.9 16.6 %shard_map.389 = (bf16[8,512,512]{2,1,0:T(8,128)(2,1)}, bf16[8,512,512]{2,1,0:T(8,128)(2,1)}, bf16[8,512,512]{2,1,0:T(8,128)(2,1)}, bf16[4,512,512]{2,1,0:T(8,128)(2,1)}) custom-call(bf16[512,512]{1,0:T(8,128)(2,1)} %get-tuple-element.288.refs_0_, bf16[512,2048]{1,0:T(8,128)(2,1)} %get-tuple-element.289.refs_1_, ...), custom_call_target="tpu_custom_call" | custom-call | flops 16499999744 | bytes 52500000 | tf_op jit(solution)/shard_map/pallas_call | solution.py:462
  126.5 1.6 maximum_select_fusion
  128.1 7.8 %shard_map.390 = (bf16[256,512]{1,0:T(8,128)(2,1)}, bf16[256,512]{1,0:T(8,128)(2,1)}, bf16[256,512]{1,0:T(8,128)(2,1)}, bf16[256,512]{1,0:T(8,128)(2,1)}, bf16[2...) custom-call(s32[6]{0:T(128)} %concatenate.249.refs_0_, ...), custom_call_target="tpu_custom_call" | custom-call | flops 11000000512 | bytes 35000000 | tf_op jit(solution)/shard_map/pallas_call | solution.py:462
  135.9 7.2 %all-gather.4.cloned.1.call-done.refs_1_ = bf16[8,2,128,512]{3,2,1,0:T(8,128)(2,1)} async-done(((bf16[1,2,128,512]{3,2,1,0:T(8,128)(2,1)}), bf16[8,2,128,512]{3,2,1,0:T(8,128)(2,1)}) %all-gather.4.cloned.1.call-update) | async-done | bytes 2097168 | tf_op jit(solution)/shard_map/all_gather | solution.py:880
  143.1 16.5 %shard_map.391 = (bf16[256,512]{1,0:T(8,128)(2,1)}, bf16[8,2,128,512]{3,2,1,0:T(8,128)(2,1)}, bf16[8,2,128,512]{3,2,1,0:T(8,128)(2,1)}, f32[2,8,128]{2,1,0:T(8,1...) custom-call(s32[6]{0:T(128)} %concatenate.236.refs_0_, ...), custom_call_target="tpu_custom_call" | custom-call | flops 15399999488 | bytes 49000000 | tf_op jit(solution)/shard_map/pallas_call | solution.py:462
  159.6 18.0 %shard_map.392 = (bf16[256,512]{1,0:T(8,128)(2,1)}, bf16[8,2,128,512]{3,2,1,0:T(8,128)(2,1)}, bf16[8,2,128,512]{3,2,1,0:T(8,128)(2,1)}, bf16[4,2,128,512]{3,2,1,0:T(8,128)(2,1)}, bf16[4,2,128,512]{3,2,1,0:T(8,128)(2,1)}) custom-call(s32[6]{0:T(128)} %concatenate.236.refs_0_, bf16[256,512]{1,0:T(8,128)(2,1)} %get-tuple-element.325.refs_3_.refs_1_, ...), custom_call_target="tpu_custom_call" | custom-call | flops 15399999488 | bytes 49000000 | tf_op jit(solution)/shard_map/pallas_call | solution.py:462
  178.8 16.9 %shard_map.393 = (bf16[8,256,512]{2,1,0:T(8,128)(2,1)}, bf16[8,256,512]{2,1,0:T(8,128)(2,1)}, bf16[256,512]{1,0:T(8,128)(2,1)}, bf16[256,512]{1,0:T(8,128)(2,1)}...) custom-call(s32[6]{0:T(128)} %concatenate.249.refs_0_, ...), custom_call_target="tpu_custom_call" | custom-call | flops 24199999488 | bytes 77000000 | tf_op jit(solution)/shard_map/pallas_call | solution.py:462
  196.8 8.9 %collective-permute-start.7 = (bf16[2,128,512]{2,1,0:T(8,128)(2,1)S(1)}, bf16[2,128,512]{2,1,0:T(8,128)(2,1)S(1)}, u32[]{:S(2)}, u32[]{:S(2)}) collective-permute-start(bf16[2,128,512]{2,1,0:T(8,128)(2,1)S(1)} %get-tuple-element.510), channel_id=1, source_target_pairs={{0,6},{2,4},{4,2},{6,0},{1,7},{3,5},{5,3},{7,1},{8,14},{10,12},{12... | collective-permute-start | bytes 786440 | tf_op jit(solution)/shard_map/ppermute | solution.py:824
  206.3 15.3 %shard_map.394 = (bf16[8,256,512]{2,1,0:T(8,128)(2,1)}, bf16[8,256,512]{2,1,0:T(8,128)(2,1)}) custom-call(s32[1]{0:T(128)} %bitcast.8.refs_0_.info, bf16[256,512]{1,0:T(8,128)(2,1)} %get-tuple-element.358.refs_1_, bf16[256,512]{1,0:T(8,128)(2,1)} %get-tuple-element.342.refs_2_.refs_19_, bf16[2048,512]{1,0:T(8,128)(2,1)} %bitcast.109, ...), custom_call_target="tpu_custom_call" | custom-call | flops 16499999744 | bytes 52500000 | tf_op jit(solution)/shard_map/pallas_call | solution.py:462
  221.7 1.5 collective-permute-start.15
  223.2 5.0 %collective-permute-done.6 = bf16[2,128,512]{2,1,0:T(8,128)(2,1)} collective-permute-done((bf16[2,128,512]{2,1,0:T(8,128)(2,1)S(1)}, bf16[2,128,512]{2,1,0:T(8,128)(2,1)}, u32[]{:S(2)}, u32[]{:S(2)}) %collective-permute-start.6) | collective-permute-done | bytes 262176 | tf_op jit(solution)/shard_map/ppermute | solution.py:824
  228.2 2.0 add_convert_fusion.2
  230.2 11.0 %shard_map.395 = (bf16[8,256,512]{2,1,0:T(8,128)(2,1)}, bf16[8,256,512]{2,1,0:T(8,128)(2,1)}, bf16[256,512]{1,0:T(8,128)(2,1)}, bf16[256,512]{1,0:T(8,128)(2,1)}...) custom-call(s32[1]{0:T(128)} %bitcast.8.refs_0_.info, ...), custom_call_target="tpu_custom_call" | custom-call | flops 13200000000 | bytes 42000000 | tf_op jit(solution)/shard_map/pallas_call | solution.py:462
  242.1 2.0 add_convert_fusion.3
  244.1 1.5 collective-permute-start.12
  245.6 20.6 %shard_map.396 = (bf16[4,256,512]{2,1,0:T(8,128)(2,1)}, bf16[4,256,512]{2,1,0:T(8,128)(2,1)}, bf16[4,2,128,512]{3,2,1,0:T(8,128)(2,1)}, bf16[4,2,128,512]{3,2,1,0:T(8,128)(2,1)}, f32[256,512]{1,0:T(8,128)}) custom-call(s32[6]{0:T(128)} %concatenate.236.refs_0_, bf16[256,512]{1,0:T(8,128)(2,1)} %get-tuple-element.329.refs_1_, ...), custom_call_target="tpu_custom_call" | custom-call | flops 20899999744 | bytes 66500000 | tf_op jit(solution)/shard_map/pallas_call | solution.py:462
  266.3 1.8 pad_maximum_fusion
  271.0 1.5 add_convert_fusion.13
  273.9 1.6 collective-permute-start.20
  275.5 11.9 %collective-permute-done.18 = bf16[8,64,512]{2,1,0:T(8,128)(2,1)S(1)} collective-permute-done((bf16[8,64,512]{2,1,0:T(8,128)(2,1)S(1)}, bf16[8,64,512]{2,1,0:T(8,128)(2,1)S(1)}, u32[]{:S(2)}, u32[]{:S(2)}) %collective-permute-start.18) | collective-permute-done | bytes 524320 | tf_op jit(solution)/shard_map/ppermute | solution.py:824
  287.6 2.7 collective-permute-start.23
  290.3 4.2 collective-permute-done.17
  294.9 3.3 collective-permute-start.21
  300.2 3.0 collective-permute-done.22
  305.5 1.4 collective-permute-start.24
  306.9 1.9 collective-permute-start.33
  308.8 1.7 collective-permute-start.32
  310.5 12.0 %collective-permute-done.25 = bf16[2,128,512]{2,1,0:T(8,128)(2,1)} collective-permute-done((bf16[2,128,512]{2,1,0:T(8,128)(2,1)}, bf16[2,128,512]{2,1,0:T(8,128)(2,1)}, u32[]{:S(2)}, u32[]{:S(2)}) %collective-permute-start.25) | collective-permute-done | bytes 262176 | tf_op jit(solution)/shard_map/ppermute | solution.py:824
  322.6 1.8 convert_add_fusion.1
  326.0 2.1 collective-permute-start.30
  328.3 2.6 collective-permute-done.31
  330.9 2.6 collective-permute-start.28
  333.5 1.7 collective-permute-start.26
  335.6 4.5 collective-permute-done.30
  343.0 2.1 collective-permute-done.27
  345.2 1.5 collective-permute-start.41
  347.3 15.1 %collective-permute-done.37 = bf16[272,512]{1,0:T(8,128)(2,1)S(1)} collective-permute-done((bf16[272,512]{1,0:T(8,128)(2,1)S(1)}, bf16[272,512]{1,0:T(8,128)(2,1)S(1)}, u32[]{:S(2)}, u32[]{:S(2)}) %collective-permute-start.37) | collective-permute-done | bytes 278560 | tf_op jit(solution)/shard_map/ppermute | solution.py:824
  363.8 1.6 collective-permute-start.36
  365.4 6.9 %collective-permute-done.40 = bf16[8,16,512]{2,1,0:T(8,128)(2,1)S(1)} collective-permute-done((bf16[8,16,512]{2,1,0:T(8,128)(2,1)S(1)}, bf16[8,16,512]{2,1,0:T(8,128)(2,1)S(1)}, u32[]{:S(2)}, u32[]{:S(2)}) %collective-permute-start.40) | collective-permute-done | bytes 131104 | tf_op jit(solution)/shard_map/ppermute | solution.py:824
  372.3 2.1 collective-permute-start.34
  374.5 2.3 collective-permute-start.46
  377.2 8.0 %collective-permute-done.35 = bf16[8,16,512]{2,1,0:T(8,128)(2,1)S(1)} collective-permute-done((bf16[8,16,512]{2,1,0:T(8,128)(2,1)S(1)}, bf16[8,16,512]{2,1,0:T(8,128)(2,1)S(1)}, u32[]{:S(2)}, u32[]{:S(2)}) %collective-permute-start.35) | collective-permute-done | bytes 131104 | tf_op jit(solution)/shard_map/ppermute | solution.py:824
  387.5 2.5 collective-permute-done.45
  391.6 6.3 %collective-permute-done.50 = bf16[4,128,512]{2,1,0:T(8,128)(2,1)S(1)} collective-permute-done((bf16[4,128,512]{2,1,0:T(8,128)(2,1)S(1)}, bf16[4,128,512]{2,1,0:T(8,128)(2,1)S(1)}, u32[]{:S(2)}, u32[]{:S(2)}) %collective-permute-start.50) | collective-permute-done | bytes 524320 | tf_op jit(solution)/shard_map/ppermute | solution.py:824
  398.4 8.9 %collective-permute-done.49 = bf16[8,128,512]{2,1,0:T(8,128)(2,1)S(1)} collective-permute-done((bf16[8,128,512]{2,1,0:T(8,128)(2,1)S(1)}, bf16[8,128,512]{2,1,0:T(8,128)(2,1)S(1)}, u32[]{:S(2)}, u32[]{:S(2)}) %collective-permute-start.49) | collective-permute-done | bytes 1048608 | tf_op jit(solution)/shard_map/ppermute | solution.py:824
  408.2 1.8 collective-permute-start.48
  410.3 1.8 collective-permute-start.43
  412.2 10.4 %collective-permute-done.48 = bf16[8,64,512]{2,1,0:T(8,128)(2,1)S(1)} collective-permute-done((bf16[8,64,512]{2,1,0:T(8,128)(2,1)S(1)}, bf16[8,64,512]{2,1,0:T(8,128)(2,1)S(1)}, u32[]{:S(2)}, u32[]{:S(2)}) %collective-permute-start.48) | collective-permute-done | bytes 524320 | tf_op jit(solution)/shard_map/ppermute | solution.py:824
  426.2 3.4 collective-permute-start.51
  430.6 3.1 shard_map.397
  433.7 4.5 shard_map.398
  438.3 9.5 %collective-permute-done.52 = bf16[8,128,512]{2,1,0:T(8,128)(2,1)S(1)} collective-permute-done((bf16[8,128,512]{2,1,0:T(8,128)(2,1)S(1)}, bf16[8,128,512]{2,1,0:T(8,128)(2,1)S(1)}, u32[]{:S(2)}, u32[]{:S(2)}) %collective-permute-start.52) | collective-permute-done | bytes 1048608 | tf_op jit(solution)/shard_map/ppermute | solution.py:824
  452.2 1.8 convert_add_fusion
  454.0 4.5 shard_map.399
  458.6 4.5 shard_map.400
  (202 shorter events, 40.6 us)
Async XLA Ops:
  7.2 68.1 %all-gather.6.cloned.1.call-start = ((), (), s32[]{:S(2)}) async-start(), calls=%async_computation.1 | async-start | bytes 2359296 | tf_op jit(solution)/shard_map/all_gather | solution.py:880
  7.9 135.2 %all-gather.4.cloned.1.call-start = ((), (), s32[]{:S(2)}) async-start(), calls=%async_computation | async-start | bytes 2359296 | tf_op jit(solution)/shard_map/all_gather | solution.py:880
  29.1 38.0 %collective-permute-start.2 = (bf16[1,1,2,128,512]{4,3,2,1,0:T(8,128)(2,1)S(1)}, bf16[1,1,2,128,512]{4,3,2,1,0:T(8,128)(2,1)S(1)}, u32[]{:S(2)}, u32[]{:S(2)}) collective-permute-start(bf16[1,1,2,128,512]{4,3,2,1,0:T(8,128)(2,1)S(1)} %bitcast.91), channel_id=1, source_target_pairs={{0,6},{2,4},{4,2},{6,0},{1,7},{3,5},{5,3},{7,1},{8,14},{10,12},{12... | collective-permute-start | bytes 786440 | tf_op jit(solution)/shard_map/ppermute | solution.py:824
  34.2 39.8 %collective-permute-start.1 = (bf16[1,1,2,128,512]{4,3,2,1,0:T(8,128)(2,1)S(1)}, bf16[1,1,2,128,512]{4,3,2,1,0:T(8,128)(2,1)S(1)}, u32[]{:S(2)}, u32[]{:S(2)}) collective-permute-start(bf16[1,1,2,128,512]{4,3,2,1,0:T(8,128)(2,1)S(1)} %bitcast.92), channel_id=1, source_target_pairs={{0,4},{2,6},{4,0},{6,2},{1,5},{3,7},{5,1},{7,3},{8,12},{10,14},{12... | collective-permute-start | bytes 786440 | tf_op jit(solution)/shard_map/ppermute | solution.py:824
  34.2 39.8 %collective-permute-start = (bf16[1,1,2,128,512]{4,3,2,1,0:T(8,128)(2,1)S(1)}, bf16[1,1,2,128,512]{4,3,2,1,0:T(8,128)(2,1)S(1)}, u32[]{:S(2)}, u32[]{:S(2)}) collective-permute-start(bf16[1,1,2,128,512]{4,3,2,1,0:T(8,128)(2,1)S(1)} %bitcast.93), channel_id=1, source_target_pairs={{0,2},{2,0},{4,6},{6,4},{1,3},{3,1},{5,7},{7,5},{8,10},{10,8},{12,... | collective-permute-start | bytes 786440 | tf_op jit(solution)/shard_map/ppermute | solution.py:824
  75.3 17.4 %copy-start = (bf16[4,1,2,128,512]{4,3,2,1,0:T(8,128)(2,1)S(1)}, bf16[4,1,2,128,512]{4,3,2,1,0:T(8,128)(2,1)}, u32[]{:S(2)}) copy-start(bf16[4,1,2,128,512]{4,3,2,1,0:T(8,128)(2,1)} %maximum_select_fusion.4.refs_10_) | copy-start | bytes 3145732
  92.8 33.7 %collective-permute-start.3 = (bf16[4,1,2,128,512]{4,3,2,1,0:T(8,128)(2,1)S(1)}, bf16[4,1,2,128,512]{4,3,2,1,0:T(8,128)(2,1)S(1)}, u32[]{:S(2)}, u32[]{:S(2)}) collective-permute-start(bf16[4,1,2,128,512]{4,3,2,1,0:T(8,128)(2,1)S(1)} %copy-done), channel_id=1, source_target_pairs={{0,1},{1,0},{2,3},{3,2},{4,5},{5,4},{6,7},{7,6},{8,9},{9,8},{10,11... | collective-permute-start | bytes 3145736 | tf_op jit(solution)/shard_map/ppermute | solution.py:824
  177.6 18.2 %collective-permute-start.4 = (bf16[4,2,128,512]{3,2,1,0:T(8,128)(2,1)}, bf16[4,2,128,512]{3,2,1,0:T(8,128)(2,1)S(1)}, u32[]{:S(2)}, u32[]{:S(2)}) collective-permute-start(bf16[4,2,128,512]{3,2,1,0:T(8,128)(2,1)} %get-tuple-element.340), channel_id=1, source_target_pairs={{0,1},{1,0},{2,3},{3,2},{4,5},{5,4},{6,7},{7,6},{8,9},{9,8},{10,11... | collective-permute-start | bytes 3145736 | tf_op jit(solution)/shard_map/ppermute | solution.py:824
  195.7 32.5 %collective-permute-start.8 = (bf16[8,256,512]{2,1,0:T(8,128)(2,1)}, bf16[8,256,512]{2,1,0:T(8,128)(2,1)S(1)}, u32[]{:S(2)}, u32[]{:S(2)}) collective-permute-start(bf16[8,256,512]{2,1,0:T(8,128)(2,1)} %get-tuple-element.357), channel_id=1, source_target_pairs={{0,8},{8,0},{1,9},{9,1},{2,10},{10,2},{3,11},{11,3},{4,12},{12,4},... | collective-permute-start | bytes 6291464 | tf_op jit(solution)/shard_map/ppermute | solution.py:824
  196.8 24.9 %collective-permute-start.7 = (bf16[2,128,512]{2,1,0:T(8,128)(2,1)S(1)}, bf16[2,128,512]{2,1,0:T(8,128)(2,1)S(1)}, u32[]{:S(2)}, u32[]{:S(2)}) collective-permute-start(bf16[2,128,512]{2,1,0:T(8,128)(2,1)S(1)} %get-tuple-element.510), channel_id=1, source_target_pairs={{0,6},{2,4},{4,2},{6,0},{1,7},{3,5},{5,3},{7,1},{8,14},{10,12},{12... | collective-permute-start | bytes 786440 | tf_op jit(solution)/shard_map/ppermute | solution.py:824
  205.7 22.5 %collective-permute-start.6 = (bf16[2,128,512]{2,1,0:T(8,128)(2,1)S(1)}, bf16[2,128,512]{2,1,0:T(8,128)(2,1)}, u32[]{:S(2)}, u32[]{:S(2)}) collective-permute-start(bf16[2,128,512]{2,1,0:T(8,128)(2,1)S(1)} %get-tuple-element.511), channel_id=1, source_target_pairs={{0,4},{2,6},{4,0},{6,2},{1,5},{3,7},{5,1},{7,3},{8,12},{10,14},{12... | collective-permute-start | bytes 786440 | tf_op jit(solution)/shard_map/ppermute | solution.py:824
  205.7 22.5 %collective-permute-start.5 = (bf16[2,128,512]{2,1,0:T(8,128)(2,1)S(1)}, bf16[2,128,512]{2,1,0:T(8,128)(2,1)}, u32[]{:S(2)}, u32[]{:S(2)}) collective-permute-start(bf16[2,128,512]{2,1,0:T(8,128)(2,1)S(1)} %get-tuple-element.512), channel_id=1, source_target_pairs={{0,2},{2,0},{4,6},{6,4},{1,3},{3,1},{5,7},{7,5},{8,10},{10,8},{12,... | collective-permute-start | bytes 786440 | tf_op jit(solution)/shard_map/ppermute | solution.py:824
  206.3 21.9 %copy-start.3 = (bf16[8,256,512]{2,1,0:T(8,128)(2,1)S(1)}, bf16[8,256,512]{2,1,0:T(8,128)(2,1)}, u32[]{:S(2)}) copy-start(bf16[8,256,512]{2,1,0:T(8,128)(2,1)} %get-tuple-element.380) | copy-start | bytes 6291460
  221.6 20.5 %collective-permute-start.9 = (bf16[8,256,512]{2,1,0:T(8,128)(2,1)}, bf16[8,256,512]{2,1,0:T(8,128)(2,1)S(1)}, u32[]{:S(2)}, u32[]{:S(2)}) collective-permute-start(bf16[8,256,512]{2,1,0:T(8,128)(2,1)} %get-tuple-element.387), channel_id=1, source_target_pairs={{0,8},{8,0},{1,9},{9,1},{2,10},{10,2},{3,11},{11,3},{4,12},{12,4},... | collective-permute-start | bytes 6291464 | tf_op jit(solution)/shard_map/ppermute | solution.py:824
  221.7 46.5 %collective-permute-start.15 = (bf16[4,2,128,512]{3,2,1,0:T(8,128)(2,1)}, bf16[4,2,128,512]{3,2,1,0:T(8,128)(2,1)S(1)}, u32[]{:S(2)}, u32[]{:S(2)}) collective-permute-start(bf16[4,2,128,512]{3,2,1,0:T(8,128)(2,1)} %get-tuple-element.401), channel_id=1, source_target_pairs={{0,1},{1,0},{2,3},{3,2},{4,5},{5,4},{6,7},{7,6},{8,9},{9,8},{10,11... | collective-permute-start | bytes 3145736 | tf_op jit(solution)/shard_map/ppermute | solution.py:824
  230.2 38.0 %collective-permute-start.13 = (bf16[8,128,512]{2,1,0:T(8,128)(2,1)}, bf16[8,128,512]{2,1,0:T(8,128)(2,1)}, u32[]{:S(2)}, u32[]{:S(2)}) collective-permute-start(bf16[8,128,512]{2,1,0:T(8,128)(2,1)} %get-tuple-element.498), channel_id=1, source_target_pairs={{0,16},{16,0},{1,17},{17,1},{2,18},{18,2},{3,19},{19,3},{4,20},{20... | collective-permute-start | bytes 3145736 | tf_op jit(solution)/shard_map/ppermute | solution.py:824
  241.3 26.9 %collective-permute-start.14 = (bf16[8,256,512]{2,1,0:T(8,128)(2,1)}, bf16[8,256,512]{2,1,0:T(8,128)(2,1)S(1)}, u32[]{:S(2)}, u32[]{:S(2)}) collective-permute-start(bf16[8,256,512]{2,1,0:T(8,128)(2,1)} %get-tuple-element.399), channel_id=1, source_target_pairs={{0,8},{8,0},{1,9},{9,1},{2,10},{10,2},{3,11},{11,3},{4,12},{12,4},... | collective-permute-start | bytes 6291464 | tf_op jit(solution)/shard_map/ppermute | solution.py:824
  244.1 54.9 %collective-permute-start.12 = (bf16[8,128,512]{2,1,0:T(8,128)(2,1)}, bf16[8,128,512]{2,1,0:T(8,128)(2,1)S(1)}, u32[]{:S(2)}, u32[]{:S(2)}) collective-permute-start(bf16[8,128,512]{2,1,0:T(8,128)(2,1)} %get-tuple-element.500), channel_id=1, source_target_pairs={{0,1},{1,0},{2,3},{3,2},{4,5},{5,4},{6,7},{7,6},{8,9},{9,8},{10,11... | collective-permute-start | bytes 3145736 | tf_op jit(solution)/shard_map/ppermute | solution.py:824
  268.1 5.2 %collective-permute-start.10 = (bf16[1040,512]{1,0:T(8,128)(2,1)S(1)}, bf16[1040,512]{1,0:T(8,128)(2,1)S(1)}, u32[]{:S(2)}, u32[]{:S(2)}) collective-permute-start(bf16[1040,512]{1,0:T(8,128)(2,1)S(1)} %get-tuple-element.558), channel_id=1, source_target_pairs={{0,8},{8,0},{1,9},{9,1},{2,10},{10,2},{3,11},{11,3},{4,12},{12,4},... | collective-permute-start | bytes 3194888 | tf_op jit(solution)/shard_map/ppermute | solution.py:824
  269.2 25.4 %collective-permute-start.17 = (bf16[8,128,512]{2,1,0:T(8,128)(2,1)S(1)}, bf16[8,128,512]{2,1,0:T(8,128)(2,1)S(1)}, u32[]{:S(2)}, u32[]{:S(2)}) collective-permute-start(bf16[8,128,512]{2,1,0:T(8,128)(2,1)S(1)} %get-tuple-element.496), channel_id=1, source_target_pairs={{0,16},{16,0},{1,17},{17,1},{2,18},{18,2},{3,19},{19,3},{4,20},{20... | collective-permute-start | bytes 3145736 | tf_op jit(solution)/shard_map/ppermute | solution.py:824
  270.1 24.8 %collective-permute-start.16 = (bf16[2,2,128,512]{3,2,1,0:T(8,128)(2,1)S(1)}, bf16[2,2,128,512]{3,2,1,0:T(8,128)(2,1)S(1)}, u32[]{:S(2)}, u32[]{:S(2)}) collective-permute-start(bf16[2,2,128,512]{3,2,1,0:T(8,128)(2,1)S(1)} %add_convert_fusion.15), channel_id=1, source_target_pairs={{0,2},{2,0},{4,6},{6,4},{1,3},{3,1},{5,7},{7,5},{8,10},{10,8},{12,... | collective-permute-start | bytes 1572872 | tf_op jit(solution)/shard_map/ppermute | solution.py:824
  272.6 14.8 %collective-permute-start.18 = (bf16[8,64,512]{2,1,0:T(8,128)(2,1)S(1)}, bf16[8,64,512]{2,1,0:T(8,128)(2,1)S(1)}, u32[]{:S(2)}, u32[]{:S(2)}) collective-permute-start(bf16[8,64,512]{2,1,0:T(8,128)(2,1)S(1)} %get-tuple-element.508), channel_id=1, source_target_pairs={{0,1},{1,0},{2,3},{3,2},{4,5},{5,4},{6,7},{7,6},{8,9},{9,8},{10,11... | collective-permute-start | bytes 1572872 | tf_op jit(solution)/shard_map/ppermute | solution.py:824
  273.9 29.8 %collective-permute-start.20 = (bf16[528,512]{1,0:T(8,128)(2,1)S(1)}, bf16[528,512]{1,0:T(8,128)(2,1)S(1)}, u32[]{:S(2)}, u32[]{:S(2)}) collective-permute-start(bf16[528,512]{1,0:T(8,128)(2,1)S(1)} %get-tuple-element.556), channel_id=1, source_target_pairs={{0,1},{1,0},{2,3},{3,2},{4,5},{5,4},{6,7},{7,6},{8,9},{9,8},{10,11... | collective-permute-start | bytes 1622024 | tf_op jit(solution)/shard_map/ppermute | solution.py:824
  287.6 12.6 %collective-permute-start.23 = (bf16[8,16,512]{2,1,0:T(8,128)(2,1)S(1)}, bf16[8,16,512]{2,1,0:T(8,128)(2,1)S(1)}, u32[]{:S(2)}, u32[]{:S(2)}) collective-permute-start(bf16[8,16,512]{2,1,0:T(8,128)(2,1)S(1)} %get-tuple-element.536), channel_id=1, source_target_pairs={{0,6},{2,4},{4,2},{6,0},{1,7},{3,5},{5,3},{7,1},{8,14},{10,12},{12... | collective-permute-start | bytes 393224 | tf_op jit(solution)/shard_map/ppermute | solution.py:824
  294.5 8.6 %collective-permute-start.22 = (bf16[8,16,512]{2,1,0:T(8,128)(2,1)S(1)}, bf16[8,16,512]{2,1,0:T(8,128)(2,1)S(1)}, u32[]{:S(2)}, u32[]{:S(2)}) collective-permute-start(bf16[8,16,512]{2,1,0:T(8,128)(2,1)S(1)} %get-tuple-element.537), channel_id=1, source_target_pairs={{0,4},{2,6},{4,0},{6,2},{1,5},{3,7},{5,1},{7,3},{8,12},{10,14},{12... | collective-permute-start | bytes 393224 | tf_op jit(solution)/shard_map/ppermute | solution.py:824
  294.9 8.8 %collective-permute-start.21 = (bf16[8,16,512]{2,1,0:T(8,128)(2,1)S(1)}, bf16[8,16,512]{2,1,0:T(8,128)(2,1)S(1)}, u32[]{:S(2)}, u32[]{:S(2)}) collective-permute-start(bf16[8,16,512]{2,1,0:T(8,128)(2,1)S(1)} %get-tuple-element.538), channel_id=1, source_target_pairs={{0,2},{2,0},{4,6},{6,4},{1,3},{3,1},{5,7},{7,5},{8,10},{10,8},{12,... | collective-permute-start | bytes 393224 | tf_op jit(solution)/shard_map/ppermute | solution.py:824
  303.8 18.8 %copy-start.14 = (f32[256,512]{1,0:T(8,128)S(1)}, f32[256,512]{1,0:T(8,128)}, u32[]{:S(2)}) copy-start(f32[256,512]{1,0:T(8,128)} %get-tuple-element.425) | copy-start | bytes 1572868
  303.9 18.7 %collective-permute-start.25 = (bf16[2,128,512]{2,1,0:T(8,128)(2,1)}, bf16[2,128,512]{2,1,0:T(8,128)(2,1)}, u32[]{:S(2)}, u32[]{:S(2)}) collective-permute-start(bf16[2,128,512]{2,1,0:T(8,128)(2,1)} %get-tuple-element.532), channel_id=1, source_target_pairs={{0,4},{2,6},{4,0},{6,2},{1,5},{3,7},{5,1},{7,3},{8,12},{10,14},{12... | collective-permute-start | bytes 786440 | tf_op jit(solution)/shard_map/ppermute | solution.py:824
  304.0 22.0 %collective-permute-start.19 = (bf16[8,64,512]{2,1,0:T(8,128)(2,1)}, bf16[8,64,512]{2,1,0:T(8,128)(2,1)S(1)}, u32[]{:S(2)}, u32[]{:S(2)}) collective-permute-start(bf16[8,64,512]{2,1,0:T(8,128)(2,1)} %get-tuple-element.506), channel_id=1, source_target_pairs={{0,16},{16,0},{1,17},{17,1},{2,18},{18,2},{3,19},{19,3},{4,20},{20... | collective-permute-start | bytes 1572872 | tf_op jit(solution)/shard_map/ppermute | solution.py:824
  305.5 18.9 %collective-permute-start.24 = (bf16[272,512]{1,0:T(8,128)(2,1)}, bf16[272,512]{1,0:T(8,128)(2,1)}, u32[]{:S(2)}, u32[]{:S(2)}) collective-permute-start(bf16[272,512]{1,0:T(8,128)(2,1)} %get-tuple-element.554), channel_id=1, source_target_pairs={{0,16},{16,0},{1,17},{17,1},{2,18},{18,2},{3,19},{19,3},{4,20},{20... | collective-permute-start | bytes 835592 | tf_op jit(solution)/shard_map/ppermute | solution.py:824
  306.9 21.3 %collective-permute-start.33 = (bf16[8,16,512]{2,1,0:T(8,128)(2,1)S(1)}, bf16[8,16,512]{2,1,0:T(8,128)(2,1)S(1)}, u32[]{:S(2)}, u32[]{:S(2)}) collective-permute-start(bf16[8,16,512]{2,1,0:T(8,128)(2,1)S(1)} %add_convert_fusion.43), channel_id=1, source_target_pairs={{0,6},{2,4},{4,2},{6,0},{1,7},{3,5},{5,3},{7,1},{8,14},{10,12},{12... | collective-permute-start | bytes 393224 | tf_op jit(solution)/shard_map/ppermute | solution.py:824
  308.8 19.5 %collective-permute-start.32 = (bf16[8,16,512]{2,1,0:T(8,128)(2,1)S(1)}, bf16[8,16,512]{2,1,0:T(8,128)(2,1)S(1)}, u32[]{:S(2)}, u32[]{:S(2)}) collective-permute-start(bf16[8,16,512]{2,1,0:T(8,128)(2,1)S(1)} %add_convert_fusion.43), channel_id=1, source_target_pairs={{0,4},{2,6},{4,0},{6,2},{1,5},{3,7},{5,1},{7,3},{8,12},{10,14},{12... | collective-permute-start | bytes 393224 | tf_op jit(solution)/shard_map/ppermute | solution.py:824
  322.6 8.3 %collective-permute-start.31 = (bf16[8,16,512]{2,1,0:T(8,128)(2,1)S(1)}, bf16[8,16,512]{2,1,0:T(8,128)(2,1)S(1)}, u32[]{:S(2)}, u32[]{:S(2)}) collective-permute-start(bf16[8,16,512]{2,1,0:T(8,128)(2,1)S(1)} %add_convert_fusion.43), channel_id=1, source_target_pairs={{0,2},{2,0},{4,6},{6,4},{1,3},{3,1},{5,7},{7,5},{8,10},{10,8},{12,... | collective-permute-start | bytes 393224 | tf_op jit(solution)/shard_map/ppermute | solution.py:824
  324.4 16.4 %collective-permute-start.29 = (bf16[8,64,512]{2,1,0:T(8,128)(2,1)S(1)}, bf16[8,64,512]{2,1,0:T(8,128)(2,1)S(1)}, u32[]{:S(2)}, u32[]{:S(2)}) collective-permute-start(bf16[8,64,512]{2,1,0:T(8,128)(2,1)S(1)} %get-tuple-element.502), channel_id=1, source_target_pairs={{0,1},{1,0},{2,3},{3,2},{4,5},{5,4},{6,7},{7,6},{8,9},{9,8},{10,11... | collective-permute-start | bytes 1572872 | tf_op jit(solution)/shard_map/ppermute | solution.py:824
  326.0 14.2 %collective-permute-start.30 = (bf16[272,512]{1,0:T(8,128)(2,1)S(1)}, bf16[272,512]{1,0:T(8,128)(2,1)S(1)}, u32[]{:S(2)}, u32[]{:S(2)}) collective-permute-start(bf16[272,512]{1,0:T(8,128)(2,1)S(1)} %add_convert_fusion.19), channel_id=1, source_target_pairs={{0,2},{2,0},{4,6},{6,4},{1,3},{3,1},{5,7},{7,5},{8,10},{10,8},{12,... | collective-permute-start | bytes 835592 | tf_op jit(solution)/shard_map/ppermute | solution.py:824
  330.9 11.4 %collective-permute-start.28 = (bf16[8,16,512]{2,1,0:T(8,128)(2,1)S(1)}, bf16[8,16,512]{2,1,0:T(8,128)(2,1)S(1)}, u32[]{:S(2)}, u32[]{:S(2)}) collective-permute-start(bf16[8,16,512]{2,1,0:T(8,128)(2,1)S(1)} %get-tuple-element.528), channel_id=1, source_target_pairs={{0,6},{2,4},{4,2},{6,0},{1,7},{3,5},{5,3},{7,1},{8,14},{10,12},{12... | collective-permute-start | bytes 393224 | tf_op jit(solution)/shard_map/ppermute | solution.py:824
  333.5 11.6 %collective-permute-start.27 = (bf16[8,16,512]{2,1,0:T(8,128)(2,1)S(1)}, bf16[8,16,512]{2,1,0:T(8,128)(2,1)S(1)}, u32[]{:S(2)}, u32[]{:S(2)}) collective-permute-start(bf16[8,16,512]{2,1,0:T(8,128)(2,1)S(1)} %get-tuple-element.529), channel_id=1, source_target_pairs={{0,4},{2,6},{4,0},{6,2},{1,5},{3,7},{5,1},{7,3},{8,12},{10,14},{12... | collective-permute-start | bytes 393224 | tf_op jit(solution)/shard_map/ppermute | solution.py:824
  333.5 13.2 %collective-permute-start.26 = (bf16[8,16,512]{2,1,0:T(8,128)(2,1)S(1)}, bf16[8,16,512]{2,1,0:T(8,128)(2,1)S(1)}, u32[]{:S(2)}, u32[]{:S(2)}) collective-permute-start(bf16[8,16,512]{2,1,0:T(8,128)(2,1)S(1)} %get-tuple-element.530), channel_id=1, source_target_pairs={{0,2},{2,0},{4,6},{6,4},{1,3},{3,1},{5,7},{7,5},{8,10},{10,8},{12,... | collective-permute-start | bytes 393224 | tf_op jit(solution)/shard_map/ppermute | solution.py:824
  340.2 22.3 %collective-permute-start.42 = (bf16[8,64,512]{2,1,0:T(8,128)(2,1)S(1)}, bf16[8,64,512]{2,1,0:T(8,128)(2,1)S(1)}, u32[]{:S(2)}, u32[]{:S(2)}) collective-permute-start(bf16[8,64,512]{2,1,0:T(8,128)(2,1)S(1)} %maximum_select_fusion.11), channel_id=1, source_target_pairs={{0,1},{1,0},{2,3},{3,2},{4,5},{5,4},{6,7},{7,6},{8,9},{9,8},{10,11... | collective-permute-start | bytes 1572872 | tf_op jit(solution)/shard_map/ppermute | solution.py:824
  340.8 21.6 %collective-permute-start.37 = (bf16[272,512]{1,0:T(8,128)(2,1)S(1)}, bf16[272,512]{1,0:T(8,128)(2,1)S(1)}, u32[]{:S(2)}, u32[]{:S(2)}) collective-permute-start(bf16[272,512]{1,0:T(8,128)(2,1)S(1)} %add_convert_fusion.18), channel_id=1, source_target_pairs={{0,4},{2,6},{4,0},{6,2},{1,5},{3,7},{5,1},{7,3},{8,12},{10,14},{12... | collective-permute-start | bytes 835592 | tf_op jit(solution)/shard_map/ppermute | solution.py:824
  342.3 43.9 %collective-permute-start.11 = (bf16[4,2,128,512]{3,2,1,0:T(8,128)(2,1)S(1)}, bf16[4,2,128,512]{3,2,1,0:T(8,128)(2,1)S(1)}, u32[]{:S(2)}, u32[]{:S(2)}) collective-permute-start(bf16[4,2,128,512]{3,2,1,0:T(8,128)(2,1)S(1)} %copy-done.24), channel_id=1, source_target_pairs={{0,1},{1,0},{2,3},{3,2},{4,5},{5,4},{6,7},{7,6},{8,9},{9,8},{10,11... | collective-permute-start | bytes 3145736 | tf_op jit(solution)/shard_map/ppermute | solution.py:824
  345.2 18.7 %collective-permute-start.41 = (bf16[8,16,512]{2,1,0:T(8,128)(2,1)S(1)}, bf16[8,16,512]{2,1,0:T(8,128)(2,1)S(1)}, u32[]{:S(2)}, u32[]{:S(2)}) collective-permute-start(bf16[8,16,512]{2,1,0:T(8,128)(2,1)S(1)} %get-tuple-element.524), channel_id=1, source_target_pairs={{0,6},{2,4},{4,2},{6,0},{1,7},{3,5},{5,3},{7,1},{8,14},{10,12},{12... | collective-permute-start | bytes 393224 | tf_op jit(solution)/shard_map/ppermute | solution.py:824
  346.7 25.6 %collective-permute-start.40 = (bf16[8,16,512]{2,1,0:T(8,128)(2,1)S(1)}, bf16[8,16,512]{2,1,0:T(8,128)(2,1)S(1)}, u32[]{:S(2)}, u32[]{:S(2)}) collective-permute-start(bf16[8,16,512]{2,1,0:T(8,128)(2,1)S(1)} %get-tuple-element.525), channel_id=1, source_target_pairs={{0,4},{2,6},{4,0},{6,2},{1,5},{3,7},{5,1},{7,3},{8,12},{10,14},{12... | collective-permute-start | bytes 393224 | tf_op jit(solution)/shard_map/ppermute | solution.py:824
  362.4 9.9 %collective-permute-start.39 = (bf16[8,16,512]{2,1,0:T(8,128)(2,1)S(1)}, bf16[8,16,512]{2,1,0:T(8,128)(2,1)S(1)}, u32[]{:S(2)}, u32[]{:S(2)}) collective-permute-start(bf16[8,16,512]{2,1,0:T(8,128)(2,1)S(1)} %get-tuple-element.526), channel_id=1, source_target_pairs={{0,2},{2,0},{4,6},{6,4},{1,3},{3,1},{5,7},{7,5},{8,10},{10,8},{12,... | collective-permute-start | bytes 393224 | tf_op jit(solution)/shard_map/ppermute | solution.py:824
  362.5 12.0 %collective-permute-start.38 = (bf16[4,64,512]{2,1,0:T(8,128)(2,1)S(1)}, bf16[4,64,512]{2,1,0:T(8,128)(2,1)S(1)}, u32[]{:S(2)}, u32[]{:S(2)}) collective-permute-start(bf16[4,64,512]{2,1,0:T(8,128)(2,1)S(1)} %bitcast.76), channel_id=1, source_target_pairs={{0,16},{16,0},{1,17},{17,1},{2,18},{18,2},{3,19},{19,3},{4,20},{20... | collective-permute-start | bytes 786440 | tf_op jit(solution)/shard_map/ppermute | solution.py:824
  363.8 23.3 %copy-start.11 = (bf16[4,2,128,512]{3,2,1,0:T(8,128)(2,1)S(1)}, bf16[4,2,128,512]{3,2,1,0:T(8,128)(2,1)}, u32[]{:S(2)}) copy-start(bf16[4,2,128,512]{3,2,1,0:T(8,128)(2,1)} %get-tuple-element.456) | copy-start | bytes 3145732
  363.8 13.2 %collective-permute-start.36 = (bf16[8,16,512]{2,1,0:T(8,128)(2,1)S(1)}, bf16[8,16,512]{2,1,0:T(8,128)(2,1)S(1)}, u32[]{:S(2)}, u32[]{:S(2)}) collective-permute-start(bf16[8,16,512]{2,1,0:T(8,128)(2,1)S(1)} %add_convert_fusion.37), channel_id=1, source_target_pairs={{0,6},{2,4},{4,2},{6,0},{1,7},{3,5},{5,3},{7,1},{8,14},{10,12},{12... | collective-permute-start | bytes 393224 | tf_op jit(solution)/shard_map/ppermute | solution.py:824
  372.3 12.8 %collective-permute-start.35 = (bf16[8,16,512]{2,1,0:T(8,128)(2,1)S(1)}, bf16[8,16,512]{2,1,0:T(8,128)(2,1)S(1)}, u32[]{:S(2)}, u32[]{:S(2)}) collective-permute-start(bf16[8,16,512]{2,1,0:T(8,128)(2,1)S(1)} %add_convert_fusion.37), channel_id=1, source_target_pairs={{0,4},{2,6},{4,0},{6,2},{1,5},{3,7},{5,1},{7,3},{8,12},{10,14},{12... | collective-permute-start | bytes 393224 | tf_op jit(solution)/shard_map/ppermute | solution.py:824
  372.3 12.8 %collective-permute-start.34 = (bf16[8,16,512]{2,1,0:T(8,128)(2,1)S(1)}, bf16[8,16,512]{2,1,0:T(8,128)(2,1)S(1)}, u32[]{:S(2)}, u32[]{:S(2)}) collective-permute-start(bf16[8,16,512]{2,1,0:T(8,128)(2,1)S(1)} %add_convert_fusion.37), channel_id=1, source_target_pairs={{0,2},{2,0},{4,6},{6,4},{1,3},{3,1},{5,7},{7,5},{8,10},{10,8},{12,... | collective-permute-start | bytes 393224 | tf_op jit(solution)/shard_map/ppermute | solution.py:824
  374.5 12.9 %collective-permute-start.46 = (bf16[8,16,512]{2,1,0:T(8,128)(2,1)S(1)}, bf16[8,16,512]{2,1,0:T(8,128)(2,1)S(1)}, u32[]{:S(2)}, u32[]{:S(2)}) collective-permute-start(bf16[8,16,512]{2,1,0:T(8,128)(2,1)S(1)} %add_convert_fusion.33), channel_id=1, source_target_pairs={{0,6},{2,4},{4,2},{6,0},{1,7},{3,5},{5,3},{7,1},{8,14},{10,12},{12... | collective-permute-start | bytes 393224 | tf_op jit(solution)/shard_map/ppermute | solution.py:824
  377.1 12.8 %collective-permute-start.45 = (bf16[8,16,512]{2,1,0:T(8,128)(2,1)S(1)}, bf16[8,16,512]{2,1,0:T(8,128)(2,1)S(1)}, u32[]{:S(2)}, u32[]{:S(2)}) collective-permute-start(bf16[8,16,512]{2,1,0:T(8,128)(2,1)S(1)} %add_convert_fusion.33), channel_id=1, source_target_pairs={{0,4},{2,6},{4,0},{6,2},{1,5},{3,7},{5,1},{7,3},{8,12},{10,14},{12... | collective-permute-start | bytes 393224 | tf_op jit(solution)/shard_map/ppermute | solution.py:824
  385.1 6.1 %collective-permute-start.44 = (bf16[8,16,512]{2,1,0:T(8,128)(2,1)S(1)}, bf16[8,16,512]{2,1,0:T(8,128)(2,1)S(1)}, u32[]{:S(2)}, u32[]{:S(2)}) collective-permute-start(bf16[8,16,512]{2,1,0:T(8,128)(2,1)S(1)} %add_convert_fusion.33), channel_id=1, source_target_pairs={{0,2},{2,0},{4,6},{6,4},{1,3},{3,1},{5,7},{7,5},{8,10},{10,8},{12,... | collective-permute-start | bytes 393224 | tf_op jit(solution)/shard_map/ppermute | solution.py:824
  385.2 22.1 %collective-permute-start.49 = (bf16[8,128,512]{2,1,0:T(8,128)(2,1)S(1)}, bf16[8,128,512]{2,1,0:T(8,128)(2,1)S(1)}, u32[]{:S(2)}, u32[]{:S(2)}) collective-permute-start(bf16[8,128,512]{2,1,0:T(8,128)(2,1)S(1)} %maximum_select_fusion.5), channel_id=1, source_target_pairs={{0,16},{16,0},{1,17},{17,1},{2,18},{18,2},{3,19},{19,3},{4,20},{20... | collective-permute-start | bytes 3145736 | tf_op jit(solution)/shard_map/ppermute | solution.py:824
  386.1 11.8 %collective-permute-start.50 = (bf16[4,128,512]{2,1,0:T(8,128)(2,1)S(1)}, bf16[4,128,512]{2,1,0:T(8,128)(2,1)S(1)}, u32[]{:S(2)}, u32[]{:S(2)}) collective-permute-start(bf16[4,128,512]{2,1,0:T(8,128)(2,1)S(1)} %maximum_select_fusion.12), channel_id=1, source_target_pairs={{0,1},{1,0},{2,3},{3,2},{4,5},{5,4},{6,7},{7,6},{8,9},{9,8},{10,11... | collective-permute-start | bytes 1572872 | tf_op jit(solution)/shard_map/ppermute | solution.py:824
  408.1 22.5 %collective-permute-start.53 = (bf16[8,256,512]{2,1,0:T(8,128)(2,1)S(1)}, bf16[8,256,512]{2,1,0:T(8,128)(2,1)}, u32[]{:S(2)}, u32[]{:S(2)}) collective-permute-start(bf16[8,256,512]{2,1,0:T(8,128)(2,1)S(1)} %maximum_select_fusion.1.refs_0_.mine), channel_id=1, source_target_pairs={{0,8},{8,0},{1,9},{9,1},{2,10},{10,2},{3,11},{11,3},{4,12},{12,4},... | collective-permute-start | bytes 6291464 | tf_op jit(solution)/shard_map/ppermute | solution.py:824
  408.2 14.3 %collective-permute-start.48 = (bf16[8,64,512]{2,1,0:T(8,128)(2,1)S(1)}, bf16[8,64,512]{2,1,0:T(8,128)(2,1)S(1)}, u32[]{:S(2)}, u32[]{:S(2)}) collective-permute-start(bf16[8,64,512]{2,1,0:T(8,128)(2,1)S(1)} %maximum_select_fusion.13), channel_id=1, source_target_pairs={{0,16},{16,0},{1,17},{17,1},{2,18},{18,2},{3,19},{19,3},{4,20},{20... | collective-permute-start | bytes 1572872 | tf_op jit(solution)/shard_map/ppermute | solution.py:824
  410.0 19.6 %collective-permute-start.54 = (bf16[4,256,512]{2,1,0:T(8,128)(2,1)S(1)}, bf16[4,256,512]{2,1,0:T(8,128)(2,1)S(1)}, u32[]{:S(2)}, u32[]{:S(2)}) collective-permute-start(bf16[4,256,512]{2,1,0:T(8,128)(2,1)S(1)} %maximum_select_fusion.6.mine), channel_id=1, source_target_pairs={{0,8},{8,0},{1,9},{9,1},{2,10},{10,2},{3,11},{11,3},{4,12},{12,4},... | collective-permute-start | bytes 3145736 | tf_op jit(solution)/shard_map/ppermute | solution.py:824
  410.2 14.2 %collective-permute-start.47 = (bf16[8,64,512]{2,1,0:T(8,128)(2,1)S(1)}, bf16[8,64,512]{2,1,0:T(8,128)(2,1)S(1)}, u32[]{:S(2)}, u32[]{:S(2)}) collective-permute-start(bf16[8,64,512]{2,1,0:T(8,128)(2,1)S(1)} %maximum_select_fusion.14), channel_id=1, source_target_pairs={{0,1},{1,0},{2,3},{3,2},{4,5},{5,4},{6,7},{7,6},{8,9},{9,8},{10,11... | collective-permute-start | bytes 1572872 | tf_op jit(solution)/shard_map/ppermute | solution.py:824
  410.3 15.1 %collective-permute-start.43 = (bf16[2,2,128,512]{3,2,1,0:T(8,128)(2,1)S(1)}, bf16[2,2,128,512]{3,2,1,0:T(8,128)(2,1)S(1)}, u32[]{:S(2)}, u32[]{:S(2)}) collective-permute-start(bf16[2,2,128,512]{3,2,1,0:T(8,128)(2,1)S(1)} %add_convert_fusion.6), channel_id=1, source_target_pairs={{0,2},{2,0},{4,6},{6,4},{1,3},{3,1},{5,7},{7,5},{8,10},{10,8},{12,... | collective-permute-start | bytes 1572872 | tf_op jit(solution)/shard_map/ppermute | solution.py:824
  423.0 24.8 %collective-permute-start.52 = (bf16[8,128,512]{2,1,0:T(8,128)(2,1)S(1)}, bf16[8,128,512]{2,1,0:T(8,128)(2,1)S(1)}, u32[]{:S(2)}, u32[]{:S(2)}) collective-permute-start(bf16[8,128,512]{2,1,0:T(8,128)(2,1)S(1)} %maximum_select_fusion.7), channel_id=1, source_target_pairs={{0,1},{1,0},{2,3},{3,2},{4,5},{5,4},{6,7},{7,6},{8,9},{9,8},{10,11... | collective-permute-start | bytes 3145736 | tf_op jit(solution)/shard_map/ppermute | solution.py:824
  424.8 24.7 %collective-permute-start.55 = (bf16[8,128,512]{2,1,0:T(8,128)(2,1)S(1)}, bf16[8,128,512]{2,1,0:T(8,128)(2,1)S(1)}, u32[]{:S(2)}, u32[]{:S(2)}) collective-permute-start(bf16[8,128,512]{2,1,0:T(8,128)(2,1)S(1)} %maximum_select_fusion.8), channel_id=1, source_target_pairs={{0,16},{16,0},{1,17},{17,1},{2,18},{18,2},{3,19},{19,3},{4,20},{20... | collective-permute-start | bytes 3145736 | tf_op jit(solution)/shard_map/ppermute | solution.py:824
  426.2 22.3 %collective-permute-start.51 = (bf16[2,128,512]{2,1,0:T(8,128)(2,1)}, bf16[2,128,512]{2,1,0:T(8,128)(2,1)}, u32[]{:S(2)}, u32[]{:S(2)}) collective-permute-start(bf16[2,128,512]{2,1,0:T(8,128)(2,1)} %get-tuple-element.514), channel_id=1, source_target_pairs={{0,4},{2,6},{4,0},{6,2},{1,5},{3,7},{5,1},{7,3},{8,12},{10,14},{12... | collective-permute-start | bytes 786440 | tf_op jit(solution)/shard_map/ppermute | solution.py:824
  448.5 5.6 %collective-permute-start.57 = (bf16[8,256,512]{2,1,0:T(8,128)(2,1)S(1)}, bf16[8,256,512]{2,1,0:T(8,128)(2,1)}, u32[]{:S(2)}, u32[]{:S(2)}) collective-permute-start(bf16[8,256,512]{2,1,0:T(8,128)(2,1)S(1)} %maximum_select_fusion.2.mine.refs_0_), channel_id=1, source_target_pairs={{0,8},{8,0},{1,9},{9,1},{2,10},{10,2},{3,11},{11,3},{4,12},{12,4},... | collective-permute-start | bytes 6291464 | tf_op jit(solution)/shard_map/ppermute | solution.py:824
  450.1 8.5 %collective-permute-start.56 = (bf16[8,256,512]{2,1,0:T(8,128)(2,1)S(1)}, bf16[8,256,512]{2,1,0:T(8,128)(2,1)}, u32[]{:S(2)}, u32[]{:S(2)}) collective-permute-start(bf16[8,256,512]{2,1,0:T(8,128)(2,1)S(1)} %maximum_select_fusion.3.mine.refs_0_), channel_id=1, source_target_pairs={{0,8},{8,0},{1,9},{9,1},{2,10},{10,2},{3,11},{11,3},{4,12},{12,4},... | collective-permute-start | bytes 6291464 | tf_op jit(solution)/shard_map/ppermute | solution.py:824
  (23 other events, 217.8 us)
Sparse Core Ops, SparseCore 0:
  10.1 62.3 all-gather.5
  92.9 50.1 all-gather.3
